TPU v7x, 32 devices: a whole 2x2x4 slice. The times are simulated.
32 devices in a mesh: dp: 4 (over y, x), ctx: 8 (over z, core).
Axes of the slice: x: 2, y: 2, z: 4, core: 2. Of those that a mesh axis runs over, the one named last changes fastest.
Arguments:
- segment_ids: int32 [4, 1024], P('dp'), may hold values from 0 to 7, never falling along the last dimension, each value on 1 to 512 neighbouring positions
- queries: bfloat16 [4, 1024, 2048], P('dp', 'ctx'), may hold values from -600 to 600
- keys: bfloat16 [4, 1024, 1024], P('dp', 'ctx'), may hold values from -600 to 600
- values: bfloat16 [4, 1024, 1024], P('dp', 'ctx'), may hold values from -6 to 6
- query_gain: float32 [256], replicated, may hold values from 0.1 to 1.9
- key_gain: float32 [256], replicated, may hold values from 0.1 to 1.9
- out_grad: bfloat16 [4, 1024, 2048], P('dp', 'ctx'), may hold values from -9 to 9
Outputs:
- attended: bfloat16 [4, 1024, 2048], P('dp', 'ctx')
- query_grad: bfloat16 [4, 1024, 2048], P('dp', 'ctx')
- key_grad: bfloat16 [4, 1024, 1024], P('dp', 'ctx')
- value_grad: bfloat16 [4, 1024, 1024], P('dp', 'ctx')
- query_gain_grad: float32 [256], replicated
- key_gain_grad: float32 [256], replicated
Inputs may be any that keep to these rules, and one draw needn't show every extreme that they name: `segment_ids`: in each packed sequence the document numbers never fall along the positions; every document holds 1 to 512 positions and one holds exactly 512.
All inputs are finite; a program needn't handle non-finite values.
Results may differ from a plain program's by a relative error of at most 0.0081.
Values may be sent and summed in bfloat16 or wider, within the bound.
No kernel may reach another device: no remote copies, remote signals or barrier semaphores. Data moves between devices by JAX's collectives and lax.ppermute only.
A program may use at most 64 MiB of HBM per device.

v0:
```python
import jax
import jax.numpy as jnp
from jax import lax
from jax.sharding import PartitionSpec as P

HEADS = 8
KV_HEADS = 4
HEAD_DIM = 256
GREACH = 4


epsilon = 1e-06


def from_behind(array, axis, by):
    size = lax.axis_size(axis)
    pairs = [(i, i + by) for i in range(size) if 0 <= i + by < size]
    return lax.ppermute(array, axis, pairs)


def normalize(field, gain_vec):
    as_float = field.astype(jnp.float32)
    inverse = lax.rsqrt(jnp.mean(as_float * as_float, -1, keepdims=True) + epsilon)
    normed = as_float * inverse
    return (normed, inverse, normed * gain_vec)


def norm_backward(upstream, normed, inverse, gain_vec):
    scaled = upstream * gain_vec
    grad_in = inverse * (scaled - normed * jnp.mean(scaled * normed, -1, keepdims=True))
    return (grad_in, jnp.sum(upstream * normed, axis=(0, 1)))


def front_row(field):
    return jnp.concatenate(
        [jnp.zeros((field.shape[0], 1, field.shape[2]), field.dtype), field], axis=1
    )


def shards(segment_ids, queries, keys, values, query_gain, key_gain, out_grad):
    tok_rows = queries.shape[1]
    groups = HEADS // KV_HEADS
    kv_width = KV_HEADS * HEAD_DIM
    reach_rows = GREACH * tok_rows
    position = lax.axis_index("ctx")
    q_normed, q_inverse, q_gained = normalize(
        queries[0].reshape(tok_rows, HEADS, HEAD_DIM), query_gain
    )
    q_scaled = (q_gained * HEAD_DIM ** (-0.5)).astype(jnp.bfloat16)
    k_normed, k_inverse, k_gained = normalize(
        keys[0].reshape(tok_rows, KV_HEADS, HEAD_DIM), key_gain
    )
    own_block = jnp.stack([k_gained.astype(jnp.bfloat16).reshape(tok_rows, kv_width), values[0]])
    earlier = []
    moving = own_block
    for distance in range(1, GREACH + 1):
        outgoing = moving if distance < GREACH else moving[:, 1:]
        moving = from_behind(outgoing, "ctx", 1)
        if distance == GREACH:
            moving = front_row(moving)
        earlier.append(moving)
    key_band = jnp.concatenate(earlier[::-1] + [own_block], axis=1)
    band_keys = key_band[0].reshape(-1, KV_HEADS, HEAD_DIM)
    band_values = key_band[1].reshape(-1, KV_HEADS, HEAD_DIM)
    seg_row = segment_ids[0]
    seg_padded = jnp.concatenate([jnp.full((reach_rows,), -1, jnp.int32), seg_row])
    first_row = position * tok_rows
    key_seg = lax.dynamic_slice_in_dim(seg_padded, first_row, reach_rows + tok_rows)
    query_seg = lax.dynamic_slice_in_dim(seg_row, first_row, tok_rows)
    column_ids = jnp.arange(reach_rows + tok_rows)[None, :]
    row_ids = jnp.arange(tok_rows)[:, None]
    in_window = (column_ids <= row_ids + reach_rows) & (column_ids > row_ids)
    live_mask = (query_seg[:, None] == key_seg[None, :]) & in_window
    q_heads = q_scaled.reshape(tok_rows, KV_HEADS, groups, HEAD_DIM).transpose(1, 2, 0, 3)
    grad_heads = out_grad[0].reshape(tok_rows, KV_HEADS, groups, HEAD_DIM).transpose(1, 2, 0, 3)
    scores = jnp.einsum("kgid,jkd->kgij", q_heads, band_keys, preferred_element_type=jnp.float32)
    weights = jnp.where(live_mask, jnp.exp(scores), 0.0)
    probs = weights / jnp.sum(weights, -1, keepdims=True)
    probs_low = probs.astype(jnp.bfloat16)
    attended = jnp.einsum(
        "kgij,jkd->ikgd", probs_low, band_values, preferred_element_type=jnp.float32
    )
    attended = attended.astype(jnp.bfloat16).reshape(1, tok_rows, HEADS * HEAD_DIM)
    dprob = jnp.einsum(
        "kgid,jkd->kgij", grad_heads, band_values, preferred_element_type=jnp.float32
    )
    centre = jnp.sum(probs * dprob, -1, keepdims=True)
    dscore = (probs * (dprob - centre)).astype(jnp.bfloat16)
    dq_scaled = jnp.einsum("kgij,jkd->ikgd", dscore, band_keys, preferred_element_type=jnp.float32)
    dq_scaled = dq_scaled.reshape(tok_rows, HEADS, HEAD_DIM)
    key_parts = jnp.einsum("kgij,kgid->kjd", dscore, q_heads, preferred_element_type=jnp.float32)
    value_parts = jnp.einsum(
        "kgij,kgid->kjd", probs_low, grad_heads, preferred_element_type=jnp.float32
    )
    grad_parts = jnp.stack(
        [
            key_parts.astype(jnp.bfloat16).transpose(1, 0, 2).reshape(-1, kv_width),
            value_parts.astype(jnp.bfloat16).transpose(1, 0, 2).reshape(-1, kv_width),
        ]
    )

    def portion(distance):
        return grad_parts[:, (GREACH - distance) * tok_rows : (GREACH - distance + 1) * tok_rows]

    summed = lax.optimization_barrier(portion(0)).astype(jnp.float32)
    for distance in range(1, GREACH + 1):
        outgoing = portion(distance) if distance < GREACH else portion(distance)[:, 1:]
        arrived = from_behind(outgoing, "ctx", -distance)
        if distance == GREACH:
            arrived = front_row(arrived)
        summed = summed + arrived.astype(jnp.float32)
    dk_rounded = summed[0].reshape(tok_rows, KV_HEADS, HEAD_DIM)
    value_grad = summed[1].astype(jnp.bfloat16).reshape(1, tok_rows, kv_width)
    query_grad, query_gain_part = norm_backward(
        dq_scaled * HEAD_DIM ** (-0.5), q_normed, q_inverse, query_gain
    )
    key_grad, key_gain_part = norm_backward(dk_rounded, k_normed, k_inverse, key_gain)
    query_gain_sum, key_gain_sum = lax.psum((query_gain_part, key_gain_part), ("dp", "ctx"))
    factor = (lax.axis_size("dp") * queries.shape[0] * lax.axis_size("ctx") * tok_rows) ** (-0.5)
    return (
        attended,
        query_grad.astype(jnp.bfloat16).reshape(1, tok_rows, HEADS * HEAD_DIM),
        key_grad.astype(jnp.bfloat16).reshape(1, tok_rows, kv_width),
        value_grad,
        query_gain_sum * factor,
        key_gain_sum * factor,
    )


def solution(mesh):
    placed = (
        P("dp", None),
        P("dp", "ctx", None),
        P("dp", "ctx", None),
        P("dp", "ctx", None),
        P(),
        P(),
        P("dp", "ctx", None),
    )
    return jax.shard_map(
        shards,
        mesh=mesh,
        in_specs=placed,
        out_specs=(
            P("dp", "ctx", None),
            P("dp", "ctx", None),
            P("dp", "ctx", None),
            P("dp", "ctx", None),
            P(),
            P(),
        ),
        check_vma=False,
    )
```

profile of v0, /device:TPU:0, one launch (start us, length us, event | category | flops | bytes accessed | tf_op | source)
XLA Modules:
  0.0 173.4 jit_solution(13086853470905780915)
XLA Ops:
  0.6 1.2 copy.87
  1.8 1.1 copy.86
  4.8 2.4 %collective-permute-start = (bf16[2,128,1024]{1,2,0:T(8,128)(2,1)S(1)}, bf16[2,128,1024]{1,2,0:T(8,128)(2,1)S(1)}, u32[]{:S(2)}, u32[]{:S(2)}) collective-permute-start(bf16[2,128,1024]{1,2,0:T(8,128)(2,1)S(1)} %pad_maximum_fusion.1), channel_id=1, source_target_pairs={{0,1},{1,2},{2,3},{3,4},{4,5},{5,6},{6,7},{8,9},{9,10},{10,11},{11... | collective-permute-start | bytes 1572872 | tf_op jit(solution)/shard_map/ppermute | solution.py:18
  7.2 1.5 collective-permute-done
  8.7 9.2 %collective-permute-start.1 = (bf16[2,128,1024]{1,2,0:T(8,128)(2,1)S(1)}, bf16[2,128,1024]{1,2,0:T(8,128)(2,1)S(1)}, u32[]{:S(2)}, u32[]{:S(2)}) collective-permute-start(bf16[2,128,1024]{1,2,0:T(8,128)(2,1)S(1)} %collective-permute-done), channel_id=1, source_target_pairs={{0,1},{1,2},{2,3},{3,4},{4,5},{5,6},{6,7},{8,9},{9,10},{10,11},{11... | collective-permute-start | bytes 1572872 | tf_op jit(solution)/shard_map/ppermute | solution.py:18
  19.4 9.0 %collective-permute-start.2 = (bf16[2,128,1024]{1,2,0:T(8,128)(2,1)S(1)}, bf16[2,128,1024]{1,2,0:T(8,128)(2,1)S(1)}, u32[]{:S(2)}, u32[]{:S(2)}) collective-permute-start(bf16[2,128,1024]{1,2,0:T(8,128)(2,1)S(1)} %collective-permute-done.1), channel_id=1, source_target_pairs={{0,1},{1,2},{2,3},{3,4},{4,5},{5,6},{6,7},{8,9},{9,10},{10,11},{11... | collective-permute-start | bytes 1572872 | tf_op jit(solution)/shard_map/ppermute | solution.py:18
  28.4 1.2 copy.88
  29.9 1.1 mul.214
  31.1 1.0 copy.115
  32.3 6.7 %collective-permute-start.3 = (bf16[2,127,1024]{1,2,0:T(8,128)(2,1)S(1)}, bf16[2,127,1024]{1,2,0:T(8,128)(2,1)S(1)}, u32[]{:S(2)}, u32[]{:S(2)}) collective-permute-start(bf16[2,127,1024]{1,2,0:T(8,128)(2,1)S(1)} %slice.43), channel_id=1, source_target_pairs={{0,1},{1,2},{2,3},{3,4},{4,5},{5,6},{6,7},{8,9},{9,10},{10,11},{11... | collective-permute-start | bytes 1560584 | tf_op jit(solution)/shard_map/ppermute | solution.py:18
  39.4 1.2 collective-permute-done.3
  41.4 0.9 broadcast.135
  42.2 4.4 %concatenate.9 = bf16[2,640,1024]{1,2,0:T(8,128)(2,1)S(1)} concatenate(bf16[2,1,1024]{1,2,0:T(8,128)(2,1)} %broadcast.135, bf16[2,127,1024]{1,2,0:T(8,128)(2,1)} %copy-done.11, bf16[2,128,1024]{1,2,0:T(8,128)(2,1)} %copy-done.6, bf16[2,128,1024]{1,2,0:T(8,128)(2,1)} %copy-done.10, bf16[2,128,1024]{1,2,0:T(8,128)(2,1)} %copy-done.9, bf16[2,128,1024]{1,2,0:T(8,128)(2,1)} %copy-done.5), dimensions={1} | concatenate | bytes 5242880 | tf_op jit(solution)/shard_map/concatenate | solution.py:62
  46.9 1.0 copy-done
  47.9 0.9 fusion.4
  48.8 0.9 convolution_convert_fusion
  49.8 1.1 fusion
  51.6 1.7 fusion.6
  54.7 1.2 fusion.14
  55.9 1.0 pad_maximum_fusion
  56.9 1.0 copy.99
  58.3 1.2 mul.228
  59.4 2.6 %copy.97 = f32[1,128,2048]{2,1,0:T(8,128)} copy(f32[1,128,2048]{1,2,0:T(8,128)} %bitcast.120) | data formatting | bytes 2097152 | tf_op jit(solution)/shard_map/reshape | solution.py:90
  62.1 1.3 collective-permute-start.6
  63.3 1.3 collective-permute-start.5
  64.6 1.3 collective-permute-start.4
  65.9 1.3 collective-permute-start.7
  67.3 2.3 %multiply_convert_fusion = bf16[1,128,2048]{2,1,0:T(8,128)(2,1)} fusion(f32[1,128,2048]{2,1,0:T(8,128)S(1)} %copy-done.2, f32[1,128,2048]{2,1,0:T(8,128)S(1)} %copy-done.3, f32[1,128,2048]{2,1,0:T(8,128)} %copy.97, bf16[1,128,2048]{2,1,0:T(8,128)(2,1)S(1)} %copy-done.1, f32[2048]{0:T(1024)S(1)} %bitcast.129), kind=kLoop, calls=%fused_computation.26 | loop fusion | flops 1835008 | bytes 4202496 | tf_op jit(solution)/shard_map/convert_element_type | solution.py:122
  69.6 62.6 %collective-permute-done.7 = bf16[2,127,1024]{1,2,0:T(8,128)(2,1)S(1)} collective-permute-done((bf16[2,127,1024]{1,2,0:T(8,128)(2,1)}, bf16[2,127,1024]{1,2,0:T(8,128)(2,1)S(1)}, u32[]{:S(2)}, u32[]{:S(2)}) %collective-permute-start.7) | collective-permute-done | bytes 520224 | tf_op jit(solution)/shard_map/ppermute | solution.py:18
  133.2 0.9 copy.100
  134.1 0.8 copy.101
  135.0 37.9 %all-reduce.2 = (f32[256]{0:T(256)S(1)}, f32[256]{0:T(256)S(1)}) all-reduce(f32[256]{0:T(256)S(1)} %get-tuple-element.42, f32[256]{0:T(256)S(1)} %reduce_sum.88), channel_id=1, replica_groups=mesh['dp'=4,'ctx'=8] {'dp','ctx'}, use_global_device_ids=true, to_apply=%region_7.8 | all-reduce | flops 512 | bytes 4096 | tf_op jit(solution)/shard_map/psum | solution.py:118
  (71 shorter events, 9.3 us)
Async XLA Ops:
  0.6 17.2 %copy-start.1 = (bf16[1,128,2048]{2,1,0:T(8,128)(2,1)S(1)}, bf16[1,128,2048]{2,1,0:T(8,128)(2,1)}, u32[]{:S(2)}) copy-start(bf16[1,128,2048]{2,1,0:T(8,128)(2,1)} %param.8) | copy-start | bytes 1572868
  4.8 13.2 %copy-start.5 = (bf16[2,128,1024]{1,2,0:T(8,128)(2,1)}, bf16[2,128,1024]{1,2,0:T(8,128)(2,1)S(1)}, u32[]{:S(2)}) copy-start(bf16[2,128,1024]{1,2,0:T(8,128)(2,1)S(1)} %pad_maximum_fusion.1) | copy-start | bytes 1572868
  4.8 3.9 %collective-permute-start = (bf16[2,128,1024]{1,2,0:T(8,128)(2,1)S(1)}, bf16[2,128,1024]{1,2,0:T(8,128)(2,1)S(1)}, u32[]{:S(2)}, u32[]{:S(2)}) collective-permute-start(bf16[2,128,1024]{1,2,0:T(8,128)(2,1)S(1)} %pad_maximum_fusion.1), channel_id=1, source_target_pairs={{0,1},{1,2},{2,3},{3,4},{4,5},{5,6},{6,7},{8,9},{9,10},{10,11},{11... | collective-permute-start | bytes 1572872 | tf_op jit(solution)/shard_map/ppermute | solution.py:18
  8.7 21.0 %copy-start.9 = (bf16[2,128,1024]{1,2,0:T(8,128)(2,1)}, bf16[2,128,1024]{1,2,0:T(8,128)(2,1)S(1)}, u32[]{:S(2)}) copy-start(bf16[2,128,1024]{1,2,0:T(8,128)(2,1)S(1)} %collective-permute-done) | copy-start | bytes 1572868
  8.7 10.7 %collective-permute-start.1 = (bf16[2,128,1024]{1,2,0:T(8,128)(2,1)S(1)}, bf16[2,128,1024]{1,2,0:T(8,128)(2,1)S(1)}, u32[]{:S(2)}, u32[]{:S(2)}) collective-permute-start(bf16[2,128,1024]{1,2,0:T(8,128)(2,1)S(1)} %collective-permute-done), channel_id=1, source_target_pairs={{0,1},{1,2},{2,3},{3,4},{4,5},{5,6},{6,7},{8,9},{9,10},{10,11},{11... | collective-permute-start | bytes 1572872 | tf_op jit(solution)/shard_map/ppermute | solution.py:18
  18.6 12.5 %copy-start.7 = (bf16[1,128,2048]{2,1,0:T(8,128)(2,1)S(1)}, bf16[1,128,2048]{2,1,0:T(8,128)(2,1)}, u32[]{:S(2)}) copy-start(bf16[1,128,2048]{2,1,0:T(8,128)(2,1)} %param.13) | copy-start | bytes 1572868
  19.4 12.7 %copy-start.10 = (bf16[2,128,1024]{1,2,0:T(8,128)(2,1)}, bf16[2,128,1024]{1,2,0:T(8,128)(2,1)S(1)}, u32[]{:S(2)}) copy-start(bf16[2,128,1024]{1,2,0:T(8,128)(2,1)S(1)} %collective-permute-done.1) | copy-start | bytes 1572868
  19.4 12.7 %collective-permute-start.2 = (bf16[2,128,1024]{1,2,0:T(8,128)(2,1)S(1)}, bf16[2,128,1024]{1,2,0:T(8,128)(2,1)S(1)}, u32[]{:S(2)}, u32[]{:S(2)}) collective-permute-start(bf16[2,128,1024]{1,2,0:T(8,128)(2,1)S(1)} %collective-permute-done.1), channel_id=1, source_target_pairs={{0,1},{1,2},{2,3},{3,4},{4,5},{5,6},{6,7},{8,9},{9,10},{10,11},{11... | collective-permute-start | bytes 1572872 | tf_op jit(solution)/shard_map/ppermute | solution.py:18
  28.4 3.7 %copy-start.12 = (f32[256]{0:T(256)S(1)}, f32[256]{0:T(256)}, u32[]{:S(2)}) copy-start(f32[256]{0:T(256)} %param.11) | copy-start | bytes 3076
  29.7 9.4 %copy-start.14 = (s32[1,1024]{1,0:T(1,128)S(1)}, s32[1,1024]{1,0:T(1,128)}, u32[]{:S(2)}) copy-start(s32[1,1024]{1,0:T(1,128)} %param.7) | copy-start | bytes 12292
  32.1 8.5 %copy-start.6 = (bf16[2,128,1024]{1,2,0:T(8,128)(2,1)}, bf16[2,128,1024]{1,2,0:T(8,128)(2,1)S(1)}, u32[]{:S(2)}) copy-start(bf16[2,128,1024]{1,2,0:T(8,128)(2,1)S(1)} %collective-permute-done.2) | copy-start | bytes 1572868
  32.3 8.2 %collective-permute-start.3 = (bf16[2,127,1024]{1,2,0:T(8,128)(2,1)S(1)}, bf16[2,127,1024]{1,2,0:T(8,128)(2,1)S(1)}, u32[]{:S(2)}, u32[]{:S(2)}) collective-permute-start(bf16[2,127,1024]{1,2,0:T(8,128)(2,1)S(1)} %slice.43), channel_id=1, source_target_pairs={{0,1},{1,2},{2,3},{3,4},{4,5},{5,6},{6,7},{8,9},{9,10},{10,11},{11... | collective-permute-start | bytes 1560584 | tf_op jit(solution)/shard_map/ppermute | solution.py:18
  40.6 0.8 copy-start.11
  46.7 1.2 copy-start
  48.8 1.0 copy-start.8
  58.1 9.2 %copy-start.2 = (f32[1,128,2048]{2,1,0:T(8,128)S(1)}, f32[1,128,2048]{2,1,0:T(8,128)}, u32[]{:S(2)}) copy-start(f32[1,128,2048]{2,1,0:T(8,128)} %mul.214) | copy-start | bytes 3145732
  59.4 7.8 %copy-start.3 = (f32[1,128,2048]{2,1,0:T(8,128)S(1)}, f32[1,128,2048]{2,1,0:T(8,128)}, u32[]{:S(2)}) copy-start(f32[1,128,2048]{2,1,0:T(8,128)} %mul.228) | copy-start | bytes 3145732
  62.1 70.1 %collective-permute-start.6 = (bf16[2,128,1024]{1,2,0:T(8,128)(2,1)}, bf16[2,128,1024]{1,2,0:T(8,128)(2,1)S(1)}, u32[]{:S(2)}, u32[]{:S(2)}) collective-permute-start(bf16[2,128,1024]{1,2,0:T(8,128)(2,1)} %get-tuple-element.51), channel_id=1, source_target_pairs={{3,0},{4,1},{5,2},{6,3},{7,4},{11,8},{12,9},{13,10},{14,11},{15,12... | collective-permute-start | bytes 1572872 | tf_op jit(solution)/shard_map/ppermute | solution.py:18
  63.3 68.8 %collective-permute-start.5 = (bf16[2,128,1024]{1,2,0:T(8,128)(2,1)}, bf16[2,128,1024]{1,2,0:T(8,128)(2,1)S(1)}, u32[]{:S(2)}, u32[]{:S(2)}) collective-permute-start(bf16[2,128,1024]{1,2,0:T(8,128)(2,1)} %get-tuple-element.50), channel_id=1, source_target_pairs={{2,0},{3,1},{4,2},{5,3},{6,4},{7,5},{10,8},{11,9},{12,10},{13,11},... | collective-permute-start | bytes 1572872 | tf_op jit(solution)/shard_map/ppermute | solution.py:18
  64.6 67.5 %collective-permute-start.4 = (bf16[2,128,1024]{1,2,0:T(8,128)(2,1)}, bf16[2,128,1024]{1,2,0:T(8,128)(2,1)S(1)}, u32[]{:S(2)}, u32[]{:S(2)}) collective-permute-start(bf16[2,128,1024]{1,2,0:T(8,128)(2,1)} %get-tuple-element.49), channel_id=1, source_target_pairs={{1,0},{2,1},{3,2},{4,3},{5,4},{6,5},{7,6},{9,8},{10,9},{11,10},{12... | collective-permute-start | bytes 1572872 | tf_op jit(solution)/shard_map/ppermute | solution.py:18
  65.9 66.2 %collective-permute-start.7 = (bf16[2,127,1024]{1,2,0:T(8,128)(2,1)}, bf16[2,127,1024]{1,2,0:T(8,128)(2,1)S(1)}, u32[]{:S(2)}, u32[]{:S(2)}) collective-permute-start(bf16[2,127,1024]{1,2,0:T(8,128)(2,1)} %pad_maximum_fusion), channel_id=1, source_target_pairs={{4,0},{5,1},{6,2},{7,3},{12,8},{13,9},{14,10},{15,11},{20,16},{21,... | collective-permute-start | bytes 1560584 | tf_op jit(solution)/shard_map/ppermute | solution.py:18
  69.6 63.1 %copy-start.4 = (f32[128,4,256]{0,2,1:T(8,128)S(1)}, f32[128,4,256]{0,2,1:T(8,128)}, u32[]{:S(2)}) copy-start(f32[128,4,256]{0,2,1:T(8,128)} %get-tuple-element.47) | copy-start | bytes 1572868
  69.6 63.1 %copy-start.13 = (f32[256]{0:T(256)S(1)}, f32[256]{0:T(256)}, u32[]{:S(2)}) copy-start(f32[256]{0:T(256)} %param.12) | copy-start | bytes 3076
where the time goes:
time: 175 us; the launch traced here: 173 us
  waiting for transfers between devices  66 us (38%)
  blocking collectives  37.9 us (22%)
  starting transfers between devices  32.5 us (19%)
  local copies, waits for them, and re-layouts  21.7 us (12%)
  other arithmetic  8.35 us (5%)
  matrix products  5.93 us (3%)
    ppermute x8, waiting for transfers between devices, from_behind(): return lax.ppermute(array, axis, pairs)  66 us
    psum x1, blocking collectives, shards(): lax.psum((query_gain_part, key_gain_part), ('dp', 'ctx'))  37.9 us
    ppermute x8, starting transfers between devices, from_behind(): return lax.ppermute(array, axis, pairs)  32.5 us
    unnamed x40, local copies, waits for them, and re-layouts  8.05 us
    concatenate x1, local copies, waits for them, and re-layouts, shards(): key_band = jnp.concatenate(earlier[::-1] + [own_block], axis=1)  4.45 us
  transfers between devices with their start and end apart: 8, of which 4 were waited for; matrix products, arithmetic and copies ran while one was open for 4% of the time, Pallas kernels for 0%

commit v1 on v0

v1 whole, which is shorter than its diff:
```python
import functools

import jax
import jax.numpy as jnp
from jax import lax
from jax.experimental import pallas as pl
from jax.experimental.pallas import tpu as pltpu
from jax.sharding import PartitionSpec as P

HEADS = 8
KV_HEADS = 4
HEAD_DIM = 256
WINDOW = 512
GROUPS = HEADS // KV_HEADS
MY_KV = KV_HEADS // 2
EPSILON = 1e-06
BF16 = jnp.bfloat16
F32 = jnp.float32


def call(body, out_shape, flops, moved, name):
    return pl.pallas_call(
        body,
        out_shape=out_shape,
        compiler_params=pltpu.CompilerParams(vmem_limit_bytes=48 * 2**20),
        cost_estimate=pl.CostEstimate(flops=flops, bytes_accessed=moved, transcendentals=0),
        name=name,
    )


def shape(rows, cols, dtype=BF16):
    return jax.ShapeDtypeStruct((rows, cols), dtype)


def core_index():
    return lax.axis_index("ctx") % 2


def cols(first, width):
    return pl.ds(pl.multiple_of(first * HEAD_DIM, HEAD_DIM), width * HEAD_DIM)


def first_payload(keys, values, straight, cross):
    core = core_index()
    for out, side in ((straight, core), (cross, 1 - core)):
        out[:, :HEAD_DIM] = keys[0, :, cols(side * MY_KV, 1)]
        out[:, HEAD_DIM:] = values[0, :, cols(side * MY_KV, 1)]


def swap_payload(keys, values, queries, out_grad, out):
    other = 1 - core_index()
    kv = MY_KV * HEAD_DIM
    out[:, :kv] = keys[0, :, cols(other * MY_KV, MY_KV)]
    out[:, kv : 2 * kv] = values[0, :, cols(other * MY_KV, MY_KV)]
    wide = MY_KV * GROUPS
    out[:, 2 * kv : 4 * kv] = queries[0, :, cols(other * wide, wide)]
    out[:, 4 * kv :] = out_grad[0, :, cols(other * wide, wide)]


def second_payload(keys, values, swapped, out):
    core = core_index()
    rows = keys.shape[1]
    kv = MY_KV * HEAD_DIM
    out[:rows, :HEAD_DIM] = keys[0, :, cols(core * MY_KV + 1, 1)]
    out[:rows, HEAD_DIM:] = values[0, :, cols(core * MY_KV + 1, 1)]
    out[rows:, :HEAD_DIM] = swapped[:, HEAD_DIM : 2 * HEAD_DIM]
    out[rows:, HEAD_DIM:] = swapped[:, kv + HEAD_DIM : kv + 2 * HEAD_DIM]


def normalize(field):
    inverse = lax.rsqrt(jnp.mean(field * field, -1, keepdims=True) + EPSILON)
    return field * inverse, inverse


def dot(left, right, over):
    return lax.dot_general(left, right, ((over[:1], over[1:]), ((), ())), preferred_element_type=F32)


def attend(
    chunk, segments, queries, out_grad, keys, values, swapped, near_a, near_b, far, query_gain, key_gain,
    own_attended, own_query_grad, own_part, swap_out, near_part, far_part, gains,
):
    core = core_index()
    chip = lax.axis_index("ctx") // 2
    rows = queries.shape[1]
    pair = 2 * rows
    kv = MY_KV * HEAD_DIM
    wide = GROUPS * HEAD_DIM
    gain_q = query_gain[...]
    gain_k = key_gain[...]

    def segment(tile, half):
        block = 2 * (chip + tile - 2) + jnp.where(half == 0, core, 1 - core)
        first = pl.multiple_of(jnp.maximum(block, 0) * rows, rows)
        return jnp.where(block >= 0, segments[:, pl.ds(first, rows)], -1)

    key_seg = jnp.concatenate([segment(tile, half) for tile in range(3) for half in range(2)], 1)
    query_seg = jnp.concatenate(
        [jnp.broadcast_to(segment(2, half), (rows, rows)).T[:, :1] for half in range(2)], 0
    )

    def place(index):
        half = (index // rows) % 2
        return index % rows + rows * jnp.where(half == 0, core, 1 - core) + (index // pair) * pair

    query_place = place(lax.broadcasted_iota(jnp.int32, (pair, 1), 0)) + 2 * pair
    key_place = place(lax.broadcasted_iota(jnp.int32, (1, 3 * pair), 1))
    behind = query_place - key_place
    live = (query_seg == key_seg) & (behind >= 0) & (behind < WINDOW)
    live = jnp.concatenate([live] * GROUPS, 0)

    own_head = core * MY_KV + chunk
    at_k = slice(chunk * HEAD_DIM, (chunk + 1) * HEAD_DIM)
    at_v = slice(kv + chunk * HEAD_DIM, kv + (chunk + 1) * HEAD_DIM)
    band_k = jnp.concatenate(
        [far[:, :HEAD_DIM], near_a[:, :HEAD_DIM], near_b[:, :HEAD_DIM], keys[0, :, cols(own_head, 1)], swapped[:, at_k]], 0
    )
    band_v = jnp.concatenate(
        [far[:, HEAD_DIM:], near_a[:, HEAD_DIM:], near_b[:, HEAD_DIM:], values[0, :, cols(own_head, 1)], swapped[:, at_v]], 0
    )
    k_normed, _ = normalize(band_k.astype(F32))
    k_rounded = (k_normed * gain_k).astype(BF16)

    def heads(field, base):
        first = own_head * GROUPS
        return jnp.concatenate(
            [
                part
                for g in range(GROUPS)
                for part in (
                    field[0, :, cols(first + g, 1)],
                    swapped[:, base + chunk * wide + g * HEAD_DIM : base + chunk * wide + (g + 1) * HEAD_DIM],
                )
            ],
            0,
        )

    q_normed, q_inverse = normalize(heads(queries, 2 * kv).astype(F32))
    q_scaled = (q_normed * gain_q * HEAD_DIM ** (-0.5)).astype(BF16)
    grads = heads(out_grad, 4 * kv)

    scores = dot(q_scaled, k_rounded, (1, 1))
    weights = jnp.where(live, jnp.exp(scores), 0.0)
    probs = weights * (1.0 / jnp.sum(weights, -1, keepdims=True))
    probs_low = probs.astype(BF16)
    attended = dot(probs_low, band_v, (1, 0)).astype(BF16)
    dprob = dot(grads, band_v, (1, 1))
    centre = jnp.sum(probs * dprob, -1, keepdims=True)
    dscore = (probs * (dprob - centre)).astype(BF16)
    key_parts = dot(dscore, q_scaled, (0, 0))
    value_parts = dot(probs_low, grads, (0, 0))
    far_part[:, :HEAD_DIM] = key_parts[:pair].astype(BF16)
    far_part[:, HEAD_DIM:] = value_parts[:pair].astype(BF16)
    near_part[:, :HEAD_DIM] = key_parts[pair : 2 * pair]
    near_part[:, HEAD_DIM:] = value_parts[pair : 2 * pair]
    own_part[:, :HEAD_DIM] = key_parts[2 * pair : 2 * pair + rows]
    own_part[:, HEAD_DIM:] = value_parts[2 * pair : 2 * pair + rows]
    swap_out[:, 2 * wide : 2 * wide + HEAD_DIM] = key_parts[2 * pair + rows :].astype(BF16)
    swap_out[:, 2 * wide + HEAD_DIM :] = value_parts[2 * pair + rows :].astype(BF16)

    dq = dot(dscore, k_rounded, (1, 0)) * HEAD_DIM ** (-0.5)
    scaled = dq * gain_q
    query_grad = q_inverse * (scaled - q_normed * jnp.mean(scaled * q_normed, -1, keepdims=True))
    query_grad = query_grad.astype(BF16)
    for g in range(GROUPS):
        here = slice(g * HEAD_DIM, (g + 1) * HEAD_DIM)
        top = g * pair
        own_attended[:, here] = attended[top : top + rows]
        own_query_grad[:, here] = query_grad[top : top + rows]
        swap_out[:, here] = attended[top + rows : top + pair]
        swap_out[:, wide + g * HEAD_DIM : wide + (g + 1) * HEAD_DIM] = query_grad[top + rows : top + pair]
    gains[0:1, :] = jnp.sum(dq * q_normed, 0, keepdims=True)
    gains[1:2, :] = jnp.sum(key_parts * k_normed, 0, keepdims=True)


def assemble(att_0, att_1, grad_0, grad_1, swap_0, swap_1, attended, query_grad):
    core = core_index()
    wide = GROUPS * HEAD_DIM
    for chunk, (att, grad, swap) in enumerate(((att_0, grad_0, swap_0), (att_1, grad_1, swap_1))):
        mine = cols((core * MY_KV + chunk) * GROUPS, GROUPS)
        other = cols(((1 - core) * MY_KV + chunk) * GROUPS, GROUPS)
        attended[0, :, mine] = att[...]
        query_grad[0, :, mine] = grad[...]
        attended[0, :, other] = swap[:, :wide]
        query_grad[0, :, other] = swap[:, wide : 2 * wide]


def finish(
    keys, key_gain, part_0, part_1, swap_0, swap_1, straight_0, straight_1, cross_0, cross_1, key_grad, value_grad
):
    core = core_index()
    gain_k = key_gain[...]
    base = 2 * GROUPS * HEAD_DIM
    for chunk, (part, swap, straight, cross) in enumerate(
        ((part_0, swap_0, straight_0, cross_0), (part_1, swap_1, straight_1, cross_1))
    ):
        for side, local, arrived in (
            (core, part[...], straight),
            (1 - core, swap[:, base:].astype(F32), cross),
        ):
            here = cols(side * MY_KV + chunk, 1)
            total = local + arrived[...].astype(F32)
            normed, inverse = normalize(keys[0, :, here].astype(F32))
            scaled = total[:, :HEAD_DIM] * gain_k
            grad = inverse * (scaled - normed * jnp.mean(scaled * normed, -1, keepdims=True))
            key_grad[0, :, here] = grad.astype(BF16)
            value_grad[0, :, here] = total[:, HEAD_DIM:].astype(BF16)


def shards(segment_ids, queries, keys, values, query_gain, key_gain, out_grad):
    rows = queries.shape[1]
    pair = 2 * rows
    size = lax.axis_size("ctx")
    kv = MY_KV * HEAD_DIM
    wide = GROUPS * HEAD_DIM
    gain_q = query_gain.reshape(1, HEAD_DIM)
    gain_k = key_gain.reshape(1, HEAD_DIM)

    def move(field, by, cross=False):
        pairs = [(i, (i ^ 1 if cross else i) + by) for i in range(size) if 0 <= (i ^ 1 if cross else i) + by < size]
        return lax.ppermute(field, "ctx", pairs)

    straight, cross = call(
        first_payload, (shape(rows, 2 * HEAD_DIM),) * 2, 0, 2**19, "first_payload"
    )(keys, values)
    near_a0 = move(straight, 2)
    near_b0 = move(cross, 2, cross=True)
    swapped = call(swap_payload, shape(rows, 6 * kv), 0, 3 * 2**19, "swap_payload")(keys, values, queries, out_grad)
    swapped = move(swapped, 0, cross=True)
    near_1 = call(second_payload, shape(pair, 2 * HEAD_DIM), 0, 2**19, "second_payload")(keys, values, swapped)
    near_1 = move(near_1, 2)
    far_0 = move(jnp.concatenate([near_a0, near_b0], 0), 2)
    far_1 = move(near_1, 2)

    def chunk_call(chunk, near_a, near_b, far):
        return call(
            functools.partial(attend, chunk),
            (
                shape(rows, wide),
                shape(rows, wide),
                shape(rows, 2 * HEAD_DIM, F32),
                shape(rows, 2 * wide + 2 * HEAD_DIM),
                shape(pair, 2 * HEAD_DIM, F32),
                shape(pair, 2 * HEAD_DIM),
                shape(2, HEAD_DIM, F32),
            ),
            6 * 2 * GROUPS * pair * 3 * pair * HEAD_DIM,
            4 * 2**20,
            "attend",
        )(segment_ids, queries, out_grad, keys, values, swapped, near_a, near_b, far, gain_q, gain_k)

    def descend(near_part, far_part):
        arrived = move(far_part, -2)
        total = (near_part + arrived.astype(F32)).astype(BF16)
        return move(total[:rows], -2), move(total[rows:], -2, cross=True)

    att_0, grad_0, part_0, swap_0, near_part_0, far_part_0, gains_0 = chunk_call(0, near_a0, near_b0, far_0)
    straight_0, cross_0 = descend(near_part_0, far_part_0)
    swap_0 = move(swap_0, 0, cross=True)
    att_1, grad_1, part_1, swap_1, near_part_1, far_part_1, gains_1 = chunk_call(1, near_1[:rows], near_1[rows:], far_1)
    straight_1, cross_1 = descend(near_part_1, far_part_1)
    swap_1 = move(swap_1, 0, cross=True)

    gains = lax.all_gather(gains_0 + gains_1, ("dp", "ctx"))
    attended, query_grad = call(
        assemble, (jax.ShapeDtypeStruct(queries.shape, BF16),) * 2, 0, 2 * 2**20, "assemble"
    )(att_0, att_1, grad_0, grad_1, swap_0, swap_1)
    key_grad, value_grad = call(
        finish, (jax.ShapeDtypeStruct(keys.shape, BF16),) * 2, 0, 2 * 2**20, "finish"
    )(keys, gain_k, part_0, part_1, swap_0, swap_1, straight_0, straight_1, cross_0, cross_1)

    factor = (lax.axis_size("dp") * queries.shape[0] * size * rows) ** (-0.5)
    gains = jnp.sum(gains, 0) * factor
    return attended, query_grad, key_grad, value_grad, gains[0], gains[1]


def solution(mesh):
    block = P("dp", "ctx", None)
    return jax.shard_map(
        shards,
        mesh=mesh,
        in_specs=(P("dp", None), block, block, block, P(), P(), block),
        out_specs=(block, block, block, block, P(), P()),
        check_vma=False,
    )
```

time: 175 us -> 106 us (0.61)
  waiting for transfers between devices: 66 us -> 16 us
  local copies, waits for them, and re-layouts: 21.7 us -> 5.98 us
  blocking collectives: 37.9 us -> 45.5 us
  Pallas kernels: 0 us -> 7.45 us
  other arithmetic: 8.35 us -> 1.18 us
  matrix products: 5.93 us -> 0 us
  starting transfers between devices: 32.5 us -> 28.7 us
    ppermute x8 -> x14, waiting for transfers between devices: 66 us -> 16 us  [move(): return lax.ppermute(field, 'ctx', pairs)]
    all_gather x0 -> x1, blocking collectives: none -> 45.5 us  [shards(): gains = lax.all_gather(gains_0 + gains_1, ('dp', 'ctx'))]
    psum x1 -> x0, blocking collectives: 37.9 us -> none  [shards(): lax.psum((query_gain_part, key_gain_part), ('dp', 'ctx'))]
    pallas_call x0 -> x7, Pallas kernels: none -> 7.45 us  [the longest x2 5.25 us: chunk_call(): call(functools.partial(attend, chunk), (shape(rows, wide), shape(rows, wi...]
    dot_general x6 -> x0, matrix products: 5.93 us -> none  [the longest x1 1.68 us: shards(): jnp.einsum('kgij,jkd->ikgd', dscore, band_keys, preferred_element_type=jn...]
    concatenate x1 -> x0, local copies, waits for them, and re-layouts: 4.45 us -> none  [shards(): key_band = jnp.concatenate(earlier[::-1] + [own_block], axis=1)]
    ppermute x8 -> x14, starting transfers between devices: 32.5 us -> 28.7 us  [move(): return lax.ppermute(field, 'ctx', pairs)]
    unnamed x40 -> x20, local copies, waits for them, and re-layouts: 8.05 us -> 4.66 us
  transfers between devices with their start and end apart: 8 -> 14, of which waited for: 4 -> 7; matrix products, arithmetic and copies ran while one was open for 4% -> 2% of each run, Pallas kernels for 0% -> 6%
where the time goes in v1:
time: 106 us
  blocking collectives  45.5 us (43%)
  starting transfers between devices  28.7 us (27%)
  waiting for transfers between devices  16 us (15%)
  Pallas kernels  7.45 us (7%)
  local copies, waits for them, and re-layouts  5.98 us (6%)
  other arithmetic  1.18 us (1%)
    all_gather x1, blocking collectives, shards(): gains = lax.all_gather(gains_0 + gains_1, ('dp', 'ctx'))  45.5 us
    ppermute x14, starting transfers between devices, move(): return lax.ppermute(field, 'ctx', pairs)  28.7 us
    ppermute x14, waiting for transfers between devices, move(): return lax.ppermute(field, 'ctx', pairs)  16 us
    pallas_call x2, Pallas kernels, chunk_call(): call(functools.partial(attend, chunk), (shape(rows, wide), shape(rows, wi...  5.25 us
    unnamed x20, local copies, waits for them, and re-layouts  4.66 us
  transfers between devices with their start and end apart: 14, of which 7 were waited for; matrix products, arithmetic and copies ran while one was open for 2% of the time, Pallas kernels for 6%

profile of v1, /device:TPU:0, one launch (start us, length us, event | category | flops | bytes accessed | tf_op | source)
XLA Modules:
  0.0 105.7 jit_solution(3761137209948326054)
XLA Ops:
  0.6 0.9 copy-done
  1.6 0.9 copy-done.2
  2.5 1.0 copy-done.3
  3.6 1.0 copy-done.5
  4.7 0.5 collective-permute-start
  5.2 4.5 %collective-permute-start.1 = (bf16[128,512]{1,0:T(8,128)(2,1)S(1)}, bf16[128,512]{1,0:T(8,128)(2,1)S(1)}, u32[]{:S(2)}, u32[]{:S(2)}) collective-permute-start(bf16[128,512]{1,0:T(8,128)(2,1)S(1)} %get-tuple-element.26), channel_id=1, source_target_pairs={{0,2},{1,3},{2,4},{3,5},{4,6},{5,7},{8,10},{9,11},{10,12},{11,13},... | collective-permute-start | bytes 393224 | tf_op jit(solution)/shard_map/ppermute | solution.py:221
  9.8 3.3 %collective-permute-start.2 = (bf16[128,512]{1,0:T(8,128)(2,1)S(1)}, bf16[128,512]{1,0:T(8,128)(2,1)S(1)}, u32[]{:S(2)}, u32[]{:S(2)}) collective-permute-start(bf16[128,512]{1,0:T(8,128)(2,1)S(1)} %get-tuple-element.27), channel_id=1, source_target_pairs={{0,3},{1,2},{2,5},{3,4},{4,7},{5,6},{8,11},{9,10},{10,13},{11,12},... | collective-permute-start | bytes 393224 | tf_op jit(solution)/shard_map/ppermute | solution.py:221
  13.1 3.4 %collective-permute-done.2.near_b = bf16[128,512]{1,0:T(8,128)(2,1)S(1)} collective-permute-done((bf16[128,512]{1,0:T(8,128)(2,1)S(1)}, bf16[128,512]{1,0:T(8,128)(2,1)S(1)}, u32[]{:S(2)}, u32[]{:S(2)}) %collective-permute-start.2) | collective-permute-done | bytes 131104 | tf_op jit(solution)/shard_map/ppermute | solution.py:221
  16.6 4.2 %collective-permute-start.3 = (bf16[256,512]{1,0:T(8,128)(2,1)S(1)}, bf16[256,512]{1,0:T(8,128)(2,1)S(1)}, u32[]{:S(2)}, u32[]{:S(2)}) collective-permute-start(bf16[256,512]{1,0:T(8,128)(2,1)S(1)} %pad_maximum_fusion), channel_id=1, source_target_pairs={{0,2},{1,3},{2,4},{3,5},{4,6},{5,7},{8,10},{9,11},{10,12},{11,13},... | collective-permute-start | bytes 786440 | tf_op jit(solution)/shard_map/ppermute | solution.py:221
  20.9 3.5 %collective-permute-start.4 = (bf16[256,512]{1,0:T(8,128)(2,1)S(1)}, bf16[256,512]{1,0:T(8,128)(2,1)S(1)}, u32[]{:S(2)}, u32[]{:S(2)}) collective-permute-start(bf16[256,512]{1,0:T(8,128)(2,1)S(1)} %second_payload.1), channel_id=1, source_target_pairs={{0,2},{1,3},{2,4},{3,5},{4,6},{5,7},{8,10},{9,11},{10,12},{11,13},... | collective-permute-start | bytes 786440 | tf_op jit(solution)/shard_map/ppermute | solution.py:221
  24.4 3.1 %collective-permute-done.3.far = bf16[256,512]{1,0:T(8,128)(2,1)S(1)} collective-permute-done((bf16[256,512]{1,0:T(8,128)(2,1)S(1)}, bf16[256,512]{1,0:T(8,128)(2,1)S(1)}, u32[]{:S(2)}, u32[]{:S(2)}) %collective-permute-start.3) | collective-permute-done | bytes 262176 | tf_op jit(solution)/shard_map/ppermute | solution.py:221
  27.5 0.7 copy-done.7
  28.2 2.4 %attend.2 = (bf16[128,512]{1,0:T(8,128)(2,1)S(1)}, bf16[128,512]{1,0:T(8,128)(2,1)S(1)}, f32[128,512]{1,0:T(8,128)S(1)}, bf16[128,1536]{1,0:T(8,128)(2,1)S(1)}, ...) custom-call(s32[1,1024]{1,0:T(1,128)S(1)} %copy-done.8, ...), custom_call_target="tpu_custom_call" | custom-call | flops 1207959552 | bytes 4194304 | tf_op jit(solution)/shard_map/attend/pallas_call | solution.py:236
  30.6 1.3 %collective-permute-start.8 = (bf16[256,512]{1,0:T(8,128)(2,1)S(1)}, bf16[256,512]{1,0:T(8,128)(2,1)S(1)}, u32[]{:S(2)}, u32[]{:S(2)}) collective-permute-start(bf16[256,512]{1,0:T(8,128)(2,1)S(1)} %get-tuple-element.39), channel_id=1, source_target_pairs={{2,0},{3,1},{4,2},{5,3},{6,4},{7,5},{10,8},{11,9},{12,10},{13,11},... | collective-permute-start | bytes 786440 | tf_op jit(solution)/shard_map/ppermute | solution.py:221
  32.0 0.3 collective-permute-done.4
  32.3 4.7 %collective-permute-start.5 = (bf16[256,512]{1,0:T(8,128)(2,1)S(1)}, bf16[256,512]{1,0:T(8,128)(2,1)S(1)}, u32[]{:S(2)}, u32[]{:S(2)}) collective-permute-start(bf16[256,512]{1,0:T(8,128)(2,1)S(1)} %collective-permute-done.4), channel_id=1, source_target_pairs={{0,2},{1,3},{2,4},{3,5},{4,6},{5,7},{8,10},{9,11},{10,12},{11,13},... | collective-permute-start | bytes 786440 | tf_op jit(solution)/shard_map/ppermute | solution.py:221
  37.0 2.9 %collective-permute-done.8 = bf16[256,512]{1,0:T(8,128)(2,1)S(1)} collective-permute-done((bf16[256,512]{1,0:T(8,128)(2,1)S(1)}, bf16[256,512]{1,0:T(8,128)(2,1)S(1)}, u32[]{:S(2)}, u32[]{:S(2)}) %collective-permute-start.8) | collective-permute-done | bytes 262176 | tf_op jit(solution)/shard_map/ppermute | solution.py:221
  39.9 0.1 add_convert_fusion.1
  40.0 0.7 fusion.1
  40.7 1.3 %collective-permute-start.12 = (bf16[128,512]{1,0:T(8,128)(2,1)}, bf16[128,512]{1,0:T(8,128)(2,1)S(1)}, u32[]{:S(2)}, u32[]{:S(2)}) collective-permute-start(bf16[128,512]{1,0:T(8,128)(2,1)} %get-tuple-element.48), channel_id=1, source_target_pairs={{2,1},{3,0},{4,3},{5,2},{6,5},{7,4},{10,9},{11,8},{12,11},{13,10},... | collective-permute-start | bytes 393224 | tf_op jit(solution)/shard_map/ppermute | solution.py:221
  42.0 1.3 %collective-permute-start.9 = (bf16[128,512]{1,0:T(8,128)(2,1)}, bf16[128,512]{1,0:T(8,128)(2,1)S(1)}, u32[]{:S(2)}, u32[]{:S(2)}) collective-permute-start(bf16[128,512]{1,0:T(8,128)(2,1)} %get-tuple-element.49), channel_id=1, source_target_pairs={{2,0},{3,1},{4,2},{5,3},{6,4},{7,5},{10,8},{11,9},{12,10},{13,11},... | collective-permute-start | bytes 393224 | tf_op jit(solution)/shard_map/ppermute | solution.py:221
  43.3 2.8 %attend.3 = (bf16[128,512]{1,0:T(8,128)(2,1)S(1)}, bf16[128,512]{1,0:T(8,128)(2,1)S(1)}, f32[128,512]{1,0:T(8,128)S(1)}, bf16[128,1536]{1,0:T(8,128)(2,1)S(1)}, ...) custom-call(s32[1,1024]{1,0:T(1,128)S(1)} %copy-done.8, ...), custom_call_target="tpu_custom_call" | custom-call | flops 1207959552 | bytes 4194304 | tf_op jit(solution)/shard_map/attend/pallas_call | solution.py:236
  46.2 1.3 %collective-permute-start.10 = (bf16[256,512]{1,0:T(8,128)(2,1)}, bf16[256,512]{1,0:T(8,128)(2,1)}, u32[]{:S(2)}, u32[]{:S(2)}) collective-permute-start(bf16[256,512]{1,0:T(8,128)(2,1)} %get-tuple-element.41), channel_id=1, source_target_pairs={{2,0},{3,1},{4,2},{5,3},{6,4},{7,5},{10,8},{11,9},{12,10},{13,11},... | collective-permute-start | bytes 786440 | tf_op jit(solution)/shard_map/ppermute | solution.py:221
  47.5 45.5 %all-gather.1 = f32[32,2,256]{2,1,0:T(2,128)S(1)} all-gather(f32[1,2,256]{2,1,0:T(2,128)S(1)} %add_bitcast_fusion), channel_id=2, replica_groups=mesh['dp'=4,'ctx'=8] {'dp','ctx'}, dimensions={0}, use_global_device_ids=true | all-gather | bytes 67584 | tf_op jit(solution)/shard_map/all_gather | solution.py:264
  93.1 1.0 add_convert_fusion
  94.2 1.3 %collective-permute-start.13 = (bf16[128,512]{1,0:T(8,128)(2,1)S(1)}, bf16[128,512]{1,0:T(8,128)(2,1)S(1)}, u32[]{:S(2)}, u32[]{:S(2)}) collective-permute-start(bf16[128,512]{1,0:T(8,128)(2,1)S(1)} %get-tuple-element.46), channel_id=1, source_target_pairs={{2,1},{3,0},{4,3},{5,2},{6,5},{7,4},{10,9},{11,8},{12,11},{13,10},... | collective-permute-start | bytes 393224 | tf_op jit(solution)/shard_map/ppermute | solution.py:221
  95.5 1.3 %collective-permute-start.11 = (bf16[128,512]{1,0:T(8,128)(2,1)S(1)}, bf16[128,512]{1,0:T(8,128)(2,1)S(1)}, u32[]{:S(2)}, u32[]{:S(2)}) collective-permute-start(bf16[128,512]{1,0:T(8,128)(2,1)S(1)} %get-tuple-element.47), channel_id=1, source_target_pairs={{2,0},{3,1},{4,2},{5,3},{6,4},{7,5},{10,8},{11,9},{12,10},{13,11},... | collective-permute-start | bytes 393224 | tf_op jit(solution)/shard_map/ppermute | solution.py:221
  96.8 0.6 fusion.3
  97.4 1.0 assemble.1
  98.4 3.0 %collective-permute-done.13.cross_1 = bf16[128,512]{1,0:T(8,128)(2,1)S(1)} collective-permute-done((bf16[128,512]{1,0:T(8,128)(2,1)S(1)}, bf16[128,512]{1,0:T(8,128)(2,1)S(1)}, u32[]{:S(2)}, u32[]{:S(2)}) %collective-permute-start.13) | collective-permute-done | bytes 131104 | tf_op jit(solution)/shard_map/ppermute | solution.py:221
  101.4 3.3 %collective-permute-done.11.straight_1 = bf16[128,512]{1,0:T(8,128)(2,1)S(1)} collective-permute-done((bf16[128,512]{1,0:T(8,128)(2,1)S(1)}, bf16[128,512]{1,0:T(8,128)(2,1)S(1)}, u32[]{:S(2)}, u32[]{:S(2)}) %collective-permute-start.11) | collective-permute-done | bytes 131104 | tf_op jit(solution)/shard_map/ppermute | solution.py:221
  104.7 1.0 finish.1
  (34 shorter events, 0.5 us)
Async XLA Ops:
  0.6 1.0 copy-start
  1.6 0.9 copy-start.2
  2.5 1.0 copy-start.3
  3.6 1.0 copy-start.5
  4.7 16.2 %collective-permute-start = (bf16[128,3072]{1,0:T(8,128)(2,1)S(1)}, bf16[128,3072]{1,0:T(8,128)(2,1)S(1)}, u32[]{:S(2)}, u32[]{:S(2)}) collective-permute-start(bf16[128,3072]{1,0:T(8,128)(2,1)S(1)} %swap_payload.1), channel_id=1, source_target_pairs={{0,1},{1,0},{2,3},{3,2},{4,5},{5,4},{6,7},{7,6},{8,9},{9,8},{10,11... | collective-permute-start | bytes 2359304 | tf_op jit(solution)/shard_map/ppermute | solution.py:221
  5.2 7.9 %collective-permute-start.1 = (bf16[128,512]{1,0:T(8,128)(2,1)S(1)}, bf16[128,512]{1,0:T(8,128)(2,1)S(1)}, u32[]{:S(2)}, u32[]{:S(2)}) collective-permute-start(bf16[128,512]{1,0:T(8,128)(2,1)S(1)} %get-tuple-element.26), channel_id=1, source_target_pairs={{0,2},{1,3},{2,4},{3,5},{4,6},{5,7},{8,10},{9,11},{10,12},{11,13},... | collective-permute-start | bytes 393224 | tf_op jit(solution)/shard_map/ppermute | solution.py:221
  9.8 6.8 %collective-permute-start.2 = (bf16[128,512]{1,0:T(8,128)(2,1)S(1)}, bf16[128,512]{1,0:T(8,128)(2,1)S(1)}, u32[]{:S(2)}, u32[]{:S(2)}) collective-permute-start(bf16[128,512]{1,0:T(8,128)(2,1)S(1)} %get-tuple-element.27), channel_id=1, source_target_pairs={{0,3},{1,2},{2,5},{3,4},{4,7},{5,6},{8,11},{9,10},{10,13},{11,12},... | collective-permute-start | bytes 393224 | tf_op jit(solution)/shard_map/ppermute | solution.py:221
  16.6 10.9 %copy-start.4 = (bf16[1,128,2048]{2,1,0:T(8,128)(2,1)S(1)}, bf16[1,128,2048]{2,1,0:T(8,128)(2,1)}, u32[]{:S(2)}) copy-start(bf16[1,128,2048]{2,1,0:T(8,128)(2,1)} %queries.5) | copy-start | bytes 1572868
  16.6 10.9 %copy-start.6 = (bf16[1,128,2048]{2,1,0:T(8,128)(2,1)S(1)}, bf16[1,128,2048]{2,1,0:T(8,128)(2,1)}, u32[]{:S(2)}) copy-start(bf16[1,128,2048]{2,1,0:T(8,128)(2,1)} %out_grad.5) | copy-start | bytes 1572868
  16.6 10.9 %copy-start.8 = (s32[1,1024]{1,0:T(1,128)S(1)}, s32[1,1024]{1,0:T(1,128)}, u32[]{:S(2)}) copy-start(s32[1,1024]{1,0:T(1,128)} %segments.3) | copy-start | bytes 12292
  16.6 10.9 %collective-permute-start.3 = (bf16[256,512]{1,0:T(8,128)(2,1)S(1)}, bf16[256,512]{1,0:T(8,128)(2,1)S(1)}, u32[]{:S(2)}, u32[]{:S(2)}) collective-permute-start(bf16[256,512]{1,0:T(8,128)(2,1)S(1)} %pad_maximum_fusion), channel_id=1, source_target_pairs={{0,2},{1,3},{2,4},{3,5},{4,6},{5,7},{8,10},{9,11},{10,12},{11,13},... | collective-permute-start | bytes 786440 | tf_op jit(solution)/shard_map/ppermute | solution.py:221
  20.9 6.6 %copy-start.9 = (f32[256]{0:T(256)S(1)}, f32[256]{0:T(256)}, u32[]{:S(2)}) copy-start(f32[256]{0:T(256)} %param.11) | copy-start | bytes 3076
  20.9 11.4 %collective-permute-start.4 = (bf16[256,512]{1,0:T(8,128)(2,1)S(1)}, bf16[256,512]{1,0:T(8,128)(2,1)S(1)}, u32[]{:S(2)}, u32[]{:S(2)}) collective-permute-start(bf16[256,512]{1,0:T(8,128)(2,1)S(1)} %second_payload.1), channel_id=1, source_target_pairs={{0,2},{1,3},{2,4},{3,5},{4,6},{5,7},{8,10},{9,11},{10,12},{11,13},... | collective-permute-start | bytes 786440 | tf_op jit(solution)/shard_map/ppermute | solution.py:221
  27.5 0.7 copy-start.7
  30.6 9.3 %collective-permute-start.8 = (bf16[256,512]{1,0:T(8,128)(2,1)S(1)}, bf16[256,512]{1,0:T(8,128)(2,1)S(1)}, u32[]{:S(2)}, u32[]{:S(2)}) collective-permute-start(bf16[256,512]{1,0:T(8,128)(2,1)S(1)} %get-tuple-element.39), channel_id=1, source_target_pairs={{2,0},{3,1},{4,2},{5,3},{6,4},{7,5},{10,8},{11,9},{12,10},{13,11},... | collective-permute-start | bytes 786440 | tf_op jit(solution)/shard_map/ppermute | solution.py:221
  31.9 63.6 %collective-permute-start.6 = (bf16[128,1536]{1,0:T(8,128)(2,1)S(1)}, bf16[128,1536]{1,0:T(8,128)(2,1)S(1)}, u32[]{:S(2)}, u32[]{:S(2)}) collective-permute-start(bf16[128,1536]{1,0:T(8,128)(2,1)S(1)} %get-tuple-element.32), channel_id=1, source_target_pairs={{0,1},{1,0},{2,3},{3,2},{4,5},{5,4},{6,7},{7,6},{8,9},{9,8},{10,11... | collective-permute-start | bytes 1179656 | tf_op jit(solution)/shard_map/ppermute | solution.py:221
  32.3 11.0 %collective-permute-start.5 = (bf16[256,512]{1,0:T(8,128)(2,1)S(1)}, bf16[256,512]{1,0:T(8,128)(2,1)S(1)}, u32[]{:S(2)}, u32[]{:S(2)}) collective-permute-start(bf16[256,512]{1,0:T(8,128)(2,1)S(1)} %collective-permute-done.4), channel_id=1, source_target_pairs={{0,2},{1,3},{2,4},{3,5},{4,6},{5,7},{8,10},{9,11},{10,12},{11,13},... | collective-permute-start | bytes 786440 | tf_op jit(solution)/shard_map/ppermute | solution.py:221
  40.7 57.7 %collective-permute-start.12 = (bf16[128,512]{1,0:T(8,128)(2,1)}, bf16[128,512]{1,0:T(8,128)(2,1)S(1)}, u32[]{:S(2)}, u32[]{:S(2)}) collective-permute-start(bf16[128,512]{1,0:T(8,128)(2,1)} %get-tuple-element.48), channel_id=1, source_target_pairs={{2,1},{3,0},{4,3},{5,2},{6,5},{7,4},{10,9},{11,8},{12,11},{13,10},... | collective-permute-start | bytes 393224 | tf_op jit(solution)/shard_map/ppermute | solution.py:221
  42.0 56.4 %collective-permute-start.9 = (bf16[128,512]{1,0:T(8,128)(2,1)}, bf16[128,512]{1,0:T(8,128)(2,1)S(1)}, u32[]{:S(2)}, u32[]{:S(2)}) collective-permute-start(bf16[128,512]{1,0:T(8,128)(2,1)} %get-tuple-element.49), channel_id=1, source_target_pairs={{2,0},{3,1},{4,2},{5,3},{6,4},{7,5},{10,8},{11,9},{12,10},{13,11},... | collective-permute-start | bytes 393224 | tf_op jit(solution)/shard_map/ppermute | solution.py:221
  46.2 47.0 %collective-permute-start.10 = (bf16[256,512]{1,0:T(8,128)(2,1)}, bf16[256,512]{1,0:T(8,128)(2,1)}, u32[]{:S(2)}, u32[]{:S(2)}) collective-permute-start(bf16[256,512]{1,0:T(8,128)(2,1)} %get-tuple-element.41), channel_id=1, source_target_pairs={{2,0},{3,1},{4,2},{5,3},{6,4},{7,5},{10,8},{11,9},{12,10},{13,11},... | collective-permute-start | bytes 786440 | tf_op jit(solution)/shard_map/ppermute | solution.py:221
  47.4 49.9 %collective-permute-start.7 = (bf16[128,1536]{1,0:T(8,128)(2,1)S(1)}, bf16[128,1536]{1,0:T(8,128)(2,1)S(1)}, u32[]{:S(2)}, u32[]{:S(2)}) collective-permute-start(bf16[128,1536]{1,0:T(8,128)(2,1)S(1)} %get-tuple-element.33), channel_id=1, source_target_pairs={{0,1},{1,0},{2,3},{3,2},{4,5},{5,4},{6,7},{7,6},{8,9},{9,8},{10,11... | collective-permute-start | bytes 1179656 | tf_op jit(solution)/shard_map/ppermute | solution.py:221
  94.2 7.2 %collective-permute-start.13 = (bf16[128,512]{1,0:T(8,128)(2,1)S(1)}, bf16[128,512]{1,0:T(8,128)(2,1)S(1)}, u32[]{:S(2)}, u32[]{:S(2)}) collective-permute-start(bf16[128,512]{1,0:T(8,128)(2,1)S(1)} %get-tuple-element.46), channel_id=1, source_target_pairs={{2,1},{3,0},{4,3},{5,2},{6,5},{7,4},{10,9},{11,8},{12,11},{13,10},... | collective-permute-start | bytes 393224 | tf_op jit(solution)/shard_map/ppermute | solution.py:221
  95.5 9.2 %collective-permute-start.11 = (bf16[128,512]{1,0:T(8,128)(2,1)S(1)}, bf16[128,512]{1,0:T(8,128)(2,1)S(1)}, u32[]{:S(2)}, u32[]{:S(2)}) collective-permute-start(bf16[128,512]{1,0:T(8,128)(2,1)S(1)} %get-tuple-element.47), channel_id=1, source_target_pairs={{2,0},{3,1},{4,2},{5,3},{6,4},{7,5},{10,8},{11,9},{12,10},{13,11},... | collective-permute-start | bytes 393224 | tf_op jit(solution)/shard_map/ppermute | solution.py:221
  97.4 7.3 %copy-start.1 = (bf16[1,128,1024]{2,1,0:T(8,128)(2,1)S(1)}, bf16[1,128,1024]{2,1,0:T(8,128)(2,1)}, u32[]{:S(2)}) copy-start(bf16[1,128,1024]{2,1,0:T(8,128)(2,1)} %keys.11) | copy-start | bytes 786436

commit v2 on v0

v2 whole, which is shorter than its diff:
```python
import functools

import jax
import jax.numpy as jnp
from jax import lax
from jax.experimental import pallas as pl
from jax.experimental.pallas import tpu as pltpu
from jax.sharding import PartitionSpec as P

HEADS = 8
KV_HEADS = 4
HEAD_DIM = 256
WINDOW = 512
GREACH = 4
GROUPS = HEADS // KV_HEADS
EPSILON = 1e-06
BF16 = jnp.bfloat16
F32 = jnp.float32
CHUNKS = ((0, 1), (1, 1), (2, 1), (3, 1))
LAG = 2

VMEM = pl.BlockSpec(memory_space=pltpu.VMEM)
ANY = pl.BlockSpec(memory_space=pl.ANY)


def call(body, name, ins, outs, after=(), flops=0, moved=2**18, in_specs=None, out_specs=None, **more):
    names = list(ins)

    def kernel(*refs):
        used = len(names) + len(after)
        body(*refs[: len(names)], *refs[used:])

    specs = [(in_specs or {}).get(key, VMEM) for key in names] + [ANY] * len(after)
    return pl.pallas_call(
        kernel,
        out_shape=list(outs.values()),
        in_specs=specs,
        out_specs=[(out_specs or {}).get(key, VMEM) for key in outs],
        compiler_params=pltpu.CompilerParams(vmem_limit_bytes=40 * 2**20),
        cost_estimate=pl.CostEstimate(flops=flops, bytes_accessed=moved, transcendentals=0),
        name=name,
        **more,
    )(*ins.values(), *after)


def shape(rows, cols, dtype=BF16):
    return jax.ShapeDtypeStruct((rows, cols), dtype)


def core_index():
    return lax.axis_index("ctx") % 2


def payload(chunks, places, keys, values, *rest):
    outs, sems = rest[:-1], rest[-1]
    copies = []
    for index, ((first, count), (out, at)) in enumerate(zip(chunks, places)):
        here = pl.ds(first * HEAD_DIM, count * HEAD_DIM)
        for side, field in enumerate((keys, values)):
            to = outs[out].at[:, pl.ds(at + side * count * HEAD_DIM, count * HEAD_DIM)]
            copies.append(pltpu.make_async_copy(field.at[0, :, here], to, sems.at[2 * index + side]))
    for copy in copies:
        copy.start()
    for copy in copies:
        copy.wait()


def normalize(field):
    inverse = lax.rsqrt(jnp.mean(field * field, -1, keepdims=True) + EPSILON)
    return field * inverse, inverse


def dot(left, right, over):
    return lax.dot_general(left, right, ((over[:1], over[1:]), ((), ())), preferred_element_type=F32)


def attend(
    count, at_own, at_x, at_near, at_y, at_far, segments, queries, out_grad, own, across_x, arrived_near, across_y, arrived_far,
    query_gain, key_gain, *rest,
):
    attended, query_grad, part_own, part_near, part_far, part_swap, gains = rest[-7:]
    position = lax.axis_index("ctx")
    rows = queries.shape[1]
    band = (GREACH + 1) * rows
    gain_q = query_gain[...]
    gain_k = key_gain[...]

    def segment(distance):
        block = position - distance
        first = pl.multiple_of(jnp.maximum(block, 0) * rows, rows)
        return jnp.where(block >= 0, segments[:, pl.ds(first, rows)], -1)

    key_seg = jnp.concatenate([segment(distance) for distance in range(GREACH, -1, -1)], 1)
    query_seg = jnp.broadcast_to(segment(0), (rows, rows)).T[:, :1]
    back = (
        lax.broadcasted_iota(jnp.int32, (rows, band), 0)
        - lax.broadcasted_iota(jnp.int32, (rows, band), 1)
        + GREACH * rows
    )
    live = (query_seg == key_seg) & (back >= 0) & (back < WINDOW)
    live = jnp.concatenate([live] * GROUPS, 0)

    query_gains = jnp.zeros((1, HEAD_DIM), F32)
    key_gains = jnp.zeros((1, HEAD_DIM), F32)
    blocks = ((arrived_far, at_far), (across_y, at_y), (arrived_near, at_near), (across_x, at_x), (own, at_own))

    def band_of(index):
        return jnp.concatenate(
            [field[:, at + index * HEAD_DIM : at + (index + 1) * HEAD_DIM] for field, at in blocks], 0
        )

    for head in range(count):
        at_k = slice(head * HEAD_DIM, (head + 1) * HEAD_DIM)
        at_v = slice((count + head) * HEAD_DIM, (count + head + 1) * HEAD_DIM)
        at_q = [slice((head * GROUPS + g) * HEAD_DIM, (head * GROUPS + g + 1) * HEAD_DIM) for g in range(GROUPS)]
        band_v = band_of(count + head)
        k_normed, _ = normalize(band_of(head).astype(F32))
        k_rounded = (k_normed * gain_k).astype(BF16)
        q_normed, q_inverse = normalize(jnp.concatenate([queries[0, :, at] for at in at_q], 0).astype(F32))
        q_scaled = (q_normed * gain_q * HEAD_DIM ** (-0.5)).astype(BF16)
        grads = jnp.concatenate([out_grad[0, :, at] for at in at_q], 0)

        scores = dot(q_scaled, k_rounded, (1, 1))
        weights = jnp.where(live, jnp.exp(scores), 0.0)
        probs = weights * (1.0 / jnp.sum(weights, -1, keepdims=True))
        probs_low = probs.astype(BF16)
        dprob = dot(grads, band_v, (1, 1))
        centre = jnp.sum(probs * dprob, -1, keepdims=True)
        dscore = (probs * (dprob - centre)).astype(BF16)
        key_parts = dot(dscore, q_scaled, (0, 0))
        value_parts = dot(probs_low, grads, (0, 0))
        for at, parts in ((at_k, key_parts), (at_v, value_parts)):
            part_far[:, at] = parts[:rows]
            part_swap[:rows, at] = parts[rows : 2 * rows].astype(BF16)
            part_near[:, at] = parts[2 * rows : 3 * rows]
            part_swap[rows:, at] = parts[3 * rows : 4 * rows].astype(BF16)
            part_own[:, at] = parts[4 * rows :]

        output = dot(probs_low, band_v, (1, 0)).astype(BF16)
        dq = dot(dscore, k_rounded, (1, 0)) * HEAD_DIM ** (-0.5)
        scaled = dq * gain_q
        grad = q_inverse * (scaled - q_normed * jnp.mean(scaled * q_normed, -1, keepdims=True))
        grad = grad.astype(BF16)
        for g, at in enumerate(at_q):
            attended[0, :, at] = output[g * rows : (g + 1) * rows]
            query_grad[0, :, at] = grad[g * rows : (g + 1) * rows]
        query_gains = query_gains + jnp.sum(dq * q_normed, 0, keepdims=True)
        key_gains = key_gains + jnp.sum(key_parts * k_normed, 0, keepdims=True)
    gains[0:1, :] = query_gains
    gains[1:2, :] = key_gains


def finish(count, at, keys, key_gain, part_own, swapped, arrived, *rest):
    key_grad, value_grad = rest[-2:]
    rows = part_own.shape[0]
    gain_k = key_gain[...]
    for head in range(count):

        def total(index):
            here = slice(index * HEAD_DIM, (index + 1) * HEAD_DIM)
            there = slice(at + index * HEAD_DIM, at + (index + 1) * HEAD_DIM)
            extra = jnp.where(core_index() == 0, swapped[rows:, here].astype(F32), 0.0)
            return part_own[:, here] + extra + arrived[:, there].astype(F32)

        out = slice(head * HEAD_DIM, (head + 1) * HEAD_DIM)
        normed, inverse = normalize(keys[0, :, out].astype(F32))
        scaled = total(head) * gain_k
        grad = inverse * (scaled - normed * jnp.mean(scaled * normed, -1, keepdims=True))
        key_grad[0, :, out] = grad.astype(BF16)
        value_grad[0, :, out] = total(count + head).astype(BF16)


def columns(rows, width, first):
    return pl.BlockSpec((1, rows, width), lambda i: (0, 0, first // width))


def move(field, axis, target):
    size = lax.axis_size(axis)
    return lax.ppermute(field, axis, [(i, target(i)) for i in range(size) if 0 <= target(i) < size])


def up(field):
    return move(field, "ctx", lambda i: i + 2)


def down(field):
    return move(field, "ctx", lambda i: i - 2)


def swap(field):
    return move(field, "ctx", lambda i: i ^ 1)


def total_over(field, axis):
    step = 1
    while step < lax.axis_size(axis):
        field = field + move(field, axis, lambda i: i ^ step)
        step *= 2
    return field


def shards(segment_ids, queries, keys, values, query_gain, key_gain, out_grad):
    rows = queries.shape[1]
    gain_q = query_gain.reshape(1, HEAD_DIM)
    gain_k = key_gain.reshape(1, HEAD_DIM)
    amount = len(CHUNKS)
    width = [2 * count * HEAD_DIM for _, count in CHUNKS] + [0] * LAG
    pinned = [pltpu.with_memory_space_constraint(field, pltpu.HBM) for field in (keys, values)]

    def gather(chunks, after=(), joined=False):
        each = [2 * count * HEAD_DIM for _, count in chunks]
        places = [(0, sum(each[:i])) if joined else (i, 0) for i in range(len(chunks))]
        return call(
            functools.partial(payload, chunks, places),
            "payload",
            dict(keys=pinned[0], values=pinned[1]),
            {i: shape(rows, wide) for i, wide in enumerate([sum(each)] if joined else each)},
            after,
            in_specs=dict(keys=ANY, values=ANY),
            scratch_shapes=[pltpu.SemaphoreType.DMA((2 * len(chunks),))],
        )

    own = list(gather(CHUNKS[:LAG], joined=True))
    arrived = up(own[0])
    near = {chunk: (arrived, sum(width[:chunk])) for chunk in range(LAG)}
    own = [(own[0], sum(width[:chunk])) for chunk in range(LAG)]
    own += [(field, 0) for field in gather(CHUNKS[LAG:], own[0][:1])]
    far, next_behind, third_behind = {}, {}, {}

    def climb(steps, after=()):
        ins, outs, jobs = {}, {}, []

        def use(place, chunk):
            field, at = place
            key = next((key for key, value in ins.items() if value is field), f"in{len(ins)}")
            ins[key] = field
            return key, slice(at, at + width[chunk])

        across = 0
        for step in steps:
            rise = 0
            if step + LAG < amount:
                jobs.append((f"rise{step}", rise, use(own[step + LAG], step + LAG), None))
                rise += width[step + LAG]
            if step < amount:
                jobs.append((f"rise{step}", rise, use(near[step], step), None))
                outs[f"rise{step}"] = shape(rows, rise + width[step])
                jobs.append(("across", across, use(own[step], step), use(near[step], step)))
                next_behind[step] = across
                across += width[step]
            if step >= LAG:
                chunk = step - LAG
                jobs.append(("across", across, use(near[chunk], chunk), use(far[chunk], chunk)))
                third_behind[chunk] = across
                across += width[chunk]
        outs["across"] = shape(rows, across)

        def body(*refs):
            ref = dict(zip(list(ins) + list(outs), refs))
            for to, at, (key, here), other in jobs:
                value = ref[key][:, here]
                if other is not None:
                    value = jnp.where(core_index() == 0, value, ref[other[0]][:, other[1]])
                ref[to][:, at : at + value.shape[1]] = value

        made = dict(zip(outs, call(body, "climb", ins, outs, after)))
        exchanged = swap(made["across"])
        for step in steps:
            if step < amount:
                arrived = up(made[f"rise{step}"])
                ahead = 0
                if step + LAG < amount:
                    near[step + LAG] = (arrived, 0)
                    ahead = width[step + LAG]
                far[step] = (arrived, ahead)
                next_behind[step] = (exchanged, next_behind[step])
            if step >= LAG:
                third_behind[step - LAG] = (exchanged, third_behind[step - LAG])
        return [made["across"]]

    parts, sunk = [], {}

    def sink(step, after=()):
        fresh, older = step < amount, step >= LAG
        mine, below = width[step], width[step - LAG] if older else 0
        ins = {}
        if fresh:
            ins.update(far=parts[step]["far"], swapped=parts[step]["swap"])
        if older:
            ins.update(
                near=parts[step - LAG]["near"], swapped_old=parts[step - LAG]["swap"], arrived=sunk[step - LAG]
            )

        def body(*refs):
            ref = dict(zip(list(ins) + ["out"], refs))
            first = core_index() == 0
            if fresh:
                extra = jnp.where(first, 0.0, ref["swapped"][:rows, :].astype(F32))
                ref["out"][:, :mine] = (ref["far"][...] + extra).astype(BF16)
            if older:
                swapped = ref["swapped_old"]
                extra = jnp.where(first, swapped[:rows, :], swapped[rows:, :]).astype(F32)
                arrived = ref["arrived"][:, :below].astype(F32)
                ref["out"][:, mine:] = (ref["near"][...] + extra + arrived).astype(BF16)

        (total,) = call(body, "sink", ins, dict(out=shape(rows, mine + below)), after)
        sunk[step] = down(total)
        return total

    outputs, key_outputs, gains, last = [], [], 0.0, []
    order = climb(range(LAG))
    for chunk, (first, count) in enumerate(CHUNKS):
        order = climb([chunk + LAG], order)
        wide = columns(rows, GROUPS * count * HEAD_DIM, GROUPS * first * HEAD_DIM)
        held = (own, next_behind, near, third_behind, far)
        *outputs, part_own, part_near, part_far, part_swap, chunk_gains = call(
            functools.partial(attend, count, *(place[chunk][1] for place in held)),
            "attend",
            dict(
                segments=segment_ids, queries=queries, out_grad=out_grad, own=own[chunk][0],
                **{f"behind{i}": place[chunk][0] for i, place in enumerate(held[1:])}, gain_q=gain_q, gain_k=gain_k,
            ),
            dict(
                attended=jax.ShapeDtypeStruct(queries.shape, BF16),
                query_grad=jax.ShapeDtypeStruct(queries.shape, BF16),
                own=shape(rows, width[chunk], F32), near=shape(rows, width[chunk], F32),
                far=shape(rows, width[chunk], F32), swap=shape(2 * rows, width[chunk]),
                gains=shape(2, HEAD_DIM, F32),
            ),
            [*outputs, *last, *([sunk[chunk - LAG]] if chunk >= LAG else [])],
            flops=12 * GROUPS * rows * (GREACH + 1) * rows * count * HEAD_DIM,
            moved=2**21,
            grid=(1,),
            in_specs=dict(queries=wide, out_grad=wide),
            out_specs=dict(attended=wide, query_grad=wide),
            input_output_aliases={10 + i: i for i in range(len(outputs))},
        )
        gains = gains + chunk_gains
        parts.append(dict(own=part_own, near=part_near, far=part_far, swap=swap(part_swap)))
        last = [sink(chunk)]

    for step in range(amount, amount + LAG):
        sink(step)
    for chunk, (first, count) in enumerate(CHUNKS):
        narrow = columns(rows, count * HEAD_DIM, first * HEAD_DIM)
        key_outputs = call(
            functools.partial(finish, count, width[chunk + LAG]),
            "finish",
            dict(
                keys=keys, gain=gain_k, own=parts[chunk]["own"], swapped=parts[chunk]["swap"], arrived=sunk[chunk + LAG]
            ),
            dict(
                key_grad=jax.ShapeDtypeStruct(keys.shape, BF16), value_grad=jax.ShapeDtypeStruct(keys.shape, BF16)
            ),
            key_outputs,
            grid=(1,),
            in_specs=dict(keys=narrow),
            out_specs=dict(key_grad=narrow, value_grad=narrow),
            input_output_aliases={5 + i: i for i in range(len(key_outputs))},
        )

    gains = total_over(total_over(gains, "ctx"), "dp")
    factor = (lax.axis_size("dp") * queries.shape[0] * lax.axis_size("ctx") * rows) ** (-0.5)
    gains = gains * factor
    return *outputs, *key_outputs, gains[0], gains[1]


def solution(mesh):
    block = P("dp", "ctx", None)
    return jax.shard_map(
        shards,
        mesh=mesh,
        in_specs=(P("dp", None), block, block, block, P(), P(), block),
        out_specs=(block, block, block, block, P(), P()),
        check_vma=False,
    )
```

time: 175 us -> 110 us (0.63)
  blocking collectives: 37.9 us -> 0 us
  local copies, waits for them, and re-layouts: 21.7 us -> 1.23 us
  Pallas kernels: 0 us -> 13.5 us
  waiting for transfers between devices: 66 us -> 54.1 us
  other arithmetic: 8.35 us -> 0.02 us
  starting transfers between devices: 32.5 us -> 39.5 us
  matrix products: 5.93 us -> 0 us
    psum x1 -> x0, blocking collectives: 37.9 us -> none  [shards(): lax.psum((query_gain_part, key_gain_part), ('dp', 'ctx'))]
    pallas_call x0 -> x21, Pallas kernels: none -> 13.5 us  [call(): pl.pallas_call(kernel, out_shape=list(outs.values()), in_specs=specs, out...]
    ppermute x8 -> x25, waiting for transfers between devices: 66 us -> 54.1 us  [move(): lax.ppermute(field, axis, [(i, target(i)) for i in range(size) if 0 <= ta...]
    unnamed x40 -> x12, local copies, waits for them, and re-layouts: 8.05 us -> 0.66 us
    ppermute x8 -> x25, starting transfers between devices: 32.5 us -> 39.5 us  [move(): lax.ppermute(field, axis, [(i, target(i)) for i in range(size) if 0 <= ta...]
    dot_general x6 -> x0, matrix products: 5.93 us -> none  [the longest x1 1.68 us: shards(): jnp.einsum('kgij,jkd->ikgd', dscore, band_keys, preferred_element_type=jn...]
    concatenate x1 -> x0, local copies, waits for them, and re-layouts: 4.45 us -> none  [shards(): key_band = jnp.concatenate(earlier[::-1] + [own_block], axis=1)]
    convert_element_type x3 -> x0, other arithmetic: 3.21 us -> none  [the longest x1 2.33 us: shards(): query_grad.astype(jnp.bfloat16).reshape(1, tok_rows, HEADS * HEAD_DIM)]
  transfers between devices with their start and end apart: 8 -> 25, of which waited for: 4 -> 16; matrix products, arithmetic and copies ran while one was open for 4% -> 1% of each run, Pallas kernels for 0% -> 5%
where the time goes in v2:
time: 110 us; the launch traced here: 109 us
  waiting for transfers between devices  54.1 us (49%)
  starting transfers between devices  39.5 us (36%)
  Pallas kernels  13.5 us (12%)
  local copies, waits for them, and re-layouts  1.23 us (1%)
    ppermute x25, waiting for transfers between devices, move(): lax.ppermute(field, axis, [(i, target(i)) for i in range(size) if 0 <= ta...  54.1 us
    ppermute x25, starting transfers between devices, move(): lax.ppermute(field, axis, [(i, target(i)) for i in range(size) if 0 <= ta...  39.5 us
    pallas_call x21, Pallas kernels, call(): pl.pallas_call(kernel, out_shape=list(outs.values()), in_specs=specs, out...  13.5 us
  transfers between devices with their start and end apart: 25, of which 16 were waited for; matrix products, arithmetic and copies ran while one was open for 1% of the time, Pallas kernels for 5%

profile of v2, /device:TPU:0, one launch (start us, length us, event | category | flops | bytes accessed | tf_op | source)
XLA Modules:
  0.0 109.3 jit_solution(17912329322178822032)
XLA Ops:
  1.6 4.9 %collective-permute-start = (bf16[128,1024]{1,0:T(8,128)(2,1)S(1)}, bf16[128,1024]{1,0:T(8,128)(2,1)S(1)}, u32[]{:S(2)}, u32[]{:S(2)}) collective-permute-start(bf16[128,1024]{1,0:T(8,128)(2,1)S(1)} %payload.2.refs_2_.refs_3_), channel_id=1, source_target_pairs={{0,2},{1,3},{2,4},{3,5},{4,6},{5,7},{8,10},{9,11},{10,12},{11,13},... | collective-permute-start | bytes 786440 | tf_op jit(solution)/shard_map/ppermute | solution.py:179
  7.5 4.5 %collective-permute-done.refs_1_.refs_2_.refs_5_ = bf16[128,1024]{1,0:T(8,128)(2,1)S(1)} collective-permute-done((bf16[128,1024]{1,0:T(8,128)(2,1)S(1)}, bf16[128,1024]{1,0:T(8,128)(2,1)S(1)}, u32[]{:S(2)}, u32[]{:S(2)}) %collective-permute-start) | collective-permute-done | bytes 262176 | tf_op jit(solution)/shard_map/ppermute | solution.py:179
  12.2 4.5 %collective-permute-start.2 = (bf16[128,1024]{1,0:T(8,128)(2,1)S(1)}, bf16[128,1024]{1,0:T(8,128)(2,1)S(1)}, u32[]{:S(2)}, u32[]{:S(2)}) collective-permute-start(bf16[128,1024]{1,0:T(8,128)(2,1)S(1)} %get-tuple-element.54), channel_id=1, source_target_pairs={{0,2},{1,3},{2,4},{3,5},{4,6},{5,7},{8,10},{9,11},{10,12},{11,13},... | collective-permute-start | bytes 786440 | tf_op jit(solution)/shard_map/ppermute | solution.py:179
  16.8 4.6 %collective-permute-done.2.refs_0_.refs_7_.refs_5_ = bf16[128,1024]{1,0:T(8,128)(2,1)S(1)} collective-permute-done((bf16[128,1024]{1,0:T(8,128)(2,1)S(1)}, bf16[128,1024]{1,0:T(8,128)(2,1)S(1)}, u32[]{:S(2)}, u32[]{:S(2)}) %collective-permute-start.2) | collective-permute-done | bytes 262176 | tf_op jit(solution)/shard_map/ppermute | solution.py:179
  21.5 4.4 %collective-permute-start.1 = (bf16[128,1024]{1,0:T(8,128)(2,1)S(1)}, bf16[128,1024]{1,0:T(8,128)(2,1)S(1)}, u32[]{:S(2)}, u32[]{:S(2)}) collective-permute-start(bf16[128,1024]{1,0:T(8,128)(2,1)S(1)} %get-tuple-element.53), channel_id=1, source_target_pairs={{0,2},{1,3},{2,4},{3,5},{4,6},{5,7},{8,10},{9,11},{10,12},{11,13},... | collective-permute-start | bytes 786440 | tf_op jit(solution)/shard_map/ppermute | solution.py:179
  26.6 1.9 %attend.4 = (bf16[1,128,2048]{2,1,0:T(8,128)(2,1)}, bf16[1,128,2048]{2,1,0:T(8,128)(2,1)}, f32[128,512]{1,0:T(8,128)S(1)}, f32[128,512]{1,0:T(8,128)S(1)}, f32[1...) custom-call(s32[1,1024]{1,0:T(1,128)S(1)} %copy-done.3, ...), custom_call_target="tpu_custom_call" | custom-call | flops 503316480 | bytes 2097152 | tf_op jit(solution)/shard_map/attend/pallas_call | solution.py:34
  28.7 3.3 %collective-permute-done.1.refs_0_.refs_7_.refs_5_ = bf16[128,1024]{1,0:T(8,128)(2,1)S(1)} collective-permute-done((bf16[128,1024]{1,0:T(8,128)(2,1)S(1)}, bf16[128,1024]{1,0:T(8,128)(2,1)S(1)}, u32[]{:S(2)}, u32[]{:S(2)}) %collective-permute-start.1) | collective-permute-done | bytes 262176 | tf_op jit(solution)/shard_map/ppermute | solution.py:179
  32.3 1.5 %collective-permute-done.3.refs_6_.refs_4_ = bf16[128,1024]{1,0:T(8,128)(2,1)S(1)} collective-permute-done((bf16[128,1024]{1,0:T(8,128)(2,1)S(1)}, bf16[128,1024]{1,0:T(8,128)(2,1)S(1)}, u32[]{:S(2)}, u32[]{:S(2)}) %collective-permute-start.3) | collective-permute-done | bytes 262176 | tf_op jit(solution)/shard_map/ppermute | solution.py:179
  33.7 1.9 %attend.5 = (bf16[1,128,2048]{2,1,0:T(8,128)(2,1)}, bf16[1,128,2048]{2,1,0:T(8,128)(2,1)}, f32[128,512]{1,0:T(8,128)S(1)}, f32[128,512]{1,0:T(8,128)S(1)}, f32[1...) custom-call(s32[1,1024]{1,0:T(1,128)S(1)} %copy-done.3, ...), custom_call_target="tpu_custom_call", output_to_operand_aliasing={{0}: (10, {}), {1}: (11, {})} | custom-call | flops 503316480 | bytes 2097152 | tf_op jit(solution)/shard_map/attend/pallas_call | solution.py:34
  35.8 4.4 %collective-permute-start.5 = (bf16[128,512]{1,0:T(8,128)(2,1)S(1)}, bf16[128,512]{1,0:T(8,128)(2,1)S(1)}, u32[]{:S(2)}, u32[]{:S(2)}) collective-permute-start(bf16[128,512]{1,0:T(8,128)(2,1)S(1)} %get-tuple-element.59), channel_id=1, source_target_pairs={{0,2},{1,3},{2,4},{3,5},{4,6},{5,7},{8,10},{9,11},{10,12},{11,13},... | collective-permute-start | bytes 393224 | tf_op jit(solution)/shard_map/ppermute | solution.py:179
  40.2 3.3 %collective-permute-done.5.refs_1_.refs_7_ = bf16[128,512]{1,0:T(8,128)(2,1)S(1)} collective-permute-done((bf16[128,512]{1,0:T(8,128)(2,1)S(1)}, bf16[128,512]{1,0:T(8,128)(2,1)S(1)}, u32[]{:S(2)}, u32[]{:S(2)}) %collective-permute-start.5) | collective-permute-done | bytes 131104 | tf_op jit(solution)/shard_map/ppermute | solution.py:179
  43.6 1.3 %collective-permute-start.12 = (bf16[128,512]{1,0:T(8,128)(2,1)S(1)}, bf16[128,512]{1,0:T(8,128)(2,1)S(1)}, u32[]{:S(2)}, u32[]{:S(2)}) collective-permute-start(bf16[128,512]{1,0:T(8,128)(2,1)S(1)} %sink.6.refs_12_), channel_id=1, source_target_pairs={{2,0},{3,1},{4,2},{5,3},{6,4},{7,5},{10,8},{11,9},{12,10},{13,11},... | collective-permute-start | bytes 393224 | tf_op jit(solution)/shard_map/ppermute | solution.py:179
  44.9 7.2 %collective-permute-done.12.refs_13_.refs_4_ = bf16[128,512]{1,0:T(8,128)(2,1)S(1)} collective-permute-done((bf16[128,512]{1,0:T(8,128)(2,1)S(1)}, bf16[128,512]{1,0:T(8,128)(2,1)S(1)}, u32[]{:S(2)}, u32[]{:S(2)}) %collective-permute-start.12) | collective-permute-done | bytes 131104 | tf_op jit(solution)/shard_map/ppermute | solution.py:179
  52.1 1.9 %attend.6 = (bf16[1,128,2048]{2,1,0:T(8,128)(2,1)}, bf16[1,128,2048]{2,1,0:T(8,128)(2,1)}, f32[128,512]{1,0:T(8,128)S(1)}, f32[128,512]{1,0:T(8,128)S(1)}, f32[1...) custom-call(s32[1,1024]{1,0:T(1,128)S(1)} %copy-done.3, ...), custom_call_target="tpu_custom_call", output_to_operand_aliasing={{0}: (10, {}), {1}: (11, {})} | custom-call | flops 503316480 | bytes 2097152 | tf_op jit(solution)/shard_map/attend/pallas_call | solution.py:34
  54.0 3.6 %collective-permute-start.4 = (bf16[128,512]{1,0:T(8,128)(2,1)S(1)}, bf16[128,512]{1,0:T(8,128)(2,1)S(1)}, u32[]{:S(2)}, u32[]{:S(2)}) collective-permute-start(bf16[128,512]{1,0:T(8,128)(2,1)S(1)} %get-tuple-element.58), channel_id=1, source_target_pairs={{0,2},{1,3},{2,4},{3,5},{4,6},{5,7},{8,10},{9,11},{10,12},{11,13},... | collective-permute-start | bytes 393224 | tf_op jit(solution)/shard_map/ppermute | solution.py:179
  57.6 3.4 %collective-permute-done.4.refs_1_.refs_7_ = bf16[128,512]{1,0:T(8,128)(2,1)S(1)} collective-permute-done((bf16[128,512]{1,0:T(8,128)(2,1)S(1)}, bf16[128,512]{1,0:T(8,128)(2,1)S(1)}, u32[]{:S(2)}, u32[]{:S(2)}) %collective-permute-start.4) | collective-permute-done | bytes 131104 | tf_op jit(solution)/shard_map/ppermute | solution.py:179
  61.2 1.3 %collective-permute-start.14 = (bf16[128,512]{1,0:T(8,128)(2,1)S(1)}, bf16[128,512]{1,0:T(8,128)(2,1)S(1)}, u32[]{:S(2)}, u32[]{:S(2)}) collective-permute-start(bf16[128,512]{1,0:T(8,128)(2,1)S(1)} %sink.7.refs_12_), channel_id=1, source_target_pairs={{2,0},{3,1},{4,2},{5,3},{6,4},{7,5},{10,8},{11,9},{12,10},{13,11},... | collective-permute-start | bytes 393224 | tf_op jit(solution)/shard_map/ppermute | solution.py:179
  62.6 7.1 %collective-permute-done.14.refs_13_.refs_4_ = bf16[128,512]{1,0:T(8,128)(2,1)S(1)} collective-permute-done((bf16[128,512]{1,0:T(8,128)(2,1)S(1)}, bf16[128,512]{1,0:T(8,128)(2,1)S(1)}, u32[]{:S(2)}, u32[]{:S(2)}) %collective-permute-start.14) | collective-permute-done | bytes 131104 | tf_op jit(solution)/shard_map/ppermute | solution.py:179
  69.7 1.9 %attend.7 = (bf16[1,128,2048]{2,1,0:T(8,128)(2,1)}, bf16[1,128,2048]{2,1,0:T(8,128)(2,1)}, f32[128,512]{1,0:T(8,128)S(1)}, f32[128,512]{1,0:T(8,128)S(1)}, f32[1...) custom-call(s32[1,1024]{1,0:T(1,128)S(1)} %copy-done.3, ...), custom_call_target="tpu_custom_call", output_to_operand_aliasing={{0}: (10, {}), {1}: (11, {})} | custom-call | flops 503316480 | bytes 2097152 | tf_op jit(solution)/shard_map/attend/pallas_call | solution.py:34
  71.6 1.3 %collective-permute-start.18 = (bf16[128,1024]{1,0:T(8,128)(2,1)S(1)}, bf16[128,1024]{1,0:T(8,128)(2,1)S(1)}, u32[]{:S(2)}, u32[]{:S(2)}) collective-permute-start(bf16[128,1024]{1,0:T(8,128)(2,1)S(1)} %sink.8.refs_12_), channel_id=1, source_target_pairs={{2,0},{3,1},{4,2},{5,3},{6,4},{7,5},{10,8},{11,9},{12,10},{13,11},... | collective-permute-start | bytes 786440 | tf_op jit(solution)/shard_map/ppermute | solution.py:179
  73.2 1.3 %collective-permute-start.16 = (bf16[128,1024]{1,0:T(8,128)(2,1)S(1)}, bf16[128,1024]{1,0:T(8,128)(2,1)S(1)}, u32[]{:S(2)}, u32[]{:S(2)}) collective-permute-start(bf16[128,1024]{1,0:T(8,128)(2,1)S(1)} %sink.9), channel_id=1, source_target_pairs={{2,0},{3,1},{4,2},{5,3},{6,4},{7,5},{10,8},{11,9},{12,10},{13,11},... | collective-permute-start | bytes 786440 | tf_op jit(solution)/shard_map/ppermute | solution.py:179
  75.8 3.0 %collective-permute-start.21 = (f32[2,256]{1,0:T(2,128)S(1)}, f32[2,256]{1,0:T(2,128)S(1)}, u32[]{:S(2)}, u32[]{:S(2)}) collective-permute-start(f32[2,256]{1,0:T(2,128)S(1)} %add.27), channel_id=1, source_target_pairs={{0,2},{1,3},{2,0},{3,1},{4,6},{5,7},{6,4},{7,5},{8,10},{9,11},{10,... | collective-permute-start | bytes 6152 | tf_op jit(solution)/shard_map/ppermute | solution.py:179
  78.8 9.1 %collective-permute-done.21 = f32[2,256]{1,0:T(2,128)S(1)} collective-permute-done((f32[2,256]{1,0:T(2,128)S(1)}, f32[2,256]{1,0:T(2,128)S(1)}, u32[]{:S(2)}, u32[]{:S(2)}) %collective-permute-start.21) | collective-permute-done | bytes 2080 | tf_op jit(solution)/shard_map/ppermute | solution.py:179
  87.9 2.7 %collective-permute-start.22 = (f32[2,256]{1,0:T(2,128)S(1)}, f32[2,256]{1,0:T(2,128)S(1)}, u32[]{:S(2)}, u32[]{:S(2)}) collective-permute-start(f32[2,256]{1,0:T(2,128)S(1)} %add.28), channel_id=1, source_target_pairs={{0,4},{1,5},{2,6},{3,7},{4,0},{5,1},{6,2},{7,3},{8,12},{9,13},{10,... | collective-permute-start | bytes 6152 | tf_op jit(solution)/shard_map/ppermute | solution.py:179
  90.6 1.7 %collective-permute-done.22 = f32[2,256]{1,0:T(2,128)S(1)} collective-permute-done((f32[2,256]{1,0:T(2,128)S(1)}, f32[2,256]{1,0:T(2,128)S(1)}, u32[]{:S(2)}, u32[]{:S(2)}) %collective-permute-start.22) | collective-permute-done | bytes 2080 | tf_op jit(solution)/shard_map/ppermute | solution.py:179
  92.4 1.5 %collective-permute-start.23 = (f32[2,256]{1,0:T(2,128)S(1)}, f32[2,256]{1,0:T(2,128)S(1)}, u32[]{:S(2)}, u32[]{:S(2)}) collective-permute-start(f32[2,256]{1,0:T(2,128)S(1)} %add.29), channel_id=1, source_target_pairs={{0,8},{8,0},{16,24},{24,16},{1,9},{9,1},{17,25},{25,17},{2,10},{10... | collective-permute-start | bytes 6152 | tf_op jit(solution)/shard_map/ppermute | solution.py:179
  93.9 2.1 %collective-permute-done.23 = f32[2,256]{1,0:T(2,128)S(1)} collective-permute-done((f32[2,256]{1,0:T(2,128)S(1)}, f32[2,256]{1,0:T(2,128)S(1)}, u32[]{:S(2)}, u32[]{:S(2)}) %collective-permute-start.23) | collective-permute-done | bytes 2080 | tf_op jit(solution)/shard_map/ppermute | solution.py:179
  95.9 1.5 %collective-permute-start.24 = (f32[2,256]{1,0:T(2,128)S(1)}, f32[2,256]{1,0:T(2,128)S(1)}, u32[]{:S(2)}, u32[]{:S(2)}) collective-permute-start(f32[2,256]{1,0:T(2,128)S(1)} %add.30), channel_id=1, source_target_pairs={{0,16},{8,24},{16,0},{24,8},{1,17},{9,25},{17,1},{25,9},{2,18},{10... | collective-permute-start | bytes 6152 | tf_op jit(solution)/shard_map/ppermute | solution.py:179
  97.5 2.1 %collective-permute-done.24 = f32[2,256]{1,0:T(2,128)S(1)} collective-permute-done((f32[2,256]{1,0:T(2,128)S(1)}, f32[2,256]{1,0:T(2,128)S(1)}, u32[]{:S(2)}, u32[]{:S(2)}) %collective-permute-start.24) | collective-permute-done | bytes 2080 | tf_op jit(solution)/shard_map/ppermute | solution.py:179
  99.6 1.3 %collective-permute-start.19 = (bf16[128,512]{1,0:T(8,128)(2,1)S(1)}, bf16[128,512]{1,0:T(8,128)(2,1)S(1)}, u32[]{:S(2)}, u32[]{:S(2)}) collective-permute-start(bf16[128,512]{1,0:T(8,128)(2,1)S(1)} %sink.11), channel_id=1, source_target_pairs={{2,0},{3,1},{4,2},{5,3},{6,4},{7,5},{10,8},{11,9},{12,10},{13,11},... | collective-permute-start | bytes 393224 | tf_op jit(solution)/shard_map/ppermute | solution.py:179
  101.0 1.3 %collective-permute-start.17 = (bf16[128,512]{1,0:T(8,128)(2,1)S(1)}, bf16[128,512]{1,0:T(8,128)(2,1)S(1)}, u32[]{:S(2)}, u32[]{:S(2)}) collective-permute-start(bf16[128,512]{1,0:T(8,128)(2,1)S(1)} %sink.10), channel_id=1, source_target_pairs={{2,0},{3,1},{4,2},{5,3},{6,4},{7,5},{10,8},{11,9},{12,10},{13,11},... | collective-permute-start | bytes 393224 | tf_op jit(solution)/shard_map/ppermute | solution.py:179
  104.5 2.0 %collective-permute-done.19.refs_4_ = bf16[128,512]{1,0:T(8,128)(2,1)S(1)} collective-permute-done((bf16[128,512]{1,0:T(8,128)(2,1)S(1)}, bf16[128,512]{1,0:T(8,128)(2,1)S(1)}, u32[]{:S(2)}, u32[]{:S(2)}) %collective-permute-start.19) | collective-permute-done | bytes 131104 | tf_op jit(solution)/shard_map/ppermute | solution.py:179
  (58 shorter events, 10.4 us)
Async XLA Ops:
  1.6 10.5 %collective-permute-start = (bf16[128,1024]{1,0:T(8,128)(2,1)S(1)}, bf16[128,1024]{1,0:T(8,128)(2,1)S(1)}, u32[]{:S(2)}, u32[]{:S(2)}) collective-permute-start(bf16[128,1024]{1,0:T(8,128)(2,1)S(1)} %payload.2.refs_2_.refs_3_), channel_id=1, source_target_pairs={{0,2},{1,3},{2,4},{3,5},{4,6},{5,7},{8,10},{9,11},{10,12},{11,13},... | collective-permute-start | bytes 786440 | tf_op jit(solution)/shard_map/ppermute | solution.py:179
  12.1 13.8 %copy-start.2 = (bf16[1,128,2048]{2,1,0:T(8,128)(2,1)S(1)}, bf16[1,128,2048]{2,1,0:T(8,128)(2,1)}, u32[]{:S(2)}) copy-start(bf16[1,128,2048]{2,1,0:T(8,128)(2,1)} %refs_2_.7) | copy-start | bytes 1572868
  12.2 13.8 %copy-start.1 = (bf16[1,128,2048]{2,1,0:T(8,128)(2,1)S(1)}, bf16[1,128,2048]{2,1,0:T(8,128)(2,1)}, u32[]{:S(2)}) copy-start(bf16[1,128,2048]{2,1,0:T(8,128)(2,1)} %refs_1_.11) | copy-start | bytes 1572868
  12.2 9.2 %collective-permute-start.2 = (bf16[128,1024]{1,0:T(8,128)(2,1)S(1)}, bf16[128,1024]{1,0:T(8,128)(2,1)S(1)}, u32[]{:S(2)}, u32[]{:S(2)}) collective-permute-start(bf16[128,1024]{1,0:T(8,128)(2,1)S(1)} %get-tuple-element.54), channel_id=1, source_target_pairs={{0,2},{1,3},{2,4},{3,5},{4,6},{5,7},{8,10},{9,11},{10,12},{11,13},... | collective-permute-start | bytes 786440 | tf_op jit(solution)/shard_map/ppermute | solution.py:179
  16.7 9.2 %collective-permute-start.9 = (bf16[128,1024]{1,0:T(8,128)(2,1)S(1)}, bf16[128,1024]{1,0:T(8,128)(2,1)S(1)}, u32[]{:S(2)}, u32[]{:S(2)}) collective-permute-start(bf16[128,1024]{1,0:T(8,128)(2,1)S(1)} %get-tuple-element.55.refs_3_), channel_id=1, source_target_pairs={{0,1},{1,0},{2,3},{3,2},{4,5},{5,4},{6,7},{7,6},{8,9},{9,8},{10,11... | collective-permute-start | bytes 786440 | tf_op jit(solution)/shard_map/ppermute | solution.py:179
  21.4 4.6 %copy-start.5 = (f32[256]{0:T(256)S(1)}, f32[256]{0:T(256)}, u32[]{:S(2)}) copy-start(f32[256]{0:T(256)} %param.11) | copy-start | bytes 3076
  21.4 4.6 %copy-start.3 = (s32[1,1024]{1,0:T(1,128)S(1)}, s32[1,1024]{1,0:T(1,128)}, u32[]{:S(2)}) copy-start(s32[1,1024]{1,0:T(1,128)} %refs_0_.15) | copy-start | bytes 12292
  21.4 4.5 %collective-permute-start.7 = (bf16[128,1024]{1,0:T(8,128)(2,1)S(1)}, bf16[128,1024]{1,0:T(8,128)(2,1)S(1)}, u32[]{:S(2)}, u32[]{:S(2)}) collective-permute-start(bf16[128,1024]{1,0:T(8,128)(2,1)S(1)} %get-tuple-element.56.refs_3_), channel_id=1, source_target_pairs={{0,1},{1,0},{2,3},{3,2},{4,5},{5,4},{6,7},{7,6},{8,9},{9,8},{10,11... | collective-permute-start | bytes 786440 | tf_op jit(solution)/shard_map/ppermute | solution.py:179
  21.5 10.6 %collective-permute-start.1 = (bf16[128,1024]{1,0:T(8,128)(2,1)S(1)}, bf16[128,1024]{1,0:T(8,128)(2,1)S(1)}, u32[]{:S(2)}, u32[]{:S(2)}) collective-permute-start(bf16[128,1024]{1,0:T(8,128)(2,1)S(1)} %get-tuple-element.53), channel_id=1, source_target_pairs={{0,2},{1,3},{2,4},{3,5},{4,6},{5,7},{8,10},{9,11},{10,12},{11,13},... | collective-permute-start | bytes 786440 | tf_op jit(solution)/shard_map/ppermute | solution.py:179
  25.9 0.7 copy-start.4
  28.5 3.7 %collective-permute-start.10 = (bf16[256,512]{1,0:T(8,128)(2,1)S(1)}, bf16[256,512]{1,0:T(8,128)(2,1)S(1)}, u32[]{:S(2)}, u32[]{:S(2)}) collective-permute-start(bf16[256,512]{1,0:T(8,128)(2,1)S(1)} %get-tuple-element.63), channel_id=1, source_target_pairs={{0,1},{1,0},{2,3},{3,2},{4,5},{5,4},{6,7},{7,6},{8,9},{9,8},{10,11... | collective-permute-start | bytes 786440 | tf_op jit(solution)/shard_map/ppermute | solution.py:179
  32.1 1.6 %collective-permute-start.3 = (bf16[128,1024]{1,0:T(8,128)(2,1)S(1)}, bf16[128,1024]{1,0:T(8,128)(2,1)S(1)}, u32[]{:S(2)}, u32[]{:S(2)}) collective-permute-start(bf16[128,1024]{1,0:T(8,128)(2,1)S(1)} %get-tuple-element.57.refs_2_), channel_id=1, source_target_pairs={{0,1},{1,0},{2,3},{3,2},{4,5},{5,4},{6,7},{7,6},{8,9},{9,8},{10,11... | collective-permute-start | bytes 786440 | tf_op jit(solution)/shard_map/ppermute | solution.py:179
  35.7 9.2 %collective-permute-start.11 = (bf16[256,512]{1,0:T(8,128)(2,1)S(1)}, bf16[256,512]{1,0:T(8,128)(2,1)S(1)}, u32[]{:S(2)}, u32[]{:S(2)}) collective-permute-start(bf16[256,512]{1,0:T(8,128)(2,1)S(1)} %get-tuple-element.67), channel_id=1, source_target_pairs={{0,1},{1,0},{2,3},{3,2},{4,5},{5,4},{6,7},{7,6},{8,9},{9,8},{10,11... | collective-permute-start | bytes 786440 | tf_op jit(solution)/shard_map/ppermute | solution.py:179
  35.8 7.7 %collective-permute-start.5 = (bf16[128,512]{1,0:T(8,128)(2,1)S(1)}, bf16[128,512]{1,0:T(8,128)(2,1)S(1)}, u32[]{:S(2)}, u32[]{:S(2)}) collective-permute-start(bf16[128,512]{1,0:T(8,128)(2,1)S(1)} %get-tuple-element.59), channel_id=1, source_target_pairs={{0,2},{1,3},{2,4},{3,5},{4,6},{5,7},{8,10},{9,11},{10,12},{11,13},... | collective-permute-start | bytes 393224 | tf_op jit(solution)/shard_map/ppermute | solution.py:179
  43.5 1.4 %collective-permute-start.8 = (bf16[128,512]{1,0:T(8,128)(2,1)S(1)}, bf16[128,512]{1,0:T(8,128)(2,1)S(1)}, u32[]{:S(2)}, u32[]{:S(2)}) collective-permute-start(bf16[128,512]{1,0:T(8,128)(2,1)S(1)} %climb.8.refs_2_), channel_id=1, source_target_pairs={{0,1},{1,0},{2,3},{3,2},{4,5},{5,4},{6,7},{7,6},{8,9},{9,8},{10,11... | collective-permute-start | bytes 393224 | tf_op jit(solution)/shard_map/ppermute | solution.py:179
  43.6 8.5 %collective-permute-start.12 = (bf16[128,512]{1,0:T(8,128)(2,1)S(1)}, bf16[128,512]{1,0:T(8,128)(2,1)S(1)}, u32[]{:S(2)}, u32[]{:S(2)}) collective-permute-start(bf16[128,512]{1,0:T(8,128)(2,1)S(1)} %sink.6.refs_12_), channel_id=1, source_target_pairs={{2,0},{3,1},{4,2},{5,3},{6,4},{7,5},{10,8},{11,9},{12,10},{13,11},... | collective-permute-start | bytes 393224 | tf_op jit(solution)/shard_map/ppermute | solution.py:179
  54.0 8.5 %collective-permute-start.13 = (bf16[256,512]{1,0:T(8,128)(2,1)S(1)}, bf16[256,512]{1,0:T(8,128)(2,1)S(1)}, u32[]{:S(2)}, u32[]{:S(2)}) collective-permute-start(bf16[256,512]{1,0:T(8,128)(2,1)S(1)} %get-tuple-element.71), channel_id=1, source_target_pairs={{0,1},{1,0},{2,3},{3,2},{4,5},{5,4},{6,7},{7,6},{8,9},{9,8},{10,11... | collective-permute-start | bytes 786440 | tf_op jit(solution)/shard_map/ppermute | solution.py:179
  54.0 7.0 %collective-permute-start.4 = (bf16[128,512]{1,0:T(8,128)(2,1)S(1)}, bf16[128,512]{1,0:T(8,128)(2,1)S(1)}, u32[]{:S(2)}, u32[]{:S(2)}) collective-permute-start(bf16[128,512]{1,0:T(8,128)(2,1)S(1)} %get-tuple-element.58), channel_id=1, source_target_pairs={{0,2},{1,3},{2,4},{3,5},{4,6},{5,7},{8,10},{9,11},{10,12},{11,13},... | collective-permute-start | bytes 393224 | tf_op jit(solution)/shard_map/ppermute | solution.py:179
  61.1 1.5 %collective-permute-start.6 = (bf16[128,512]{1,0:T(8,128)(2,1)S(1)}, bf16[128,512]{1,0:T(8,128)(2,1)S(1)}, u32[]{:S(2)}, u32[]{:S(2)}) collective-permute-start(bf16[128,512]{1,0:T(8,128)(2,1)S(1)} %climb.9), channel_id=1, source_target_pairs={{0,1},{1,0},{2,3},{3,2},{4,5},{5,4},{6,7},{7,6},{8,9},{9,8},{10,11... | collective-permute-start | bytes 393224 | tf_op jit(solution)/shard_map/ppermute | solution.py:179
  61.2 8.5 %collective-permute-start.14 = (bf16[128,512]{1,0:T(8,128)(2,1)S(1)}, bf16[128,512]{1,0:T(8,128)(2,1)S(1)}, u32[]{:S(2)}, u32[]{:S(2)}) collective-permute-start(bf16[128,512]{1,0:T(8,128)(2,1)S(1)} %sink.7.refs_12_), channel_id=1, source_target_pairs={{2,0},{3,1},{4,2},{5,3},{6,4},{7,5},{10,8},{11,9},{12,10},{13,11},... | collective-permute-start | bytes 393224 | tf_op jit(solution)/shard_map/ppermute | solution.py:179
  71.6 1.5 %collective-permute-start.15 = (bf16[256,512]{1,0:T(8,128)(2,1)S(1)}, bf16[256,512]{1,0:T(8,128)(2,1)S(1)}, u32[]{:S(2)}, u32[]{:S(2)}) collective-permute-start(bf16[256,512]{1,0:T(8,128)(2,1)S(1)} %get-tuple-element.76), channel_id=1, source_target_pairs={{0,1},{1,0},{2,3},{3,2},{4,5},{5,4},{6,7},{7,6},{8,9},{9,8},{10,11... | collective-permute-start | bytes 786440 | tf_op jit(solution)/shard_map/ppermute | solution.py:179
  71.6 27.9 %collective-permute-start.18 = (bf16[128,1024]{1,0:T(8,128)(2,1)S(1)}, bf16[128,1024]{1,0:T(8,128)(2,1)S(1)}, u32[]{:S(2)}, u32[]{:S(2)}) collective-permute-start(bf16[128,1024]{1,0:T(8,128)(2,1)S(1)} %sink.8.refs_12_), channel_id=1, source_target_pairs={{2,0},{3,1},{4,2},{5,3},{6,4},{7,5},{10,8},{11,9},{12,10},{13,11},... | collective-permute-start | bytes 786440 | tf_op jit(solution)/shard_map/ppermute | solution.py:179
  73.2 27.7 %collective-permute-start.16 = (bf16[128,1024]{1,0:T(8,128)(2,1)S(1)}, bf16[128,1024]{1,0:T(8,128)(2,1)S(1)}, u32[]{:S(2)}, u32[]{:S(2)}) collective-permute-start(bf16[128,1024]{1,0:T(8,128)(2,1)S(1)} %sink.9), channel_id=1, source_target_pairs={{2,0},{3,1},{4,2},{5,3},{6,4},{7,5},{10,8},{11,9},{12,10},{13,11},... | collective-permute-start | bytes 786440 | tf_op jit(solution)/shard_map/ppermute | solution.py:179
  74.5 1.2 %collective-permute-start.20 = (f32[2,256]{1,0:T(2,128)S(1)}, f32[2,256]{1,0:T(2,128)S(1)}, u32[]{:S(2)}, u32[]{:S(2)}) collective-permute-start(f32[2,256]{1,0:T(2,128)S(1)} %add_add_fusion), channel_id=1, source_target_pairs={{0,1},{1,0},{2,3},{3,2},{4,5},{5,4},{6,7},{7,6},{8,9},{9,8},{10,11... | collective-permute-start | bytes 6152 | tf_op jit(solution)/shard_map/ppermute | solution.py:179
  75.8 12.1 %collective-permute-start.21 = (f32[2,256]{1,0:T(2,128)S(1)}, f32[2,256]{1,0:T(2,128)S(1)}, u32[]{:S(2)}, u32[]{:S(2)}) collective-permute-start(f32[2,256]{1,0:T(2,128)S(1)} %add.27), channel_id=1, source_target_pairs={{0,2},{1,3},{2,0},{3,1},{4,6},{5,7},{6,4},{7,5},{8,10},{9,11},{10,... | collective-permute-start | bytes 6152 | tf_op jit(solution)/shard_map/ppermute | solution.py:179
  87.9 4.5 %collective-permute-start.22 = (f32[2,256]{1,0:T(2,128)S(1)}, f32[2,256]{1,0:T(2,128)S(1)}, u32[]{:S(2)}, u32[]{:S(2)}) collective-permute-start(f32[2,256]{1,0:T(2,128)S(1)} %add.28), channel_id=1, source_target_pairs={{0,4},{1,5},{2,6},{3,7},{4,0},{5,1},{6,2},{7,3},{8,12},{9,13},{10,... | collective-permute-start | bytes 6152 | tf_op jit(solution)/shard_map/ppermute | solution.py:179
  92.4 3.6 %collective-permute-start.23 = (f32[2,256]{1,0:T(2,128)S(1)}, f32[2,256]{1,0:T(2,128)S(1)}, u32[]{:S(2)}, u32[]{:S(2)}) collective-permute-start(f32[2,256]{1,0:T(2,128)S(1)} %add.29), channel_id=1, source_target_pairs={{0,8},{8,0},{16,24},{24,16},{1,9},{9,1},{17,25},{25,17},{2,10},{10... | collective-permute-start | bytes 6152 | tf_op jit(solution)/shard_map/ppermute | solution.py:179
  95.9 3.6 %collective-permute-start.24 = (f32[2,256]{1,0:T(2,128)S(1)}, f32[2,256]{1,0:T(2,128)S(1)}, u32[]{:S(2)}, u32[]{:S(2)}) collective-permute-start(f32[2,256]{1,0:T(2,128)S(1)} %add.30), channel_id=1, source_target_pairs={{0,16},{8,24},{16,0},{24,8},{1,17},{9,25},{17,1},{25,9},{2,18},{10... | collective-permute-start | bytes 6152 | tf_op jit(solution)/shard_map/ppermute | solution.py:179
  99.6 6.9 %collective-permute-start.19 = (bf16[128,512]{1,0:T(8,128)(2,1)S(1)}, bf16[128,512]{1,0:T(8,128)(2,1)S(1)}, u32[]{:S(2)}, u32[]{:S(2)}) collective-permute-start(bf16[128,512]{1,0:T(8,128)(2,1)S(1)} %sink.11), channel_id=1, source_target_pairs={{2,0},{3,1},{4,2},{5,3},{6,4},{7,5},{10,8},{11,9},{12,10},{13,11},... | collective-permute-start | bytes 393224 | tf_op jit(solution)/shard_map/ppermute | solution.py:179
  100.9 2.0 %copy-start = (bf16[1,128,1024]{2,1,0:T(8,128)(2,1)S(1)}, bf16[1,128,1024]{2,1,0:T(8,128)(2,1)}, u32[]{:S(2)}) copy-start(bf16[1,128,1024]{2,1,0:T(8,128)(2,1)} %refs_0_.19) | copy-start | bytes 786436
  101.0 7.5 %collective-permute-start.17 = (bf16[128,512]{1,0:T(8,128)(2,1)S(1)}, bf16[128,512]{1,0:T(8,128)(2,1)S(1)}, u32[]{:S(2)}, u32[]{:S(2)}) collective-permute-start(bf16[128,512]{1,0:T(8,128)(2,1)S(1)} %sink.10), channel_id=1, source_target_pairs={{2,0},{3,1},{4,2},{5,3},{6,4},{7,5},{10,8},{11,9},{12,10},{13,11},... | collective-permute-start | bytes 393224 | tf_op jit(solution)/shard_map/ppermute | solution.py:179

commit v3 on v2

--- a/solution.py
+++ b/solution.py
@@ -19,11 +19,13 @@
 CHUNKS = ((0, 1), (1, 1), (2, 1), (3, 1))
 LAG = 2
 
+PIECES = 4
+
 VMEM = pl.BlockSpec(memory_space=pltpu.VMEM)
 ANY = pl.BlockSpec(memory_space=pl.ANY)
 
 
-def call(body, name, ins, outs, after=(), flops=0, moved=2**18, in_specs=None, out_specs=None, **more):
+def call(body, name, ins, outs, after=(), cost=0, in_specs=None, out_specs=None, **more):
     names = list(ins)
 
     def kernel(*refs):
@@ -37,7 +39,7 @@
         in_specs=specs,
         out_specs=[(out_specs or {}).get(key, VMEM) for key in outs],
         compiler_params=pltpu.CompilerParams(vmem_limit_bytes=40 * 2**20),
-        cost_estimate=pl.CostEstimate(flops=flops, bytes_accessed=moved, transcendentals=0),
+        cost_estimate=pl.CostEstimate(flops=cost, bytes_accessed=1, transcendentals=0),
         name=name,
         **more,
     )(*ins.values(), *after)
@@ -57,8 +59,12 @@
     for index, ((first, count), (out, at)) in enumerate(zip(chunks, places)):
         here = pl.ds(first * HEAD_DIM, count * HEAD_DIM)
         for side, field in enumerate((keys, values)):
-            to = outs[out].at[:, pl.ds(at + side * count * HEAD_DIM, count * HEAD_DIM)]
-            copies.append(pltpu.make_async_copy(field.at[0, :, here], to, sems.at[2 * index + side]))
+            to = pl.ds(at + side * count * HEAD_DIM, count * HEAD_DIM)
+            for piece in range(PIECES):
+                share = field.shape[1] // PIECES
+                rows = pl.ds(piece * share, share)
+                sem = sems.at[(2 * index + side) * PIECES + piece]
+                copies.append(pltpu.make_async_copy(field.at[0, rows, here], outs[out].at[rows, to], sem))
     for copy in copies:
         copy.start()
     for copy in copies:
@@ -75,10 +81,10 @@
 
 
 def attend(
-    count, at_own, at_x, at_near, at_y, at_far, segments, queries, out_grad, own, across_x, arrived_near, across_y, arrived_far,
+    first, count, at_own, at_x, at_near, at_y, at_far, segments, queries, out_grad, own, across_x, arrived_near, across_y, arrived_far,
     query_gain, key_gain, *rest,
 ):
-    attended, query_grad, part_own, part_near, part_far, part_swap, gains = rest[-7:]
+    attended, query_grad, part_own, part_near, part_far, part_third, part_next, gains = rest
     position = lax.axis_index("ctx")
     rows = queries.shape[1]
     band = (GREACH + 1) * rows
@@ -113,12 +119,13 @@
         at_k = slice(head * HEAD_DIM, (head + 1) * HEAD_DIM)
         at_v = slice((count + head) * HEAD_DIM, (count + head + 1) * HEAD_DIM)
         at_q = [slice((head * GROUPS + g) * HEAD_DIM, (head * GROUPS + g + 1) * HEAD_DIM) for g in range(GROUPS)]
+        from_q = [slice(at.start + first * GROUPS * HEAD_DIM, at.stop + first * GROUPS * HEAD_DIM) for at in at_q]
         band_v = band_of(count + head)
         k_normed, _ = normalize(band_of(head).astype(F32))
         k_rounded = (k_normed * gain_k).astype(BF16)
-        q_normed, q_inverse = normalize(jnp.concatenate([queries[0, :, at] for at in at_q], 0).astype(F32))
+        q_normed, q_inverse = normalize(jnp.concatenate([queries[0, :, at] for at in from_q], 0).astype(F32))
         q_scaled = (q_normed * gain_q * HEAD_DIM ** (-0.5)).astype(BF16)
-        grads = jnp.concatenate([out_grad[0, :, at] for at in at_q], 0)
+        grads = jnp.concatenate([out_grad[0, :, at] for at in from_q], 0)
 
         scores = dot(q_scaled, k_rounded, (1, 1))
         weights = jnp.where(live, jnp.exp(scores), 0.0)
@@ -131,9 +138,9 @@
         value_parts = dot(probs_low, grads, (0, 0))
         for at, parts in ((at_k, key_parts), (at_v, value_parts)):
             part_far[:, at] = parts[:rows]
-            part_swap[:rows, at] = parts[rows : 2 * rows].astype(BF16)
+            part_third[:, at] = parts[rows : 2 * rows].astype(BF16)
             part_near[:, at] = parts[2 * rows : 3 * rows]
-            part_swap[rows:, at] = parts[3 * rows : 4 * rows].astype(BF16)
+            part_next[:, at] = parts[3 * rows : 4 * rows].astype(BF16)
             part_own[:, at] = parts[4 * rows :]
 
         output = dot(probs_low, band_v, (1, 0)).astype(BF16)
@@ -142,12 +149,23 @@
         grad = q_inverse * (scaled - q_normed * jnp.mean(scaled * q_normed, -1, keepdims=True))
         grad = grad.astype(BF16)
         for g, at in enumerate(at_q):
-            attended[0, :, at] = output[g * rows : (g + 1) * rows]
-            query_grad[0, :, at] = grad[g * rows : (g + 1) * rows]
+            attended[:, at] = output[g * rows : (g + 1) * rows]
+            query_grad[:, at] = grad[g * rows : (g + 1) * rows]
         query_gains = query_gains + jnp.sum(dq * q_normed, 0, keepdims=True)
         key_gains = key_gains + jnp.sum(key_parts * k_normed, 0, keepdims=True)
     gains[0:1, :] = query_gains
     gains[1:2, :] = key_gains
+
+
+def assemble(*refs):
+    amount = len(CHUNKS)
+    for index, out in enumerate(refs[-2:]):
+        for (first, count), part in zip(CHUNKS, refs[index * amount : (index + 1) * amount]):
+            out[0, :, first * GROUPS * HEAD_DIM : (first + count) * GROUPS * HEAD_DIM] = part[...]
+
+
+def add(left, right, out):
+    out[...] = left[...] + right[...]
 
 
 def finish(count, at, keys, key_gain, part_own, swapped, arrived, *rest):
@@ -159,7 +177,7 @@
         def total(index):
             here = slice(index * HEAD_DIM, (index + 1) * HEAD_DIM)
             there = slice(at + index * HEAD_DIM, at + (index + 1) * HEAD_DIM)
-            extra = jnp.where(core_index() == 0, swapped[rows:, here].astype(F32), 0.0)
+            extra = jnp.where(core_index() == 0, swapped[:, here].astype(F32), 0.0)
             return part_own[:, here] + extra + arrived[:, there].astype(F32)
 
         out = slice(head * HEAD_DIM, (head + 1) * HEAD_DIM)
@@ -191,10 +209,10 @@
     return move(field, "ctx", lambda i: i ^ 1)
 
 
-def total_over(field, axis):
-    step = 1
-    while step < lax.axis_size(axis):
-        field = field + move(field, axis, lambda i: i ^ step)
+def total_over(field, axis, first, last, after=()):
+    step = first
+    while step < min(last, lax.axis_size(axis)):
+        (field,) = call(add, "add", dict(a=field, b=move(field, axis, lambda i: i ^ step)), dict(o=field), after)
         step *= 2
     return field
 
@@ -217,7 +235,7 @@
             {i: shape(rows, wide) for i, wide in enumerate([sum(each)] if joined else each)},
             after,
             in_specs=dict(keys=ANY, values=ANY),
-            scratch_shapes=[pltpu.SemaphoreType.DMA((2 * len(chunks),))],
+            scratch_shapes=[pltpu.SemaphoreType.DMA((2 * len(chunks) * PIECES,))],
         )
 
     own = list(gather(CHUNKS[:LAG], joined=True))
@@ -236,7 +254,12 @@
             ins[key] = field
             return key, slice(at, at + width[chunk])
 
-        across = 0
+        def exchange(to, kept, chunk, first, second):
+            at = outs[to].shape[1] if to in outs else 0
+            jobs.append((to, at, use(first[chunk], chunk), use(second[chunk], chunk)))
+            outs[to] = shape(rows, at + width[chunk])
+            kept[chunk] = (to, at)
+
         for step in steps:
             rise = 0
             if step + LAG < amount:
@@ -245,15 +268,9 @@
             if step < amount:
                 jobs.append((f"rise{step}", rise, use(near[step], step), None))
                 outs[f"rise{step}"] = shape(rows, rise + width[step])
-                jobs.append(("across", across, use(own[step], step), use(near[step], step)))
-                next_behind[step] = across
-                across += width[step]
+                exchange("next", next_behind, step, own, near)
             if step >= LAG:
-                chunk = step - LAG
-                jobs.append(("across", across, use(near[chunk], chunk), use(far[chunk], chunk)))
-                third_behind[chunk] = across
-                across += width[chunk]
-        outs["across"] = shape(rows, across)
+                exchange("third", third_behind, step - LAG, near, far)
 
         def body(*refs):
             ref = dict(zip(list(ins) + list(outs), refs))
@@ -263,8 +280,8 @@
                     value = jnp.where(core_index() == 0, value, ref[other[0]][:, other[1]])
                 ref[to][:, at : at + value.shape[1]] = value
 
-        made = dict(zip(outs, call(body, "climb", ins, outs, after)))
-        exchanged = swap(made["across"])
+        made = dict(zip(outs, call(body, "climb", ins, outs, after, cost=10**9 * max(0, steps[0] - LAG))))
+        exchanged = {to: swap(made[to]) for to in ("next", "third") if to in made}
         for step in steps:
             if step < amount:
                 arrived = up(made[f"rise{step}"])
@@ -273,10 +290,10 @@
                     near[step + LAG] = (arrived, 0)
                     ahead = width[step + LAG]
                 far[step] = (arrived, ahead)
-                next_behind[step] = (exchanged, next_behind[step])
+                next_behind[step] = (exchanged["next"], next_behind[step][1])
             if step >= LAG:
-                third_behind[step - LAG] = (exchanged, third_behind[step - LAG])
-        return [made["across"]]
+                third_behind[step - LAG] = (exchanged["third"], third_behind[step - LAG][1])
+        return [next(iter(made.values()))]
 
     parts, sunk = [], {}
 
@@ -285,21 +302,20 @@
         mine, below = width[step], width[step - LAG] if older else 0
         ins = {}
         if fresh:
-            ins.update(far=parts[step]["far"], swapped=parts[step]["swap"])
+            ins.update(far=parts[step]["far"], third=parts[step]["third"])
         if older:
-            ins.update(
-                near=parts[step - LAG]["near"], swapped_old=parts[step - LAG]["swap"], arrived=sunk[step - LAG]
-            )
+            chunk = step - LAG
+            ins.update(near=parts[chunk]["near"], arrived=sunk[chunk])
+            ins.update(third_old=parts[chunk]["third"], next_old=parts[chunk]["next"])
 
         def body(*refs):
             ref = dict(zip(list(ins) + ["out"], refs))
             first = core_index() == 0
             if fresh:
-                extra = jnp.where(first, 0.0, ref["swapped"][:rows, :].astype(F32))
+                extra = jnp.where(first, 0.0, ref["third"][...].astype(F32))
                 ref["out"][:, :mine] = (ref["far"][...] + extra).astype(BF16)
             if older:
-                swapped = ref["swapped_old"]
-                extra = jnp.where(first, swapped[:rows, :], swapped[rows:, :]).astype(F32)
+                extra = jnp.where(first, ref["third_old"][...], ref["next_old"][...]).astype(F32)
                 arrived = ref["arrived"][:, :below].astype(F32)
                 ref["out"][:, mine:] = (ref["near"][...] + extra + arrived).astype(BF16)
 
@@ -307,62 +323,72 @@
         sunk[step] = down(total)
         return total
 
-    outputs, key_outputs, gains, last = [], [], 0.0, []
+    made, gains, last, token = [], [], [], []
     order = climb(range(LAG))
     for chunk, (first, count) in enumerate(CHUNKS):
-        order = climb([chunk + LAG], order)
-        wide = columns(rows, GROUPS * count * HEAD_DIM, GROUPS * first * HEAD_DIM)
+        order = climb([chunk + LAG], order + token + ([sunk[chunk - LAG]] if chunk >= LAG else []))
         held = (own, next_behind, near, third_behind, far)
-        *outputs, part_own, part_near, part_far, part_swap, chunk_gains = call(
-            functools.partial(attend, count, *(place[chunk][1] for place in held)),
+        wide = shape(rows, GROUPS * count * HEAD_DIM)
+        whole, low = shape(rows, width[chunk], F32), shape(rows, width[chunk])
+        result = call(
+            functools.partial(attend, first, count, *(place[chunk][1] for place in held)),
             "attend",
             dict(
                 segments=segment_ids, queries=queries, out_grad=out_grad, own=own[chunk][0],
                 **{f"behind{i}": place[chunk][0] for i, place in enumerate(held[1:])}, gain_q=gain_q, gain_k=gain_k,
             ),
             dict(
-                attended=jax.ShapeDtypeStruct(queries.shape, BF16),
-                query_grad=jax.ShapeDtypeStruct(queries.shape, BF16),
-                own=shape(rows, width[chunk], F32), near=shape(rows, width[chunk], F32),
-                far=shape(rows, width[chunk], F32), swap=shape(2 * rows, width[chunk]),
+                attended=wide, query_grad=wide, own=whole, near=whole, far=whole, third=low, next=low,
                 gains=shape(2, HEAD_DIM, F32),
             ),
-            [*outputs, *last, *([sunk[chunk - LAG]] if chunk >= LAG else [])],
-            flops=12 * GROUPS * rows * (GREACH + 1) * rows * count * HEAD_DIM,
-            moved=2**21,
-            grid=(1,),
-            in_specs=dict(queries=wide, out_grad=wide),
-            out_specs=dict(attended=wide, query_grad=wide),
-            input_output_aliases={10 + i: i for i in range(len(outputs))},
+            last,
         )
-        gains = gains + chunk_gains
-        parts.append(dict(own=part_own, near=part_near, far=part_far, swap=swap(part_swap)))
-        last = [sink(chunk)]
+        made.append(result[:2])
+        gains.append(result[7])
+        token = [result[7]]
+        parts.append(
+            dict(own=result[2], near=result[3], far=result[4], third=swap(result[5]), next=swap(result[6]))
+        )
+        last = [sink(chunk, last)]
 
     for step in range(amount, amount + LAG):
-        sink(step)
+        last = [sink(step, last)]
+    key_outputs = []
     for chunk, (first, count) in enumerate(CHUNKS):
         narrow = columns(rows, count * HEAD_DIM, first * HEAD_DIM)
         key_outputs = call(
             functools.partial(finish, count, width[chunk + LAG]),
             "finish",
             dict(
-                keys=keys, gain=gain_k, own=parts[chunk]["own"], swapped=parts[chunk]["swap"], arrived=sunk[chunk + LAG]
+                keys=keys, gain=gain_k, own=parts[chunk]["own"], next=parts[chunk]["next"], arrived=sunk[chunk + LAG]
             ),
             dict(
                 key_grad=jax.ShapeDtypeStruct(keys.shape, BF16), value_grad=jax.ShapeDtypeStruct(keys.shape, BF16)
             ),
             key_outputs,
+            cost=2**32,
             grid=(1,),
             in_specs=dict(keys=narrow),
             out_specs=dict(key_grad=narrow, value_grad=narrow),
             input_output_aliases={5 + i: i for i in range(len(key_outputs))},
         )
-
-    gains = total_over(total_over(gains, "ctx"), "dp")
+    attended, query_grad = call(
+        assemble,
+        "assemble",
+        {(i, chunk): made[chunk][i] for i in range(2) for chunk in range(amount)},
+        dict(a=jax.ShapeDtypeStruct(queries.shape, BF16), b=jax.ShapeDtypeStruct(queries.shape, BF16)),
+        last,
+    )
+
+    total = gains[0]
+    for more in gains[1:]:
+        (total,) = call(add, "add", dict(a=total, b=more), dict(o=more))
+    total = total_over(total, "dp", 1, lax.axis_size("dp"))
+    total = total_over(total, "ctx", 1, 2, last)
+    total = total_over(total, "ctx", 2, lax.axis_size("ctx"))
     factor = (lax.axis_size("dp") * queries.shape[0] * lax.axis_size("ctx") * rows) ** (-0.5)
-    gains = gains * factor
-    return *outputs, *key_outputs, gains[0], gains[1]
+    total = total * factor
+    return attended, query_grad, *key_outputs, total[0], total[1]
 
 
 def solution(mesh):

time: 110 us -> 87.3 us (0.79)
  waiting for transfers between devices: 54.1 us -> 31.3 us
  starting transfers between devices: 39.5 us -> 41.1 us
  Pallas kernels: 13.5 us -> 12.1 us
    ppermute x25 -> x31, waiting for transfers between devices: 54.1 us -> 31.3 us  [move(): lax.ppermute(field, axis, [(i, target(i)) for i in range(size) if 0 <= ta...]
    ppermute x25 -> x31, starting transfers between devices: 39.5 us -> 41.1 us  [move(): lax.ppermute(field, axis, [(i, target(i)) for i in range(size) if 0 <= ta...]
    pallas_call x21 -> x30, Pallas kernels: 13.5 us -> 12.1 us  [call(): pl.pallas_call(kernel, out_shape=list(outs.values()), in_specs=specs, out...]
  transfers between devices with their start and end apart: 25 -> 31, of which waited for: 16 -> 11; matrix products, arithmetic and copies ran while one was open for 1% -> 1% of each run, Pallas kernels for 5% -> 12%
where the time goes in v3:
time: 87.3 us; the launch traced here: 86.7 us
  starting transfers between devices  41.1 us (47%)
  waiting for transfers between devices  31.3 us (36%)
  Pallas kernels  12.1 us (14%)
  local copies, waits for them, and re-layouts  1.26 us (1%)
  between operations  0.98 us (1%)
    ppermute x31, starting transfers between devices, move(): lax.ppermute(field, axis, [(i, target(i)) for i in range(size) if 0 <= ta...  41.1 us
    ppermute x31, waiting for transfers between devices, move(): lax.ppermute(field, axis, [(i, target(i)) for i in range(size) if 0 <= ta...  31.3 us
    pallas_call x30, Pallas kernels, call(): pl.pallas_call(kernel, out_shape=list(outs.values()), in_specs=specs, out...  12.1 us
  transfers between devices with their start and end apart: 31, of which 11 were waited for; matrix products, arithmetic and copies ran while one was open for 1% of the time, Pallas kernels for 12%

profile of v3, /device:TPU:0, one launch (start us, length us, event | category | flops | bytes accessed | tf_op | source)
XLA Modules:
  0.0 86.7 jit_solution(4025753246041039278)
XLA Ops:
  0.6 1.0 %payload.2.refs_2_.refs_3_ = bf16[128,1024]{1,0:T(8,128)(2,1)S(1)} custom-call(bf16[1,128,1024]{2,1,0:T(8,128)(2,1)} %refs_0_.19, bf16[1,128,1024]{2,1,0:T(8,128)(2,1)} %refs_1_.7), custom_call_target="tpu_custom_call" | custom-call | bytes 1 | tf_op jit(solution)/shard_map/payload/pallas_call | solution.py:36
  1.7 4.9 %collective-permute-start = (bf16[128,1024]{1,0:T(8,128)(2,1)S(1)}, bf16[128,1024]{1,0:T(8,128)(2,1)S(1)}, u32[]{:S(2)}, u32[]{:S(2)}) collective-permute-start(bf16[128,1024]{1,0:T(8,128)(2,1)S(1)} %payload.2.refs_2_.refs_3_), channel_id=1, source_target_pairs={{0,2},{1,3},{2,4},{3,5},{4,6},{5,7},{8,10},{9,11},{10,12},{11,13},... | collective-permute-start | bytes 786440 | tf_op jit(solution)/shard_map/ppermute | solution.py:197
  6.6 1.0 %payload.3 = (bf16[128,512]{1,0:T(8,128)(2,1)S(1)}, bf16[128,512]{1,0:T(8,128)(2,1)S(1)}) custom-call(bf16[1,128,1024]{2,1,0:T(8,128)(2,1)} %refs_0_.19, bf16[1,128,1024]{2,1,0:T(8,128)(2,1)} %refs_1_.7, bf16[128,1024]{1,0:T(8,128)(2,1)S(1)} %payload.2.refs_2_.refs_3_), custom_call_target="tpu_custom_call" | custom-call | bytes 1 | tf_op jit(solution)/shard_map/payload/pallas_call | solution.py:36
  7.7 4.5 %collective-permute-done.refs_1_.refs_2_.refs_5_ = bf16[128,1024]{1,0:T(8,128)(2,1)S(1)} collective-permute-done((bf16[128,1024]{1,0:T(8,128)(2,1)S(1)}, bf16[128,1024]{1,0:T(8,128)(2,1)S(1)}, u32[]{:S(2)}, u32[]{:S(2)}) %collective-permute-start) | collective-permute-done | bytes 262176 | tf_op jit(solution)/shard_map/ppermute | solution.py:197
  12.2 4.5 %collective-permute-start.2 = (bf16[128,1024]{1,0:T(8,128)(2,1)S(1)}, bf16[128,1024]{1,0:T(8,128)(2,1)S(1)}, u32[]{:S(2)}, u32[]{:S(2)}) collective-permute-start(bf16[128,1024]{1,0:T(8,128)(2,1)S(1)} %get-tuple-element.62.refs_3_), channel_id=1, source_target_pairs={{0,2},{1,3},{2,4},{3,5},{4,6},{5,7},{8,10},{9,11},{10,12},{11,13},... | collective-permute-start | bytes 786440 | tf_op jit(solution)/shard_map/ppermute | solution.py:197
  16.9 3.5 %collective-permute-start.4 = (bf16[128,1024]{1,0:T(8,128)(2,1)S(1)}, bf16[128,1024]{1,0:T(8,128)(2,1)S(1)}, u32[]{:S(2)}, u32[]{:S(2)}) collective-permute-start(bf16[128,1024]{1,0:T(8,128)(2,1)S(1)} %get-tuple-element.65), channel_id=1, source_target_pairs={{0,2},{1,3},{2,4},{3,5},{4,6},{5,7},{8,10},{9,11},{10,12},{11,13},... | collective-permute-start | bytes 786440 | tf_op jit(solution)/shard_map/ppermute | solution.py:197
  20.3 1.5 %collective-permute-done.2.refs_0_.refs_7_.refs_5_ = bf16[128,1024]{1,0:T(8,128)(2,1)S(1)} collective-permute-done((bf16[128,1024]{1,0:T(8,128)(2,1)S(1)}, bf16[128,1024]{1,0:T(8,128)(2,1)S(1)}, u32[]{:S(2)}, u32[]{:S(2)}) %collective-permute-start.2) | collective-permute-done | bytes 262176 | tf_op jit(solution)/shard_map/ppermute | solution.py:197
  22.0 1.3 %collective-permute-done.3.refs_6_ = bf16[128,512]{1,0:T(8,128)(2,1)S(1)} collective-permute-done((bf16[128,512]{1,0:T(8,128)(2,1)S(1)}, bf16[128,512]{1,0:T(8,128)(2,1)S(1)}, u32[]{:S(2)}, u32[]{:S(2)}) %collective-permute-start.3) | collective-permute-done | bytes 131104 | tf_op jit(solution)/shard_map/ppermute | solution.py:197
  24.0 1.3 %attend.4 = (bf16[128,512]{1,0:T(8,128)(2,1)S(1)}, bf16[128,512]{1,0:T(8,128)(2,1)S(1)}, f32[128,512]{1,0:T(8,128)S(1)}, f32[128,512]{1,0:T(8,128)S(1)}, f32[128...) custom-call(s32[1,1024]{1,0:T(1,128)S(1)} %copy-done.3, ...), custom_call_target="tpu_custom_call" | custom-call | bytes 1 | tf_op jit(solution)/shard_map/attend/pallas_call | solution.py:36
  25.5 1.5 %collective-permute-done.4.refs_0_.refs_7_.refs_5_ = bf16[128,1024]{1,0:T(8,128)(2,1)S(1)} collective-permute-done((bf16[128,1024]{1,0:T(8,128)(2,1)S(1)}, bf16[128,1024]{1,0:T(8,128)(2,1)S(1)}, u32[]{:S(2)}, u32[]{:S(2)}) %collective-permute-start.4) | collective-permute-done | bytes 262176 | tf_op jit(solution)/shard_map/ppermute | solution.py:197
  27.2 4.4 %collective-permute-start.8 = (bf16[128,512]{1,0:T(8,128)(2,1)S(1)}, bf16[128,512]{1,0:T(8,128)(2,1)S(1)}, u32[]{:S(2)}, u32[]{:S(2)}) collective-permute-start(bf16[128,512]{1,0:T(8,128)(2,1)S(1)} %get-tuple-element.66.refs_3_), channel_id=1, source_target_pairs={{0,2},{1,3},{2,4},{3,5},{4,6},{5,7},{8,10},{9,11},{10,12},{11,13},... | collective-permute-start | bytes 393224 | tf_op jit(solution)/shard_map/ppermute | solution.py:197
  31.6 1.3 %collective-permute-start.9 = (bf16[128,512]{1,0:T(8,128)(2,1)S(1)}, bf16[128,512]{1,0:T(8,128)(2,1)S(1)}, u32[]{:S(2)}, u32[]{:S(2)}) collective-permute-start(bf16[128,512]{1,0:T(8,128)(2,1)S(1)} %sink.6.refs_10_.refs_2_), channel_id=1, source_target_pairs={{2,0},{3,1},{4,2},{5,3},{6,4},{7,5},{10,8},{11,9},{12,10},{13,11},... | collective-permute-start | bytes 393224 | tf_op jit(solution)/shard_map/ppermute | solution.py:197
  33.2 1.3 %attend.5 = (bf16[128,512]{1,0:T(8,128)(2,1)S(1)}, bf16[128,512]{1,0:T(8,128)(2,1)S(1)}, f32[128,512]{1,0:T(8,128)S(1)}, f32[128,512]{1,0:T(8,128)S(1)}, f32[128...) custom-call(s32[1,1024]{1,0:T(1,128)S(1)} %copy-done.3, ...), custom_call_target="tpu_custom_call" | custom-call | bytes 1 | tf_op jit(solution)/shard_map/attend/pallas_call | solution.py:36
  35.0 4.2 %collective-permute-done.9.refs_4_.refs_3_ = bf16[128,512]{1,0:T(8,128)(2,1)S(1)} collective-permute-done((bf16[128,512]{1,0:T(8,128)(2,1)S(1)}, bf16[128,512]{1,0:T(8,128)(2,1)S(1)}, u32[]{:S(2)}, u32[]{:S(2)}) %collective-permute-start.9) | collective-permute-done | bytes 131104 | tf_op jit(solution)/shard_map/ppermute | solution.py:197
  39.2 3.5 %collective-permute-start.13 = (bf16[128,512]{1,0:T(8,128)(2,1)S(1)}, bf16[128,512]{1,0:T(8,128)(2,1)S(1)}, u32[]{:S(2)}, u32[]{:S(2)}) collective-permute-start(bf16[128,512]{1,0:T(8,128)(2,1)S(1)} %get-tuple-element.73.refs_2_), channel_id=1, source_target_pairs={{0,2},{1,3},{2,4},{3,5},{4,6},{5,7},{8,10},{9,11},{10,12},{11,13},... | collective-permute-start | bytes 393224 | tf_op jit(solution)/shard_map/ppermute | solution.py:197
  42.8 1.3 %collective-permute-start.14 = (bf16[128,512]{1,0:T(8,128)(2,1)S(1)}, bf16[128,512]{1,0:T(8,128)(2,1)S(1)}, u32[]{:S(2)}, u32[]{:S(2)}) collective-permute-start(bf16[128,512]{1,0:T(8,128)(2,1)S(1)} %sink.7.refs_10_.refs_6_), channel_id=1, source_target_pairs={{2,0},{3,1},{4,2},{5,3},{6,4},{7,5},{10,8},{11,9},{12,10},{13,11},... | collective-permute-start | bytes 393224 | tf_op jit(solution)/shard_map/ppermute | solution.py:197
  44.7 1.2 %attend.6 = (bf16[128,512]{1,0:T(8,128)(2,1)S(1)}, bf16[128,512]{1,0:T(8,128)(2,1)S(1)}, f32[128,512]{1,0:T(8,128)S(1)}, f32[128,512]{1,0:T(8,128)S(1)}, f32[128...) custom-call(s32[1,1024]{1,0:T(1,128)S(1)} %copy-done.3, ...), custom_call_target="tpu_custom_call" | custom-call | bytes 1 | tf_op jit(solution)/shard_map/attend/pallas_call | solution.py:36
  46.2 4.1 %collective-permute-done.14.refs_4_.refs_3_ = bf16[128,512]{1,0:T(8,128)(2,1)S(1)} collective-permute-done((bf16[128,512]{1,0:T(8,128)(2,1)S(1)}, bf16[128,512]{1,0:T(8,128)(2,1)S(1)}, u32[]{:S(2)}, u32[]{:S(2)}) %collective-permute-start.14) | collective-permute-done | bytes 131104 | tf_op jit(solution)/shard_map/ppermute | solution.py:197
  50.5 1.3 %collective-permute-start.22 = (bf16[128,1024]{1,0:T(8,128)(2,1)S(1)}, bf16[128,1024]{1,0:T(8,128)(2,1)S(1)}, u32[]{:S(2)}, u32[]{:S(2)}) collective-permute-start(bf16[128,1024]{1,0:T(8,128)(2,1)S(1)} %sink.8.refs_10_.refs_6_), channel_id=1, source_target_pairs={{2,0},{3,1},{4,2},{5,3},{6,4},{7,5},{10,8},{11,9},{12,10},{13,11},... | collective-permute-start | bytes 786440 | tf_op jit(solution)/shard_map/ppermute | solution.py:197
  52.4 1.3 %attend.7 = (bf16[128,512]{1,0:T(8,128)(2,1)S(1)}, bf16[128,512]{1,0:T(8,128)(2,1)S(1)}, f32[128,512]{1,0:T(8,128)S(1)}, f32[128,512]{1,0:T(8,128)S(1)}, f32[128...) custom-call(s32[1,1024]{1,0:T(1,128)S(1)} %copy-done.3, ...), custom_call_target="tpu_custom_call" | custom-call | bytes 1 | tf_op jit(solution)/shard_map/attend/pallas_call | solution.py:36
  54.2 1.5 %collective-permute-start.26 = (f32[2,256]{1,0:T(2,128)S(1)}, f32[2,256]{1,0:T(2,128)S(1)}, u32[]{:S(2)}, u32[]{:S(2)}) collective-permute-start(f32[2,256]{1,0:T(2,128)S(1)} %add.10.refs_0_), channel_id=1, source_target_pairs={{0,8},{8,0},{16,24},{24,16},{1,9},{9,1},{17,25},{25,17},{2,10},{10... | collective-permute-start | bytes 6152 | tf_op jit(solution)/shard_map/ppermute | solution.py:197
  55.8 2.1 %collective-permute-done.26.refs_1_ = f32[2,256]{1,0:T(2,128)S(1)} collective-permute-done((f32[2,256]{1,0:T(2,128)S(1)}, f32[2,256]{1,0:T(2,128)S(1)}, u32[]{:S(2)}, u32[]{:S(2)}) %collective-permute-start.26) | collective-permute-done | bytes 2080 | tf_op jit(solution)/shard_map/ppermute | solution.py:197
  57.9 1.5 %collective-permute-start.27 = (f32[2,256]{1,0:T(2,128)S(1)}, f32[2,256]{1,0:T(2,128)S(1)}, u32[]{:S(2)}, u32[]{:S(2)}) collective-permute-start(f32[2,256]{1,0:T(2,128)S(1)} %add.11.refs_0_), channel_id=1, source_target_pairs={{0,16},{8,24},{16,0},{24,8},{1,17},{9,25},{17,1},{25,9},{2,18},{10... | collective-permute-start | bytes 6152 | tf_op jit(solution)/shard_map/ppermute | solution.py:197
  59.4 2.1 %collective-permute-done.27.refs_1_ = f32[2,256]{1,0:T(2,128)S(1)} collective-permute-done((f32[2,256]{1,0:T(2,128)S(1)}, f32[2,256]{1,0:T(2,128)S(1)}, u32[]{:S(2)}, u32[]{:S(2)}) %collective-permute-start.27) | collective-permute-done | bytes 2080 | tf_op jit(solution)/shard_map/ppermute | solution.py:197
  62.1 1.3 %collective-permute-start.20 = (bf16[128,1024]{1,0:T(8,128)(2,1)S(1)}, bf16[128,1024]{1,0:T(8,128)(2,1)S(1)}, u32[]{:S(2)}, u32[]{:S(2)}) collective-permute-start(bf16[128,1024]{1,0:T(8,128)(2,1)S(1)} %sink.9.refs_4_), channel_id=1, source_target_pairs={{2,0},{3,1},{4,2},{5,3},{6,4},{7,5},{10,8},{11,9},{12,10},{13,11},... | collective-permute-start | bytes 786440 | tf_op jit(solution)/shard_map/ppermute | solution.py:197
  63.5 1.3 %collective-permute-start.25 = (bf16[128,512]{1,0:T(8,128)(2,1)S(1)}, bf16[128,512]{1,0:T(8,128)(2,1)S(1)}, u32[]{:S(2)}, u32[]{:S(2)}) collective-permute-start(bf16[128,512]{1,0:T(8,128)(2,1)S(1)} %sink.10.refs_4_), channel_id=1, source_target_pairs={{2,0},{3,1},{4,2},{5,3},{6,4},{7,5},{10,8},{11,9},{12,10},{13,11},... | collective-permute-start | bytes 393224 | tf_op jit(solution)/shard_map/ppermute | solution.py:197
  65.6 7.8 %collective-permute-done.20.refs_1_.refs_4_ = bf16[128,1024]{1,0:T(8,128)(2,1)S(1)} collective-permute-done((bf16[128,1024]{1,0:T(8,128)(2,1)S(1)}, bf16[128,1024]{1,0:T(8,128)(2,1)S(1)}, u32[]{:S(2)}, u32[]{:S(2)}) %collective-permute-start.20) | collective-permute-done | bytes 262176 | tf_op jit(solution)/shard_map/ppermute | solution.py:197
  73.5 1.3 %collective-permute-start.24 = (bf16[128,512]{1,0:T(8,128)(2,1)S(1)}, bf16[128,512]{1,0:T(8,128)(2,1)S(1)}, u32[]{:S(2)}, u32[]{:S(2)}) collective-permute-start(bf16[128,512]{1,0:T(8,128)(2,1)S(1)} %sink.11.refs_8_.refs_2_), channel_id=1, source_target_pairs={{2,0},{3,1},{4,2},{5,3},{6,4},{7,5},{10,8},{11,9},{12,10},{13,11},... | collective-permute-start | bytes 393224 | tf_op jit(solution)/shard_map/ppermute | solution.py:197
  74.8 2.7 %collective-permute-start.29 = (f32[2,256]{1,0:T(2,128)S(1)}, f32[2,256]{1,0:T(2,128)S(1)}, u32[]{:S(2)}, u32[]{:S(2)}) collective-permute-start(f32[2,256]{1,0:T(2,128)S(1)} %add.13.refs_0_), channel_id=1, source_target_pairs={{0,2},{1,3},{2,0},{3,1},{4,6},{5,7},{6,4},{7,5},{8,10},{9,11},{10,... | collective-permute-start | bytes 6152 | tf_op jit(solution)/shard_map/ppermute | solution.py:197
  78.4 2.0 %collective-permute-done.29.refs_1_ = f32[2,256]{1,0:T(2,128)S(1)} collective-permute-done((f32[2,256]{1,0:T(2,128)S(1)}, f32[2,256]{1,0:T(2,128)S(1)}, u32[]{:S(2)}, u32[]{:S(2)}) %collective-permute-start.29) | collective-permute-done | bytes 2080 | tf_op jit(solution)/shard_map/ppermute | solution.py:197
  80.4 3.0 %collective-permute-start.30 = (f32[2,256]{1,0:T(2,128)S(1)}, f32[2,256]{1,0:T(2,128)S(1)}, u32[]{:S(2)}, u32[]{:S(2)}) collective-permute-start(f32[2,256]{1,0:T(2,128)S(1)} %add.14.refs_0_), channel_id=1, source_target_pairs={{0,4},{1,5},{2,6},{3,7},{4,0},{5,1},{6,2},{7,3},{8,12},{9,13},{10,... | collective-permute-start | bytes 6152 | tf_op jit(solution)/shard_map/ppermute | solution.py:197
  84.3 1.0 %assemble.1 = (bf16[1,128,2048]{2,1,0:T(8,128)(2,1)}, bf16[1,128,2048]{2,1,0:T(8,128)(2,1)}) custom-call(bf16[128,512]{1,0:T(8,128)(2,1)S(1)} %get-tuple-element.64.refs_0_, bf16[128,512]{1,0:T(8,128)(2,1)S(1)} %get-tuple-element.71.refs_1_, bf16[128,512]{1,0:T(8,128)(2,1)S(1)} %get-tuple-element.77.refs_2_, bf16[128,512]{1,0:T(8,128)(2,1)S(1)} %get-tuple-element.84.refs_3_, ...), custom_call_target="tpu_custom_call" | custom-call | bytes 1 | tf_op jit(solution)/shard_map/assemble/pallas_call | solution.py:36
  (74 shorter events, 9.0 us)
Async XLA Ops:
  1.7 10.5 %collective-permute-start = (bf16[128,1024]{1,0:T(8,128)(2,1)S(1)}, bf16[128,1024]{1,0:T(8,128)(2,1)S(1)}, u32[]{:S(2)}, u32[]{:S(2)}) collective-permute-start(bf16[128,1024]{1,0:T(8,128)(2,1)S(1)} %payload.2.refs_2_.refs_3_), channel_id=1, source_target_pairs={{0,2},{1,3},{2,4},{3,5},{4,6},{5,7},{8,10},{9,11},{10,12},{11,13},... | collective-permute-start | bytes 786440 | tf_op jit(solution)/shard_map/ppermute | solution.py:197
  12.2 11.2 %copy-start.1 = (bf16[1,128,2048]{2,1,0:T(8,128)(2,1)S(1)}, bf16[1,128,2048]{2,1,0:T(8,128)(2,1)}, u32[]{:S(2)}) copy-start(bf16[1,128,2048]{2,1,0:T(8,128)(2,1)} %refs_2_.7) | copy-start | bytes 1572868
  12.2 9.7 %collective-permute-start.2 = (bf16[128,1024]{1,0:T(8,128)(2,1)S(1)}, bf16[128,1024]{1,0:T(8,128)(2,1)S(1)}, u32[]{:S(2)}, u32[]{:S(2)}) collective-permute-start(bf16[128,1024]{1,0:T(8,128)(2,1)S(1)} %get-tuple-element.62.refs_3_), channel_id=1, source_target_pairs={{0,2},{1,3},{2,4},{3,5},{4,6},{5,7},{8,10},{9,11},{10,12},{11,13},... | collective-permute-start | bytes 786440 | tf_op jit(solution)/shard_map/ppermute | solution.py:197
  16.8 5.2 %collective-permute-start.1 = (bf16[128,1024]{1,0:T(8,128)(2,1)S(1)}, bf16[128,1024]{1,0:T(8,128)(2,1)S(1)}, u32[]{:S(2)}, u32[]{:S(2)}) collective-permute-start(bf16[128,1024]{1,0:T(8,128)(2,1)S(1)} %get-tuple-element.61), channel_id=1, source_target_pairs={{0,1},{1,0},{2,3},{3,2},{4,5},{5,4},{6,7},{7,6},{8,9},{9,8},{10,11... | collective-permute-start | bytes 786440 | tf_op jit(solution)/shard_map/ppermute | solution.py:197
  16.9 10.2 %collective-permute-start.4 = (bf16[128,1024]{1,0:T(8,128)(2,1)S(1)}, bf16[128,1024]{1,0:T(8,128)(2,1)S(1)}, u32[]{:S(2)}, u32[]{:S(2)}) collective-permute-start(bf16[128,1024]{1,0:T(8,128)(2,1)S(1)} %get-tuple-element.65), channel_id=1, source_target_pairs={{0,2},{1,3},{2,4},{3,5},{4,6},{5,7},{8,10},{9,11},{10,12},{11,13},... | collective-permute-start | bytes 786440 | tf_op jit(solution)/shard_map/ppermute | solution.py:197
  21.9 1.4 %collective-permute-start.3 = (bf16[128,512]{1,0:T(8,128)(2,1)S(1)}, bf16[128,512]{1,0:T(8,128)(2,1)S(1)}, u32[]{:S(2)}, u32[]{:S(2)}) collective-permute-start(bf16[128,512]{1,0:T(8,128)(2,1)S(1)} %get-tuple-element.63), channel_id=1, source_target_pairs={{0,1},{1,0},{2,3},{3,2},{4,5},{5,4},{6,7},{7,6},{8,9},{9,8},{10,11... | collective-permute-start | bytes 393224 | tf_op jit(solution)/shard_map/ppermute | solution.py:197
  25.3 6.3 %collective-permute-start.6 = (bf16[128,512]{1,0:T(8,128)(2,1)S(1)}, bf16[128,512]{1,0:T(8,128)(2,1)S(1)}, u32[]{:S(2)}, u32[]{:S(2)}) collective-permute-start(bf16[128,512]{1,0:T(8,128)(2,1)S(1)} %get-tuple-element.70), channel_id=1, source_target_pairs={{0,1},{1,0},{2,3},{3,2},{4,5},{5,4},{6,7},{7,6},{8,9},{9,8},{10,11... | collective-permute-start | bytes 393224 | tf_op jit(solution)/shard_map/ppermute | solution.py:197
  27.1 6.1 %collective-permute-start.5 = (bf16[128,512]{1,0:T(8,128)(2,1)S(1)}, bf16[128,512]{1,0:T(8,128)(2,1)S(1)}, u32[]{:S(2)}, u32[]{:S(2)}) collective-permute-start(bf16[128,512]{1,0:T(8,128)(2,1)S(1)} %get-tuple-element.68), channel_id=1, source_target_pairs={{0,1},{1,0},{2,3},{3,2},{4,5},{5,4},{6,7},{7,6},{8,9},{9,8},{10,11... | collective-permute-start | bytes 393224 | tf_op jit(solution)/shard_map/ppermute | solution.py:197
  27.2 7.8 %collective-permute-start.8 = (bf16[128,512]{1,0:T(8,128)(2,1)S(1)}, bf16[128,512]{1,0:T(8,128)(2,1)S(1)}, u32[]{:S(2)}, u32[]{:S(2)}) collective-permute-start(bf16[128,512]{1,0:T(8,128)(2,1)S(1)} %get-tuple-element.66.refs_3_), channel_id=1, source_target_pairs={{0,2},{1,3},{2,4},{3,5},{4,6},{5,7},{8,10},{9,11},{10,12},{11,13},... | collective-permute-start | bytes 393224 | tf_op jit(solution)/shard_map/ppermute | solution.py:197
  31.6 7.5 %collective-permute-start.9 = (bf16[128,512]{1,0:T(8,128)(2,1)S(1)}, bf16[128,512]{1,0:T(8,128)(2,1)S(1)}, u32[]{:S(2)}, u32[]{:S(2)}) collective-permute-start(bf16[128,512]{1,0:T(8,128)(2,1)S(1)} %sink.6.refs_10_.refs_2_), channel_id=1, source_target_pairs={{2,0},{3,1},{4,2},{5,3},{6,4},{7,5},{10,8},{11,9},{12,10},{13,11},... | collective-permute-start | bytes 393224 | tf_op jit(solution)/shard_map/ppermute | solution.py:197
  32.9 11.4 %collective-permute-start.7 = (bf16[128,512]{1,0:T(8,128)(2,1)S(1)}, bf16[128,512]{1,0:T(8,128)(2,1)S(1)}, u32[]{:S(2)}, u32[]{:S(2)}) collective-permute-start(bf16[128,512]{1,0:T(8,128)(2,1)S(1)} %get-tuple-element.72), channel_id=1, source_target_pairs={{0,1},{1,0},{2,3},{3,2},{4,5},{5,4},{6,7},{7,6},{8,9},{9,8},{10,11... | collective-permute-start | bytes 393224 | tf_op jit(solution)/shard_map/ppermute | solution.py:197
  34.5 8.2 %collective-permute-start.11 = (bf16[128,512]{1,0:T(8,128)(2,1)S(1)}, bf16[128,512]{1,0:T(8,128)(2,1)S(1)}, u32[]{:S(2)}, u32[]{:S(2)}) collective-permute-start(bf16[128,512]{1,0:T(8,128)(2,1)S(1)} %get-tuple-element.76), channel_id=1, source_target_pairs={{0,1},{1,0},{2,3},{3,2},{4,5},{5,4},{6,7},{7,6},{8,9},{9,8},{10,11... | collective-permute-start | bytes 393224 | tf_op jit(solution)/shard_map/ppermute | solution.py:197
  39.2 5.5 %collective-permute-start.10 = (bf16[128,512]{1,0:T(8,128)(2,1)S(1)}, bf16[128,512]{1,0:T(8,128)(2,1)S(1)}, u32[]{:S(2)}, u32[]{:S(2)}) collective-permute-start(bf16[128,512]{1,0:T(8,128)(2,1)S(1)} %climb.8.refs_2_), channel_id=1, source_target_pairs={{0,1},{1,0},{2,3},{3,2},{4,5},{5,4},{6,7},{7,6},{8,9},{9,8},{10,11... | collective-permute-start | bytes 393224 | tf_op jit(solution)/shard_map/ppermute | solution.py:197
  39.2 7.0 %collective-permute-start.13 = (bf16[128,512]{1,0:T(8,128)(2,1)S(1)}, bf16[128,512]{1,0:T(8,128)(2,1)S(1)}, u32[]{:S(2)}, u32[]{:S(2)}) collective-permute-start(bf16[128,512]{1,0:T(8,128)(2,1)S(1)} %get-tuple-element.73.refs_2_), channel_id=1, source_target_pairs={{0,2},{1,3},{2,4},{3,5},{4,6},{5,7},{8,10},{9,11},{10,12},{11,13},... | collective-permute-start | bytes 393224 | tf_op jit(solution)/shard_map/ppermute | solution.py:197
  42.8 7.5 %collective-permute-start.14 = (bf16[128,512]{1,0:T(8,128)(2,1)S(1)}, bf16[128,512]{1,0:T(8,128)(2,1)S(1)}, u32[]{:S(2)}, u32[]{:S(2)}) collective-permute-start(bf16[128,512]{1,0:T(8,128)(2,1)S(1)} %sink.7.refs_10_.refs_6_), channel_id=1, source_target_pairs={{2,0},{3,1},{4,2},{5,3},{6,4},{7,5},{10,8},{11,9},{12,10},{13,11},... | collective-permute-start | bytes 393224 | tf_op jit(solution)/shard_map/ppermute | solution.py:197
  44.1 6.3 %collective-permute-start.17 = (bf16[128,512]{1,0:T(8,128)(2,1)S(1)}, bf16[128,512]{1,0:T(8,128)(2,1)S(1)}, u32[]{:S(2)}, u32[]{:S(2)}) collective-permute-start(bf16[128,512]{1,0:T(8,128)(2,1)S(1)} %get-tuple-element.83), channel_id=1, source_target_pairs={{0,1},{1,0},{2,3},{3,2},{4,5},{5,4},{6,7},{7,6},{8,9},{9,8},{10,11... | collective-permute-start | bytes 393224 | tf_op jit(solution)/shard_map/ppermute | solution.py:197
  44.4 8.0 %collective-permute-start.12 = (bf16[128,512]{1,0:T(8,128)(2,1)S(1)}, bf16[128,512]{1,0:T(8,128)(2,1)S(1)}, u32[]{:S(2)}, u32[]{:S(2)}) collective-permute-start(bf16[128,512]{1,0:T(8,128)(2,1)S(1)} %get-tuple-element.78), channel_id=1, source_target_pairs={{0,1},{1,0},{2,3},{3,2},{4,5},{5,4},{6,7},{7,6},{8,9},{9,8},{10,11... | collective-permute-start | bytes 393224 | tf_op jit(solution)/shard_map/ppermute | solution.py:197
  45.9 4.5 %collective-permute-start.16 = (bf16[128,512]{1,0:T(8,128)(2,1)S(1)}, bf16[128,512]{1,0:T(8,128)(2,1)S(1)}, u32[]{:S(2)}, u32[]{:S(2)}) collective-permute-start(bf16[128,512]{1,0:T(8,128)(2,1)S(1)} %get-tuple-element.81), channel_id=1, source_target_pairs={{0,1},{1,0},{2,3},{3,2},{4,5},{5,4},{6,7},{7,6},{8,9},{9,8},{10,11... | collective-permute-start | bytes 393224 | tf_op jit(solution)/shard_map/ppermute | solution.py:197
  50.3 2.0 %collective-permute-start.15 = (bf16[128,512]{1,0:T(8,128)(2,1)S(1)}, bf16[128,512]{1,0:T(8,128)(2,1)S(1)}, u32[]{:S(2)}, u32[]{:S(2)}) collective-permute-start(bf16[128,512]{1,0:T(8,128)(2,1)S(1)} %climb.9), channel_id=1, source_target_pairs={{0,1},{1,0},{2,3},{3,2},{4,5},{5,4},{6,7},{7,6},{8,9},{9,8},{10,11... | collective-permute-start | bytes 393224 | tf_op jit(solution)/shard_map/ppermute | solution.py:197
  50.5 12.9 %collective-permute-start.22 = (bf16[128,1024]{1,0:T(8,128)(2,1)S(1)}, bf16[128,1024]{1,0:T(8,128)(2,1)S(1)}, u32[]{:S(2)}, u32[]{:S(2)}) collective-permute-start(bf16[128,1024]{1,0:T(8,128)(2,1)S(1)} %sink.8.refs_10_.refs_6_), channel_id=1, source_target_pairs={{2,0},{3,1},{4,2},{5,3},{6,4},{7,5},{10,8},{11,9},{12,10},{13,11},... | collective-permute-start | bytes 786440 | tf_op jit(solution)/shard_map/ppermute | solution.py:197
  51.8 9.7 %collective-permute-start.19 = (bf16[128,512]{1,0:T(8,128)(2,1)S(1)}, bf16[128,512]{1,0:T(8,128)(2,1)S(1)}, u32[]{:S(2)}, u32[]{:S(2)}) collective-permute-start(bf16[128,512]{1,0:T(8,128)(2,1)S(1)} %get-tuple-element.93), channel_id=1, source_target_pairs={{0,1},{1,0},{2,3},{3,2},{4,5},{5,4},{6,7},{7,6},{8,9},{9,8},{10,11... | collective-permute-start | bytes 393224 | tf_op jit(solution)/shard_map/ppermute | solution.py:197
  53.6 8.3 %collective-permute-start.18 = (bf16[128,512]{1,0:T(8,128)(2,1)S(1)}, bf16[128,512]{1,0:T(8,128)(2,1)S(1)}, u32[]{:S(2)}, u32[]{:S(2)}) collective-permute-start(bf16[128,512]{1,0:T(8,128)(2,1)S(1)} %get-tuple-element.91), channel_id=1, source_target_pairs={{0,1},{1,0},{2,3},{3,2},{4,5},{5,4},{6,7},{7,6},{8,9},{9,8},{10,11... | collective-permute-start | bytes 393224 | tf_op jit(solution)/shard_map/ppermute | solution.py:197
  53.7 9.6 %collective-permute-start.23 = (bf16[128,512]{1,0:T(8,128)(2,1)S(1)}, bf16[128,512]{1,0:T(8,128)(2,1)S(1)}, u32[]{:S(2)}, u32[]{:S(2)}) collective-permute-start(bf16[128,512]{1,0:T(8,128)(2,1)S(1)} %get-tuple-element.96), channel_id=1, source_target_pairs={{0,1},{1,0},{2,3},{3,2},{4,5},{5,4},{6,7},{7,6},{8,9},{9,8},{10,11... | collective-permute-start | bytes 393224 | tf_op jit(solution)/shard_map/ppermute | solution.py:197
  54.2 3.6 %collective-permute-start.26 = (f32[2,256]{1,0:T(2,128)S(1)}, f32[2,256]{1,0:T(2,128)S(1)}, u32[]{:S(2)}, u32[]{:S(2)}) collective-permute-start(f32[2,256]{1,0:T(2,128)S(1)} %add.10.refs_0_), channel_id=1, source_target_pairs={{0,8},{8,0},{16,24},{24,16},{1,9},{9,1},{17,25},{25,17},{2,10},{10... | collective-permute-start | bytes 6152 | tf_op jit(solution)/shard_map/ppermute | solution.py:197
  57.9 3.6 %collective-permute-start.27 = (f32[2,256]{1,0:T(2,128)S(1)}, f32[2,256]{1,0:T(2,128)S(1)}, u32[]{:S(2)}, u32[]{:S(2)}) collective-permute-start(f32[2,256]{1,0:T(2,128)S(1)} %add.11.refs_0_), channel_id=1, source_target_pairs={{0,16},{8,24},{16,0},{24,8},{1,17},{9,25},{17,1},{25,9},{2,18},{10... | collective-permute-start | bytes 6152 | tf_op jit(solution)/shard_map/ppermute | solution.py:197
  61.5 4.1 %collective-permute-start.21 = (bf16[128,512]{1,0:T(8,128)(2,1)S(1)}, bf16[128,512]{1,0:T(8,128)(2,1)S(1)}, u32[]{:S(2)}, u32[]{:S(2)}) collective-permute-start(bf16[128,512]{1,0:T(8,128)(2,1)S(1)} %get-tuple-element.94), channel_id=1, source_target_pairs={{0,1},{1,0},{2,3},{3,2},{4,5},{5,4},{6,7},{7,6},{8,9},{9,8},{10,11... | collective-permute-start | bytes 393224 | tf_op jit(solution)/shard_map/ppermute | solution.py:197
  61.5 13.3 %collective-permute-start.28 = (f32[2,256]{1,0:T(2,128)S(1)}, f32[2,256]{1,0:T(2,128)S(1)}, u32[]{:S(2)}, u32[]{:S(2)}) collective-permute-start(f32[2,256]{1,0:T(2,128)S(1)} %add.12.refs_0_), channel_id=1, source_target_pairs={{0,1},{1,0},{2,3},{3,2},{4,5},{5,4},{6,7},{7,6},{8,9},{9,8},{10,11... | collective-permute-start | bytes 6152 | tf_op jit(solution)/shard_map/ppermute | solution.py:197
  62.1 11.4 %collective-permute-start.20 = (bf16[128,1024]{1,0:T(8,128)(2,1)S(1)}, bf16[128,1024]{1,0:T(8,128)(2,1)S(1)}, u32[]{:S(2)}, u32[]{:S(2)}) collective-permute-start(bf16[128,1024]{1,0:T(8,128)(2,1)S(1)} %sink.9.refs_4_), channel_id=1, source_target_pairs={{2,0},{3,1},{4,2},{5,3},{6,4},{7,5},{10,8},{11,9},{12,10},{13,11},... | collective-permute-start | bytes 786440 | tf_op jit(solution)/shard_map/ppermute | solution.py:197
  63.5 20.0 %collective-permute-start.25 = (bf16[128,512]{1,0:T(8,128)(2,1)S(1)}, bf16[128,512]{1,0:T(8,128)(2,1)S(1)}, u32[]{:S(2)}, u32[]{:S(2)}) collective-permute-start(bf16[128,512]{1,0:T(8,128)(2,1)S(1)} %sink.10.refs_4_), channel_id=1, source_target_pairs={{2,0},{3,1},{4,2},{5,3},{6,4},{7,5},{10,8},{11,9},{12,10},{13,11},... | collective-permute-start | bytes 393224 | tf_op jit(solution)/shard_map/ppermute | solution.py:197
  73.5 12.4 %collective-permute-start.24 = (bf16[128,512]{1,0:T(8,128)(2,1)S(1)}, bf16[128,512]{1,0:T(8,128)(2,1)S(1)}, u32[]{:S(2)}, u32[]{:S(2)}) collective-permute-start(bf16[128,512]{1,0:T(8,128)(2,1)S(1)} %sink.11.refs_8_.refs_2_), channel_id=1, source_target_pairs={{2,0},{3,1},{4,2},{5,3},{6,4},{7,5},{10,8},{11,9},{12,10},{13,11},... | collective-permute-start | bytes 393224 | tf_op jit(solution)/shard_map/ppermute | solution.py:197
  74.8 5.6 %collective-permute-start.29 = (f32[2,256]{1,0:T(2,128)S(1)}, f32[2,256]{1,0:T(2,128)S(1)}, u32[]{:S(2)}, u32[]{:S(2)}) collective-permute-start(f32[2,256]{1,0:T(2,128)S(1)} %add.13.refs_0_), channel_id=1, source_target_pairs={{0,2},{1,3},{2,0},{3,1},{4,6},{5,7},{6,4},{7,5},{8,10},{9,11},{10,... | collective-permute-start | bytes 6152 | tf_op jit(solution)/shard_map/ppermute | solution.py:197
  80.4 4.9 %collective-permute-start.30 = (f32[2,256]{1,0:T(2,128)S(1)}, f32[2,256]{1,0:T(2,128)S(1)}, u32[]{:S(2)}, u32[]{:S(2)}) collective-permute-start(f32[2,256]{1,0:T(2,128)S(1)} %add.14.refs_0_), channel_id=1, source_target_pairs={{0,4},{1,5},{2,6},{3,7},{4,0},{5,1},{6,2},{7,3},{8,12},{9,13},{10,... | collective-permute-start | bytes 6152 | tf_op jit(solution)/shard_map/ppermute | solution.py:197
  (5 other events, 16.1 us)

commit v4 on v3

--- a/solution.py
+++ b/solution.py
@@ -16,7 +16,7 @@
 EPSILON = 1e-06
 BF16 = jnp.bfloat16
 F32 = jnp.float32
-CHUNKS = ((0, 1), (1, 1), (2, 1), (3, 1))
+CHUNKS = ((0, 2), (2, 2))
 LAG = 2
 
 PIECES = 4
@@ -53,18 +53,19 @@
     return lax.axis_index("ctx") % 2
 
 
-def payload(chunks, places, keys, values, *rest):
-    outs, sems = rest[:-1], rest[-1]
-    copies = []
-    for index, ((first, count), (out, at)) in enumerate(zip(chunks, places)):
+def payload(chunks, keys, values, *rest):
+    extra = len(rest[:-1]) - len(chunks)
+    small, outs, kept, sems = rest[: extra // 2], rest[extra // 2 : -1 - extra // 2], rest[-1 - extra // 2 : -1], rest[-1]
+    copies = [pltpu.make_async_copy(old, new, sems.at[i]) for i, (old, new) in enumerate(zip(small, kept))]
+    for (first, count), out in zip(chunks, outs):
         here = pl.ds(first * HEAD_DIM, count * HEAD_DIM)
         for side, field in enumerate((keys, values)):
-            to = pl.ds(at + side * count * HEAD_DIM, count * HEAD_DIM)
+            to = pl.ds(side * count * HEAD_DIM, count * HEAD_DIM)
             for piece in range(PIECES):
                 share = field.shape[1] // PIECES
                 rows = pl.ds(piece * share, share)
-                sem = sems.at[(2 * index + side) * PIECES + piece]
-                copies.append(pltpu.make_async_copy(field.at[0, rows, here], outs[out].at[rows, to], sem))
+                sem = sems.at[len(copies)]
+                copies.append(pltpu.make_async_copy(field.at[0, rows, here], out.at[rows, to], sem))
     for copy in copies:
         copy.start()
     for copy in copies:
@@ -81,10 +82,10 @@
 
 
 def attend(
-    first, count, at_own, at_x, at_near, at_y, at_far, segments, queries, out_grad, own, across_x, arrived_near, across_y, arrived_far,
-    query_gain, key_gain, *rest,
+    first, count, at_own, at_x, at_near, at_far, segments, queries, out_grad, own, across_x, arrived_near, arrived_far,
+    across_k, across_v,    query_gain, key_gain, *rest,
 ):
-    attended, query_grad, part_own, part_near, part_far, part_third, part_next, gains = rest
+    attended, query_grad, part_own, part_near, part_far, third_k, third_v, part_next, gains = rest
     position = lax.axis_index("ctx")
     rows = queries.shape[1]
     band = (GREACH + 1) * rows
@@ -108,9 +109,10 @@
 
     query_gains = jnp.zeros((1, HEAD_DIM), F32)
     key_gains = jnp.zeros((1, HEAD_DIM), F32)
-    blocks = ((arrived_far, at_far), (across_y, at_y), (arrived_near, at_near), (across_x, at_x), (own, at_own))
 
     def band_of(index):
+        third = (across_k, 0) if index < count else (across_v, -count * HEAD_DIM)
+        blocks = ((arrived_far, at_far), third, (arrived_near, at_near), (across_x, at_x), (own, at_own))
         return jnp.concatenate(
             [field[:, at + index * HEAD_DIM : at + (index + 1) * HEAD_DIM] for field, at in blocks], 0
         )
@@ -136,9 +138,9 @@
         dscore = (probs * (dprob - centre)).astype(BF16)
         key_parts = dot(dscore, q_scaled, (0, 0))
         value_parts = dot(probs_low, grads, (0, 0))
-        for at, parts in ((at_k, key_parts), (at_v, value_parts)):
+        for at, parts, third in ((at_k, key_parts, third_k), (at_v, value_parts, third_v)):
             part_far[:, at] = parts[:rows]
-            part_third[:, at] = parts[rows : 2 * rows].astype(BF16)
+            third[:, at_k] = parts[rows : 2 * rows].astype(BF16)
             part_near[:, at] = parts[2 * rows : 3 * rows]
             part_next[:, at] = parts[3 * rows : 4 * rows].astype(BF16)
             part_own[:, at] = parts[4 * rows :]
@@ -164,8 +166,13 @@
             out[0, :, first * GROUPS * HEAD_DIM : (first + count) * GROUPS * HEAD_DIM] = part[...]
 
 
-def add(left, right, out):
-    out[...] = left[...] + right[...]
+def add(*refs):
+    refs[-1][...] = sum(ref[...] for ref in refs[1:-1]) + refs[0][...]
+
+
+def scale(factor, total, query_gains, key_gains):
+    query_gains[...] = total[0:1, :] * factor
+    key_gains[...] = total[1:2, :] * factor
 
 
 def finish(count, at, keys, key_gain, part_own, swapped, arrived, *rest):
@@ -209,11 +216,12 @@
     return move(field, "ctx", lambda i: i ^ 1)
 
 
-def total_over(field, axis, first, last, after=()):
-    step = first
-    while step < min(last, lax.axis_size(axis)):
-        (field,) = call(add, "add", dict(a=field, b=move(field, axis, lambda i: i ^ step)), dict(o=field), after)
-        step *= 2
+def total_over(field, axis, unit, most, after=()):
+    while unit < lax.axis_size(axis):
+        group = min(most, lax.axis_size(axis) // unit)
+        others = [move(field, axis, lambda i: i ^ (by * unit)) for by in range(1, group)]
+        (field,) = call(add, "add", dict(enumerate([field, *others])), dict(o=shape(*field.shape, F32)), after)
+        unit *= group
     return field
 
 
@@ -223,26 +231,30 @@
     gain_k = key_gain.reshape(1, HEAD_DIM)
     amount = len(CHUNKS)
     width = [2 * count * HEAD_DIM for _, count in CHUNKS] + [0] * LAG
-    pinned = [pltpu.with_memory_space_constraint(field, pltpu.HBM) for field in (keys, values)]
-
-    def gather(chunks, after=(), joined=False):
-        each = [2 * count * HEAD_DIM for _, count in chunks]
-        places = [(0, sum(each[:i])) if joined else (i, 0) for i in range(len(chunks))]
-        return call(
-            functools.partial(payload, chunks, places),
+    def gather(chunks, small=(), after=()):
+        sources = [pltpu.with_memory_space_constraint(field, pltpu.HBM) for field in (keys, values, *small)]
+        made = call(
+            functools.partial(payload, chunks),
             "payload",
-            dict(keys=pinned[0], values=pinned[1]),
-            {i: shape(rows, wide) for i, wide in enumerate([sum(each)] if joined else each)},
+            dict(enumerate(sources)),
+            dict(
+                enumerate(
+                    [shape(rows, 2 * count * HEAD_DIM) for _, count in chunks]
+                    + [jax.ShapeDtypeStruct(field.shape, field.dtype) for field in small]
+                )
+            ),
             after,
-            in_specs=dict(keys=ANY, values=ANY),
-            scratch_shapes=[pltpu.SemaphoreType.DMA((2 * len(chunks) * PIECES,))],
+            in_specs=dict.fromkeys(range(len(sources)), ANY),
+            scratch_shapes=[pltpu.SemaphoreType.DMA((2 * len(chunks) * PIECES + len(small),))],
         )
-
-    own = list(gather(CHUNKS[:LAG], joined=True))
-    arrived = up(own[0])
-    near = {chunk: (arrived, sum(width[:chunk])) for chunk in range(LAG)}
-    own = [(own[0], sum(width[:chunk])) for chunk in range(LAG)]
-    own += [(field, 0) for field in gather(CHUNKS[LAG:], own[0][:1])]
+        return made[: len(chunks)], made[len(chunks) :]
+
+    own, _ = gather(CHUNKS[:1])
+    near = {0: (up(own[0]), 0)}
+    more, (segments, gain_q, gain_k) = gather(CHUNKS[1:], (segment_ids, gain_q, gain_k), own)
+    own = [(field, 0) for field in (*own, *more)]
+    for chunk in range(1, LAG):
+        near[chunk] = (up(own[chunk][0]), 0)
     far, next_behind, third_behind = {}, {}, {}
 
     def climb(steps, after=()):
@@ -254,11 +266,12 @@
             ins[key] = field
             return key, slice(at, at + width[chunk])
 
-        def exchange(to, kept, chunk, first, second):
-            at = outs[to].shape[1] if to in outs else 0
-            jobs.append((to, at, use(first[chunk], chunk), use(second[chunk], chunk)))
-            outs[to] = shape(rows, at + width[chunk])
-            kept[chunk] = (to, at)
+        def exchange(to, chunk, first, second, halves=1):
+            part = width[chunk] // halves
+            for half in range(halves):
+                pick = [(key, slice(at.start + half * part, at.start + (half + 1) * part)) for key, at in (use(first[chunk], chunk), use(second[chunk], chunk))]
+                jobs.append((f"{to}{half}", 0, *pick))
+                outs[f"{to}{half}"] = shape(rows, part)
 
         for step in steps:
             rise = 0
@@ -268,9 +281,9 @@
             if step < amount:
                 jobs.append((f"rise{step}", rise, use(near[step], step), None))
                 outs[f"rise{step}"] = shape(rows, rise + width[step])
-                exchange("next", next_behind, step, own, near)
+                exchange("next", step, own, near)
             if step >= LAG:
-                exchange("third", third_behind, step - LAG, near, far)
+                exchange("third", step - LAG, near, far, 2)
 
         def body(*refs):
             ref = dict(zip(list(ins) + list(outs), refs))
@@ -280,8 +293,7 @@
                     value = jnp.where(core_index() == 0, value, ref[other[0]][:, other[1]])
                 ref[to][:, at : at + value.shape[1]] = value
 
-        made = dict(zip(outs, call(body, "climb", ins, outs, after, cost=10**9 * max(0, steps[0] - LAG))))
-        exchanged = {to: swap(made[to]) for to in ("next", "third") if to in made}
+        made = dict(zip(outs, call(body, "climb", ins, outs, after, cost=10**9 * steps[0])))
         for step in steps:
             if step < amount:
                 arrived = up(made[f"rise{step}"])
@@ -290,9 +302,9 @@
                     near[step + LAG] = (arrived, 0)
                     ahead = width[step + LAG]
                 far[step] = (arrived, ahead)
-                next_behind[step] = (exchanged["next"], next_behind[step][1])
+                next_behind[step] = (swap(made["next0"]), 0)
             if step >= LAG:
-                third_behind[step - LAG] = (exchanged["third"], third_behind[step - LAG][1])
+                third_behind[step - LAG] = [swap(made["third0"]), swap(made["third1"])]
         return [next(iter(made.values()))]
 
     parts, sunk = [], {}
@@ -302,56 +314,62 @@
         mine, below = width[step], width[step - LAG] if older else 0
         ins = {}
         if fresh:
-            ins.update(far=parts[step]["far"], third=parts[step]["third"])
+            ins.update(far=parts[step]["far"], third_k=parts[step]["third_k"], third_v=parts[step]["third_v"])
         if older:
             chunk = step - LAG
             ins.update(near=parts[chunk]["near"], arrived=sunk[chunk])
-            ins.update(third_old=parts[chunk]["third"], next_old=parts[chunk]["next"])
+            ins.update(old_k=parts[chunk]["third_k"], old_v=parts[chunk]["third_v"], next_old=parts[chunk]["next"])
 
         def body(*refs):
             ref = dict(zip(list(ins) + ["out"], refs))
             first = core_index() == 0
             if fresh:
-                extra = jnp.where(first, 0.0, ref["third"][...].astype(F32))
-                ref["out"][:, :mine] = (ref["far"][...] + extra).astype(BF16)
+                for half, extra in ((slice(0, mine // 2), ref["third_k"]), (slice(mine // 2, mine), ref["third_v"])):
+                    extra = jnp.where(first, 0.0, extra[...].astype(F32))
+                    ref["out"][:, half] = (ref["far"][:, half] + extra).astype(BF16)
             if older:
-                extra = jnp.where(first, ref["third_old"][...], ref["next_old"][...]).astype(F32)
-                arrived = ref["arrived"][:, :below].astype(F32)
-                ref["out"][:, mine:] = (ref["near"][...] + extra + arrived).astype(BF16)
+                for half, extra in ((slice(0, below // 2), ref["old_k"]), (slice(below // 2, below), ref["old_v"])):
+                    extra = jnp.where(first, extra[...], ref["next_old"][:, half]).astype(F32)
+                    total = ref["near"][:, half] + extra + ref["arrived"][:, half].astype(F32)
+                    ref["out"][:, mine + half.start : mine + half.stop] = total.astype(BF16)
 
         (total,) = call(body, "sink", ins, dict(out=shape(rows, mine + below)), after)
         sunk[step] = down(total)
         return total
 
     made, gains, last, token = [], [], [], []
-    order = climb(range(LAG))
+    order = []
+    for step in range(LAG):
+        order = climb([step], order)
     for chunk, (first, count) in enumerate(CHUNKS):
-        order = climb([chunk + LAG], order + token + ([sunk[chunk - LAG]] if chunk >= LAG else []))
-        held = (own, next_behind, near, third_behind, far)
+        order = climb([chunk + LAG], order + token)
+        held = (own, next_behind, near, far)
         wide = shape(rows, GROUPS * count * HEAD_DIM)
-        whole, low = shape(rows, width[chunk], F32), shape(rows, width[chunk])
+        whole, low, half = shape(rows, width[chunk], F32), shape(rows, width[chunk]), shape(rows, width[chunk] // 2)
         result = call(
             functools.partial(attend, first, count, *(place[chunk][1] for place in held)),
             "attend",
             dict(
-                segments=segment_ids, queries=queries, out_grad=out_grad, own=own[chunk][0],
-                **{f"behind{i}": place[chunk][0] for i, place in enumerate(held[1:])}, gain_q=gain_q, gain_k=gain_k,
+                segments=segments, queries=queries, out_grad=out_grad, own=own[chunk][0],
+                **{f"behind{i}": place[chunk][0] for i, place in enumerate(held[1:])},
+                third_k=third_behind[chunk][0], third_v=third_behind[chunk][1], gain_q=gain_q, gain_k=gain_k,
             ),
             dict(
-                attended=wide, query_grad=wide, own=whole, near=whole, far=whole, third=low, next=low,
+                attended=wide, query_grad=wide, own=whole, near=whole, far=whole,
+                third_k=half, third_v=half, next=low,
                 gains=shape(2, HEAD_DIM, F32),
             ),
             last,
         )
         made.append(result[:2])
-        gains.append(result[7])
-        token = [result[7]]
-        parts.append(
-            dict(own=result[2], near=result[3], far=result[4], third=swap(result[5]), next=swap(result[6]))
-        )
+        gains.append(result[8])
+        token = [result[8]]
+        parts.append(dict(zip(("own", "near", "far"), result[2:5])))
+        parts[-1].update(third_k=swap(result[5]), third_v=swap(result[6]), next=swap(result[7]))
         last = [sink(chunk, last)]
 
     for step in range(amount, amount + LAG):
+        order_gains = last
         last = [sink(step, last)]
     key_outputs = []
     for chunk, (first, count) in enumerate(CHUNKS):
@@ -366,7 +384,7 @@
                 key_grad=jax.ShapeDtypeStruct(keys.shape, BF16), value_grad=jax.ShapeDtypeStruct(keys.shape, BF16)
             ),
             key_outputs,
-            cost=2**32,
+            cost=2**31 * (1 + chunk),
             grid=(1,),
             in_specs=dict(keys=narrow),
             out_specs=dict(key_grad=narrow, value_grad=narrow),
@@ -380,15 +398,14 @@
         last,
     )
 
-    total = gains[0]
-    for more in gains[1:]:
-        (total,) = call(add, "add", dict(a=total, b=more), dict(o=more))
-    total = total_over(total, "dp", 1, lax.axis_size("dp"))
-    total = total_over(total, "ctx", 1, 2, last)
-    total = total_over(total, "ctx", 2, lax.axis_size("ctx"))
+    (total,) = call(add, "add", dict(enumerate(gains)), dict(o=shape(2, HEAD_DIM, F32)))
+    (total,) = call(add, "add", dict(a=total, b=swap(total)), dict(o=shape(2, HEAD_DIM, F32)), order_gains)
+    total = total_over(total, "dp", 1, 2, last)
+    total = total_over(total, "ctx", 2, 4)
     factor = (lax.axis_size("dp") * queries.shape[0] * lax.axis_size("ctx") * rows) ** (-0.5)
-    total = total * factor
-    return attended, query_grad, *key_outputs, total[0], total[1]
+    row = shape(1, HEAD_DIM, F32)
+    query_gains, key_gains = call(functools.partial(scale, factor), "scale", dict(t=total), dict(a=row, b=row))
+    return attended, query_grad, *key_outputs, query_gains[0], key_gains[0]
 
 
 def solution(mesh):

time: 87.3 us -> 71.8 us (0.82)
  starting transfers between devices: 41.1 us -> 34.7 us
  waiting for transfers between devices: 31.3 us -> 25.3 us
  Pallas kernels: 12.1 us -> 10.5 us
  local copies, waits for them, and re-layouts: 1.26 us -> 0.02 us
    ppermute x31 -> x26, starting transfers between devices: 41.1 us -> 34.7 us  [move(): lax.ppermute(field, axis, [(i, target(i)) for i in range(size) if 0 <= ta...]
    ppermute x31 -> x26, waiting for transfers between devices: 31.3 us -> 25.3 us  [move(): lax.ppermute(field, axis, [(i, target(i)) for i in range(size) if 0 <= ta...]
    pallas_call x30 -> x21, Pallas kernels: 12.1 us -> 10.5 us  [call(): pl.pallas_call(kernel, out_shape=list(outs.values()), in_specs=specs, out...]
  transfers between devices with their start and end apart: 31 -> 26, of which waited for: 11 -> 15; matrix products, arithmetic and copies ran while one was open for 1% -> 0% of each run, Pallas kernels for 12% -> 12%
where the time goes in v4:
time: 71.8 us; the launch traced here: 71.3 us
  starting transfers between devices  34.7 us (48%)
  waiting for transfers between devices  25.3 us (35%)
  Pallas kernels  10.5 us (15%)
  between operations  0.85 us (1%)
    ppermute x26, starting transfers between devices, move(): lax.ppermute(field, axis, [(i, target(i)) for i in range(size) if 0 <= ta...  34.7 us
    ppermute x26, waiting for transfers between devices, move(): lax.ppermute(field, axis, [(i, target(i)) for i in range(size) if 0 <= ta...  25.3 us
    pallas_call x21, Pallas kernels, call(): pl.pallas_call(kernel, out_shape=list(outs.values()), in_specs=specs, out...  10.5 us
  transfers between devices with their start and end apart: 26, of which 15 were waited for; matrix products, arithmetic and copies ran while one was open for 0% of the time, Pallas kernels for 12%

profile of v4, /device:TPU:0, one launch (start us, length us, event | category | flops | bytes accessed | tf_op | source)
XLA Modules:
  0.0 71.3 jit_solution(12772586946904901036)
XLA Ops:
  0.6 0.9 %payload.2.refs_5_.refs_1_.refs_3_ = bf16[128,1024]{1,0:T(8,128)(2,1)S(1)} custom-call(bf16[1,128,1024]{2,1,0:T(8,128)(2,1)} %refs_0_.7, bf16[1,128,1024]{2,1,0:T(8,128)(2,1)} %refs_1_.5), custom_call_target="tpu_custom_call" | custom-call | bytes 1 | tf_op jit(solution)/shard_map/payload/pallas_call | solution.py:36
  1.6 4.9 %collective-permute-start = (bf16[128,1024]{1,0:T(8,128)(2,1)S(1)}, bf16[128,1024]{1,0:T(8,128)(2,1)S(1)}, u32[]{:S(2)}, u32[]{:S(2)}) collective-permute-start(bf16[128,1024]{1,0:T(8,128)(2,1)S(1)} %payload.2.refs_5_.refs_1_.refs_3_), channel_id=1, source_target_pairs={{0,2},{1,3},{2,4},{3,5},{4,6},{5,7},{8,10},{9,11},{10,12},{11,13},... | collective-permute-start | bytes 786440 | tf_op jit(solution)/shard_map/ppermute | solution.py:204
  6.5 1.0 %payload.3 = (bf16[128,1024]{1,0:T(8,128)(2,1)S(1)}, s32[1,1024]{1,0:T(1,128)S(1)}, f32[1,256]{1,0:T(1,128)S(1)}, f32[1,256]{1,0:T(1,128)S(1)}) custom-call(bf16[1,128,1024]{2,1,0:T(8,128)(2,1)} %refs_0_.7, bf16[1,128,1024]{2,1,0:T(8,128)(2,1)} %refs_1_.5, s32[1,1024]{1,0:T(1,128)} %refs_2_.3, f32[1,256]{1,0:T(1,128)} %bitcast.4, f32[1,256]{1,0:T(1,128)} %bitcast.5, ...), custom_call_target="tpu_custom_call" | custom-call | bytes 1 | tf_op jit(solution)/shard_map/payload/pallas_call | solution.py:36
  7.6 3.5 %collective-permute-start.3 = (bf16[128,1024]{1,0:T(8,128)(2,1)S(1)}, bf16[128,1024]{1,0:T(8,128)(2,1)S(1)}, u32[]{:S(2)}, u32[]{:S(2)}) collective-permute-start(bf16[128,1024]{1,0:T(8,128)(2,1)S(1)} %get-tuple-element.47.refs_1_.refs_3_), channel_id=1, source_target_pairs={{0,2},{1,3},{2,4},{3,5},{4,6},{5,7},{8,10},{9,11},{10,12},{11,13},... | collective-permute-start | bytes 786440 | tf_op jit(solution)/shard_map/ppermute | solution.py:204
  11.1 2.2 %collective-permute-done.refs_0_.refs_5_ = bf16[128,1024]{1,0:T(8,128)(2,1)S(1)} collective-permute-done((bf16[128,1024]{1,0:T(8,128)(2,1)S(1)}, bf16[128,1024]{1,0:T(8,128)(2,1)S(1)}, u32[]{:S(2)}, u32[]{:S(2)}) %collective-permute-start) | collective-permute-done | bytes 262176 | tf_op jit(solution)/shard_map/ppermute | solution.py:204
  13.3 4.4 %collective-permute-start.2 = (bf16[128,1024]{1,0:T(8,128)(2,1)S(1)}, bf16[128,1024]{1,0:T(8,128)(2,1)S(1)}, u32[]{:S(2)}, u32[]{:S(2)}) collective-permute-start(bf16[128,1024]{1,0:T(8,128)(2,1)S(1)} %get-tuple-element.46.refs_2_), channel_id=1, source_target_pairs={{0,2},{1,3},{2,4},{3,5},{4,6},{5,7},{8,10},{9,11},{10,12},{11,13},... | collective-permute-start | bytes 786440 | tf_op jit(solution)/shard_map/ppermute | solution.py:204
  17.7 1.1 %collective-permute-done.3.refs_0_.refs_5_ = bf16[128,1024]{1,0:T(8,128)(2,1)S(1)} collective-permute-done((bf16[128,1024]{1,0:T(8,128)(2,1)S(1)}, bf16[128,1024]{1,0:T(8,128)(2,1)S(1)}, u32[]{:S(2)}, u32[]{:S(2)}) %collective-permute-start.3) | collective-permute-done | bytes 262176 | tf_op jit(solution)/shard_map/ppermute | solution.py:204
  18.9 4.5 %collective-permute-start.7 = (bf16[128,1024]{1,0:T(8,128)(2,1)S(1)}, bf16[128,1024]{1,0:T(8,128)(2,1)S(1)}, u32[]{:S(2)}, u32[]{:S(2)}) collective-permute-start(bf16[128,1024]{1,0:T(8,128)(2,1)S(1)} %get-tuple-element.48.refs_2_), channel_id=1, source_target_pairs={{0,2},{1,3},{2,4},{3,5},{4,6},{5,7},{8,10},{9,11},{10,12},{11,13},... | collective-permute-start | bytes 786440 | tf_op jit(solution)/shard_map/ppermute | solution.py:204
  23.4 1.0 %collective-permute-done.2.refs_1_.refs_6_ = bf16[128,1024]{1,0:T(8,128)(2,1)S(1)} collective-permute-done((bf16[128,1024]{1,0:T(8,128)(2,1)S(1)}, bf16[128,1024]{1,0:T(8,128)(2,1)S(1)}, u32[]{:S(2)}, u32[]{:S(2)}) %collective-permute-start.2) | collective-permute-done | bytes 262176 | tf_op jit(solution)/shard_map/ppermute | solution.py:204
  25.1 0.8 %collective-permute-done.4.refs_7_ = bf16[128,512]{1,0:T(8,128)(2,1)S(1)} collective-permute-done((bf16[128,512]{1,0:T(8,128)(2,1)S(1)}, bf16[128,512]{1,0:T(8,128)(2,1)S(1)}, u32[]{:S(2)}, u32[]{:S(2)}) %collective-permute-start.4) | collective-permute-done | bytes 131104 | tf_op jit(solution)/shard_map/ppermute | solution.py:204
  26.1 2.2 %attend.2 = (bf16[128,1024]{1,0:T(8,128)(2,1)S(1)}, bf16[128,1024]{1,0:T(8,128)(2,1)S(1)}, f32[128,1024]{1,0:T(8,128)S(1)}, f32[128,1024]{1,0:T(8,128)S(1)}, f32...) custom-call(s32[1,1024]{1,0:T(1,128)S(1)} %get-tuple-element.44.refs, ...), custom_call_target="tpu_custom_call" | custom-call | bytes 1 | tf_op jit(solution)/shard_map/attend/pallas_call | solution.py:36
  30.2 1.3 %collective-permute-start.16 = (bf16[128,1024]{1,0:T(8,128)(2,1)S(1)}, bf16[128,1024]{1,0:T(8,128)(2,1)S(1)}, u32[]{:S(2)}, u32[]{:S(2)}) collective-permute-start(bf16[128,1024]{1,0:T(8,128)(2,1)S(1)} %sink.4.refs_11_.refs_3_), channel_id=1, source_target_pairs={{2,0},{3,1},{4,2},{5,3},{6,4},{7,5},{10,8},{11,9},{12,10},{13,11},... | collective-permute-start | bytes 786440 | tf_op jit(solution)/shard_map/ppermute | solution.py:204
  31.5 2.3 %attend.3 = (bf16[128,1024]{1,0:T(8,128)(2,1)S(1)}, bf16[128,1024]{1,0:T(8,128)(2,1)S(1)}, f32[128,1024]{1,0:T(8,128)S(1)}, f32[128,1024]{1,0:T(8,128)S(1)}, f32...) custom-call(s32[1,1024]{1,0:T(1,128)S(1)} %get-tuple-element.44.refs, ...), custom_call_target="tpu_custom_call" | custom-call | bytes 1 | tf_op jit(solution)/shard_map/attend/pallas_call | solution.py:36
  34.5 0.7 collective-permute-done.12.refs_1_.refs_2_
  35.4 1.3 %collective-permute-start.14 = (bf16[128,1024]{1,0:T(8,128)(2,1)S(1)}, bf16[128,1024]{1,0:T(8,128)(2,1)S(1)}, u32[]{:S(2)}, u32[]{:S(2)}) collective-permute-start(bf16[128,1024]{1,0:T(8,128)(2,1)S(1)} %sink.5.refs_5_), channel_id=1, source_target_pairs={{2,0},{3,1},{4,2},{5,3},{6,4},{7,5},{10,8},{11,9},{12,10},{13,11},... | collective-permute-start | bytes 786440 | tf_op jit(solution)/shard_map/ppermute | solution.py:204
  36.8 4.5 %collective-permute-done.16.refs_1_ = bf16[128,1024]{1,0:T(8,128)(2,1)S(1)} collective-permute-done((bf16[128,1024]{1,0:T(8,128)(2,1)S(1)}, bf16[128,1024]{1,0:T(8,128)(2,1)S(1)}, u32[]{:S(2)}, u32[]{:S(2)}) %collective-permute-start.16) | collective-permute-done | bytes 262176 | tf_op jit(solution)/shard_map/ppermute | solution.py:204
  41.3 1.3 %collective-permute-start.19 = (bf16[128,1024]{1,0:T(8,128)(2,1)S(1)}, bf16[128,1024]{1,0:T(8,128)(2,1)S(1)}, u32[]{:S(2)}, u32[]{:S(2)}) collective-permute-start(bf16[128,1024]{1,0:T(8,128)(2,1)S(1)} %sink.6.refs_5_.refs_2_), channel_id=1, source_target_pairs={{2,0},{3,1},{4,2},{5,3},{6,4},{7,5},{10,8},{11,9},{12,10},{13,11},... | collective-permute-start | bytes 786440 | tf_op jit(solution)/shard_map/ppermute | solution.py:204
  42.6 4.9 %collective-permute-done.14.refs_1_ = bf16[128,1024]{1,0:T(8,128)(2,1)S(1)} collective-permute-done((bf16[128,1024]{1,0:T(8,128)(2,1)S(1)}, bf16[128,1024]{1,0:T(8,128)(2,1)S(1)}, u32[]{:S(2)}, u32[]{:S(2)}) %collective-permute-start.14) | collective-permute-done | bytes 262176 | tf_op jit(solution)/shard_map/ppermute | solution.py:204
  47.6 1.3 %collective-permute-start.18 = (bf16[128,1024]{1,0:T(8,128)(2,1)S(1)}, bf16[128,1024]{1,0:T(8,128)(2,1)S(1)}, u32[]{:S(2)}, u32[]{:S(2)}) collective-permute-start(bf16[128,1024]{1,0:T(8,128)(2,1)S(1)} %sink.7.refs_4_.refs_2_), channel_id=1, source_target_pairs={{2,0},{3,1},{4,2},{5,3},{6,4},{7,5},{10,8},{11,9},{12,10},{13,11},... | collective-permute-start | bytes 786440 | tf_op jit(solution)/shard_map/ppermute | solution.py:204
  49.0 1.1 %collective-permute-done.20.refs_1_ = f32[2,256]{1,0:T(2,128)S(1)} collective-permute-done((f32[2,256]{1,0:T(2,128)S(1)}, f32[2,256]{1,0:T(2,128)S(1)}, u32[]{:S(2)}, u32[]{:S(2)}) %collective-permute-start.20) | collective-permute-done | bytes 2080 | tf_op jit(solution)/shard_map/ppermute | solution.py:204
  50.2 1.5 %collective-permute-start.21 = (f32[2,256]{1,0:T(2,128)S(1)}, f32[2,256]{1,0:T(2,128)S(1)}, u32[]{:S(2)}, u32[]{:S(2)}) collective-permute-start(f32[2,256]{1,0:T(2,128)S(1)} %add.6.refs_0_), channel_id=1, source_target_pairs={{0,8},{8,0},{16,24},{24,16},{1,9},{9,1},{17,25},{25,17},{2,10},{10... | collective-permute-start | bytes 6152 | tf_op jit(solution)/shard_map/ppermute | solution.py:204
  51.6 2.1 %collective-permute-done.21.refs_1_ = f32[2,256]{1,0:T(2,128)S(1)} collective-permute-done((f32[2,256]{1,0:T(2,128)S(1)}, f32[2,256]{1,0:T(2,128)S(1)}, u32[]{:S(2)}, u32[]{:S(2)}) %collective-permute-start.21) | collective-permute-done | bytes 2080 | tf_op jit(solution)/shard_map/ppermute | solution.py:204
  53.8 1.5 %collective-permute-start.22 = (f32[2,256]{1,0:T(2,128)S(1)}, f32[2,256]{1,0:T(2,128)S(1)}, u32[]{:S(2)}, u32[]{:S(2)}) collective-permute-start(f32[2,256]{1,0:T(2,128)S(1)} %add.7.refs_0_), channel_id=1, source_target_pairs={{0,16},{8,24},{16,0},{24,8},{1,17},{9,25},{17,1},{25,9},{2,18},{10... | collective-permute-start | bytes 6152 | tf_op jit(solution)/shard_map/ppermute | solution.py:204
  55.3 2.1 %collective-permute-done.22.refs_1_ = f32[2,256]{1,0:T(2,128)S(1)} collective-permute-done((f32[2,256]{1,0:T(2,128)S(1)}, f32[2,256]{1,0:T(2,128)S(1)}, u32[]{:S(2)}, u32[]{:S(2)}) %collective-permute-start.22) | collective-permute-done | bytes 2080 | tf_op jit(solution)/shard_map/ppermute | solution.py:204
  57.3 2.7 %collective-permute-start.23 = (f32[2,256]{1,0:T(2,128)S(1)}, f32[2,256]{1,0:T(2,128)S(1)}, u32[]{:S(2)}, u32[]{:S(2)}) collective-permute-start(f32[2,256]{1,0:T(2,128)S(1)} %add.8.refs_0_), channel_id=1, source_target_pairs={{0,2},{1,3},{2,0},{3,1},{4,6},{5,7},{6,4},{7,5},{8,10},{9,11},{10,... | collective-permute-start | bytes 6152 | tf_op jit(solution)/shard_map/ppermute | solution.py:204
  60.0 3.5 %collective-permute-start.24 = (f32[2,256]{1,0:T(2,128)S(1)}, f32[2,256]{1,0:T(2,128)S(1)}, u32[]{:S(2)}, u32[]{:S(2)}) collective-permute-start(f32[2,256]{1,0:T(2,128)S(1)} %add.8.refs_0_), channel_id=1, source_target_pairs={{0,4},{1,5},{2,6},{3,7},{4,0},{5,1},{6,2},{7,3},{8,12},{9,13},{10,... | collective-permute-start | bytes 6152 | tf_op jit(solution)/shard_map/ppermute | solution.py:204
  63.5 1.0 %assemble.1 = (bf16[1,128,2048]{2,1,0:T(8,128)(2,1)}, bf16[1,128,2048]{2,1,0:T(8,128)(2,1)}) custom-call(bf16[128,1024]{1,0:T(8,128)(2,1)S(1)} %get-tuple-element.53.refs_0_, bf16[128,1024]{1,0:T(8,128)(2,1)S(1)} %get-tuple-element.61.refs_1_, bf16[128,1024]{1,0:T(8,128)(2,1)S(1)} %get-tuple-element.62.refs_2_, ...), custom_call_target="tpu_custom_call" | custom-call | bytes 1 | tf_op jit(solution)/shard_map/assemble/pallas_call | solution.py:36
  64.6 0.5 collective-permute-done.24.refs_2_
  65.1 3.8 %collective-permute-done.25.refs_3_ = f32[2,256]{1,0:T(2,128)S(1)} collective-permute-done((f32[2,256]{1,0:T(2,128)S(1)}, f32[2,256]{1,0:T(2,128)S(1)}, u32[]{:S(2)}, u32[]{:S(2)}) %collective-permute-start.25) | collective-permute-done | bytes 2080 | tf_op jit(solution)/shard_map/ppermute | solution.py:204
  68.9 0.6 scale.1
  69.5 0.9 %finish.2 = (bf16[1,128,1024]{2,1,0:T(8,128)(2,1)}, bf16[1,128,1024]{2,1,0:T(8,128)(2,1)}) custom-call(bf16[1,128,1024]{2,1,0:T(8,128)(2,1)S(1)} %copy-done.2, f32[1,256]{1,0:T(1,128)S(1)} %get-tuple-element.52.refs_10_.refs_1_, f32[128,1024]{1,0:T(8,128)S(1)} %get-tuple-element.74.refs_2_, bf16[128,1024]{1,0:T(8,128)(2,1)S(1)} %collective-permute-done.17.refs_4_.refs_3_, ...), custom_call_target="tpu_custom_call" | custom-call | flops 2147483648 | bytes 1 | tf_op jit(solution)/shard_map/finish/pallas_call | solution.py:36
  70.4 0.9 %finish.3 = (bf16[1,128,1024]{2,1,0:T(8,128)(2,1)}, bf16[1,128,1024]{2,1,0:T(8,128)(2,1)}) custom-call(bf16[1,128,1024]{2,1,0:T(8,128)(2,1)S(1)} %copy-done.2, f32[1,256]{1,0:T(1,128)S(1)} %get-tuple-element.52.refs_10_.refs_1_, f32[128,1024]{1,0:T(8,128)S(1)} %get-tuple-element.73.refs_2_, ...), custom_call_target="tpu_custom_call", output_to_operand_aliasing={{0}: (5, {}), {1}: (6, {})} | custom-call | flops 4294967296 | bytes 1 | tf_op jit(solution)/shard_map/finish/pallas_call | solution.py:36
  (47 shorter events, 4.2 us)
Async XLA Ops:
  1.6 11.6 %collective-permute-start = (bf16[128,1024]{1,0:T(8,128)(2,1)S(1)}, bf16[128,1024]{1,0:T(8,128)(2,1)S(1)}, u32[]{:S(2)}, u32[]{:S(2)}) collective-permute-start(bf16[128,1024]{1,0:T(8,128)(2,1)S(1)} %payload.2.refs_5_.refs_1_.refs_3_), channel_id=1, source_target_pairs={{0,2},{1,3},{2,4},{3,5},{4,6},{5,7},{8,10},{9,11},{10,12},{11,13},... | collective-permute-start | bytes 786440 | tf_op jit(solution)/shard_map/ppermute | solution.py:204
  7.6 11.3 %collective-permute-start.3 = (bf16[128,1024]{1,0:T(8,128)(2,1)S(1)}, bf16[128,1024]{1,0:T(8,128)(2,1)S(1)}, u32[]{:S(2)}, u32[]{:S(2)}) collective-permute-start(bf16[128,1024]{1,0:T(8,128)(2,1)S(1)} %get-tuple-element.47.refs_1_.refs_3_), channel_id=1, source_target_pairs={{0,2},{1,3},{2,4},{3,5},{4,6},{5,7},{8,10},{9,11},{10,12},{11,13},... | collective-permute-start | bytes 786440 | tf_op jit(solution)/shard_map/ppermute | solution.py:204
  13.3 11.2 %collective-permute-start.2 = (bf16[128,1024]{1,0:T(8,128)(2,1)S(1)}, bf16[128,1024]{1,0:T(8,128)(2,1)S(1)}, u32[]{:S(2)}, u32[]{:S(2)}) collective-permute-start(bf16[128,1024]{1,0:T(8,128)(2,1)S(1)} %get-tuple-element.46.refs_2_), channel_id=1, source_target_pairs={{0,2},{1,3},{2,4},{3,5},{4,6},{5,7},{8,10},{9,11},{10,12},{11,13},... | collective-permute-start | bytes 786440 | tf_op jit(solution)/shard_map/ppermute | solution.py:204
  17.7 7.5 %collective-permute-start.1 = (bf16[128,1024]{1,0:T(8,128)(2,1)S(1)}, bf16[128,1024]{1,0:T(8,128)(2,1)S(1)}, u32[]{:S(2)}, u32[]{:S(2)}) collective-permute-start(bf16[128,1024]{1,0:T(8,128)(2,1)S(1)} %get-tuple-element.45), channel_id=1, source_target_pairs={{0,1},{1,0},{2,3},{3,2},{4,5},{5,4},{6,7},{7,6},{8,9},{9,8},{10,11... | collective-permute-start | bytes 786440 | tf_op jit(solution)/shard_map/ppermute | solution.py:204
  18.9 7.2 %copy-start = (bf16[1,128,2048]{2,1,0:T(8,128)(2,1)S(1)}, bf16[1,128,2048]{2,1,0:T(8,128)(2,1)}, u32[]{:S(2)}) copy-start(bf16[1,128,2048]{2,1,0:T(8,128)(2,1)} %refs_1_.7) | copy-start | bytes 1572868
  18.9 7.2 %copy-start.1 = (bf16[1,128,2048]{2,1,0:T(8,128)(2,1)S(1)}, bf16[1,128,2048]{2,1,0:T(8,128)(2,1)}, u32[]{:S(2)}) copy-start(bf16[1,128,2048]{2,1,0:T(8,128)(2,1)} %refs_2_.5) | copy-start | bytes 1572868
  18.9 10.0 %collective-permute-start.7 = (bf16[128,1024]{1,0:T(8,128)(2,1)S(1)}, bf16[128,1024]{1,0:T(8,128)(2,1)S(1)}, u32[]{:S(2)}, u32[]{:S(2)}) collective-permute-start(bf16[128,1024]{1,0:T(8,128)(2,1)S(1)} %get-tuple-element.48.refs_2_), channel_id=1, source_target_pairs={{0,2},{1,3},{2,4},{3,5},{4,6},{5,7},{8,10},{9,11},{10,12},{11,13},... | collective-permute-start | bytes 786440 | tf_op jit(solution)/shard_map/ppermute | solution.py:204
  24.5 1.4 %collective-permute-start.4 = (bf16[128,512]{1,0:T(8,128)(2,1)S(1)}, bf16[128,512]{1,0:T(8,128)(2,1)S(1)}, u32[]{:S(2)}, u32[]{:S(2)}) collective-permute-start(bf16[128,512]{1,0:T(8,128)(2,1)S(1)} %get-tuple-element.49.refs_2_), channel_id=1, source_target_pairs={{0,1},{1,0},{2,3},{3,2},{4,5},{5,4},{6,7},{7,6},{8,9},{9,8},{10,11... | collective-permute-start | bytes 393224 | tf_op jit(solution)/shard_map/ppermute | solution.py:204
  24.6 1.5 %collective-permute-start.5 = (bf16[128,512]{1,0:T(8,128)(2,1)S(1)}, bf16[128,512]{1,0:T(8,128)(2,1)S(1)}, u32[]{:S(2)}, u32[]{:S(2)}) collective-permute-start(bf16[128,512]{1,0:T(8,128)(2,1)S(1)} %get-tuple-element.50), channel_id=1, source_target_pairs={{0,1},{1,0},{2,3},{3,2},{4,5},{5,4},{6,7},{7,6},{8,9},{9,8},{10,11... | collective-permute-start | bytes 393224 | tf_op jit(solution)/shard_map/ppermute | solution.py:204
  25.1 6.4 %collective-permute-start.6 = (bf16[128,1024]{1,0:T(8,128)(2,1)S(1)}, bf16[128,1024]{1,0:T(8,128)(2,1)S(1)}, u32[]{:S(2)}, u32[]{:S(2)}) collective-permute-start(bf16[128,1024]{1,0:T(8,128)(2,1)S(1)} %get-tuple-element.54), channel_id=1, source_target_pairs={{0,1},{1,0},{2,3},{3,2},{4,5},{5,4},{6,7},{7,6},{8,9},{9,8},{10,11... | collective-permute-start | bytes 786440 | tf_op jit(solution)/shard_map/ppermute | solution.py:204
  28.3 1.4 %collective-permute-start.10 = (bf16[128,512]{1,0:T(8,128)(2,1)S(1)}, bf16[128,512]{1,0:T(8,128)(2,1)S(1)}, u32[]{:S(2)}, u32[]{:S(2)}) collective-permute-start(bf16[128,512]{1,0:T(8,128)(2,1)S(1)} %get-tuple-element.59), channel_id=1, source_target_pairs={{0,1},{1,0},{2,3},{3,2},{4,5},{5,4},{6,7},{7,6},{8,9},{9,8},{10,11... | collective-permute-start | bytes 393224 | tf_op jit(solution)/shard_map/ppermute | solution.py:204
  28.7 1.4 %collective-permute-start.11 = (bf16[128,512]{1,0:T(8,128)(2,1)S(1)}, bf16[128,512]{1,0:T(8,128)(2,1)S(1)}, u32[]{:S(2)}, u32[]{:S(2)}) collective-permute-start(bf16[128,512]{1,0:T(8,128)(2,1)S(1)} %get-tuple-element.60), channel_id=1, source_target_pairs={{0,1},{1,0},{2,3},{3,2},{4,5},{5,4},{6,7},{7,6},{8,9},{9,8},{10,11... | collective-permute-start | bytes 393224 | tf_op jit(solution)/shard_map/ppermute | solution.py:204
  29.0 2.5 %collective-permute-start.8 = (bf16[128,512]{1,0:T(8,128)(2,1)S(1)}, bf16[128,512]{1,0:T(8,128)(2,1)S(1)}, u32[]{:S(2)}, u32[]{:S(2)}) collective-permute-start(bf16[128,512]{1,0:T(8,128)(2,1)S(1)} %get-tuple-element.56), channel_id=1, source_target_pairs={{0,1},{1,0},{2,3},{3,2},{4,5},{5,4},{6,7},{7,6},{8,9},{9,8},{10,11... | collective-permute-start | bytes 393224 | tf_op jit(solution)/shard_map/ppermute | solution.py:204
  29.4 2.1 %collective-permute-start.9 = (bf16[128,512]{1,0:T(8,128)(2,1)S(1)}, bf16[128,512]{1,0:T(8,128)(2,1)S(1)}, u32[]{:S(2)}, u32[]{:S(2)}) collective-permute-start(bf16[128,512]{1,0:T(8,128)(2,1)S(1)} %get-tuple-element.57), channel_id=1, source_target_pairs={{0,1},{1,0},{2,3},{3,2},{4,5},{5,4},{6,7},{7,6},{8,9},{9,8},{10,11... | collective-permute-start | bytes 393224 | tf_op jit(solution)/shard_map/ppermute | solution.py:204
  29.8 7.0 %collective-permute-start.17 = (bf16[128,1024]{1,0:T(8,128)(2,1)S(1)}, bf16[128,1024]{1,0:T(8,128)(2,1)S(1)}, u32[]{:S(2)}, u32[]{:S(2)}) collective-permute-start(bf16[128,1024]{1,0:T(8,128)(2,1)S(1)} %get-tuple-element.70), channel_id=1, source_target_pairs={{0,1},{1,0},{2,3},{3,2},{4,5},{5,4},{6,7},{7,6},{8,9},{9,8},{10,11... | collective-permute-start | bytes 786440 | tf_op jit(solution)/shard_map/ppermute | solution.py:204
  30.2 11.0 %collective-permute-start.16 = (bf16[128,1024]{1,0:T(8,128)(2,1)S(1)}, bf16[128,1024]{1,0:T(8,128)(2,1)S(1)}, u32[]{:S(2)}, u32[]{:S(2)}) collective-permute-start(bf16[128,1024]{1,0:T(8,128)(2,1)S(1)} %sink.4.refs_11_.refs_3_), channel_id=1, source_target_pairs={{2,0},{3,1},{4,2},{5,3},{6,4},{7,5},{10,8},{11,9},{12,10},{13,11},... | collective-permute-start | bytes 786440 | tf_op jit(solution)/shard_map/ppermute | solution.py:204
  33.8 1.4 %collective-permute-start.12 = (bf16[128,512]{1,0:T(8,128)(2,1)S(1)}, bf16[128,512]{1,0:T(8,128)(2,1)S(1)}, u32[]{:S(2)}, u32[]{:S(2)}) collective-permute-start(bf16[128,512]{1,0:T(8,128)(2,1)S(1)} %get-tuple-element.66), channel_id=1, source_target_pairs={{0,1},{1,0},{2,3},{3,2},{4,5},{5,4},{6,7},{7,6},{8,9},{9,8},{10,11... | collective-permute-start | bytes 393224 | tf_op jit(solution)/shard_map/ppermute | solution.py:204
  34.0 1.3 %collective-permute-start.13 = (bf16[128,512]{1,0:T(8,128)(2,1)S(1)}, bf16[128,512]{1,0:T(8,128)(2,1)S(1)}, u32[]{:S(2)}, u32[]{:S(2)}) collective-permute-start(bf16[128,512]{1,0:T(8,128)(2,1)S(1)} %get-tuple-element.67), channel_id=1, source_target_pairs={{0,1},{1,0},{2,3},{3,2},{4,5},{5,4},{6,7},{7,6},{8,9},{9,8},{10,11... | collective-permute-start | bytes 393224 | tf_op jit(solution)/shard_map/ppermute | solution.py:204
  34.3 8.3 %collective-permute-start.15 = (bf16[128,1024]{1,0:T(8,128)(2,1)S(1)}, bf16[128,1024]{1,0:T(8,128)(2,1)S(1)}, u32[]{:S(2)}, u32[]{:S(2)}) collective-permute-start(bf16[128,1024]{1,0:T(8,128)(2,1)S(1)} %get-tuple-element.68), channel_id=1, source_target_pairs={{0,1},{1,0},{2,3},{3,2},{4,5},{5,4},{6,7},{7,6},{8,9},{9,8},{10,11... | collective-permute-start | bytes 786440 | tf_op jit(solution)/shard_map/ppermute | solution.py:204
  35.4 12.1 %collective-permute-start.14 = (bf16[128,1024]{1,0:T(8,128)(2,1)S(1)}, bf16[128,1024]{1,0:T(8,128)(2,1)S(1)}, u32[]{:S(2)}, u32[]{:S(2)}) collective-permute-start(bf16[128,1024]{1,0:T(8,128)(2,1)S(1)} %sink.5.refs_5_), channel_id=1, source_target_pairs={{2,0},{3,1},{4,2},{5,3},{6,4},{7,5},{10,8},{11,9},{12,10},{13,11},... | collective-permute-start | bytes 786440 | tf_op jit(solution)/shard_map/ppermute | solution.py:204
  41.3 28.2 %collective-permute-start.19 = (bf16[128,1024]{1,0:T(8,128)(2,1)S(1)}, bf16[128,1024]{1,0:T(8,128)(2,1)S(1)}, u32[]{:S(2)}, u32[]{:S(2)}) collective-permute-start(bf16[128,1024]{1,0:T(8,128)(2,1)S(1)} %sink.6.refs_5_.refs_2_), channel_id=1, source_target_pairs={{2,0},{3,1},{4,2},{5,3},{6,4},{7,5},{10,8},{11,9},{12,10},{13,11},... | collective-permute-start | bytes 786440 | tf_op jit(solution)/shard_map/ppermute | solution.py:204
  47.6 22.8 %collective-permute-start.18 = (bf16[128,1024]{1,0:T(8,128)(2,1)S(1)}, bf16[128,1024]{1,0:T(8,128)(2,1)S(1)}, u32[]{:S(2)}, u32[]{:S(2)}) collective-permute-start(bf16[128,1024]{1,0:T(8,128)(2,1)S(1)} %sink.7.refs_4_.refs_2_), channel_id=1, source_target_pairs={{2,0},{3,1},{4,2},{5,3},{6,4},{7,5},{10,8},{11,9},{12,10},{13,11},... | collective-permute-start | bytes 786440 | tf_op jit(solution)/shard_map/ppermute | solution.py:204
  48.9 1.2 %collective-permute-start.20 = (f32[2,256]{1,0:T(2,128)S(1)}, f32[2,256]{1,0:T(2,128)S(1)}, u32[]{:S(2)}, u32[]{:S(2)}) collective-permute-start(f32[2,256]{1,0:T(2,128)S(1)} %add.5.refs_0_), channel_id=1, source_target_pairs={{0,1},{1,0},{2,3},{3,2},{4,5},{5,4},{6,7},{7,6},{8,9},{9,8},{10,11... | collective-permute-start | bytes 6152 | tf_op jit(solution)/shard_map/ppermute | solution.py:204
  50.2 3.6 %collective-permute-start.21 = (f32[2,256]{1,0:T(2,128)S(1)}, f32[2,256]{1,0:T(2,128)S(1)}, u32[]{:S(2)}, u32[]{:S(2)}) collective-permute-start(f32[2,256]{1,0:T(2,128)S(1)} %add.6.refs_0_), channel_id=1, source_target_pairs={{0,8},{8,0},{16,24},{24,16},{1,9},{9,1},{17,25},{25,17},{2,10},{10... | collective-permute-start | bytes 6152 | tf_op jit(solution)/shard_map/ppermute | solution.py:204
  53.8 3.6 %collective-permute-start.22 = (f32[2,256]{1,0:T(2,128)S(1)}, f32[2,256]{1,0:T(2,128)S(1)}, u32[]{:S(2)}, u32[]{:S(2)}) collective-permute-start(f32[2,256]{1,0:T(2,128)S(1)} %add.7.refs_0_), channel_id=1, source_target_pairs={{0,16},{8,24},{16,0},{24,8},{1,17},{9,25},{17,1},{25,9},{2,18},{10... | collective-permute-start | bytes 6152 | tf_op jit(solution)/shard_map/ppermute | solution.py:204
  57.3 7.2 %collective-permute-start.23 = (f32[2,256]{1,0:T(2,128)S(1)}, f32[2,256]{1,0:T(2,128)S(1)}, u32[]{:S(2)}, u32[]{:S(2)}) collective-permute-start(f32[2,256]{1,0:T(2,128)S(1)} %add.8.refs_0_), channel_id=1, source_target_pairs={{0,2},{1,3},{2,0},{3,1},{4,6},{5,7},{6,4},{7,5},{8,10},{9,11},{10,... | collective-permute-start | bytes 6152 | tf_op jit(solution)/shard_map/ppermute | solution.py:204
  60.0 5.1 %collective-permute-start.24 = (f32[2,256]{1,0:T(2,128)S(1)}, f32[2,256]{1,0:T(2,128)S(1)}, u32[]{:S(2)}, u32[]{:S(2)}) collective-permute-start(f32[2,256]{1,0:T(2,128)S(1)} %add.8.refs_0_), channel_id=1, source_target_pairs={{0,4},{1,5},{2,6},{3,7},{4,0},{5,1},{6,2},{7,3},{8,12},{9,13},{10,... | collective-permute-start | bytes 6152 | tf_op jit(solution)/shard_map/ppermute | solution.py:204
  63.5 5.4 %collective-permute-start.25 = (f32[2,256]{1,0:T(2,128)S(1)}, f32[2,256]{1,0:T(2,128)S(1)}, u32[]{:S(2)}, u32[]{:S(2)}) collective-permute-start(f32[2,256]{1,0:T(2,128)S(1)} %add.8.refs_0_), channel_id=1, source_target_pairs={{0,6},{1,7},{2,4},{3,5},{4,2},{5,3},{6,0},{7,1},{8,14},{9,15},{10,... | collective-permute-start | bytes 6152 | tf_op jit(solution)/shard_map/ppermute | solution.py:204
  63.5 6.0 %copy-start.2 = (bf16[1,128,1024]{2,1,0:T(8,128)(2,1)S(1)}, bf16[1,128,1024]{2,1,0:T(8,128)(2,1)}, u32[]{:S(2)}) copy-start(bf16[1,128,1024]{2,1,0:T(8,128)(2,1)} %refs_0_.7) | copy-start | bytes 786436

commit v5 on v4

--- a/solution.py
+++ b/solution.py
@@ -216,9 +216,10 @@
     return move(field, "ctx", lambda i: i ^ 1)
 
 
-def total_over(field, axis, unit, most, after=()):
-    while unit < lax.axis_size(axis):
-        group = min(most, lax.axis_size(axis) // unit)
+def total_over(field, axis, unit, end, most, after=()):
+    end = min(end, lax.axis_size(axis))
+    while unit < end:
+        group = min(most, end // unit)
         others = [move(field, axis, lambda i: i ^ (by * unit)) for by in range(1, group)]
         (field,) = call(add, "add", dict(enumerate([field, *others])), dict(o=shape(*field.shape, F32)), after)
         unit *= group
@@ -366,11 +367,15 @@
         token = [result[8]]
         parts.append(dict(zip(("own", "near", "far"), result[2:5])))
         parts[-1].update(third_k=swap(result[5]), third_v=swap(result[6]), next=swap(result[7]))
+        if chunk == amount - 1:
+            (total,) = call(add, "add", dict(enumerate(gains)), dict(o=shape(2, HEAD_DIM, F32)))
+            total = total_over(total, "ctx", 1, 2, 2)
+            last = [*last, total]
         last = [sink(chunk, last)]
 
+    total = total_over(total, "dp", 1, 2, 2)
     for step in range(amount, amount + LAG):
-        order_gains = last
-        last = [sink(step, last)]
+        last = [sink(step, [*last, total])]
     key_outputs = []
     for chunk, (first, count) in enumerate(CHUNKS):
         narrow = columns(rows, count * HEAD_DIM, first * HEAD_DIM)
@@ -398,10 +403,8 @@
         last,
     )
 
-    (total,) = call(add, "add", dict(enumerate(gains)), dict(o=shape(2, HEAD_DIM, F32)))
-    (total,) = call(add, "add", dict(a=total, b=swap(total)), dict(o=shape(2, HEAD_DIM, F32)), order_gains)
-    total = total_over(total, "dp", 1, 2, last)
-    total = total_over(total, "ctx", 2, 4)
+    total = total_over(total, "dp", 2, lax.axis_size("dp"), 2)
+    total = total_over(total, "ctx", 2, lax.axis_size("ctx"), 4, last)
     factor = (lax.axis_size("dp") * queries.shape[0] * lax.axis_size("ctx") * rows) ** (-0.5)
     row = shape(1, HEAD_DIM, F32)
     query_gains, key_gains = call(functools.partial(scale, factor), "scale", dict(t=total), dict(a=row, b=row))

time: 71.8 us -> 68.4 us (0.953)
  waiting for transfers between devices: 25.3 us -> 21.7 us
    ppermute x26, waiting for transfers between devices: 25.3 us -> 21.7 us  [move(): lax.ppermute(field, axis, [(i, target(i)) for i in range(size) if 0 <= ta...]
  transfers between devices with their start and end apart: 26 -> 26, of which waited for: 15 -> 13; matrix products, arithmetic and copies ran while one was open for 0% -> 0% of each run, Pallas kernels for 12% -> 13%
where the time goes in v5:
time: 68.4 us; the launch traced here: 67.9 us
  starting transfers between devices  35 us (51%)
  waiting for transfers between devices  21.7 us (32%)
  Pallas kernels  10.4 us (15%)
  between operations  0.83 us (1%)
    ppermute x26, starting transfers between devices, move(): lax.ppermute(field, axis, [(i, target(i)) for i in range(size) if 0 <= ta...  35 us
    ppermute x26, waiting for transfers between devices, move(): lax.ppermute(field, axis, [(i, target(i)) for i in range(size) if 0 <= ta...  21.7 us
    pallas_call x21, Pallas kernels, call(): pl.pallas_call(kernel, out_shape=list(outs.values()), in_specs=specs, out...  10.4 us
  transfers between devices with their start and end apart: 26, of which 13 were waited for; matrix products, arithmetic and copies ran while one was open for 0% of the time, Pallas kernels for 13%

profile of v5, /device:TPU:0, one launch (start us, length us, event | category | flops | bytes accessed | tf_op | source)
XLA Modules:
  0.0 67.9 jit_solution(3870095097630560970)
XLA Ops:
  0.6 0.9 %payload.2.refs_5_.refs_1_.refs_3_ = bf16[128,1024]{1,0:T(8,128)(2,1)S(1)} custom-call(bf16[1,128,1024]{2,1,0:T(8,128)(2,1)} %refs_0_.7, bf16[1,128,1024]{2,1,0:T(8,128)(2,1)} %refs_1_.5), custom_call_target="tpu_custom_call" | custom-call | bytes 1 | tf_op jit(solution)/shard_map/payload/pallas_call | solution.py:36
  1.6 4.9 %collective-permute-start = (bf16[128,1024]{1,0:T(8,128)(2,1)S(1)}, bf16[128,1024]{1,0:T(8,128)(2,1)S(1)}, u32[]{:S(2)}, u32[]{:S(2)}) collective-permute-start(bf16[128,1024]{1,0:T(8,128)(2,1)S(1)} %payload.2.refs_5_.refs_1_.refs_3_), channel_id=1, source_target_pairs={{0,2},{1,3},{2,4},{3,5},{4,6},{5,7},{8,10},{9,11},{10,12},{11,13},... | collective-permute-start | bytes 786440 | tf_op jit(solution)/shard_map/ppermute | solution.py:204
  6.5 1.0 %payload.3 = (bf16[128,1024]{1,0:T(8,128)(2,1)S(1)}, s32[1,1024]{1,0:T(1,128)S(1)}, f32[1,256]{1,0:T(1,128)S(1)}, f32[1,256]{1,0:T(1,128)S(1)}) custom-call(bf16[1,128,1024]{2,1,0:T(8,128)(2,1)} %refs_0_.7, bf16[1,128,1024]{2,1,0:T(8,128)(2,1)} %refs_1_.5, s32[1,1024]{1,0:T(1,128)} %refs_2_.3, f32[1,256]{1,0:T(1,128)} %bitcast.4, f32[1,256]{1,0:T(1,128)} %bitcast.5, ...), custom_call_target="tpu_custom_call" | custom-call | bytes 1 | tf_op jit(solution)/shard_map/payload/pallas_call | solution.py:36
  7.6 3.5 %collective-permute-start.3 = (bf16[128,1024]{1,0:T(8,128)(2,1)S(1)}, bf16[128,1024]{1,0:T(8,128)(2,1)S(1)}, u32[]{:S(2)}, u32[]{:S(2)}) collective-permute-start(bf16[128,1024]{1,0:T(8,128)(2,1)S(1)} %get-tuple-element.47.refs_1_.refs_3_), channel_id=1, source_target_pairs={{0,2},{1,3},{2,4},{3,5},{4,6},{5,7},{8,10},{9,11},{10,12},{11,13},... | collective-permute-start | bytes 786440 | tf_op jit(solution)/shard_map/ppermute | solution.py:204
  11.1 2.2 %collective-permute-done.refs_0_.refs_5_ = bf16[128,1024]{1,0:T(8,128)(2,1)S(1)} collective-permute-done((bf16[128,1024]{1,0:T(8,128)(2,1)S(1)}, bf16[128,1024]{1,0:T(8,128)(2,1)S(1)}, u32[]{:S(2)}, u32[]{:S(2)}) %collective-permute-start) | collective-permute-done | bytes 262176 | tf_op jit(solution)/shard_map/ppermute | solution.py:204
  13.3 4.4 %collective-permute-start.2 = (bf16[128,1024]{1,0:T(8,128)(2,1)S(1)}, bf16[128,1024]{1,0:T(8,128)(2,1)S(1)}, u32[]{:S(2)}, u32[]{:S(2)}) collective-permute-start(bf16[128,1024]{1,0:T(8,128)(2,1)S(1)} %get-tuple-element.46.refs_2_), channel_id=1, source_target_pairs={{0,2},{1,3},{2,4},{3,5},{4,6},{5,7},{8,10},{9,11},{10,12},{11,13},... | collective-permute-start | bytes 786440 | tf_op jit(solution)/shard_map/ppermute | solution.py:204
  17.7 1.1 %collective-permute-done.3.refs_0_.refs_5_ = bf16[128,1024]{1,0:T(8,128)(2,1)S(1)} collective-permute-done((bf16[128,1024]{1,0:T(8,128)(2,1)S(1)}, bf16[128,1024]{1,0:T(8,128)(2,1)S(1)}, u32[]{:S(2)}, u32[]{:S(2)}) %collective-permute-start.3) | collective-permute-done | bytes 262176 | tf_op jit(solution)/shard_map/ppermute | solution.py:204
  18.9 4.5 %collective-permute-start.7 = (bf16[128,1024]{1,0:T(8,128)(2,1)S(1)}, bf16[128,1024]{1,0:T(8,128)(2,1)S(1)}, u32[]{:S(2)}, u32[]{:S(2)}) collective-permute-start(bf16[128,1024]{1,0:T(8,128)(2,1)S(1)} %get-tuple-element.48.refs_2_), channel_id=1, source_target_pairs={{0,2},{1,3},{2,4},{3,5},{4,6},{5,7},{8,10},{9,11},{10,12},{11,13},... | collective-permute-start | bytes 786440 | tf_op jit(solution)/shard_map/ppermute | solution.py:204
  23.4 1.0 %collective-permute-done.2.refs_1_.refs_6_ = bf16[128,1024]{1,0:T(8,128)(2,1)S(1)} collective-permute-done((bf16[128,1024]{1,0:T(8,128)(2,1)S(1)}, bf16[128,1024]{1,0:T(8,128)(2,1)S(1)}, u32[]{:S(2)}, u32[]{:S(2)}) %collective-permute-start.2) | collective-permute-done | bytes 262176 | tf_op jit(solution)/shard_map/ppermute | solution.py:204
  24.6 0.5 collective-permute-start.5
  25.1 0.8 %collective-permute-done.4.refs_7_ = bf16[128,512]{1,0:T(8,128)(2,1)S(1)} collective-permute-done((bf16[128,512]{1,0:T(8,128)(2,1)S(1)}, bf16[128,512]{1,0:T(8,128)(2,1)S(1)}, u32[]{:S(2)}, u32[]{:S(2)}) %collective-permute-start.4) | collective-permute-done | bytes 131104 | tf_op jit(solution)/shard_map/ppermute | solution.py:204
  26.1 2.2 %attend.2 = (bf16[128,1024]{1,0:T(8,128)(2,1)S(1)}, bf16[128,1024]{1,0:T(8,128)(2,1)S(1)}, f32[128,1024]{1,0:T(8,128)S(1)}, f32[128,1024]{1,0:T(8,128)S(1)}, f32...) custom-call(s32[1,1024]{1,0:T(1,128)S(1)} %get-tuple-element.44.refs, ...), custom_call_target="tpu_custom_call" | custom-call | bytes 1 | tf_op jit(solution)/shard_map/attend/pallas_call | solution.py:36
  30.2 1.3 %collective-permute-start.17 = (bf16[128,1024]{1,0:T(8,128)(2,1)S(1)}, bf16[128,1024]{1,0:T(8,128)(2,1)S(1)}, u32[]{:S(2)}, u32[]{:S(2)}) collective-permute-start(bf16[128,1024]{1,0:T(8,128)(2,1)S(1)} %sink.4.refs_11_.refs_3_), channel_id=1, source_target_pairs={{2,0},{3,1},{4,2},{5,3},{6,4},{7,5},{10,8},{11,9},{12,10},{13,11},... | collective-permute-start | bytes 786440 | tf_op jit(solution)/shard_map/ppermute | solution.py:204
  31.5 2.3 %attend.3 = (bf16[128,1024]{1,0:T(8,128)(2,1)S(1)}, bf16[128,1024]{1,0:T(8,128)(2,1)S(1)}, f32[128,1024]{1,0:T(8,128)S(1)}, f32[128,1024]{1,0:T(8,128)S(1)}, f32...) custom-call(s32[1,1024]{1,0:T(1,128)S(1)} %get-tuple-element.44.refs, ...), custom_call_target="tpu_custom_call" | custom-call | bytes 1 | tf_op jit(solution)/shard_map/attend/pallas_call | solution.py:36
  34.5 1.0 %collective-permute-done.14.refs_1_ = f32[2,256]{1,0:T(2,128)S(1)} collective-permute-done((f32[2,256]{1,0:T(2,128)S(1)}, f32[2,256]{1,0:T(2,128)S(1)}, u32[]{:S(2)}, u32[]{:S(2)}) %collective-permute-start.14) | collective-permute-done | bytes 2080 | tf_op jit(solution)/shard_map/ppermute | solution.py:204
  35.8 1.3 %collective-permute-start.15 = (bf16[128,1024]{1,0:T(8,128)(2,1)S(1)}, bf16[128,1024]{1,0:T(8,128)(2,1)S(1)}, u32[]{:S(2)}, u32[]{:S(2)}) collective-permute-start(bf16[128,1024]{1,0:T(8,128)(2,1)S(1)} %sink.5.refs_5_), channel_id=1, source_target_pairs={{2,0},{3,1},{4,2},{5,3},{6,4},{7,5},{10,8},{11,9},{12,10},{13,11},... | collective-permute-start | bytes 786440 | tf_op jit(solution)/shard_map/ppermute | solution.py:204
  37.1 1.6 %collective-permute-start.19 = (f32[2,256]{1,0:T(2,128)S(1)}, f32[2,256]{1,0:T(2,128)S(1)}, u32[]{:S(2)}, u32[]{:S(2)}) collective-permute-start(f32[2,256]{1,0:T(2,128)S(1)} %add.6.refs_4_.refs_0_), channel_id=1, source_target_pairs={{0,8},{8,0},{16,24},{24,16},{1,9},{9,1},{17,25},{25,17},{2,10},{10... | collective-permute-start | bytes 6152 | tf_op jit(solution)/shard_map/ppermute | solution.py:204
  38.6 2.1 %collective-permute-done.19.refs_1_ = f32[2,256]{1,0:T(2,128)S(1)} collective-permute-done((f32[2,256]{1,0:T(2,128)S(1)}, f32[2,256]{1,0:T(2,128)S(1)}, u32[]{:S(2)}, u32[]{:S(2)}) %collective-permute-start.19) | collective-permute-done | bytes 2080 | tf_op jit(solution)/shard_map/ppermute | solution.py:204
  40.7 0.5 collective-permute-done.17.refs_1_
  41.3 1.3 %collective-permute-start.21 = (bf16[128,1024]{1,0:T(8,128)(2,1)S(1)}, bf16[128,1024]{1,0:T(8,128)(2,1)S(1)}, u32[]{:S(2)}, u32[]{:S(2)}) collective-permute-start(bf16[128,1024]{1,0:T(8,128)(2,1)S(1)} %sink.6.refs_5_), channel_id=1, source_target_pairs={{2,0},{3,1},{4,2},{5,3},{6,4},{7,5},{10,8},{11,9},{12,10},{13,11},... | collective-permute-start | bytes 786440 | tf_op jit(solution)/shard_map/ppermute | solution.py:204
  42.6 5.2 %collective-permute-done.15.refs_1_ = bf16[128,1024]{1,0:T(8,128)(2,1)S(1)} collective-permute-done((bf16[128,1024]{1,0:T(8,128)(2,1)S(1)}, bf16[128,1024]{1,0:T(8,128)(2,1)S(1)}, u32[]{:S(2)}, u32[]{:S(2)}) %collective-permute-start.15) | collective-permute-done | bytes 262176 | tf_op jit(solution)/shard_map/ppermute | solution.py:204
  48.0 1.3 %collective-permute-start.20 = (bf16[128,1024]{1,0:T(8,128)(2,1)S(1)}, bf16[128,1024]{1,0:T(8,128)(2,1)S(1)}, u32[]{:S(2)}, u32[]{:S(2)}) collective-permute-start(bf16[128,1024]{1,0:T(8,128)(2,1)S(1)} %sink.7.refs_4_), channel_id=1, source_target_pairs={{2,0},{3,1},{4,2},{5,3},{6,4},{7,5},{10,8},{11,9},{12,10},{13,11},... | collective-permute-start | bytes 786440 | tf_op jit(solution)/shard_map/ppermute | solution.py:204
  49.3 1.6 %collective-permute-start.22 = (f32[2,256]{1,0:T(2,128)S(1)}, f32[2,256]{1,0:T(2,128)S(1)}, u32[]{:S(2)}, u32[]{:S(2)}) collective-permute-start(f32[2,256]{1,0:T(2,128)S(1)} %add.7.refs_6_.refs_0_), channel_id=1, source_target_pairs={{0,16},{8,24},{16,0},{24,8},{1,17},{9,25},{17,1},{25,9},{2,18},{10... | collective-permute-start | bytes 6152 | tf_op jit(solution)/shard_map/ppermute | solution.py:204
  50.8 2.1 %collective-permute-done.22.refs_1_ = f32[2,256]{1,0:T(2,128)S(1)} collective-permute-done((f32[2,256]{1,0:T(2,128)S(1)}, f32[2,256]{1,0:T(2,128)S(1)}, u32[]{:S(2)}, u32[]{:S(2)}) %collective-permute-start.22) | collective-permute-done | bytes 2080 | tf_op jit(solution)/shard_map/ppermute | solution.py:204
  52.9 2.7 %collective-permute-start.23 = (f32[2,256]{1,0:T(2,128)S(1)}, f32[2,256]{1,0:T(2,128)S(1)}, u32[]{:S(2)}, u32[]{:S(2)}) collective-permute-start(f32[2,256]{1,0:T(2,128)S(1)} %add.8.refs_0_), channel_id=1, source_target_pairs={{0,2},{1,3},{2,0},{3,1},{4,6},{5,7},{6,4},{7,5},{8,10},{9,11},{10,... | collective-permute-start | bytes 6152 | tf_op jit(solution)/shard_map/ppermute | solution.py:204
  55.6 3.5 %collective-permute-start.24 = (f32[2,256]{1,0:T(2,128)S(1)}, f32[2,256]{1,0:T(2,128)S(1)}, u32[]{:S(2)}, u32[]{:S(2)}) collective-permute-start(f32[2,256]{1,0:T(2,128)S(1)} %add.8.refs_0_), channel_id=1, source_target_pairs={{0,4},{1,5},{2,6},{3,7},{4,0},{5,1},{6,2},{7,3},{8,12},{9,13},{10,... | collective-permute-start | bytes 6152 | tf_op jit(solution)/shard_map/ppermute | solution.py:204
  59.1 1.6 %collective-permute-done.24.refs_2_ = f32[2,256]{1,0:T(2,128)S(1)} collective-permute-done((f32[2,256]{1,0:T(2,128)S(1)}, f32[2,256]{1,0:T(2,128)S(1)}, u32[]{:S(2)}, u32[]{:S(2)}) %collective-permute-start.24) | collective-permute-done | bytes 2080 | tf_op jit(solution)/shard_map/ppermute | solution.py:204
  60.6 3.8 %collective-permute-done.25.refs_3_ = f32[2,256]{1,0:T(2,128)S(1)} collective-permute-done((f32[2,256]{1,0:T(2,128)S(1)}, f32[2,256]{1,0:T(2,128)S(1)}, u32[]{:S(2)}, u32[]{:S(2)}) %collective-permute-start.25) | collective-permute-done | bytes 2080 | tf_op jit(solution)/shard_map/ppermute | solution.py:204
  64.5 0.6 scale.1
  65.0 1.0 %assemble.1 = (bf16[1,128,2048]{2,1,0:T(8,128)(2,1)}, bf16[1,128,2048]{2,1,0:T(8,128)(2,1)}) custom-call(bf16[128,1024]{1,0:T(8,128)(2,1)S(1)} %get-tuple-element.53.refs_0_, bf16[128,1024]{1,0:T(8,128)(2,1)S(1)} %get-tuple-element.61.refs_1_, bf16[128,1024]{1,0:T(8,128)(2,1)S(1)} %get-tuple-element.62.refs_2_, ...), custom_call_target="tpu_custom_call" | custom-call | bytes 1 | tf_op jit(solution)/shard_map/assemble/pallas_call | solution.py:36
  66.1 0.9 %finish.2 = (bf16[1,128,1024]{2,1,0:T(8,128)(2,1)}, bf16[1,128,1024]{2,1,0:T(8,128)(2,1)}) custom-call(bf16[1,128,1024]{2,1,0:T(8,128)(2,1)S(1)} %copy-done.2, f32[1,256]{1,0:T(1,128)S(1)} %get-tuple-element.52.refs_10_.refs_1_, f32[128,1024]{1,0:T(8,128)S(1)} %get-tuple-element.75.refs_2_, bf16[128,1024]{1,0:T(8,128)(2,1)S(1)} %collective-permute-done.18.refs_4_.refs_3_, ...), custom_call_target="tpu_custom_call" | custom-call | flops 2147483648 | bytes 1 | tf_op jit(solution)/shard_map/finish/pallas_call | solution.py:36
  67.0 0.9 %finish.3 = (bf16[1,128,1024]{2,1,0:T(8,128)(2,1)}, bf16[1,128,1024]{2,1,0:T(8,128)(2,1)}) custom-call(bf16[1,128,1024]{2,1,0:T(8,128)(2,1)S(1)} %copy-done.2, f32[1,256]{1,0:T(1,128)S(1)} %get-tuple-element.52.refs_10_.refs_1_, f32[128,1024]{1,0:T(8,128)S(1)} %get-tuple-element.74.refs_2_, ...), custom_call_target="tpu_custom_call", output_to_operand_aliasing={{0}: (5, {}), {1}: (6, {})} | custom-call | flops 4294967296 | bytes 1 | tf_op jit(solution)/shard_map/finish/pallas_call | solution.py:36
  (47 shorter events, 3.7 us)
Async XLA Ops:
  1.6 11.6 %collective-permute-start = (bf16[128,1024]{1,0:T(8,128)(2,1)S(1)}, bf16[128,1024]{1,0:T(8,128)(2,1)S(1)}, u32[]{:S(2)}, u32[]{:S(2)}) collective-permute-start(bf16[128,1024]{1,0:T(8,128)(2,1)S(1)} %payload.2.refs_5_.refs_1_.refs_3_), channel_id=1, source_target_pairs={{0,2},{1,3},{2,4},{3,5},{4,6},{5,7},{8,10},{9,11},{10,12},{11,13},... | collective-permute-start | bytes 786440 | tf_op jit(solution)/shard_map/ppermute | solution.py:204
  7.6 11.3 %collective-permute-start.3 = (bf16[128,1024]{1,0:T(8,128)(2,1)S(1)}, bf16[128,1024]{1,0:T(8,128)(2,1)S(1)}, u32[]{:S(2)}, u32[]{:S(2)}) collective-permute-start(bf16[128,1024]{1,0:T(8,128)(2,1)S(1)} %get-tuple-element.47.refs_1_.refs_3_), channel_id=1, source_target_pairs={{0,2},{1,3},{2,4},{3,5},{4,6},{5,7},{8,10},{9,11},{10,12},{11,13},... | collective-permute-start | bytes 786440 | tf_op jit(solution)/shard_map/ppermute | solution.py:204
  13.3 11.2 %collective-permute-start.2 = (bf16[128,1024]{1,0:T(8,128)(2,1)S(1)}, bf16[128,1024]{1,0:T(8,128)(2,1)S(1)}, u32[]{:S(2)}, u32[]{:S(2)}) collective-permute-start(bf16[128,1024]{1,0:T(8,128)(2,1)S(1)} %get-tuple-element.46.refs_2_), channel_id=1, source_target_pairs={{0,2},{1,3},{2,4},{3,5},{4,6},{5,7},{8,10},{9,11},{10,12},{11,13},... | collective-permute-start | bytes 786440 | tf_op jit(solution)/shard_map/ppermute | solution.py:204
  17.7 7.5 %collective-permute-start.1 = (bf16[128,1024]{1,0:T(8,128)(2,1)S(1)}, bf16[128,1024]{1,0:T(8,128)(2,1)S(1)}, u32[]{:S(2)}, u32[]{:S(2)}) collective-permute-start(bf16[128,1024]{1,0:T(8,128)(2,1)S(1)} %get-tuple-element.45), channel_id=1, source_target_pairs={{0,1},{1,0},{2,3},{3,2},{4,5},{5,4},{6,7},{7,6},{8,9},{9,8},{10,11... | collective-permute-start | bytes 786440 | tf_op jit(solution)/shard_map/ppermute | solution.py:204
  18.9 7.2 %copy-start = (bf16[1,128,2048]{2,1,0:T(8,128)(2,1)S(1)}, bf16[1,128,2048]{2,1,0:T(8,128)(2,1)}, u32[]{:S(2)}) copy-start(bf16[1,128,2048]{2,1,0:T(8,128)(2,1)} %refs_1_.7) | copy-start | bytes 1572868
  18.9 7.2 %copy-start.1 = (bf16[1,128,2048]{2,1,0:T(8,128)(2,1)S(1)}, bf16[1,128,2048]{2,1,0:T(8,128)(2,1)}, u32[]{:S(2)}) copy-start(bf16[1,128,2048]{2,1,0:T(8,128)(2,1)} %refs_2_.5) | copy-start | bytes 1572868
  18.9 10.0 %collective-permute-start.7 = (bf16[128,1024]{1,0:T(8,128)(2,1)S(1)}, bf16[128,1024]{1,0:T(8,128)(2,1)S(1)}, u32[]{:S(2)}, u32[]{:S(2)}) collective-permute-start(bf16[128,1024]{1,0:T(8,128)(2,1)S(1)} %get-tuple-element.48.refs_2_), channel_id=1, source_target_pairs={{0,2},{1,3},{2,4},{3,5},{4,6},{5,7},{8,10},{9,11},{10,12},{11,13},... | collective-permute-start | bytes 786440 | tf_op jit(solution)/shard_map/ppermute | solution.py:204
  24.5 1.4 %collective-permute-start.4 = (bf16[128,512]{1,0:T(8,128)(2,1)S(1)}, bf16[128,512]{1,0:T(8,128)(2,1)S(1)}, u32[]{:S(2)}, u32[]{:S(2)}) collective-permute-start(bf16[128,512]{1,0:T(8,128)(2,1)S(1)} %get-tuple-element.49.refs_2_), channel_id=1, source_target_pairs={{0,1},{1,0},{2,3},{3,2},{4,5},{5,4},{6,7},{7,6},{8,9},{9,8},{10,11... | collective-permute-start | bytes 393224 | tf_op jit(solution)/shard_map/ppermute | solution.py:204
  24.6 1.5 %collective-permute-start.5 = (bf16[128,512]{1,0:T(8,128)(2,1)S(1)}, bf16[128,512]{1,0:T(8,128)(2,1)S(1)}, u32[]{:S(2)}, u32[]{:S(2)}) collective-permute-start(bf16[128,512]{1,0:T(8,128)(2,1)S(1)} %get-tuple-element.50), channel_id=1, source_target_pairs={{0,1},{1,0},{2,3},{3,2},{4,5},{5,4},{6,7},{7,6},{8,9},{9,8},{10,11... | collective-permute-start | bytes 393224 | tf_op jit(solution)/shard_map/ppermute | solution.py:204
  25.1 6.4 %collective-permute-start.6 = (bf16[128,1024]{1,0:T(8,128)(2,1)S(1)}, bf16[128,1024]{1,0:T(8,128)(2,1)S(1)}, u32[]{:S(2)}, u32[]{:S(2)}) collective-permute-start(bf16[128,1024]{1,0:T(8,128)(2,1)S(1)} %get-tuple-element.54), channel_id=1, source_target_pairs={{0,1},{1,0},{2,3},{3,2},{4,5},{5,4},{6,7},{7,6},{8,9},{9,8},{10,11... | collective-permute-start | bytes 786440 | tf_op jit(solution)/shard_map/ppermute | solution.py:204
  28.3 1.4 %collective-permute-start.10 = (bf16[128,512]{1,0:T(8,128)(2,1)S(1)}, bf16[128,512]{1,0:T(8,128)(2,1)S(1)}, u32[]{:S(2)}, u32[]{:S(2)}) collective-permute-start(bf16[128,512]{1,0:T(8,128)(2,1)S(1)} %get-tuple-element.59), channel_id=1, source_target_pairs={{0,1},{1,0},{2,3},{3,2},{4,5},{5,4},{6,7},{7,6},{8,9},{9,8},{10,11... | collective-permute-start | bytes 393224 | tf_op jit(solution)/shard_map/ppermute | solution.py:204
  28.7 1.4 %collective-permute-start.11 = (bf16[128,512]{1,0:T(8,128)(2,1)S(1)}, bf16[128,512]{1,0:T(8,128)(2,1)S(1)}, u32[]{:S(2)}, u32[]{:S(2)}) collective-permute-start(bf16[128,512]{1,0:T(8,128)(2,1)S(1)} %get-tuple-element.60), channel_id=1, source_target_pairs={{0,1},{1,0},{2,3},{3,2},{4,5},{5,4},{6,7},{7,6},{8,9},{9,8},{10,11... | collective-permute-start | bytes 393224 | tf_op jit(solution)/shard_map/ppermute | solution.py:204
  29.0 2.5 %collective-permute-start.8 = (bf16[128,512]{1,0:T(8,128)(2,1)S(1)}, bf16[128,512]{1,0:T(8,128)(2,1)S(1)}, u32[]{:S(2)}, u32[]{:S(2)}) collective-permute-start(bf16[128,512]{1,0:T(8,128)(2,1)S(1)} %get-tuple-element.56), channel_id=1, source_target_pairs={{0,1},{1,0},{2,3},{3,2},{4,5},{5,4},{6,7},{7,6},{8,9},{9,8},{10,11... | collective-permute-start | bytes 393224 | tf_op jit(solution)/shard_map/ppermute | solution.py:204
  29.4 2.1 %collective-permute-start.9 = (bf16[128,512]{1,0:T(8,128)(2,1)S(1)}, bf16[128,512]{1,0:T(8,128)(2,1)S(1)}, u32[]{:S(2)}, u32[]{:S(2)}) collective-permute-start(bf16[128,512]{1,0:T(8,128)(2,1)S(1)} %get-tuple-element.57), channel_id=1, source_target_pairs={{0,1},{1,0},{2,3},{3,2},{4,5},{5,4},{6,7},{7,6},{8,9},{9,8},{10,11... | collective-permute-start | bytes 393224 | tf_op jit(solution)/shard_map/ppermute | solution.py:204
  29.8 11.0 %collective-permute-start.18 = (bf16[128,1024]{1,0:T(8,128)(2,1)S(1)}, bf16[128,1024]{1,0:T(8,128)(2,1)S(1)}, u32[]{:S(2)}, u32[]{:S(2)}) collective-permute-start(bf16[128,1024]{1,0:T(8,128)(2,1)S(1)} %get-tuple-element.71), channel_id=1, source_target_pairs={{0,1},{1,0},{2,3},{3,2},{4,5},{5,4},{6,7},{7,6},{8,9},{9,8},{10,11... | collective-permute-start | bytes 786440 | tf_op jit(solution)/shard_map/ppermute | solution.py:204
  30.2 11.0 %collective-permute-start.17 = (bf16[128,1024]{1,0:T(8,128)(2,1)S(1)}, bf16[128,1024]{1,0:T(8,128)(2,1)S(1)}, u32[]{:S(2)}, u32[]{:S(2)}) collective-permute-start(bf16[128,1024]{1,0:T(8,128)(2,1)S(1)} %sink.4.refs_11_.refs_3_), channel_id=1, source_target_pairs={{2,0},{3,1},{4,2},{5,3},{6,4},{7,5},{10,8},{11,9},{12,10},{13,11},... | collective-permute-start | bytes 786440 | tf_op jit(solution)/shard_map/ppermute | solution.py:204
  33.8 1.9 %collective-permute-start.12 = (bf16[128,512]{1,0:T(8,128)(2,1)S(1)}, bf16[128,512]{1,0:T(8,128)(2,1)S(1)}, u32[]{:S(2)}, u32[]{:S(2)}) collective-permute-start(bf16[128,512]{1,0:T(8,128)(2,1)S(1)} %get-tuple-element.66), channel_id=1, source_target_pairs={{0,1},{1,0},{2,3},{3,2},{4,5},{5,4},{6,7},{7,6},{8,9},{9,8},{10,11... | collective-permute-start | bytes 393224 | tf_op jit(solution)/shard_map/ppermute | solution.py:204
  34.0 1.7 %collective-permute-start.13 = (bf16[128,512]{1,0:T(8,128)(2,1)S(1)}, bf16[128,512]{1,0:T(8,128)(2,1)S(1)}, u32[]{:S(2)}, u32[]{:S(2)}) collective-permute-start(bf16[128,512]{1,0:T(8,128)(2,1)S(1)} %get-tuple-element.67), channel_id=1, source_target_pairs={{0,1},{1,0},{2,3},{3,2},{4,5},{5,4},{6,7},{7,6},{8,9},{9,8},{10,11... | collective-permute-start | bytes 393224 | tf_op jit(solution)/shard_map/ppermute | solution.py:204
  34.3 1.2 %collective-permute-start.14 = (f32[2,256]{1,0:T(2,128)S(1)}, f32[2,256]{1,0:T(2,128)S(1)}, u32[]{:S(2)}, u32[]{:S(2)}) collective-permute-start(f32[2,256]{1,0:T(2,128)S(1)} %add.5.refs_0_), channel_id=1, source_target_pairs={{0,1},{1,0},{2,3},{3,2},{4,5},{5,4},{6,7},{7,6},{8,9},{9,8},{10,11... | collective-permute-start | bytes 6152 | tf_op jit(solution)/shard_map/ppermute | solution.py:204
  35.5 7.1 %collective-permute-start.16 = (bf16[128,1024]{1,0:T(8,128)(2,1)S(1)}, bf16[128,1024]{1,0:T(8,128)(2,1)S(1)}, u32[]{:S(2)}, u32[]{:S(2)}) collective-permute-start(bf16[128,1024]{1,0:T(8,128)(2,1)S(1)} %get-tuple-element.69), channel_id=1, source_target_pairs={{0,1},{1,0},{2,3},{3,2},{4,5},{5,4},{6,7},{7,6},{8,9},{9,8},{10,11... | collective-permute-start | bytes 786440 | tf_op jit(solution)/shard_map/ppermute | solution.py:204
  35.8 12.1 %collective-permute-start.15 = (bf16[128,1024]{1,0:T(8,128)(2,1)S(1)}, bf16[128,1024]{1,0:T(8,128)(2,1)S(1)}, u32[]{:S(2)}, u32[]{:S(2)}) collective-permute-start(bf16[128,1024]{1,0:T(8,128)(2,1)S(1)} %sink.5.refs_5_), channel_id=1, source_target_pairs={{2,0},{3,1},{4,2},{5,3},{6,4},{7,5},{10,8},{11,9},{12,10},{13,11},... | collective-permute-start | bytes 786440 | tf_op jit(solution)/shard_map/ppermute | solution.py:204
  37.1 3.7 %collective-permute-start.19 = (f32[2,256]{1,0:T(2,128)S(1)}, f32[2,256]{1,0:T(2,128)S(1)}, u32[]{:S(2)}, u32[]{:S(2)}) collective-permute-start(f32[2,256]{1,0:T(2,128)S(1)} %add.6.refs_4_.refs_0_), channel_id=1, source_target_pairs={{0,8},{8,0},{16,24},{24,16},{1,9},{9,1},{17,25},{25,17},{2,10},{10... | collective-permute-start | bytes 6152 | tf_op jit(solution)/shard_map/ppermute | solution.py:204
  41.3 24.8 %collective-permute-start.21 = (bf16[128,1024]{1,0:T(8,128)(2,1)S(1)}, bf16[128,1024]{1,0:T(8,128)(2,1)S(1)}, u32[]{:S(2)}, u32[]{:S(2)}) collective-permute-start(bf16[128,1024]{1,0:T(8,128)(2,1)S(1)} %sink.6.refs_5_), channel_id=1, source_target_pairs={{2,0},{3,1},{4,2},{5,3},{6,4},{7,5},{10,8},{11,9},{12,10},{13,11},... | collective-permute-start | bytes 786440 | tf_op jit(solution)/shard_map/ppermute | solution.py:204
  48.0 19.0 %collective-permute-start.20 = (bf16[128,1024]{1,0:T(8,128)(2,1)S(1)}, bf16[128,1024]{1,0:T(8,128)(2,1)S(1)}, u32[]{:S(2)}, u32[]{:S(2)}) collective-permute-start(bf16[128,1024]{1,0:T(8,128)(2,1)S(1)} %sink.7.refs_4_), channel_id=1, source_target_pairs={{2,0},{3,1},{4,2},{5,3},{6,4},{7,5},{10,8},{11,9},{12,10},{13,11},... | collective-permute-start | bytes 786440 | tf_op jit(solution)/shard_map/ppermute | solution.py:204
  49.3 3.7 %collective-permute-start.22 = (f32[2,256]{1,0:T(2,128)S(1)}, f32[2,256]{1,0:T(2,128)S(1)}, u32[]{:S(2)}, u32[]{:S(2)}) collective-permute-start(f32[2,256]{1,0:T(2,128)S(1)} %add.7.refs_6_.refs_0_), channel_id=1, source_target_pairs={{0,16},{8,24},{16,0},{24,8},{1,17},{9,25},{17,1},{25,9},{2,18},{10... | collective-permute-start | bytes 6152 | tf_op jit(solution)/shard_map/ppermute | solution.py:204
  52.9 6.2 %collective-permute-start.23 = (f32[2,256]{1,0:T(2,128)S(1)}, f32[2,256]{1,0:T(2,128)S(1)}, u32[]{:S(2)}, u32[]{:S(2)}) collective-permute-start(f32[2,256]{1,0:T(2,128)S(1)} %add.8.refs_0_), channel_id=1, source_target_pairs={{0,2},{1,3},{2,0},{3,1},{4,6},{5,7},{6,4},{7,5},{8,10},{9,11},{10,... | collective-permute-start | bytes 6152 | tf_op jit(solution)/shard_map/ppermute | solution.py:204
  55.6 5.1 %collective-permute-start.24 = (f32[2,256]{1,0:T(2,128)S(1)}, f32[2,256]{1,0:T(2,128)S(1)}, u32[]{:S(2)}, u32[]{:S(2)}) collective-permute-start(f32[2,256]{1,0:T(2,128)S(1)} %add.8.refs_0_), channel_id=1, source_target_pairs={{0,4},{1,5},{2,6},{3,7},{4,0},{5,1},{6,2},{7,3},{8,12},{9,13},{10,... | collective-permute-start | bytes 6152 | tf_op jit(solution)/shard_map/ppermute | solution.py:204
  59.1 5.4 %collective-permute-start.25 = (f32[2,256]{1,0:T(2,128)S(1)}, f32[2,256]{1,0:T(2,128)S(1)}, u32[]{:S(2)}, u32[]{:S(2)}) collective-permute-start(f32[2,256]{1,0:T(2,128)S(1)} %add.8.refs_0_), channel_id=1, source_target_pairs={{0,6},{1,7},{2,4},{3,5},{4,2},{5,3},{6,0},{7,1},{8,14},{9,15},{10,... | collective-permute-start | bytes 6152 | tf_op jit(solution)/shard_map/ppermute | solution.py:204
  65.0 1.0 %copy-start.2 = (bf16[1,128,1024]{2,1,0:T(8,128)(2,1)S(1)}, bf16[1,128,1024]{2,1,0:T(8,128)(2,1)}, u32[]{:S(2)}) copy-start(bf16[1,128,1024]{2,1,0:T(8,128)(2,1)} %refs_0_.7) | copy-start | bytes 786436

commit v6 on v5

--- a/solution.py
+++ b/solution.py
@@ -170,9 +170,10 @@
     refs[-1][...] = sum(ref[...] for ref in refs[1:-1]) + refs[0][...]
 
 
-def scale(factor, total, query_gains, key_gains):
-    query_gains[...] = total[0:1, :] * factor
-    key_gains[...] = total[1:2, :] * factor
+def scale(factor, *refs):
+    total = sum(ref[...] for ref in refs[1:-2]) + refs[0][...]
+    refs[-2][...] = total[0:1, :] * factor
+    refs[-1][...] = total[1:2, :] * factor
 
 
 def finish(count, at, keys, key_gain, part_own, swapped, arrived, *rest):
@@ -373,8 +374,11 @@
             last = [*last, total]
         last = [sink(chunk, last)]
 
-    total = total_over(total, "dp", 1, 2, 2)
+    unit = 1
     for step in range(amount, amount + LAG):
+        end = unit * 2 if step + 1 < amount + LAG else lax.axis_size("dp")
+        total = total_over(total, "dp", unit, end, 2)
+        unit = end
         last = [sink(step, [*last, total])]
     key_outputs = []
     for chunk, (first, count) in enumerate(CHUNKS):
@@ -403,11 +407,20 @@
         last,
     )
 
-    total = total_over(total, "dp", 2, lax.axis_size("dp"), 2)
-    total = total_over(total, "ctx", 2, lax.axis_size("ctx"), 4, last)
     factor = (lax.axis_size("dp") * queries.shape[0] * lax.axis_size("ctx") * rows) ** (-0.5)
     row = shape(1, HEAD_DIM, F32)
-    query_gains, key_gains = call(functools.partial(scale, factor), "scale", dict(t=total), dict(a=row, b=row))
+    chips = lax.axis_size("ctx") // 2
+    while chips > 4:
+        total = total_over(total, "ctx", chips, 2 * chips, 2)
+        chips //= 2
+    others = [move(total, "ctx", lambda i: i ^ (2 * by)) for by in range(1, chips)]
+    query_gains, key_gains = call(
+        functools.partial(scale, factor),
+        "scale",
+        dict(enumerate([total, *others])),
+        dict(a=row, b=row),
+        [pltpu.with_memory_space_constraint(field, pltpu.HBM) for field in (attended, *key_outputs)],
+    )
     return attended, query_grad, *key_outputs, query_gains[0], key_gains[0]
 
 

time: 68.4 us -> 62.6 us (0.915)
  waiting for transfers between devices: 21.7 us -> 15.5 us
    ppermute x26, waiting for transfers between devices: 21.7 us -> 15.5 us  [move(): lax.ppermute(field, axis, [(i, target(i)) for i in range(size) if 0 <= ta...]
    pallas_call x21 -> x20, Pallas kernels: 10.4 us -> 10.4 us  [call(): pl.pallas_call(kernel, out_shape=list(outs.values()), in_specs=specs, out...]
  transfers between devices with their start and end apart: 26 -> 26, of which waited for: 13 -> 14; matrix products, arithmetic and copies ran while one was open for 0% -> 0% of each run, Pallas kernels for 13% -> 14%
where the time goes in v6:
time: 62.6 us; the launch traced here: 62.1 us
  starting transfers between devices  35.3 us (56%)
  waiting for transfers between devices  15.5 us (25%)
  Pallas kernels  10.4 us (17%)
  between operations  0.82 us (1%)
    ppermute x26, starting transfers between devices, move(): lax.ppermute(field, axis, [(i, target(i)) for i in range(size) if 0 <= ta...  35.3 us
    ppermute x26, waiting for transfers between devices, move(): lax.ppermute(field, axis, [(i, target(i)) for i in range(size) if 0 <= ta...  15.5 us
    pallas_call x20, Pallas kernels, call(): pl.pallas_call(kernel, out_shape=list(outs.values()), in_specs=specs, out...  10.4 us
  transfers between devices with their start and end apart: 26, of which 14 were waited for; matrix products, arithmetic and copies ran while one was open for 0% of the time, Pallas kernels for 14%

profile of v6, /device:TPU:0, one launch (start us, length us, event | category | flops | bytes accessed | tf_op | source)
XLA Modules:
  0.0 62.1 jit_solution(12769709570234752429)
XLA Ops:
  0.6 0.9 %payload.2.refs_5_.refs_1_.refs_3_ = bf16[128,1024]{1,0:T(8,128)(2,1)S(1)} custom-call(bf16[1,128,1024]{2,1,0:T(8,128)(2,1)} %refs_0_.7, bf16[1,128,1024]{2,1,0:T(8,128)(2,1)} %refs_1_.5), custom_call_target="tpu_custom_call" | custom-call | bytes 1 | tf_op jit(solution)/shard_map/payload/pallas_call | solution.py:36
  1.6 4.9 %collective-permute-start = (bf16[128,1024]{1,0:T(8,128)(2,1)S(1)}, bf16[128,1024]{1,0:T(8,128)(2,1)S(1)}, u32[]{:S(2)}, u32[]{:S(2)}) collective-permute-start(bf16[128,1024]{1,0:T(8,128)(2,1)S(1)} %payload.2.refs_5_.refs_1_.refs_3_), channel_id=1, source_target_pairs={{0,2},{1,3},{2,4},{3,5},{4,6},{5,7},{8,10},{9,11},{10,12},{11,13},... | collective-permute-start | bytes 786440 | tf_op jit(solution)/shard_map/ppermute | solution.py:205
  6.5 1.0 %payload.3 = (bf16[128,1024]{1,0:T(8,128)(2,1)S(1)}, s32[1,1024]{1,0:T(1,128)S(1)}, f32[1,256]{1,0:T(1,128)S(1)}, f32[1,256]{1,0:T(1,128)S(1)}) custom-call(bf16[1,128,1024]{2,1,0:T(8,128)(2,1)} %refs_0_.7, bf16[1,128,1024]{2,1,0:T(8,128)(2,1)} %refs_1_.5, s32[1,1024]{1,0:T(1,128)} %refs_2_.3, f32[1,256]{1,0:T(1,128)} %bitcast.4, f32[1,256]{1,0:T(1,128)} %bitcast.5, ...), custom_call_target="tpu_custom_call" | custom-call | bytes 1 | tf_op jit(solution)/shard_map/payload/pallas_call | solution.py:36
  7.6 3.5 %collective-permute-start.3 = (bf16[128,1024]{1,0:T(8,128)(2,1)S(1)}, bf16[128,1024]{1,0:T(8,128)(2,1)S(1)}, u32[]{:S(2)}, u32[]{:S(2)}) collective-permute-start(bf16[128,1024]{1,0:T(8,128)(2,1)S(1)} %get-tuple-element.47.refs_1_.refs_3_), channel_id=1, source_target_pairs={{0,2},{1,3},{2,4},{3,5},{4,6},{5,7},{8,10},{9,11},{10,12},{11,13},... | collective-permute-start | bytes 786440 | tf_op jit(solution)/shard_map/ppermute | solution.py:205
  11.1 2.2 %collective-permute-done.refs_0_.refs_5_ = bf16[128,1024]{1,0:T(8,128)(2,1)S(1)} collective-permute-done((bf16[128,1024]{1,0:T(8,128)(2,1)S(1)}, bf16[128,1024]{1,0:T(8,128)(2,1)S(1)}, u32[]{:S(2)}, u32[]{:S(2)}) %collective-permute-start) | collective-permute-done | bytes 262176 | tf_op jit(solution)/shard_map/ppermute | solution.py:205
  13.3 4.4 %collective-permute-start.2 = (bf16[128,1024]{1,0:T(8,128)(2,1)S(1)}, bf16[128,1024]{1,0:T(8,128)(2,1)S(1)}, u32[]{:S(2)}, u32[]{:S(2)}) collective-permute-start(bf16[128,1024]{1,0:T(8,128)(2,1)S(1)} %get-tuple-element.46.refs_2_), channel_id=1, source_target_pairs={{0,2},{1,3},{2,4},{3,5},{4,6},{5,7},{8,10},{9,11},{10,12},{11,13},... | collective-permute-start | bytes 786440 | tf_op jit(solution)/shard_map/ppermute | solution.py:205
  17.7 1.1 %collective-permute-done.3.refs_0_.refs_5_ = bf16[128,1024]{1,0:T(8,128)(2,1)S(1)} collective-permute-done((bf16[128,1024]{1,0:T(8,128)(2,1)S(1)}, bf16[128,1024]{1,0:T(8,128)(2,1)S(1)}, u32[]{:S(2)}, u32[]{:S(2)}) %collective-permute-start.3) | collective-permute-done | bytes 262176 | tf_op jit(solution)/shard_map/ppermute | solution.py:205
  18.9 4.5 %collective-permute-start.7 = (bf16[128,1024]{1,0:T(8,128)(2,1)S(1)}, bf16[128,1024]{1,0:T(8,128)(2,1)S(1)}, u32[]{:S(2)}, u32[]{:S(2)}) collective-permute-start(bf16[128,1024]{1,0:T(8,128)(2,1)S(1)} %get-tuple-element.48.refs_2_), channel_id=1, source_target_pairs={{0,2},{1,3},{2,4},{3,5},{4,6},{5,7},{8,10},{9,11},{10,12},{11,13},... | collective-permute-start | bytes 786440 | tf_op jit(solution)/shard_map/ppermute | solution.py:205
  23.4 1.0 %collective-permute-done.2.refs_1_.refs_6_ = bf16[128,1024]{1,0:T(8,128)(2,1)S(1)} collective-permute-done((bf16[128,1024]{1,0:T(8,128)(2,1)S(1)}, bf16[128,1024]{1,0:T(8,128)(2,1)S(1)}, u32[]{:S(2)}, u32[]{:S(2)}) %collective-permute-start.2) | collective-permute-done | bytes 262176 | tf_op jit(solution)/shard_map/ppermute | solution.py:205
  24.6 0.5 collective-permute-start.5
  25.1 0.8 %collective-permute-done.4.refs_7_ = bf16[128,512]{1,0:T(8,128)(2,1)S(1)} collective-permute-done((bf16[128,512]{1,0:T(8,128)(2,1)S(1)}, bf16[128,512]{1,0:T(8,128)(2,1)S(1)}, u32[]{:S(2)}, u32[]{:S(2)}) %collective-permute-start.4) | collective-permute-done | bytes 131104 | tf_op jit(solution)/shard_map/ppermute | solution.py:205
  26.1 2.2 %attend.2 = (bf16[128,1024]{1,0:T(8,128)(2,1)S(1)}, bf16[128,1024]{1,0:T(8,128)(2,1)S(1)}, f32[128,1024]{1,0:T(8,128)S(1)}, f32[128,1024]{1,0:T(8,128)S(1)}, f32...) custom-call(s32[1,1024]{1,0:T(1,128)S(1)} %get-tuple-element.44.refs, ...), custom_call_target="tpu_custom_call" | custom-call | bytes 1 | tf_op jit(solution)/shard_map/attend/pallas_call | solution.py:36
  30.2 1.3 %collective-permute-start.17 = (bf16[128,1024]{1,0:T(8,128)(2,1)S(1)}, bf16[128,1024]{1,0:T(8,128)(2,1)S(1)}, u32[]{:S(2)}, u32[]{:S(2)}) collective-permute-start(bf16[128,1024]{1,0:T(8,128)(2,1)S(1)} %sink.4.refs_11_.refs_3_), channel_id=1, source_target_pairs={{2,0},{3,1},{4,2},{5,3},{6,4},{7,5},{10,8},{11,9},{12,10},{13,11},... | collective-permute-start | bytes 786440 | tf_op jit(solution)/shard_map/ppermute | solution.py:205
  31.5 2.3 %attend.3 = (bf16[128,1024]{1,0:T(8,128)(2,1)S(1)}, bf16[128,1024]{1,0:T(8,128)(2,1)S(1)}, f32[128,1024]{1,0:T(8,128)S(1)}, f32[128,1024]{1,0:T(8,128)S(1)}, f32...) custom-call(s32[1,1024]{1,0:T(1,128)S(1)} %get-tuple-element.44.refs, ...), custom_call_target="tpu_custom_call" | custom-call | bytes 1 | tf_op jit(solution)/shard_map/attend/pallas_call | solution.py:36
  34.5 1.0 %collective-permute-done.14.refs_1_ = f32[2,256]{1,0:T(2,128)S(1)} collective-permute-done((f32[2,256]{1,0:T(2,128)S(1)}, f32[2,256]{1,0:T(2,128)S(1)}, u32[]{:S(2)}, u32[]{:S(2)}) %collective-permute-start.14) | collective-permute-done | bytes 2080 | tf_op jit(solution)/shard_map/ppermute | solution.py:205
  35.8 1.3 %collective-permute-start.15 = (bf16[128,1024]{1,0:T(8,128)(2,1)S(1)}, bf16[128,1024]{1,0:T(8,128)(2,1)S(1)}, u32[]{:S(2)}, u32[]{:S(2)}) collective-permute-start(bf16[128,1024]{1,0:T(8,128)(2,1)S(1)} %sink.5.refs_5_), channel_id=1, source_target_pairs={{2,0},{3,1},{4,2},{5,3},{6,4},{7,5},{10,8},{11,9},{12,10},{13,11},... | collective-permute-start | bytes 786440 | tf_op jit(solution)/shard_map/ppermute | solution.py:205
  37.1 1.6 %collective-permute-start.19 = (f32[2,256]{1,0:T(2,128)S(1)}, f32[2,256]{1,0:T(2,128)S(1)}, u32[]{:S(2)}, u32[]{:S(2)}) collective-permute-start(f32[2,256]{1,0:T(2,128)S(1)} %add.5.refs_4_.refs_0_), channel_id=1, source_target_pairs={{0,8},{8,0},{16,24},{24,16},{1,9},{9,1},{17,25},{25,17},{2,10},{10... | collective-permute-start | bytes 6152 | tf_op jit(solution)/shard_map/ppermute | solution.py:205
  38.6 2.1 %collective-permute-done.19.refs_1_ = f32[2,256]{1,0:T(2,128)S(1)} collective-permute-done((f32[2,256]{1,0:T(2,128)S(1)}, f32[2,256]{1,0:T(2,128)S(1)}, u32[]{:S(2)}, u32[]{:S(2)}) %collective-permute-start.19) | collective-permute-done | bytes 2080 | tf_op jit(solution)/shard_map/ppermute | solution.py:205
  41.3 1.3 %collective-permute-start.22 = (bf16[128,1024]{1,0:T(8,128)(2,1)S(1)}, bf16[128,1024]{1,0:T(8,128)(2,1)S(1)}, u32[]{:S(2)}, u32[]{:S(2)}) collective-permute-start(bf16[128,1024]{1,0:T(8,128)(2,1)S(1)} %sink.6.refs_5_), channel_id=1, source_target_pairs={{2,0},{3,1},{4,2},{5,3},{6,4},{7,5},{10,8},{11,9},{12,10},{13,11},... | collective-permute-start | bytes 786440 | tf_op jit(solution)/shard_map/ppermute | solution.py:205
  42.6 1.6 %collective-permute-start.20 = (f32[2,256]{1,0:T(2,128)S(1)}, f32[2,256]{1,0:T(2,128)S(1)}, u32[]{:S(2)}, u32[]{:S(2)}) collective-permute-start(f32[2,256]{1,0:T(2,128)S(1)} %add.6.refs_6_.refs_0_), channel_id=1, source_target_pairs={{0,16},{8,24},{16,0},{24,8},{1,17},{9,25},{17,1},{25,9},{2,18},{10... | collective-permute-start | bytes 6152 | tf_op jit(solution)/shard_map/ppermute | solution.py:205
  44.2 2.1 %collective-permute-done.20.refs_1_ = f32[2,256]{1,0:T(2,128)S(1)} collective-permute-done((f32[2,256]{1,0:T(2,128)S(1)}, f32[2,256]{1,0:T(2,128)S(1)}, u32[]{:S(2)}, u32[]{:S(2)}) %collective-permute-start.20) | collective-permute-done | bytes 2080 | tf_op jit(solution)/shard_map/ppermute | solution.py:205
  46.3 1.6 %collective-permute-done.15.refs_1_ = bf16[128,1024]{1,0:T(8,128)(2,1)S(1)} collective-permute-done((bf16[128,1024]{1,0:T(8,128)(2,1)S(1)}, bf16[128,1024]{1,0:T(8,128)(2,1)S(1)}, u32[]{:S(2)}, u32[]{:S(2)}) %collective-permute-start.15) | collective-permute-done | bytes 262176 | tf_op jit(solution)/shard_map/ppermute | solution.py:205
  48.0 1.3 %collective-permute-start.21 = (bf16[128,1024]{1,0:T(8,128)(2,1)S(1)}, bf16[128,1024]{1,0:T(8,128)(2,1)S(1)}, u32[]{:S(2)}, u32[]{:S(2)}) collective-permute-start(bf16[128,1024]{1,0:T(8,128)(2,1)S(1)} %sink.7.refs_4_), channel_id=1, source_target_pairs={{2,0},{3,1},{4,2},{5,3},{6,4},{7,5},{10,8},{11,9},{12,10},{13,11},... | collective-permute-start | bytes 786440 | tf_op jit(solution)/shard_map/ppermute | solution.py:205
  49.3 3.0 %collective-permute-start.23 = (f32[2,256]{1,0:T(2,128)S(1)}, f32[2,256]{1,0:T(2,128)S(1)}, u32[]{:S(2)}, u32[]{:S(2)}) collective-permute-start(f32[2,256]{1,0:T(2,128)S(1)} %add.7.refs_6_.refs_0_), channel_id=1, source_target_pairs={{0,2},{1,3},{2,0},{3,1},{4,6},{5,7},{6,4},{7,5},{8,10},{9,11},{10,... | collective-permute-start | bytes 6152 | tf_op jit(solution)/shard_map/ppermute | solution.py:205
  52.3 3.5 %collective-permute-start.24 = (f32[2,256]{1,0:T(2,128)S(1)}, f32[2,256]{1,0:T(2,128)S(1)}, u32[]{:S(2)}, u32[]{:S(2)}) collective-permute-start(f32[2,256]{1,0:T(2,128)S(1)} %add.7.refs_6_.refs_0_), channel_id=1, source_target_pairs={{0,4},{1,5},{2,6},{3,7},{4,0},{5,1},{6,2},{7,3},{8,12},{9,13},{10,... | collective-permute-start | bytes 6152 | tf_op jit(solution)/shard_map/ppermute | solution.py:205
  55.8 1.0 %assemble.1 = (bf16[1,128,2048]{2,1,0:T(8,128)(2,1)}, bf16[1,128,2048]{2,1,0:T(8,128)(2,1)}) custom-call(bf16[128,1024]{1,0:T(8,128)(2,1)S(1)} %get-tuple-element.53.refs_0_, bf16[128,1024]{1,0:T(8,128)(2,1)S(1)} %get-tuple-element.61.refs_1_, bf16[128,1024]{1,0:T(8,128)(2,1)S(1)} %get-tuple-element.62.refs_2_, ...), custom_call_target="tpu_custom_call" | custom-call | bytes 1 | tf_op jit(solution)/shard_map/assemble/pallas_call | solution.py:36
  56.8 0.9 %finish.2 = (bf16[1,128,1024]{2,1,0:T(8,128)(2,1)}, bf16[1,128,1024]{2,1,0:T(8,128)(2,1)}) custom-call(bf16[1,128,1024]{2,1,0:T(8,128)(2,1)S(1)} %copy-done.2, f32[1,256]{1,0:T(1,128)S(1)} %get-tuple-element.52.refs_10_.refs_1_, f32[128,1024]{1,0:T(8,128)S(1)} %get-tuple-element.75.refs_2_, bf16[128,1024]{1,0:T(8,128)(2,1)S(1)} %collective-permute-done.18.refs_4_.refs_3_, ...), custom_call_target="tpu_custom_call" | custom-call | flops 2147483648 | bytes 1 | tf_op jit(solution)/shard_map/finish/pallas_call | solution.py:36
  57.7 1.1 %collective-permute-done.21.refs_4_ = bf16[128,1024]{1,0:T(8,128)(2,1)S(1)} collective-permute-done((bf16[128,1024]{1,0:T(8,128)(2,1)S(1)}, bf16[128,1024]{1,0:T(8,128)(2,1)S(1)}, u32[]{:S(2)}, u32[]{:S(2)}) %collective-permute-start.21) | collective-permute-done | bytes 262176 | tf_op jit(solution)/shard_map/ppermute | solution.py:205
  58.8 0.9 %finish.3 = (bf16[1,128,1024]{2,1,0:T(8,128)(2,1)}, bf16[1,128,1024]{2,1,0:T(8,128)(2,1)}) custom-call(bf16[1,128,1024]{2,1,0:T(8,128)(2,1)S(1)} %copy-done.2, f32[1,256]{1,0:T(1,128)S(1)} %get-tuple-element.52.refs_10_.refs_1_, f32[128,1024]{1,0:T(8,128)S(1)} %get-tuple-element.74.refs_2_, ...), custom_call_target="tpu_custom_call", output_to_operand_aliasing={{0}: (5, {}), {1}: (6, {})} | custom-call | flops 4294967296 | bytes 1 | tf_op jit(solution)/shard_map/finish/pallas_call | solution.py:36
  59.8 0.6 collective-permute-done.24.refs_2_
  60.3 1.2 %collective-permute-done.25.refs_3_ = f32[2,256]{1,0:T(2,128)S(1)} collective-permute-done((f32[2,256]{1,0:T(2,128)S(1)}, f32[2,256]{1,0:T(2,128)S(1)}, u32[]{:S(2)}, u32[]{:S(2)}) %collective-permute-start.25) | collective-permute-done | bytes 2080 | tf_op jit(solution)/shard_map/ppermute | solution.py:205
  61.6 0.6 scale.1
  (46 shorter events, 4.1 us)
Async XLA Ops:
  1.6 11.6 %collective-permute-start = (bf16[128,1024]{1,0:T(8,128)(2,1)S(1)}, bf16[128,1024]{1,0:T(8,128)(2,1)S(1)}, u32[]{:S(2)}, u32[]{:S(2)}) collective-permute-start(bf16[128,1024]{1,0:T(8,128)(2,1)S(1)} %payload.2.refs_5_.refs_1_.refs_3_), channel_id=1, source_target_pairs={{0,2},{1,3},{2,4},{3,5},{4,6},{5,7},{8,10},{9,11},{10,12},{11,13},... | collective-permute-start | bytes 786440 | tf_op jit(solution)/shard_map/ppermute | solution.py:205
  7.6 11.3 %collective-permute-start.3 = (bf16[128,1024]{1,0:T(8,128)(2,1)S(1)}, bf16[128,1024]{1,0:T(8,128)(2,1)S(1)}, u32[]{:S(2)}, u32[]{:S(2)}) collective-permute-start(bf16[128,1024]{1,0:T(8,128)(2,1)S(1)} %get-tuple-element.47.refs_1_.refs_3_), channel_id=1, source_target_pairs={{0,2},{1,3},{2,4},{3,5},{4,6},{5,7},{8,10},{9,11},{10,12},{11,13},... | collective-permute-start | bytes 786440 | tf_op jit(solution)/shard_map/ppermute | solution.py:205
  13.3 11.2 %collective-permute-start.2 = (bf16[128,1024]{1,0:T(8,128)(2,1)S(1)}, bf16[128,1024]{1,0:T(8,128)(2,1)S(1)}, u32[]{:S(2)}, u32[]{:S(2)}) collective-permute-start(bf16[128,1024]{1,0:T(8,128)(2,1)S(1)} %get-tuple-element.46.refs_2_), channel_id=1, source_target_pairs={{0,2},{1,3},{2,4},{3,5},{4,6},{5,7},{8,10},{9,11},{10,12},{11,13},... | collective-permute-start | bytes 786440 | tf_op jit(solution)/shard_map/ppermute | solution.py:205
  17.7 7.5 %collective-permute-start.1 = (bf16[128,1024]{1,0:T(8,128)(2,1)S(1)}, bf16[128,1024]{1,0:T(8,128)(2,1)S(1)}, u32[]{:S(2)}, u32[]{:S(2)}) collective-permute-start(bf16[128,1024]{1,0:T(8,128)(2,1)S(1)} %get-tuple-element.45), channel_id=1, source_target_pairs={{0,1},{1,0},{2,3},{3,2},{4,5},{5,4},{6,7},{7,6},{8,9},{9,8},{10,11... | collective-permute-start | bytes 786440 | tf_op jit(solution)/shard_map/ppermute | solution.py:205
  18.9 7.2 %copy-start = (bf16[1,128,2048]{2,1,0:T(8,128)(2,1)S(1)}, bf16[1,128,2048]{2,1,0:T(8,128)(2,1)}, u32[]{:S(2)}) copy-start(bf16[1,128,2048]{2,1,0:T(8,128)(2,1)} %refs_1_.7) | copy-start | bytes 1572868
  18.9 7.2 %copy-start.1 = (bf16[1,128,2048]{2,1,0:T(8,128)(2,1)S(1)}, bf16[1,128,2048]{2,1,0:T(8,128)(2,1)}, u32[]{:S(2)}) copy-start(bf16[1,128,2048]{2,1,0:T(8,128)(2,1)} %refs_2_.5) | copy-start | bytes 1572868
  18.9 10.0 %collective-permute-start.7 = (bf16[128,1024]{1,0:T(8,128)(2,1)S(1)}, bf16[128,1024]{1,0:T(8,128)(2,1)S(1)}, u32[]{:S(2)}, u32[]{:S(2)}) collective-permute-start(bf16[128,1024]{1,0:T(8,128)(2,1)S(1)} %get-tuple-element.48.refs_2_), channel_id=1, source_target_pairs={{0,2},{1,3},{2,4},{3,5},{4,6},{5,7},{8,10},{9,11},{10,12},{11,13},... | collective-permute-start | bytes 786440 | tf_op jit(solution)/shard_map/ppermute | solution.py:205
  24.5 1.4 %collective-permute-start.4 = (bf16[128,512]{1,0:T(8,128)(2,1)S(1)}, bf16[128,512]{1,0:T(8,128)(2,1)S(1)}, u32[]{:S(2)}, u32[]{:S(2)}) collective-permute-start(bf16[128,512]{1,0:T(8,128)(2,1)S(1)} %get-tuple-element.49.refs_2_), channel_id=1, source_target_pairs={{0,1},{1,0},{2,3},{3,2},{4,5},{5,4},{6,7},{7,6},{8,9},{9,8},{10,11... | collective-permute-start | bytes 393224 | tf_op jit(solution)/shard_map/ppermute | solution.py:205
  24.6 1.5 %collective-permute-start.5 = (bf16[128,512]{1,0:T(8,128)(2,1)S(1)}, bf16[128,512]{1,0:T(8,128)(2,1)S(1)}, u32[]{:S(2)}, u32[]{:S(2)}) collective-permute-start(bf16[128,512]{1,0:T(8,128)(2,1)S(1)} %get-tuple-element.50), channel_id=1, source_target_pairs={{0,1},{1,0},{2,3},{3,2},{4,5},{5,4},{6,7},{7,6},{8,9},{9,8},{10,11... | collective-permute-start | bytes 393224 | tf_op jit(solution)/shard_map/ppermute | solution.py:205
  25.1 6.4 %collective-permute-start.6 = (bf16[128,1024]{1,0:T(8,128)(2,1)S(1)}, bf16[128,1024]{1,0:T(8,128)(2,1)S(1)}, u32[]{:S(2)}, u32[]{:S(2)}) collective-permute-start(bf16[128,1024]{1,0:T(8,128)(2,1)S(1)} %get-tuple-element.54), channel_id=1, source_target_pairs={{0,1},{1,0},{2,3},{3,2},{4,5},{5,4},{6,7},{7,6},{8,9},{9,8},{10,11... | collective-permute-start | bytes 786440 | tf_op jit(solution)/shard_map/ppermute | solution.py:205
  28.3 1.4 %collective-permute-start.10 = (bf16[128,512]{1,0:T(8,128)(2,1)S(1)}, bf16[128,512]{1,0:T(8,128)(2,1)S(1)}, u32[]{:S(2)}, u32[]{:S(2)}) collective-permute-start(bf16[128,512]{1,0:T(8,128)(2,1)S(1)} %get-tuple-element.59), channel_id=1, source_target_pairs={{0,1},{1,0},{2,3},{3,2},{4,5},{5,4},{6,7},{7,6},{8,9},{9,8},{10,11... | collective-permute-start | bytes 393224 | tf_op jit(solution)/shard_map/ppermute | solution.py:205
  28.7 1.4 %collective-permute-start.11 = (bf16[128,512]{1,0:T(8,128)(2,1)S(1)}, bf16[128,512]{1,0:T(8,128)(2,1)S(1)}, u32[]{:S(2)}, u32[]{:S(2)}) collective-permute-start(bf16[128,512]{1,0:T(8,128)(2,1)S(1)} %get-tuple-element.60), channel_id=1, source_target_pairs={{0,1},{1,0},{2,3},{3,2},{4,5},{5,4},{6,7},{7,6},{8,9},{9,8},{10,11... | collective-permute-start | bytes 393224 | tf_op jit(solution)/shard_map/ppermute | solution.py:205
  29.0 2.5 %collective-permute-start.8 = (bf16[128,512]{1,0:T(8,128)(2,1)S(1)}, bf16[128,512]{1,0:T(8,128)(2,1)S(1)}, u32[]{:S(2)}, u32[]{:S(2)}) collective-permute-start(bf16[128,512]{1,0:T(8,128)(2,1)S(1)} %get-tuple-element.56), channel_id=1, source_target_pairs={{0,1},{1,0},{2,3},{3,2},{4,5},{5,4},{6,7},{7,6},{8,9},{9,8},{10,11... | collective-permute-start | bytes 393224 | tf_op jit(solution)/shard_map/ppermute | solution.py:205
  29.4 2.1 %collective-permute-start.9 = (bf16[128,512]{1,0:T(8,128)(2,1)S(1)}, bf16[128,512]{1,0:T(8,128)(2,1)S(1)}, u32[]{:S(2)}, u32[]{:S(2)}) collective-permute-start(bf16[128,512]{1,0:T(8,128)(2,1)S(1)} %get-tuple-element.57), channel_id=1, source_target_pairs={{0,1},{1,0},{2,3},{3,2},{4,5},{5,4},{6,7},{7,6},{8,9},{9,8},{10,11... | collective-permute-start | bytes 393224 | tf_op jit(solution)/shard_map/ppermute | solution.py:205
  29.8 11.0 %collective-permute-start.18 = (bf16[128,1024]{1,0:T(8,128)(2,1)S(1)}, bf16[128,1024]{1,0:T(8,128)(2,1)S(1)}, u32[]{:S(2)}, u32[]{:S(2)}) collective-permute-start(bf16[128,1024]{1,0:T(8,128)(2,1)S(1)} %get-tuple-element.71), channel_id=1, source_target_pairs={{0,1},{1,0},{2,3},{3,2},{4,5},{5,4},{6,7},{7,6},{8,9},{9,8},{10,11... | collective-permute-start | bytes 786440 | tf_op jit(solution)/shard_map/ppermute | solution.py:205
  30.2 11.0 %collective-permute-start.17 = (bf16[128,1024]{1,0:T(8,128)(2,1)S(1)}, bf16[128,1024]{1,0:T(8,128)(2,1)S(1)}, u32[]{:S(2)}, u32[]{:S(2)}) collective-permute-start(bf16[128,1024]{1,0:T(8,128)(2,1)S(1)} %sink.4.refs_11_.refs_3_), channel_id=1, source_target_pairs={{2,0},{3,1},{4,2},{5,3},{6,4},{7,5},{10,8},{11,9},{12,10},{13,11},... | collective-permute-start | bytes 786440 | tf_op jit(solution)/shard_map/ppermute | solution.py:205
  33.8 1.9 %collective-permute-start.12 = (bf16[128,512]{1,0:T(8,128)(2,1)S(1)}, bf16[128,512]{1,0:T(8,128)(2,1)S(1)}, u32[]{:S(2)}, u32[]{:S(2)}) collective-permute-start(bf16[128,512]{1,0:T(8,128)(2,1)S(1)} %get-tuple-element.66), channel_id=1, source_target_pairs={{0,1},{1,0},{2,3},{3,2},{4,5},{5,4},{6,7},{7,6},{8,9},{9,8},{10,11... | collective-permute-start | bytes 393224 | tf_op jit(solution)/shard_map/ppermute | solution.py:205
  34.0 1.7 %collective-permute-start.13 = (bf16[128,512]{1,0:T(8,128)(2,1)S(1)}, bf16[128,512]{1,0:T(8,128)(2,1)S(1)}, u32[]{:S(2)}, u32[]{:S(2)}) collective-permute-start(bf16[128,512]{1,0:T(8,128)(2,1)S(1)} %get-tuple-element.67), channel_id=1, source_target_pairs={{0,1},{1,0},{2,3},{3,2},{4,5},{5,4},{6,7},{7,6},{8,9},{9,8},{10,11... | collective-permute-start | bytes 393224 | tf_op jit(solution)/shard_map/ppermute | solution.py:205
  34.3 1.2 %collective-permute-start.14 = (f32[2,256]{1,0:T(2,128)S(1)}, f32[2,256]{1,0:T(2,128)S(1)}, u32[]{:S(2)}, u32[]{:S(2)}) collective-permute-start(f32[2,256]{1,0:T(2,128)S(1)} %add.4.refs_0_), channel_id=1, source_target_pairs={{0,1},{1,0},{2,3},{3,2},{4,5},{5,4},{6,7},{7,6},{8,9},{9,8},{10,11... | collective-permute-start | bytes 6152 | tf_op jit(solution)/shard_map/ppermute | solution.py:205
  35.5 10.8 %collective-permute-start.16 = (bf16[128,1024]{1,0:T(8,128)(2,1)S(1)}, bf16[128,1024]{1,0:T(8,128)(2,1)S(1)}, u32[]{:S(2)}, u32[]{:S(2)}) collective-permute-start(bf16[128,1024]{1,0:T(8,128)(2,1)S(1)} %get-tuple-element.69), channel_id=1, source_target_pairs={{0,1},{1,0},{2,3},{3,2},{4,5},{5,4},{6,7},{7,6},{8,9},{9,8},{10,11... | collective-permute-start | bytes 786440 | tf_op jit(solution)/shard_map/ppermute | solution.py:205
  35.8 12.1 %collective-permute-start.15 = (bf16[128,1024]{1,0:T(8,128)(2,1)S(1)}, bf16[128,1024]{1,0:T(8,128)(2,1)S(1)}, u32[]{:S(2)}, u32[]{:S(2)}) collective-permute-start(bf16[128,1024]{1,0:T(8,128)(2,1)S(1)} %sink.5.refs_5_), channel_id=1, source_target_pairs={{2,0},{3,1},{4,2},{5,3},{6,4},{7,5},{10,8},{11,9},{12,10},{13,11},... | collective-permute-start | bytes 786440 | tf_op jit(solution)/shard_map/ppermute | solution.py:205
  37.1 3.7 %collective-permute-start.19 = (f32[2,256]{1,0:T(2,128)S(1)}, f32[2,256]{1,0:T(2,128)S(1)}, u32[]{:S(2)}, u32[]{:S(2)}) collective-permute-start(f32[2,256]{1,0:T(2,128)S(1)} %add.5.refs_4_.refs_0_), channel_id=1, source_target_pairs={{0,8},{8,0},{16,24},{24,16},{1,9},{9,1},{17,25},{25,17},{2,10},{10... | collective-permute-start | bytes 6152 | tf_op jit(solution)/shard_map/ppermute | solution.py:205
  41.3 15.5 %collective-permute-start.22 = (bf16[128,1024]{1,0:T(8,128)(2,1)S(1)}, bf16[128,1024]{1,0:T(8,128)(2,1)S(1)}, u32[]{:S(2)}, u32[]{:S(2)}) collective-permute-start(bf16[128,1024]{1,0:T(8,128)(2,1)S(1)} %sink.6.refs_5_), channel_id=1, source_target_pairs={{2,0},{3,1},{4,2},{5,3},{6,4},{7,5},{10,8},{11,9},{12,10},{13,11},... | collective-permute-start | bytes 786440 | tf_op jit(solution)/shard_map/ppermute | solution.py:205
  42.6 3.7 %collective-permute-start.20 = (f32[2,256]{1,0:T(2,128)S(1)}, f32[2,256]{1,0:T(2,128)S(1)}, u32[]{:S(2)}, u32[]{:S(2)}) collective-permute-start(f32[2,256]{1,0:T(2,128)S(1)} %add.6.refs_6_.refs_0_), channel_id=1, source_target_pairs={{0,16},{8,24},{16,0},{24,8},{1,17},{9,25},{17,1},{25,9},{2,18},{10... | collective-permute-start | bytes 6152 | tf_op jit(solution)/shard_map/ppermute | solution.py:205
  48.0 10.9 %collective-permute-start.21 = (bf16[128,1024]{1,0:T(8,128)(2,1)S(1)}, bf16[128,1024]{1,0:T(8,128)(2,1)S(1)}, u32[]{:S(2)}, u32[]{:S(2)}) collective-permute-start(bf16[128,1024]{1,0:T(8,128)(2,1)S(1)} %sink.7.refs_4_), channel_id=1, source_target_pairs={{2,0},{3,1},{4,2},{5,3},{6,4},{7,5},{10,8},{11,9},{12,10},{13,11},... | collective-permute-start | bytes 786440 | tf_op jit(solution)/shard_map/ppermute | solution.py:205
  49.3 10.5 %collective-permute-start.23 = (f32[2,256]{1,0:T(2,128)S(1)}, f32[2,256]{1,0:T(2,128)S(1)}, u32[]{:S(2)}, u32[]{:S(2)}) collective-permute-start(f32[2,256]{1,0:T(2,128)S(1)} %add.7.refs_6_.refs_0_), channel_id=1, source_target_pairs={{0,2},{1,3},{2,0},{3,1},{4,6},{5,7},{6,4},{7,5},{8,10},{9,11},{10,... | collective-permute-start | bytes 6152 | tf_op jit(solution)/shard_map/ppermute | solution.py:205
  52.3 8.0 %collective-permute-start.24 = (f32[2,256]{1,0:T(2,128)S(1)}, f32[2,256]{1,0:T(2,128)S(1)}, u32[]{:S(2)}, u32[]{:S(2)}) collective-permute-start(f32[2,256]{1,0:T(2,128)S(1)} %add.7.refs_6_.refs_0_), channel_id=1, source_target_pairs={{0,4},{1,5},{2,6},{3,7},{4,0},{5,1},{6,2},{7,3},{8,12},{9,13},{10,... | collective-permute-start | bytes 6152 | tf_op jit(solution)/shard_map/ppermute | solution.py:205
  55.8 5.8 %collective-permute-start.25 = (f32[2,256]{1,0:T(2,128)S(1)}, f32[2,256]{1,0:T(2,128)S(1)}, u32[]{:S(2)}, u32[]{:S(2)}) collective-permute-start(f32[2,256]{1,0:T(2,128)S(1)} %add.7.refs_6_.refs_0_), channel_id=1, source_target_pairs={{0,6},{1,7},{2,4},{3,5},{4,2},{5,3},{6,0},{7,1},{8,14},{9,15},{10,... | collective-permute-start | bytes 6152 | tf_op jit(solution)/shard_map/ppermute | solution.py:205
  55.8 1.0 %copy-start.2 = (bf16[1,128,1024]{2,1,0:T(8,128)(2,1)S(1)}, bf16[1,128,1024]{2,1,0:T(8,128)(2,1)}, u32[]{:S(2)}) copy-start(bf16[1,128,1024]{2,1,0:T(8,128)(2,1)} %refs_0_.7) | copy-start | bytes 786436

commit v7 on v6

--- a/solution.py
+++ b/solution.py
@@ -20,6 +20,8 @@
 LAG = 2
 
 PIECES = 4
+
+Z_COST, S_COST, F_COST, G_COST = 2**30, 0, 2**31, 2**32
 
 VMEM = pl.BlockSpec(memory_space=pltpu.VMEM)
 ANY = pl.BlockSpec(memory_space=pl.ANY)
@@ -217,12 +219,12 @@
     return move(field, "ctx", lambda i: i ^ 1)
 
 
-def total_over(field, axis, unit, end, most, after=()):
+def total_over(field, axis, unit, end, most, cost=0):
     end = min(end, lax.axis_size(axis))
     while unit < end:
         group = min(most, end // unit)
         others = [move(field, axis, lambda i: i ^ (by * unit)) for by in range(1, group)]
-        (field,) = call(add, "add", dict(enumerate([field, *others])), dict(o=shape(*field.shape, F32)), after)
+        (field,) = call(add, "add", dict(enumerate([field, *others])), dict(o=shape(*field.shape, F32)), cost=cost)
         unit *= group
     return field
 
@@ -374,11 +376,9 @@
             last = [*last, total]
         last = [sink(chunk, last)]
 
-    unit = 1
     for step in range(amount, amount + LAG):
-        end = unit * 2 if step + 1 < amount + LAG else lax.axis_size("dp")
-        total = total_over(total, "dp", unit, end, 2)
-        unit = end
+        if step == amount:
+            total = total_over(total, "dp", 1, 2, 2)
         last = [sink(step, [*last, total])]
     key_outputs = []
     for chunk, (first, count) in enumerate(CHUNKS):
@@ -393,7 +393,7 @@
                 key_grad=jax.ShapeDtypeStruct(keys.shape, BF16), value_grad=jax.ShapeDtypeStruct(keys.shape, BF16)
             ),
             key_outputs,
-            cost=2**31 * (1 + chunk),
+            cost=(F_COST, G_COST)[chunk],
             grid=(1,),
             in_specs=dict(keys=narrow),
             out_specs=dict(key_grad=narrow, value_grad=narrow),
@@ -413,13 +413,12 @@
     while chips > 4:
         total = total_over(total, "ctx", chips, 2 * chips, 2)
         chips //= 2
-    others = [move(total, "ctx", lambda i: i ^ (2 * by)) for by in range(1, chips)]
+    total = total_over(total, "ctx", 2, 2 * chips, 4, cost=Z_COST)
+    half = lax.axis_size("dp") // 2
+    total = total_over(total, "dp", 2, half, 2)
+    others = [move(total, "dp", lambda i: i ^ half)] if half > 1 else []
     query_gains, key_gains = call(
-        functools.partial(scale, factor),
-        "scale",
-        dict(enumerate([total, *others])),
-        dict(a=row, b=row),
-        [pltpu.with_memory_space_constraint(field, pltpu.HBM) for field in (attended, *key_outputs)],
+        functools.partial(scale, factor), "scale", dict(enumerate([total, *others])), dict(a=row, b=row), cost=S_COST
     )
     return attended, query_grad, *key_outputs, query_gains[0], key_gains[0]
 

time: 62.6 us -> 64.3 us (1.027)
  starting transfers between devices: 35.3 us -> 36.2 us
  waiting for transfers between devices: 15.5 us -> 16.3 us
    ppermute x26, starting transfers between devices: 35.3 us -> 36.2 us  [move(): lax.ppermute(field, axis, [(i, target(i)) for i in range(size) if 0 <= ta...]
    ppermute x26, waiting for transfers between devices: 15.5 us -> 16.3 us  [move(): lax.ppermute(field, axis, [(i, target(i)) for i in range(size) if 0 <= ta...]
  transfers between devices with their start and end apart: 26 -> 26, of which waited for: 14 -> 13; matrix products, arithmetic and copies ran while one was open for 0% -> 0% of each run, Pallas kernels for 14% -> 13%
where the time goes in v7:
time: 64.3 us; the launch traced here: 63.8 us
  starting transfers between devices  36.2 us (56%)
  waiting for transfers between devices  16.3 us (25%)
  Pallas kernels  10.4 us (16%)
  between operations  0.83 us (1%)
    ppermute x26, starting transfers between devices, move(): lax.ppermute(field, axis, [(i, target(i)) for i in range(size) if 0 <= ta...  36.2 us
    ppermute x26, waiting for transfers between devices, move(): lax.ppermute(field, axis, [(i, target(i)) for i in range(size) if 0 <= ta...  16.3 us
    pallas_call x20, Pallas kernels, call(): pl.pallas_call(kernel, out_shape=list(outs.values()), in_specs=specs, out...  10.4 us
  transfers between devices with their start and end apart: 26, of which 13 were waited for; matrix products, arithmetic and copies ran while one was open for 0% of the time, Pallas kernels for 13%

profile of v7, /device:TPU:0, one launch (start us, length us, event | category | flops | bytes accessed | tf_op | source)
XLA Modules:
  0.0 63.8 jit_solution(17226646393504566309)
XLA Ops:
  0.6 0.9 %payload.2.refs_5_.refs_1_.refs_3_ = bf16[128,1024]{1,0:T(8,128)(2,1)S(1)} custom-call(bf16[1,128,1024]{2,1,0:T(8,128)(2,1)} %refs_0_.7, bf16[1,128,1024]{2,1,0:T(8,128)(2,1)} %refs_1_.5), custom_call_target="tpu_custom_call" | custom-call | bytes 1 | tf_op jit(solution)/shard_map/payload/pallas_call | solution.py:38
  1.6 4.9 %collective-permute-start = (bf16[128,1024]{1,0:T(8,128)(2,1)S(1)}, bf16[128,1024]{1,0:T(8,128)(2,1)S(1)}, u32[]{:S(2)}, u32[]{:S(2)}) collective-permute-start(bf16[128,1024]{1,0:T(8,128)(2,1)S(1)} %payload.2.refs_5_.refs_1_.refs_3_), channel_id=1, source_target_pairs={{0,2},{1,3},{2,4},{3,5},{4,6},{5,7},{8,10},{9,11},{10,12},{11,13},... | collective-permute-start | bytes 786440 | tf_op jit(solution)/shard_map/ppermute | solution.py:207
  6.5 1.0 %payload.3 = (bf16[128,1024]{1,0:T(8,128)(2,1)S(1)}, s32[1,1024]{1,0:T(1,128)S(1)}, f32[1,256]{1,0:T(1,128)S(1)}, f32[1,256]{1,0:T(1,128)S(1)}) custom-call(bf16[1,128,1024]{2,1,0:T(8,128)(2,1)} %refs_0_.7, bf16[1,128,1024]{2,1,0:T(8,128)(2,1)} %refs_1_.5, s32[1,1024]{1,0:T(1,128)} %refs_2_.3, f32[1,256]{1,0:T(1,128)} %bitcast.4, f32[1,256]{1,0:T(1,128)} %bitcast.5, ...), custom_call_target="tpu_custom_call" | custom-call | bytes 1 | tf_op jit(solution)/shard_map/payload/pallas_call | solution.py:38
  7.6 3.5 %collective-permute-start.3 = (bf16[128,1024]{1,0:T(8,128)(2,1)S(1)}, bf16[128,1024]{1,0:T(8,128)(2,1)S(1)}, u32[]{:S(2)}, u32[]{:S(2)}) collective-permute-start(bf16[128,1024]{1,0:T(8,128)(2,1)S(1)} %get-tuple-element.47.refs_1_.refs_3_), channel_id=1, source_target_pairs={{0,2},{1,3},{2,4},{3,5},{4,6},{5,7},{8,10},{9,11},{10,12},{11,13},... | collective-permute-start | bytes 786440 | tf_op jit(solution)/shard_map/ppermute | solution.py:207
  11.1 2.2 %collective-permute-done.refs_0_.refs_5_ = bf16[128,1024]{1,0:T(8,128)(2,1)S(1)} collective-permute-done((bf16[128,1024]{1,0:T(8,128)(2,1)S(1)}, bf16[128,1024]{1,0:T(8,128)(2,1)S(1)}, u32[]{:S(2)}, u32[]{:S(2)}) %collective-permute-start) | collective-permute-done | bytes 262176 | tf_op jit(solution)/shard_map/ppermute | solution.py:207
  13.3 4.4 %collective-permute-start.2 = (bf16[128,1024]{1,0:T(8,128)(2,1)S(1)}, bf16[128,1024]{1,0:T(8,128)(2,1)S(1)}, u32[]{:S(2)}, u32[]{:S(2)}) collective-permute-start(bf16[128,1024]{1,0:T(8,128)(2,1)S(1)} %get-tuple-element.46.refs_2_), channel_id=1, source_target_pairs={{0,2},{1,3},{2,4},{3,5},{4,6},{5,7},{8,10},{9,11},{10,12},{11,13},... | collective-permute-start | bytes 786440 | tf_op jit(solution)/shard_map/ppermute | solution.py:207
  17.7 1.1 %collective-permute-done.3.refs_0_.refs_5_ = bf16[128,1024]{1,0:T(8,128)(2,1)S(1)} collective-permute-done((bf16[128,1024]{1,0:T(8,128)(2,1)S(1)}, bf16[128,1024]{1,0:T(8,128)(2,1)S(1)}, u32[]{:S(2)}, u32[]{:S(2)}) %collective-permute-start.3) | collective-permute-done | bytes 262176 | tf_op jit(solution)/shard_map/ppermute | solution.py:207
  18.9 4.5 %collective-permute-start.7 = (bf16[128,1024]{1,0:T(8,128)(2,1)S(1)}, bf16[128,1024]{1,0:T(8,128)(2,1)S(1)}, u32[]{:S(2)}, u32[]{:S(2)}) collective-permute-start(bf16[128,1024]{1,0:T(8,128)(2,1)S(1)} %get-tuple-element.48.refs_2_), channel_id=1, source_target_pairs={{0,2},{1,3},{2,4},{3,5},{4,6},{5,7},{8,10},{9,11},{10,12},{11,13},... | collective-permute-start | bytes 786440 | tf_op jit(solution)/shard_map/ppermute | solution.py:207
  23.4 1.0 %collective-permute-done.2.refs_1_.refs_6_ = bf16[128,1024]{1,0:T(8,128)(2,1)S(1)} collective-permute-done((bf16[128,1024]{1,0:T(8,128)(2,1)S(1)}, bf16[128,1024]{1,0:T(8,128)(2,1)S(1)}, u32[]{:S(2)}, u32[]{:S(2)}) %collective-permute-start.2) | collective-permute-done | bytes 262176 | tf_op jit(solution)/shard_map/ppermute | solution.py:207
  24.6 0.5 collective-permute-start.5
  25.1 0.8 %collective-permute-done.4.refs_7_ = bf16[128,512]{1,0:T(8,128)(2,1)S(1)} collective-permute-done((bf16[128,512]{1,0:T(8,128)(2,1)S(1)}, bf16[128,512]{1,0:T(8,128)(2,1)S(1)}, u32[]{:S(2)}, u32[]{:S(2)}) %collective-permute-start.4) | collective-permute-done | bytes 131104 | tf_op jit(solution)/shard_map/ppermute | solution.py:207
  26.1 2.2 %attend.2 = (bf16[128,1024]{1,0:T(8,128)(2,1)S(1)}, bf16[128,1024]{1,0:T(8,128)(2,1)S(1)}, f32[128,1024]{1,0:T(8,128)S(1)}, f32[128,1024]{1,0:T(8,128)S(1)}, f32...) custom-call(s32[1,1024]{1,0:T(1,128)S(1)} %get-tuple-element.44.refs, ...), custom_call_target="tpu_custom_call" | custom-call | bytes 1 | tf_op jit(solution)/shard_map/attend/pallas_call | solution.py:38
  30.2 1.3 %collective-permute-start.17 = (bf16[128,1024]{1,0:T(8,128)(2,1)S(1)}, bf16[128,1024]{1,0:T(8,128)(2,1)S(1)}, u32[]{:S(2)}, u32[]{:S(2)}) collective-permute-start(bf16[128,1024]{1,0:T(8,128)(2,1)S(1)} %sink.4.refs_11_.refs_3_), channel_id=1, source_target_pairs={{2,0},{3,1},{4,2},{5,3},{6,4},{7,5},{10,8},{11,9},{12,10},{13,11},... | collective-permute-start | bytes 786440 | tf_op jit(solution)/shard_map/ppermute | solution.py:207
  31.5 2.3 %attend.3 = (bf16[128,1024]{1,0:T(8,128)(2,1)S(1)}, bf16[128,1024]{1,0:T(8,128)(2,1)S(1)}, f32[128,1024]{1,0:T(8,128)S(1)}, f32[128,1024]{1,0:T(8,128)S(1)}, f32...) custom-call(s32[1,1024]{1,0:T(1,128)S(1)} %get-tuple-element.44.refs, ...), custom_call_target="tpu_custom_call" | custom-call | bytes 1 | tf_op jit(solution)/shard_map/attend/pallas_call | solution.py:38
  34.5 1.0 %collective-permute-done.14.refs_1_ = f32[2,256]{1,0:T(2,128)S(1)} collective-permute-done((f32[2,256]{1,0:T(2,128)S(1)}, f32[2,256]{1,0:T(2,128)S(1)}, u32[]{:S(2)}, u32[]{:S(2)}) %collective-permute-start.14) | collective-permute-done | bytes 2080 | tf_op jit(solution)/shard_map/ppermute | solution.py:207
  35.8 1.3 %collective-permute-start.15 = (bf16[128,1024]{1,0:T(8,128)(2,1)S(1)}, bf16[128,1024]{1,0:T(8,128)(2,1)S(1)}, u32[]{:S(2)}, u32[]{:S(2)}) collective-permute-start(bf16[128,1024]{1,0:T(8,128)(2,1)S(1)} %sink.5.refs_5_), channel_id=1, source_target_pairs={{2,0},{3,1},{4,2},{5,3},{6,4},{7,5},{10,8},{11,9},{12,10},{13,11},... | collective-permute-start | bytes 786440 | tf_op jit(solution)/shard_map/ppermute | solution.py:207
  37.1 1.6 %collective-permute-start.19 = (f32[2,256]{1,0:T(2,128)S(1)}, f32[2,256]{1,0:T(2,128)S(1)}, u32[]{:S(2)}, u32[]{:S(2)}) collective-permute-start(f32[2,256]{1,0:T(2,128)S(1)} %add.5.refs_4_.refs_0_), channel_id=1, source_target_pairs={{0,8},{8,0},{16,24},{24,16},{1,9},{9,1},{17,25},{25,17},{2,10},{10... | collective-permute-start | bytes 6152 | tf_op jit(solution)/shard_map/ppermute | solution.py:207
  38.6 2.1 %collective-permute-done.19.refs_1_ = f32[2,256]{1,0:T(2,128)S(1)} collective-permute-done((f32[2,256]{1,0:T(2,128)S(1)}, f32[2,256]{1,0:T(2,128)S(1)}, u32[]{:S(2)}, u32[]{:S(2)}) %collective-permute-start.19) | collective-permute-done | bytes 2080 | tf_op jit(solution)/shard_map/ppermute | solution.py:207
  40.7 0.5 collective-permute-done.17.refs_1_
  41.3 1.3 %collective-permute-start.21 = (bf16[128,1024]{1,0:T(8,128)(2,1)S(1)}, bf16[128,1024]{1,0:T(8,128)(2,1)S(1)}, u32[]{:S(2)}, u32[]{:S(2)}) collective-permute-start(bf16[128,1024]{1,0:T(8,128)(2,1)S(1)} %sink.6.refs_5_), channel_id=1, source_target_pairs={{2,0},{3,1},{4,2},{5,3},{6,4},{7,5},{10,8},{11,9},{12,10},{13,11},... | collective-permute-start | bytes 786440 | tf_op jit(solution)/shard_map/ppermute | solution.py:207
  42.6 4.0 %collective-permute-start.22 = (f32[2,256]{1,0:T(2,128)S(1)}, f32[2,256]{1,0:T(2,128)S(1)}, u32[]{:S(2)}, u32[]{:S(2)}) collective-permute-start(f32[2,256]{1,0:T(2,128)S(1)} %add.6.refs_6_.refs_0_), channel_id=1, source_target_pairs={{0,2},{1,3},{2,0},{3,1},{4,6},{5,7},{6,4},{7,5},{8,10},{9,11},{10,... | collective-permute-start | bytes 6152 | tf_op jit(solution)/shard_map/ppermute | solution.py:207
  46.6 3.5 %collective-permute-start.23 = (f32[2,256]{1,0:T(2,128)S(1)}, f32[2,256]{1,0:T(2,128)S(1)}, u32[]{:S(2)}, u32[]{:S(2)}) collective-permute-start(f32[2,256]{1,0:T(2,128)S(1)} %add.6.refs_6_.refs_0_), channel_id=1, source_target_pairs={{0,4},{1,5},{2,6},{3,7},{4,0},{5,1},{6,2},{7,3},{8,12},{9,13},{10,... | collective-permute-start | bytes 6152 | tf_op jit(solution)/shard_map/ppermute | solution.py:207
  50.2 1.3 %collective-permute-start.20 = (bf16[128,1024]{1,0:T(8,128)(2,1)S(1)}, bf16[128,1024]{1,0:T(8,128)(2,1)S(1)}, u32[]{:S(2)}, u32[]{:S(2)}) collective-permute-start(bf16[128,1024]{1,0:T(8,128)(2,1)S(1)} %sink.7.refs_4_), channel_id=1, source_target_pairs={{2,0},{3,1},{4,2},{5,3},{6,4},{7,5},{10,8},{11,9},{12,10},{13,11},... | collective-permute-start | bytes 786440 | tf_op jit(solution)/shard_map/ppermute | solution.py:207
  51.5 1.9 %collective-permute-done.22.refs_1_ = f32[2,256]{1,0:T(2,128)S(1)} collective-permute-done((f32[2,256]{1,0:T(2,128)S(1)}, f32[2,256]{1,0:T(2,128)S(1)}, u32[]{:S(2)}, u32[]{:S(2)}) %collective-permute-start.22) | collective-permute-done | bytes 2080 | tf_op jit(solution)/shard_map/ppermute | solution.py:207
  53.4 1.9 %collective-permute-done.23.refs_2_ = f32[2,256]{1,0:T(2,128)S(1)} collective-permute-done((f32[2,256]{1,0:T(2,128)S(1)}, f32[2,256]{1,0:T(2,128)S(1)}, u32[]{:S(2)}, u32[]{:S(2)}) %collective-permute-start.23) | collective-permute-done | bytes 2080 | tf_op jit(solution)/shard_map/ppermute | solution.py:207
  55.3 1.5 %collective-permute-done.24.refs_3_ = f32[2,256]{1,0:T(2,128)S(1)} collective-permute-done((f32[2,256]{1,0:T(2,128)S(1)}, f32[2,256]{1,0:T(2,128)S(1)}, u32[]{:S(2)}, u32[]{:S(2)}) %collective-permute-start.24) | collective-permute-done | bytes 2080 | tf_op jit(solution)/shard_map/ppermute | solution.py:207
  56.8 1.5 %collective-permute-start.25 = (f32[2,256]{1,0:T(2,128)S(1)}, f32[2,256]{1,0:T(2,128)S(1)}, u32[]{:S(2)}, u32[]{:S(2)}) collective-permute-start(f32[2,256]{1,0:T(2,128)S(1)} %add.7.refs_0_), channel_id=1, source_target_pairs={{0,16},{8,24},{16,0},{24,8},{1,17},{9,25},{17,1},{25,9},{2,18},{10... | collective-permute-start | bytes 6152 | tf_op jit(solution)/shard_map/ppermute | solution.py:207
  58.3 2.1 %collective-permute-done.25.refs_1_ = f32[2,256]{1,0:T(2,128)S(1)} collective-permute-done((f32[2,256]{1,0:T(2,128)S(1)}, f32[2,256]{1,0:T(2,128)S(1)}, u32[]{:S(2)}, u32[]{:S(2)}) %collective-permute-start.25) | collective-permute-done | bytes 2080 | tf_op jit(solution)/shard_map/ppermute | solution.py:207
  60.3 0.6 scale.1
  60.9 1.0 %assemble.1 = (bf16[1,128,2048]{2,1,0:T(8,128)(2,1)}, bf16[1,128,2048]{2,1,0:T(8,128)(2,1)}) custom-call(bf16[128,1024]{1,0:T(8,128)(2,1)S(1)} %get-tuple-element.53.refs_0_, bf16[128,1024]{1,0:T(8,128)(2,1)S(1)} %get-tuple-element.61.refs_1_, bf16[128,1024]{1,0:T(8,128)(2,1)S(1)} %get-tuple-element.62.refs_2_, ...), custom_call_target="tpu_custom_call" | custom-call | bytes 1 | tf_op jit(solution)/shard_map/assemble/pallas_call | solution.py:38
  62.0 0.9 %finish.2 = (bf16[1,128,1024]{2,1,0:T(8,128)(2,1)}, bf16[1,128,1024]{2,1,0:T(8,128)(2,1)}) custom-call(bf16[1,128,1024]{2,1,0:T(8,128)(2,1)S(1)} %copy-done.2, f32[1,256]{1,0:T(1,128)S(1)} %get-tuple-element.52.refs_10_.refs_1_, f32[128,1024]{1,0:T(8,128)S(1)} %get-tuple-element.75.refs_2_, bf16[128,1024]{1,0:T(8,128)(2,1)S(1)} %collective-permute-done.18.refs_4_.refs_3_, ...), custom_call_target="tpu_custom_call" | custom-call | flops 2147483648 | bytes 1 | tf_op jit(solution)/shard_map/finish/pallas_call | solution.py:38
  62.9 0.9 %finish.3 = (bf16[1,128,1024]{2,1,0:T(8,128)(2,1)}, bf16[1,128,1024]{2,1,0:T(8,128)(2,1)}) custom-call(bf16[1,128,1024]{2,1,0:T(8,128)(2,1)S(1)} %copy-done.2, f32[1,256]{1,0:T(1,128)S(1)} %get-tuple-element.52.refs_10_.refs_1_, f32[128,1024]{1,0:T(8,128)S(1)} %get-tuple-element.74.refs_2_, ...), custom_call_target="tpu_custom_call", output_to_operand_aliasing={{0}: (5, {}), {1}: (6, {})} | custom-call | flops 4294967296 | bytes 1 | tf_op jit(solution)/shard_map/finish/pallas_call | solution.py:38
  (46 shorter events, 3.7 us)
Async XLA Ops:
  1.6 11.6 %collective-permute-start = (bf16[128,1024]{1,0:T(8,128)(2,1)S(1)}, bf16[128,1024]{1,0:T(8,128)(2,1)S(1)}, u32[]{:S(2)}, u32[]{:S(2)}) collective-permute-start(bf16[128,1024]{1,0:T(8,128)(2,1)S(1)} %payload.2.refs_5_.refs_1_.refs_3_), channel_id=1, source_target_pairs={{0,2},{1,3},{2,4},{3,5},{4,6},{5,7},{8,10},{9,11},{10,12},{11,13},... | collective-permute-start | bytes 786440 | tf_op jit(solution)/shard_map/ppermute | solution.py:207
  7.6 11.3 %collective-permute-start.3 = (bf16[128,1024]{1,0:T(8,128)(2,1)S(1)}, bf16[128,1024]{1,0:T(8,128)(2,1)S(1)}, u32[]{:S(2)}, u32[]{:S(2)}) collective-permute-start(bf16[128,1024]{1,0:T(8,128)(2,1)S(1)} %get-tuple-element.47.refs_1_.refs_3_), channel_id=1, source_target_pairs={{0,2},{1,3},{2,4},{3,5},{4,6},{5,7},{8,10},{9,11},{10,12},{11,13},... | collective-permute-start | bytes 786440 | tf_op jit(solution)/shard_map/ppermute | solution.py:207
  13.3 11.2 %collective-permute-start.2 = (bf16[128,1024]{1,0:T(8,128)(2,1)S(1)}, bf16[128,1024]{1,0:T(8,128)(2,1)S(1)}, u32[]{:S(2)}, u32[]{:S(2)}) collective-permute-start(bf16[128,1024]{1,0:T(8,128)(2,1)S(1)} %get-tuple-element.46.refs_2_), channel_id=1, source_target_pairs={{0,2},{1,3},{2,4},{3,5},{4,6},{5,7},{8,10},{9,11},{10,12},{11,13},... | collective-permute-start | bytes 786440 | tf_op jit(solution)/shard_map/ppermute | solution.py:207
  17.7 7.5 %collective-permute-start.1 = (bf16[128,1024]{1,0:T(8,128)(2,1)S(1)}, bf16[128,1024]{1,0:T(8,128)(2,1)S(1)}, u32[]{:S(2)}, u32[]{:S(2)}) collective-permute-start(bf16[128,1024]{1,0:T(8,128)(2,1)S(1)} %get-tuple-element.45), channel_id=1, source_target_pairs={{0,1},{1,0},{2,3},{3,2},{4,5},{5,4},{6,7},{7,6},{8,9},{9,8},{10,11... | collective-permute-start | bytes 786440 | tf_op jit(solution)/shard_map/ppermute | solution.py:207
  18.9 7.2 %copy-start = (bf16[1,128,2048]{2,1,0:T(8,128)(2,1)S(1)}, bf16[1,128,2048]{2,1,0:T(8,128)(2,1)}, u32[]{:S(2)}) copy-start(bf16[1,128,2048]{2,1,0:T(8,128)(2,1)} %refs_1_.7) | copy-start | bytes 1572868
  18.9 7.2 %copy-start.1 = (bf16[1,128,2048]{2,1,0:T(8,128)(2,1)S(1)}, bf16[1,128,2048]{2,1,0:T(8,128)(2,1)}, u32[]{:S(2)}) copy-start(bf16[1,128,2048]{2,1,0:T(8,128)(2,1)} %refs_2_.5) | copy-start | bytes 1572868
  18.9 10.0 %collective-permute-start.7 = (bf16[128,1024]{1,0:T(8,128)(2,1)S(1)}, bf16[128,1024]{1,0:T(8,128)(2,1)S(1)}, u32[]{:S(2)}, u32[]{:S(2)}) collective-permute-start(bf16[128,1024]{1,0:T(8,128)(2,1)S(1)} %get-tuple-element.48.refs_2_), channel_id=1, source_target_pairs={{0,2},{1,3},{2,4},{3,5},{4,6},{5,7},{8,10},{9,11},{10,12},{11,13},... | collective-permute-start | bytes 786440 | tf_op jit(solution)/shard_map/ppermute | solution.py:207
  24.5 1.4 %collective-permute-start.4 = (bf16[128,512]{1,0:T(8,128)(2,1)S(1)}, bf16[128,512]{1,0:T(8,128)(2,1)S(1)}, u32[]{:S(2)}, u32[]{:S(2)}) collective-permute-start(bf16[128,512]{1,0:T(8,128)(2,1)S(1)} %get-tuple-element.49.refs_2_), channel_id=1, source_target_pairs={{0,1},{1,0},{2,3},{3,2},{4,5},{5,4},{6,7},{7,6},{8,9},{9,8},{10,11... | collective-permute-start | bytes 393224 | tf_op jit(solution)/shard_map/ppermute | solution.py:207
  24.6 1.5 %collective-permute-start.5 = (bf16[128,512]{1,0:T(8,128)(2,1)S(1)}, bf16[128,512]{1,0:T(8,128)(2,1)S(1)}, u32[]{:S(2)}, u32[]{:S(2)}) collective-permute-start(bf16[128,512]{1,0:T(8,128)(2,1)S(1)} %get-tuple-element.50), channel_id=1, source_target_pairs={{0,1},{1,0},{2,3},{3,2},{4,5},{5,4},{6,7},{7,6},{8,9},{9,8},{10,11... | collective-permute-start | bytes 393224 | tf_op jit(solution)/shard_map/ppermute | solution.py:207
  25.1 6.4 %collective-permute-start.6 = (bf16[128,1024]{1,0:T(8,128)(2,1)S(1)}, bf16[128,1024]{1,0:T(8,128)(2,1)S(1)}, u32[]{:S(2)}, u32[]{:S(2)}) collective-permute-start(bf16[128,1024]{1,0:T(8,128)(2,1)S(1)} %get-tuple-element.54), channel_id=1, source_target_pairs={{0,1},{1,0},{2,3},{3,2},{4,5},{5,4},{6,7},{7,6},{8,9},{9,8},{10,11... | collective-permute-start | bytes 786440 | tf_op jit(solution)/shard_map/ppermute | solution.py:207
  28.3 1.4 %collective-permute-start.10 = (bf16[128,512]{1,0:T(8,128)(2,1)S(1)}, bf16[128,512]{1,0:T(8,128)(2,1)S(1)}, u32[]{:S(2)}, u32[]{:S(2)}) collective-permute-start(bf16[128,512]{1,0:T(8,128)(2,1)S(1)} %get-tuple-element.59), channel_id=1, source_target_pairs={{0,1},{1,0},{2,3},{3,2},{4,5},{5,4},{6,7},{7,6},{8,9},{9,8},{10,11... | collective-permute-start | bytes 393224 | tf_op jit(solution)/shard_map/ppermute | solution.py:207
  28.7 1.4 %collective-permute-start.11 = (bf16[128,512]{1,0:T(8,128)(2,1)S(1)}, bf16[128,512]{1,0:T(8,128)(2,1)S(1)}, u32[]{:S(2)}, u32[]{:S(2)}) collective-permute-start(bf16[128,512]{1,0:T(8,128)(2,1)S(1)} %get-tuple-element.60), channel_id=1, source_target_pairs={{0,1},{1,0},{2,3},{3,2},{4,5},{5,4},{6,7},{7,6},{8,9},{9,8},{10,11... | collective-permute-start | bytes 393224 | tf_op jit(solution)/shard_map/ppermute | solution.py:207
  29.0 2.5 %collective-permute-start.8 = (bf16[128,512]{1,0:T(8,128)(2,1)S(1)}, bf16[128,512]{1,0:T(8,128)(2,1)S(1)}, u32[]{:S(2)}, u32[]{:S(2)}) collective-permute-start(bf16[128,512]{1,0:T(8,128)(2,1)S(1)} %get-tuple-element.56), channel_id=1, source_target_pairs={{0,1},{1,0},{2,3},{3,2},{4,5},{5,4},{6,7},{7,6},{8,9},{9,8},{10,11... | collective-permute-start | bytes 393224 | tf_op jit(solution)/shard_map/ppermute | solution.py:207
  29.4 2.1 %collective-permute-start.9 = (bf16[128,512]{1,0:T(8,128)(2,1)S(1)}, bf16[128,512]{1,0:T(8,128)(2,1)S(1)}, u32[]{:S(2)}, u32[]{:S(2)}) collective-permute-start(bf16[128,512]{1,0:T(8,128)(2,1)S(1)} %get-tuple-element.57), channel_id=1, source_target_pairs={{0,1},{1,0},{2,3},{3,2},{4,5},{5,4},{6,7},{7,6},{8,9},{9,8},{10,11... | collective-permute-start | bytes 393224 | tf_op jit(solution)/shard_map/ppermute | solution.py:207
  29.8 11.0 %collective-permute-start.18 = (bf16[128,1024]{1,0:T(8,128)(2,1)S(1)}, bf16[128,1024]{1,0:T(8,128)(2,1)S(1)}, u32[]{:S(2)}, u32[]{:S(2)}) collective-permute-start(bf16[128,1024]{1,0:T(8,128)(2,1)S(1)} %get-tuple-element.71), channel_id=1, source_target_pairs={{0,1},{1,0},{2,3},{3,2},{4,5},{5,4},{6,7},{7,6},{8,9},{9,8},{10,11... | collective-permute-start | bytes 786440 | tf_op jit(solution)/shard_map/ppermute | solution.py:207
  30.2 11.0 %collective-permute-start.17 = (bf16[128,1024]{1,0:T(8,128)(2,1)S(1)}, bf16[128,1024]{1,0:T(8,128)(2,1)S(1)}, u32[]{:S(2)}, u32[]{:S(2)}) collective-permute-start(bf16[128,1024]{1,0:T(8,128)(2,1)S(1)} %sink.4.refs_11_.refs_3_), channel_id=1, source_target_pairs={{2,0},{3,1},{4,2},{5,3},{6,4},{7,5},{10,8},{11,9},{12,10},{13,11},... | collective-permute-start | bytes 786440 | tf_op jit(solution)/shard_map/ppermute | solution.py:207
  33.8 1.9 %collective-permute-start.12 = (bf16[128,512]{1,0:T(8,128)(2,1)S(1)}, bf16[128,512]{1,0:T(8,128)(2,1)S(1)}, u32[]{:S(2)}, u32[]{:S(2)}) collective-permute-start(bf16[128,512]{1,0:T(8,128)(2,1)S(1)} %get-tuple-element.66), channel_id=1, source_target_pairs={{0,1},{1,0},{2,3},{3,2},{4,5},{5,4},{6,7},{7,6},{8,9},{9,8},{10,11... | collective-permute-start | bytes 393224 | tf_op jit(solution)/shard_map/ppermute | solution.py:207
  34.0 1.7 %collective-permute-start.13 = (bf16[128,512]{1,0:T(8,128)(2,1)S(1)}, bf16[128,512]{1,0:T(8,128)(2,1)S(1)}, u32[]{:S(2)}, u32[]{:S(2)}) collective-permute-start(bf16[128,512]{1,0:T(8,128)(2,1)S(1)} %get-tuple-element.67), channel_id=1, source_target_pairs={{0,1},{1,0},{2,3},{3,2},{4,5},{5,4},{6,7},{7,6},{8,9},{9,8},{10,11... | collective-permute-start | bytes 393224 | tf_op jit(solution)/shard_map/ppermute | solution.py:207
  34.3 1.2 %collective-permute-start.14 = (f32[2,256]{1,0:T(2,128)S(1)}, f32[2,256]{1,0:T(2,128)S(1)}, u32[]{:S(2)}, u32[]{:S(2)}) collective-permute-start(f32[2,256]{1,0:T(2,128)S(1)} %add.4.refs_0_), channel_id=1, source_target_pairs={{0,1},{1,0},{2,3},{3,2},{4,5},{5,4},{6,7},{7,6},{8,9},{9,8},{10,11... | collective-permute-start | bytes 6152 | tf_op jit(solution)/shard_map/ppermute | solution.py:207
  35.5 14.6 %collective-permute-start.16 = (bf16[128,1024]{1,0:T(8,128)(2,1)S(1)}, bf16[128,1024]{1,0:T(8,128)(2,1)S(1)}, u32[]{:S(2)}, u32[]{:S(2)}) collective-permute-start(bf16[128,1024]{1,0:T(8,128)(2,1)S(1)} %get-tuple-element.69), channel_id=1, source_target_pairs={{0,1},{1,0},{2,3},{3,2},{4,5},{5,4},{6,7},{7,6},{8,9},{9,8},{10,11... | collective-permute-start | bytes 786440 | tf_op jit(solution)/shard_map/ppermute | solution.py:207
  35.8 14.3 %collective-permute-start.15 = (bf16[128,1024]{1,0:T(8,128)(2,1)S(1)}, bf16[128,1024]{1,0:T(8,128)(2,1)S(1)}, u32[]{:S(2)}, u32[]{:S(2)}) collective-permute-start(bf16[128,1024]{1,0:T(8,128)(2,1)S(1)} %sink.5.refs_5_), channel_id=1, source_target_pairs={{2,0},{3,1},{4,2},{5,3},{6,4},{7,5},{10,8},{11,9},{12,10},{13,11},... | collective-permute-start | bytes 786440 | tf_op jit(solution)/shard_map/ppermute | solution.py:207
  37.1 3.7 %collective-permute-start.19 = (f32[2,256]{1,0:T(2,128)S(1)}, f32[2,256]{1,0:T(2,128)S(1)}, u32[]{:S(2)}, u32[]{:S(2)}) collective-permute-start(f32[2,256]{1,0:T(2,128)S(1)} %add.5.refs_4_.refs_0_), channel_id=1, source_target_pairs={{0,8},{8,0},{16,24},{24,16},{1,9},{9,1},{17,25},{25,17},{2,10},{10... | collective-permute-start | bytes 6152 | tf_op jit(solution)/shard_map/ppermute | solution.py:207
  41.3 20.7 %collective-permute-start.21 = (bf16[128,1024]{1,0:T(8,128)(2,1)S(1)}, bf16[128,1024]{1,0:T(8,128)(2,1)S(1)}, u32[]{:S(2)}, u32[]{:S(2)}) collective-permute-start(bf16[128,1024]{1,0:T(8,128)(2,1)S(1)} %sink.6.refs_5_), channel_id=1, source_target_pairs={{2,0},{3,1},{4,2},{5,3},{6,4},{7,5},{10,8},{11,9},{12,10},{13,11},... | collective-permute-start | bytes 786440 | tf_op jit(solution)/shard_map/ppermute | solution.py:207
  42.6 10.8 %collective-permute-start.22 = (f32[2,256]{1,0:T(2,128)S(1)}, f32[2,256]{1,0:T(2,128)S(1)}, u32[]{:S(2)}, u32[]{:S(2)}) collective-permute-start(f32[2,256]{1,0:T(2,128)S(1)} %add.6.refs_6_.refs_0_), channel_id=1, source_target_pairs={{0,2},{1,3},{2,0},{3,1},{4,6},{5,7},{6,4},{7,5},{8,10},{9,11},{10,... | collective-permute-start | bytes 6152 | tf_op jit(solution)/shard_map/ppermute | solution.py:207
  46.6 8.7 %collective-permute-start.23 = (f32[2,256]{1,0:T(2,128)S(1)}, f32[2,256]{1,0:T(2,128)S(1)}, u32[]{:S(2)}, u32[]{:S(2)}) collective-permute-start(f32[2,256]{1,0:T(2,128)S(1)} %add.6.refs_6_.refs_0_), channel_id=1, source_target_pairs={{0,4},{1,5},{2,6},{3,7},{4,0},{5,1},{6,2},{7,3},{8,12},{9,13},{10,... | collective-permute-start | bytes 6152 | tf_op jit(solution)/shard_map/ppermute | solution.py:207
  50.1 6.7 %collective-permute-start.24 = (f32[2,256]{1,0:T(2,128)S(1)}, f32[2,256]{1,0:T(2,128)S(1)}, u32[]{:S(2)}, u32[]{:S(2)}) collective-permute-start(f32[2,256]{1,0:T(2,128)S(1)} %add.6.refs_6_.refs_0_), channel_id=1, source_target_pairs={{0,6},{1,7},{2,4},{3,5},{4,2},{5,3},{6,0},{7,1},{8,14},{9,15},{10,... | collective-permute-start | bytes 6152 | tf_op jit(solution)/shard_map/ppermute | solution.py:207
  50.2 12.7 %collective-permute-start.20 = (bf16[128,1024]{1,0:T(8,128)(2,1)S(1)}, bf16[128,1024]{1,0:T(8,128)(2,1)S(1)}, u32[]{:S(2)}, u32[]{:S(2)}) collective-permute-start(bf16[128,1024]{1,0:T(8,128)(2,1)S(1)} %sink.7.refs_4_), channel_id=1, source_target_pairs={{2,0},{3,1},{4,2},{5,3},{6,4},{7,5},{10,8},{11,9},{12,10},{13,11},... | collective-permute-start | bytes 786440 | tf_op jit(solution)/shard_map/ppermute | solution.py:207
  56.8 3.6 %collective-permute-start.25 = (f32[2,256]{1,0:T(2,128)S(1)}, f32[2,256]{1,0:T(2,128)S(1)}, u32[]{:S(2)}, u32[]{:S(2)}) collective-permute-start(f32[2,256]{1,0:T(2,128)S(1)} %add.7.refs_0_), channel_id=1, source_target_pairs={{0,16},{8,24},{16,0},{24,8},{1,17},{9,25},{17,1},{25,9},{2,18},{10... | collective-permute-start | bytes 6152 | tf_op jit(solution)/shard_map/ppermute | solution.py:207
  60.9 1.0 %copy-start.2 = (bf16[1,128,1024]{2,1,0:T(8,128)(2,1)S(1)}, bf16[1,128,1024]{2,1,0:T(8,128)(2,1)}, u32[]{:S(2)}) copy-start(bf16[1,128,1024]{2,1,0:T(8,128)(2,1)} %refs_0_.7) | copy-start | bytes 786436

commit v8 on v4

--- a/solution.py
+++ b/solution.py
@@ -20,6 +20,8 @@
 LAG = 2
 
 PIECES = 4
+
+GAIN_ROWS = 32
 
 VMEM = pl.BlockSpec(memory_space=pltpu.VMEM)
 ANY = pl.BlockSpec(memory_space=pl.ANY)
@@ -85,7 +87,8 @@
     first, count, at_own, at_x, at_near, at_far, segments, queries, out_grad, own, across_x, arrived_near, arrived_far,
     across_k, across_v,    query_gain, key_gain, *rest,
 ):
-    attended, query_grad, part_own, part_near, part_far, third_k, third_v, part_next, gains = rest
+    attended, query_grad, part_own, part_near, part_far, third_k, third_v, part_next, gains = rest[-9:]
+    earlier = rest[0] if len(rest) > 9 else None
     position = lax.axis_index("ctx")
     rows = queries.shape[1]
     band = (GREACH + 1) * rows
@@ -107,8 +110,11 @@
     live = (query_seg == key_seg) & (back >= 0) & (back < WINDOW)
     live = jnp.concatenate([live] * GROUPS, 0)
 
-    query_gains = jnp.zeros((1, HEAD_DIM), F32)
-    key_gains = jnp.zeros((1, HEAD_DIM), F32)
+    def folded(field):
+        return jnp.sum(field.reshape(-1, GAIN_ROWS, HEAD_DIM), 0)
+
+    query_gains = 0.0 if earlier is None else earlier[:GAIN_ROWS, :]
+    key_gains = 0.0 if earlier is None else earlier[GAIN_ROWS:, :]
 
     def band_of(index):
         third = (across_k, 0) if index < count else (across_v, -count * HEAD_DIM)
@@ -153,10 +159,10 @@
         for g, at in enumerate(at_q):
             attended[:, at] = output[g * rows : (g + 1) * rows]
             query_grad[:, at] = grad[g * rows : (g + 1) * rows]
-        query_gains = query_gains + jnp.sum(dq * q_normed, 0, keepdims=True)
-        key_gains = key_gains + jnp.sum(key_parts * k_normed, 0, keepdims=True)
-    gains[0:1, :] = query_gains
-    gains[1:2, :] = key_gains
+        query_gains = query_gains + folded(dq * q_normed)
+        key_gains = key_gains + folded(key_parts * k_normed)
+    gains[:GAIN_ROWS, :] = query_gains
+    gains[GAIN_ROWS:, :] = key_gains
 
 
 def assemble(*refs):
@@ -166,13 +172,9 @@
             out[0, :, first * GROUPS * HEAD_DIM : (first + count) * GROUPS * HEAD_DIM] = part[...]
 
 
-def add(*refs):
-    refs[-1][...] = sum(ref[...] for ref in refs[1:-1]) + refs[0][...]
-
-
 def scale(factor, total, query_gains, key_gains):
-    query_gains[...] = total[0:1, :] * factor
-    key_gains[...] = total[1:2, :] * factor
+    query_gains[...] = jnp.sum(total[:GAIN_ROWS, :], 0, keepdims=True) * factor
+    key_gains[...] = jnp.sum(total[GAIN_ROWS:, :], 0, keepdims=True) * factor
 
 
 def finish(count, at, keys, key_gain, part_own, swapped, arrived, *rest):
@@ -214,15 +216,6 @@
 
 def swap(field):
     return move(field, "ctx", lambda i: i ^ 1)
-
-
-def total_over(field, axis, unit, most, after=()):
-    while unit < lax.axis_size(axis):
-        group = min(most, lax.axis_size(axis) // unit)
-        others = [move(field, axis, lambda i: i ^ (by * unit)) for by in range(1, group)]
-        (field,) = call(add, "add", dict(enumerate([field, *others])), dict(o=shape(*field.shape, F32)), after)
-        unit *= group
-    return field
 
 
 def shards(segment_ids, queries, keys, values, query_gain, key_gain, out_grad):
@@ -353,23 +346,24 @@
                 segments=segments, queries=queries, out_grad=out_grad, own=own[chunk][0],
                 **{f"behind{i}": place[chunk][0] for i, place in enumerate(held[1:])},
                 third_k=third_behind[chunk][0], third_v=third_behind[chunk][1], gain_q=gain_q, gain_k=gain_k,
+                **({"earlier": gains[0]} if gains else {}),
             ),
             dict(
                 attended=wide, query_grad=wide, own=whole, near=whole, far=whole,
                 third_k=half, third_v=half, next=low,
-                gains=shape(2, HEAD_DIM, F32),
+                gains=shape(2 * GAIN_ROWS, HEAD_DIM, F32),
             ),
             last,
         )
         made.append(result[:2])
-        gains.append(result[8])
+        gains = [result[8]]
         token = [result[8]]
         parts.append(dict(zip(("own", "near", "far"), result[2:5])))
         parts[-1].update(third_k=swap(result[5]), third_v=swap(result[6]), next=swap(result[7]))
         last = [sink(chunk, last)]
 
+    total = lax.psum(gains[0], ("dp", "ctx"))
     for step in range(amount, amount + LAG):
-        order_gains = last
         last = [sink(step, last)]
     key_outputs = []
     for chunk, (first, count) in enumerate(CHUNKS):
@@ -398,13 +392,15 @@
         last,
     )
 
-    (total,) = call(add, "add", dict(enumerate(gains)), dict(o=shape(2, HEAD_DIM, F32)))
-    (total,) = call(add, "add", dict(a=total, b=swap(total)), dict(o=shape(2, HEAD_DIM, F32)), order_gains)
-    total = total_over(total, "dp", 1, 2, last)
-    total = total_over(total, "ctx", 2, 4)
     factor = (lax.axis_size("dp") * queries.shape[0] * lax.axis_size("ctx") * rows) ** (-0.5)
     row = shape(1, HEAD_DIM, F32)
-    query_gains, key_gains = call(functools.partial(scale, factor), "scale", dict(t=total), dict(a=row, b=row))
+    query_gains, key_gains = call(
+        functools.partial(scale, factor),
+        "scale",
+        dict(total=total),
+        dict(a=row, b=row),
+        [pltpu.with_memory_space_constraint(field, pltpu.HBM) for field in (attended, *key_outputs)],
+    )
     return attended, query_grad, *key_outputs, query_gains[0], key_gains[0]
 
 

time: 71.8 us -> 188 us (2.62)
  waiting for transfers between devices: 25.3 us -> 133 us
  between operations: 0.85 us -> 14.2 us
  starting transfers between devices: 34.7 us -> 25.5 us
    psum x0 -> x1, waiting for transfers between devices: none -> 110 us  [shards(): total = lax.psum(gains[0], ('dp', 'ctx'))]
    ppermute x26 -> x20, starting transfers between devices: 34.7 us -> 25.4 us  [move(): lax.ppermute(field, axis, [(i, target(i)) for i in range(size) if 0 <= ta...]
    ppermute x26 -> x20, waiting for transfers between devices: 25.3 us -> 23.3 us  [move(): lax.ppermute(field, axis, [(i, target(i)) for i in range(size) if 0 <= ta...]
    pallas_call x21 -> x16, Pallas kernels: 10.5 us -> 11.9 us  [call(): pl.pallas_call(kernel, out_shape=list(outs.values()), in_specs=specs, out...]
  transfers between devices with their start and end apart: 26 -> 21, of which waited for: 15 -> 13; matrix products, arithmetic and copies ran while one was open for 0% -> 0% of each run, Pallas kernels for 12% -> 6%
where the time goes in v8:
time: 188 us; the launch traced here: 186 us
  waiting for transfers between devices  133 us (71%)
  starting transfers between devices  25.5 us (14%)
  between operations  14.2 us (8%)
  Pallas kernels  11.9 us (6%)
    psum x1, waiting for transfers between devices, shards(): total = lax.psum(gains[0], ('dp', 'ctx'))  110 us
    ppermute x20, starting transfers between devices, move(): lax.ppermute(field, axis, [(i, target(i)) for i in range(size) if 0 <= ta...  25.4 us
    ppermute x20, waiting for transfers between devices, move(): lax.ppermute(field, axis, [(i, target(i)) for i in range(size) if 0 <= ta...  23.3 us
    pallas_call x16, Pallas kernels, call(): pl.pallas_call(kernel, out_shape=list(outs.values()), in_specs=specs, out...  11.9 us
  transfers between devices with their start and end apart: 21, of which 13 were waited for; matrix products, arithmetic and copies ran while one was open for 0% of the time, Pallas kernels for 6%

profile of v8, /device:TPU:0, one launch (start us, length us, event | category | flops | bytes accessed | tf_op | source)
XLA Modules:
  0.0 185.9 jit_solution(2758267526405342897)
XLA Ops:
  7.2 0.9 payload.2.refs_5_.refs_1_.refs_3_
  8.2 4.9 %collective-permute-start = (bf16[128,1024]{1,0:T(8,128)(2,1)S(1)}, bf16[128,1024]{1,0:T(8,128)(2,1)S(1)}, u32[]{:S(2)}, u32[]{:S(2)}) collective-permute-start(bf16[128,1024]{1,0:T(8,128)(2,1)S(1)} %payload.2.refs_5_.refs_1_.refs_3_), channel_id=1, source_target_pairs={{0,2},{1,3},{2,4},{3,5},{4,6},{5,7},{8,10},{9,11},{10,12},{11,13},... | collective-permute-start | bytes 786440 | tf_op jit(solution)/shard_map/ppermute | solution.py:206
  13.1 1.0 payload.3
  14.1 3.5 %collective-permute-start.3 = (bf16[128,1024]{1,0:T(8,128)(2,1)S(1)}, bf16[128,1024]{1,0:T(8,128)(2,1)S(1)}, u32[]{:S(2)}, u32[]{:S(2)}) collective-permute-start(bf16[128,1024]{1,0:T(8,128)(2,1)S(1)} %get-tuple-element.47.refs_1_.refs_3_), channel_id=1, source_target_pairs={{0,2},{1,3},{2,4},{3,5},{4,6},{5,7},{8,10},{9,11},{10,12},{11,13},... | collective-permute-start | bytes 786440 | tf_op jit(solution)/shard_map/ppermute | solution.py:206
  17.6 2.2 %collective-permute-done.refs_0_.refs_5_ = bf16[128,1024]{1,0:T(8,128)(2,1)S(1)} collective-permute-done((bf16[128,1024]{1,0:T(8,128)(2,1)S(1)}, bf16[128,1024]{1,0:T(8,128)(2,1)S(1)}, u32[]{:S(2)}, u32[]{:S(2)}) %collective-permute-start) | collective-permute-done | bytes 262176 | tf_op jit(solution)/shard_map/ppermute | solution.py:206
  19.8 4.4 %collective-permute-start.2 = (bf16[128,1024]{1,0:T(8,128)(2,1)S(1)}, bf16[128,1024]{1,0:T(8,128)(2,1)S(1)}, u32[]{:S(2)}, u32[]{:S(2)}) collective-permute-start(bf16[128,1024]{1,0:T(8,128)(2,1)S(1)} %get-tuple-element.46.refs_2_), channel_id=1, source_target_pairs={{0,2},{1,3},{2,4},{3,5},{4,6},{5,7},{8,10},{9,11},{10,12},{11,13},... | collective-permute-start | bytes 786440 | tf_op jit(solution)/shard_map/ppermute | solution.py:206
  24.3 1.1 collective-permute-done.3.refs_0_.refs_5_
  25.5 4.5 %collective-permute-start.7 = (bf16[128,1024]{1,0:T(8,128)(2,1)S(1)}, bf16[128,1024]{1,0:T(8,128)(2,1)S(1)}, u32[]{:S(2)}, u32[]{:S(2)}) collective-permute-start(bf16[128,1024]{1,0:T(8,128)(2,1)S(1)} %get-tuple-element.48.refs_2_), channel_id=1, source_target_pairs={{0,2},{1,3},{2,4},{3,5},{4,6},{5,7},{8,10},{9,11},{10,12},{11,13},... | collective-permute-start | bytes 786440 | tf_op jit(solution)/shard_map/ppermute | solution.py:206
  30.0 1.0 collective-permute-done.2.refs_1_.refs_6_
  31.1 0.5 collective-permute-start.5
  31.7 0.8 collective-permute-done.4.refs_7_
  32.7 2.2 %attend.2 = (bf16[128,1024]{1,0:T(8,128)(2,1)S(1)}, bf16[128,1024]{1,0:T(8,128)(2,1)S(1)}, f32[128,1024]{1,0:T(8,128)S(1)}, f32[128,1024]{1,0:T(8,128)S(1)}, f32...) custom-call(s32[1,1024]{1,0:T(1,128)S(1)} %get-tuple-element.44.refs, ...), custom_call_target="tpu_custom_call" | custom-call | bytes 1 | tf_op jit(solution)/shard_map/attend/pallas_call | solution.py:38
  34.9 0.4 collective-permute-start.10
  35.5 0.4 collective-permute-start.8
  36.3 0.3 collective-permute-start.17
  36.7 1.3 collective-permute-start.16
  38.1 2.8 %attend.3 = (bf16[128,1024]{1,0:T(8,128)(2,1)S(1)}, bf16[128,1024]{1,0:T(8,128)(2,1)S(1)}, f32[128,1024]{1,0:T(8,128)S(1)}, f32[128,1024]{1,0:T(8,128)S(1)}, f32...) custom-call(s32[1,1024]{1,0:T(1,128)S(1)} %get-tuple-element.44.refs, ...), custom_call_target="tpu_custom_call" | custom-call | bytes 1 | tf_op jit(solution)/shard_map/attend/pallas_call | solution.py:38
  41.0 0.3 collective-permute-start.13
  41.6 0.6 collective-permute-done.12.refs_1_.refs_2_
  42.5 1.3 collective-permute-start.14
  43.8 4.0 %collective-permute-done.16.refs_1_ = bf16[128,1024]{1,0:T(8,128)(2,1)S(1)} collective-permute-done((bf16[128,1024]{1,0:T(8,128)(2,1)S(1)}, bf16[128,1024]{1,0:T(8,128)(2,1)S(1)}, u32[]{:S(2)}, u32[]{:S(2)}) %collective-permute-start.16) | collective-permute-done | bytes 262176 | tf_op jit(solution)/shard_map/ppermute | solution.py:206
  47.9 1.3 collective-permute-start.19
  49.2 5.3 %collective-permute-done.14.refs_1_ = bf16[128,1024]{1,0:T(8,128)(2,1)S(1)} collective-permute-done((bf16[128,1024]{1,0:T(8,128)(2,1)S(1)}, bf16[128,1024]{1,0:T(8,128)(2,1)S(1)}, u32[]{:S(2)}, u32[]{:S(2)}) %collective-permute-start.14) | collective-permute-done | bytes 262176 | tf_op jit(solution)/shard_map/ppermute | solution.py:206
  54.7 1.3 collective-permute-start.18
  56.0 1.0 assemble.1
  57.0 3.1 %collective-permute-done.19.refs_4_ = bf16[128,1024]{1,0:T(8,128)(2,1)S(1)} collective-permute-done((bf16[128,1024]{1,0:T(8,128)(2,1)S(1)}, bf16[128,1024]{1,0:T(8,128)(2,1)S(1)}, u32[]{:S(2)}, u32[]{:S(2)}) %collective-permute-start.19) | collective-permute-done | bytes 262176 | tf_op jit(solution)/shard_map/ppermute | solution.py:206
  60.2 0.9 finish.2
  61.1 4.5 %collective-permute-done.18.refs_4_ = bf16[128,1024]{1,0:T(8,128)(2,1)} collective-permute-done((bf16[128,1024]{1,0:T(8,128)(2,1)S(1)}, bf16[128,1024]{1,0:T(8,128)(2,1)}, u32[]{:S(2)}, u32[]{:S(2)}) %collective-permute-start.18) | collective-permute-done | bytes 262176 | tf_op jit(solution)/shard_map/ppermute | solution.py:206
  65.6 1.9 %finish.3 = (bf16[1,128,1024]{2,1,0:T(8,128)(2,1)}, bf16[1,128,1024]{2,1,0:T(8,128)(2,1)}) custom-call(bf16[1,128,1024]{2,1,0:T(8,128)(2,1)S(1)} %copy-done.2, f32[1,256]{1,0:T(1,128)S(1)} %get-tuple-element.52.refs_10_.refs_1_, f32[128,1024]{1,0:T(8,128)S(1)} %get-tuple-element.73.refs_2_, ...), custom_call_target="tpu_custom_call", output_to_operand_aliasing={{0}: (5, {}), {1}: (6, {})} | custom-call | flops 4294967296 | bytes 1 | tf_op jit(solution)/shard_map/finish/pallas_call | solution.py:38
  67.5 110.2 %all-reduce.2.cloned.1.call-done.refs_0_ = f32[64,256]{1,0:T(8,128)} async-done(((f32[64,256]{1,0:T(8,128)}), f32[64,256]{1,0:T(8,128)}) %all-reduce.2.cloned.1.call-update) | async-done | bytes 65552 | tf_op jit(solution)/shard_map/psum | solution.py:365
  177.6 0.8 copy-done.3
  178.5 0.6 scale.1
  (35 shorter events, 2.2 us)
Async XLA Ops:
  7.2 170.5 %all-reduce.2.cloned.1.call-start = ((), (), s32[]{:S(2)}) async-start(), calls=%async_computation | async-start | bytes 131072 | tf_op jit(solution)/shard_map/psum | solution.py:365
  8.2 11.6 %collective-permute-start = (bf16[128,1024]{1,0:T(8,128)(2,1)S(1)}, bf16[128,1024]{1,0:T(8,128)(2,1)S(1)}, u32[]{:S(2)}, u32[]{:S(2)}) collective-permute-start(bf16[128,1024]{1,0:T(8,128)(2,1)S(1)} %payload.2.refs_5_.refs_1_.refs_3_), channel_id=1, source_target_pairs={{0,2},{1,3},{2,4},{3,5},{4,6},{5,7},{8,10},{9,11},{10,12},{11,13},... | collective-permute-start | bytes 786440 | tf_op jit(solution)/shard_map/ppermute | solution.py:206
  14.1 11.3 %collective-permute-start.3 = (bf16[128,1024]{1,0:T(8,128)(2,1)S(1)}, bf16[128,1024]{1,0:T(8,128)(2,1)S(1)}, u32[]{:S(2)}, u32[]{:S(2)}) collective-permute-start(bf16[128,1024]{1,0:T(8,128)(2,1)S(1)} %get-tuple-element.47.refs_1_.refs_3_), channel_id=1, source_target_pairs={{0,2},{1,3},{2,4},{3,5},{4,6},{5,7},{8,10},{9,11},{10,12},{11,13},... | collective-permute-start | bytes 786440 | tf_op jit(solution)/shard_map/ppermute | solution.py:206
  19.8 11.2 %collective-permute-start.2 = (bf16[128,1024]{1,0:T(8,128)(2,1)S(1)}, bf16[128,1024]{1,0:T(8,128)(2,1)S(1)}, u32[]{:S(2)}, u32[]{:S(2)}) collective-permute-start(bf16[128,1024]{1,0:T(8,128)(2,1)S(1)} %get-tuple-element.46.refs_2_), channel_id=1, source_target_pairs={{0,2},{1,3},{2,4},{3,5},{4,6},{5,7},{8,10},{9,11},{10,12},{11,13},... | collective-permute-start | bytes 786440 | tf_op jit(solution)/shard_map/ppermute | solution.py:206
  24.2 7.5 %collective-permute-start.1 = (bf16[128,1024]{1,0:T(8,128)(2,1)S(1)}, bf16[128,1024]{1,0:T(8,128)(2,1)S(1)}, u32[]{:S(2)}, u32[]{:S(2)}) collective-permute-start(bf16[128,1024]{1,0:T(8,128)(2,1)S(1)} %get-tuple-element.45), channel_id=1, source_target_pairs={{0,1},{1,0},{2,3},{3,2},{4,5},{5,4},{6,7},{7,6},{8,9},{9,8},{10,11... | collective-permute-start | bytes 786440 | tf_op jit(solution)/shard_map/ppermute | solution.py:206
  25.5 7.2 %copy-start = (bf16[1,128,2048]{2,1,0:T(8,128)(2,1)S(1)}, bf16[1,128,2048]{2,1,0:T(8,128)(2,1)}, u32[]{:S(2)}) copy-start(bf16[1,128,2048]{2,1,0:T(8,128)(2,1)} %refs_1_.7) | copy-start | bytes 1572868
  25.5 7.2 %copy-start.1 = (bf16[1,128,2048]{2,1,0:T(8,128)(2,1)S(1)}, bf16[1,128,2048]{2,1,0:T(8,128)(2,1)}, u32[]{:S(2)}) copy-start(bf16[1,128,2048]{2,1,0:T(8,128)(2,1)} %refs_2_.5) | copy-start | bytes 1572868
  25.5 10.0 %collective-permute-start.7 = (bf16[128,1024]{1,0:T(8,128)(2,1)S(1)}, bf16[128,1024]{1,0:T(8,128)(2,1)S(1)}, u32[]{:S(2)}, u32[]{:S(2)}) collective-permute-start(bf16[128,1024]{1,0:T(8,128)(2,1)S(1)} %get-tuple-element.48.refs_2_), channel_id=1, source_target_pairs={{0,2},{1,3},{2,4},{3,5},{4,6},{5,7},{8,10},{9,11},{10,12},{11,13},... | collective-permute-start | bytes 786440 | tf_op jit(solution)/shard_map/ppermute | solution.py:206
  31.1 1.4 collective-permute-start.4
  31.1 1.5 collective-permute-start.5
  31.6 6.4 %collective-permute-start.6 = (bf16[128,1024]{1,0:T(8,128)(2,1)S(1)}, bf16[128,1024]{1,0:T(8,128)(2,1)S(1)}, u32[]{:S(2)}, u32[]{:S(2)}) collective-permute-start(bf16[128,1024]{1,0:T(8,128)(2,1)S(1)} %get-tuple-element.54), channel_id=1, source_target_pairs={{0,1},{1,0},{2,3},{3,2},{4,5},{5,4},{6,7},{7,6},{8,9},{9,8},{10,11... | collective-permute-start | bytes 786440 | tf_op jit(solution)/shard_map/ppermute | solution.py:206
  34.9 1.4 collective-permute-start.10
  35.3 1.4 collective-permute-start.11
  35.5 2.5 %collective-permute-start.8 = (bf16[128,512]{1,0:T(8,128)(2,1)S(1)}, bf16[128,512]{1,0:T(8,128)(2,1)S(1)}, u32[]{:S(2)}, u32[]{:S(2)}) collective-permute-start(bf16[128,512]{1,0:T(8,128)(2,1)S(1)} %get-tuple-element.56), channel_id=1, source_target_pairs={{0,1},{1,0},{2,3},{3,2},{4,5},{5,4},{6,7},{7,6},{8,9},{9,8},{10,11... | collective-permute-start | bytes 393224 | tf_op jit(solution)/shard_map/ppermute | solution.py:206
  35.9 2.1 %collective-permute-start.9 = (bf16[128,512]{1,0:T(8,128)(2,1)S(1)}, bf16[128,512]{1,0:T(8,128)(2,1)S(1)}, u32[]{:S(2)}, u32[]{:S(2)}) collective-permute-start(bf16[128,512]{1,0:T(8,128)(2,1)S(1)} %get-tuple-element.57), channel_id=1, source_target_pairs={{0,1},{1,0},{2,3},{3,2},{4,5},{5,4},{6,7},{7,6},{8,9},{9,8},{10,11... | collective-permute-start | bytes 393224 | tf_op jit(solution)/shard_map/ppermute | solution.py:206
  36.3 7.4 %collective-permute-start.17 = (bf16[128,1024]{1,0:T(8,128)(2,1)S(1)}, bf16[128,1024]{1,0:T(8,128)(2,1)S(1)}, u32[]{:S(2)}, u32[]{:S(2)}) collective-permute-start(bf16[128,1024]{1,0:T(8,128)(2,1)S(1)} %get-tuple-element.70), channel_id=1, source_target_pairs={{0,1},{1,0},{2,3},{3,2},{4,5},{5,4},{6,7},{7,6},{8,9},{9,8},{10,11... | collective-permute-start | bytes 786440 | tf_op jit(solution)/shard_map/ppermute | solution.py:206
  36.7 11.0 %collective-permute-start.16 = (bf16[128,1024]{1,0:T(8,128)(2,1)S(1)}, bf16[128,1024]{1,0:T(8,128)(2,1)S(1)}, u32[]{:S(2)}, u32[]{:S(2)}) collective-permute-start(bf16[128,1024]{1,0:T(8,128)(2,1)S(1)} %sink.4.refs_12_.refs_3_), channel_id=1, source_target_pairs={{2,0},{3,1},{4,2},{5,3},{6,4},{7,5},{10,8},{11,9},{12,10},{13,11},... | collective-permute-start | bytes 786440 | tf_op jit(solution)/shard_map/ppermute | solution.py:206
  40.9 1.3 collective-permute-start.12
  41.0 1.3 collective-permute-start.13
  41.4 7.8 %collective-permute-start.15 = (bf16[128,1024]{1,0:T(8,128)(2,1)S(1)}, bf16[128,1024]{1,0:T(8,128)(2,1)S(1)}, u32[]{:S(2)}, u32[]{:S(2)}) collective-permute-start(bf16[128,1024]{1,0:T(8,128)(2,1)S(1)} %get-tuple-element.68), channel_id=1, source_target_pairs={{0,1},{1,0},{2,3},{3,2},{4,5},{5,4},{6,7},{7,6},{8,9},{9,8},{10,11... | collective-permute-start | bytes 786440 | tf_op jit(solution)/shard_map/ppermute | solution.py:206
  42.5 12.1 %collective-permute-start.14 = (bf16[128,1024]{1,0:T(8,128)(2,1)S(1)}, bf16[128,1024]{1,0:T(8,128)(2,1)S(1)}, u32[]{:S(2)}, u32[]{:S(2)}) collective-permute-start(bf16[128,1024]{1,0:T(8,128)(2,1)S(1)} %sink.5.refs_5_), channel_id=1, source_target_pairs={{2,0},{3,1},{4,2},{5,3},{6,4},{7,5},{10,8},{11,9},{12,10},{13,11},... | collective-permute-start | bytes 786440 | tf_op jit(solution)/shard_map/ppermute | solution.py:206
  47.9 12.3 %collective-permute-start.19 = (bf16[128,1024]{1,0:T(8,128)(2,1)S(1)}, bf16[128,1024]{1,0:T(8,128)(2,1)S(1)}, u32[]{:S(2)}, u32[]{:S(2)}) collective-permute-start(bf16[128,1024]{1,0:T(8,128)(2,1)S(1)} %sink.6.refs_5_), channel_id=1, source_target_pairs={{2,0},{3,1},{4,2},{5,3},{6,4},{7,5},{10,8},{11,9},{12,10},{13,11},... | collective-permute-start | bytes 786440 | tf_op jit(solution)/shard_map/ppermute | solution.py:206
  54.7 11.0 %collective-permute-start.18 = (bf16[128,1024]{1,0:T(8,128)(2,1)S(1)}, bf16[128,1024]{1,0:T(8,128)(2,1)}, u32[]{:S(2)}, u32[]{:S(2)}) collective-permute-start(bf16[128,1024]{1,0:T(8,128)(2,1)S(1)} %sink.7.refs_4_), channel_id=1, source_target_pairs={{2,0},{3,1},{4,2},{5,3},{6,4},{7,5},{10,8},{11,9},{12,10},{13,11},... | collective-permute-start | bytes 786440 | tf_op jit(solution)/shard_map/ppermute | solution.py:206
  56.0 4.2 %copy-start.2 = (bf16[1,128,1024]{2,1,0:T(8,128)(2,1)S(1)}, bf16[1,128,1024]{2,1,0:T(8,128)(2,1)}, u32[]{:S(2)}) copy-start(bf16[1,128,1024]{2,1,0:T(8,128)(2,1)} %refs_0_.7) | copy-start | bytes 786436
  177.6 0.8 copy-start.3
Sparse Core Ops, SparseCore 0:
  56.1 121.4 all-reduce.1

commit v9 on v5

--- a/solution.py
+++ b/solution.py
@@ -20,6 +20,8 @@
 LAG = 2
 
 PIECES = 4
+
+COSTS = 2**32, 0, 0, 2**31, 2**32, 2**32
 
 VMEM = pl.BlockSpec(memory_space=pltpu.VMEM)
 ANY = pl.BlockSpec(memory_space=pl.ANY)
@@ -170,9 +172,10 @@
     refs[-1][...] = sum(ref[...] for ref in refs[1:-1]) + refs[0][...]
 
 
-def scale(factor, total, query_gains, key_gains):
-    query_gains[...] = total[0:1, :] * factor
-    key_gains[...] = total[1:2, :] * factor
+def scale(factor, *refs):
+    total = sum(ref[...] for ref in refs[1:-2]) + refs[0][...]
+    refs[-2][...] = total[0:1, :] * factor
+    refs[-1][...] = total[1:2, :] * factor
 
 
 def finish(count, at, keys, key_gain, part_own, swapped, arrived, *rest):
@@ -216,12 +219,12 @@
     return move(field, "ctx", lambda i: i ^ 1)
 
 
-def total_over(field, axis, unit, end, most, after=()):
+def total_over(field, axis, unit, end, most, cost=0, after=()):
     end = min(end, lax.axis_size(axis))
     while unit < end:
         group = min(most, end // unit)
         others = [move(field, axis, lambda i: i ^ (by * unit)) for by in range(1, group)]
-        (field,) = call(add, "add", dict(enumerate([field, *others])), dict(o=shape(*field.shape, F32)), after)
+        (field,) = call(add, "add", dict(enumerate([field, *others])), dict(o=shape(*field.shape, F32)), after, cost=cost)
         unit *= group
     return field
 
@@ -373,9 +376,35 @@
             last = [*last, total]
         last = [sink(chunk, last)]
 
-    total = total_over(total, "dp", 1, 2, 2)
     for step in range(amount, amount + LAG):
-        last = [sink(step, [*last, total])]
+        last = [sink(step, last)]
+
+    factor = (lax.axis_size("dp") * queries.shape[0] * lax.axis_size("ctx") * rows) ** (-0.5)
+    row = shape(1, HEAD_DIM, F32)
+    chips = lax.axis_size("ctx") // 2
+    (total,) = call(add, "add", dict(total=total), dict(o=shape(2, HEAD_DIM, F32)), [sunk[0]], cost=COSTS[5])
+    while chips > 4:
+        total = total_over(total, "ctx", chips, 2 * chips, 2)
+        chips //= 2
+    total = total_over(total, "ctx", 2, 2 * chips, 4, COSTS[0], [sunk[amount - 1]])
+    half = lax.axis_size("dp") // 2
+    total = total_over(total, "dp", 1, half, 2, COSTS[1])
+    others = [move(total, "dp", lambda i: i ^ half)] if half else []
+    query_gains, key_gains = call(
+        functools.partial(scale, factor),
+        "scale",
+        dict(enumerate([total, *others])),
+        dict(a=row, b=row),
+        cost=COSTS[2],
+    )
+    attended, query_grad = call(
+        assemble,
+        "assemble",
+        {(i, chunk): made[chunk][i] for i in range(2) for chunk in range(amount)},
+        dict(a=jax.ShapeDtypeStruct(queries.shape, BF16), b=jax.ShapeDtypeStruct(queries.shape, BF16)),
+        last,
+    )
+    before = [pltpu.with_memory_space_constraint(field, pltpu.HBM) for field in (attended, query_gains)]
     key_outputs = []
     for chunk, (first, count) in enumerate(CHUNKS):
         narrow = columns(rows, count * HEAD_DIM, first * HEAD_DIM)
@@ -388,26 +417,13 @@
             dict(
                 key_grad=jax.ShapeDtypeStruct(keys.shape, BF16), value_grad=jax.ShapeDtypeStruct(keys.shape, BF16)
             ),
-            key_outputs,
-            cost=2**31 * (1 + chunk),
+            [*key_outputs, *(before if chunk == amount - 1 else [])],
+            cost=COSTS[3 + chunk],
             grid=(1,),
             in_specs=dict(keys=narrow),
             out_specs=dict(key_grad=narrow, value_grad=narrow),
             input_output_aliases={5 + i: i for i in range(len(key_outputs))},
         )
-    attended, query_grad = call(
-        assemble,
-        "assemble",
-        {(i, chunk): made[chunk][i] for i in range(2) for chunk in range(amount)},
-        dict(a=jax.ShapeDtypeStruct(queries.shape, BF16), b=jax.ShapeDtypeStruct(queries.shape, BF16)),
-        last,
-    )
-
-    total = total_over(total, "dp", 2, lax.axis_size("dp"), 2)
-    total = total_over(total, "ctx", 2, lax.axis_size("ctx"), 4, last)
-    factor = (lax.axis_size("dp") * queries.shape[0] * lax.axis_size("ctx") * rows) ** (-0.5)
-    row = shape(1, HEAD_DIM, F32)
-    query_gains, key_gains = call(functools.partial(scale, factor), "scale", dict(t=total), dict(a=row, b=row))
     return attended, query_grad, *key_outputs, query_gains[0], key_gains[0]
 
 

time: 68.4 us -> 61.7 us (0.902)
  waiting for transfers between devices: 21.7 us -> 16.8 us
  starting transfers between devices: 35 us -> 33.1 us
    ppermute x26, waiting for transfers between devices: 21.7 us -> 16.8 us  [move(): lax.ppermute(field, axis, [(i, target(i)) for i in range(size) if 0 <= ta...]
    ppermute x26, starting transfers between devices: 35 us -> 33.1 us  [move(): lax.ppermute(field, axis, [(i, target(i)) for i in range(size) if 0 <= ta...]
  transfers between devices with their start and end apart: 26 -> 26, of which waited for: 13 -> 15; matrix products, arithmetic and copies ran while one was open for 0% -> 0% of each run, Pallas kernels for 13% -> 14%
where the time goes in v9:
time: 61.7 us; the launch traced here: 61.3 us
  starting transfers between devices  33.1 us (54%)
  waiting for transfers between devices  16.8 us (27%)
  Pallas kernels  10.4 us (17%)
  between operations  0.84 us (1%)
    ppermute x26, starting transfers between devices, move(): lax.ppermute(field, axis, [(i, target(i)) for i in range(size) if 0 <= ta...  33.1 us
    ppermute x26, waiting for transfers between devices, move(): lax.ppermute(field, axis, [(i, target(i)) for i in range(size) if 0 <= ta...  16.8 us
    pallas_call x21, Pallas kernels, call(): pl.pallas_call(kernel, out_shape=list(outs.values()), in_specs=specs, out...  10.4 us
  transfers between devices with their start and end apart: 26, of which 15 were waited for; matrix products, arithmetic and copies ran while one was open for 0% of the time, Pallas kernels for 14%

profile of v9, /device:TPU:0, one launch (start us, length us, event | category | flops | bytes accessed | tf_op | source)
XLA Modules:
  0.0 61.3 jit_solution(16553436254627694366)
XLA Ops:
  0.6 0.9 %payload.2.refs_5_.refs_1_.refs_3_ = bf16[128,1024]{1,0:T(8,128)(2,1)S(1)} custom-call(bf16[1,128,1024]{2,1,0:T(8,128)(2,1)} %refs_0_.7, bf16[1,128,1024]{2,1,0:T(8,128)(2,1)} %refs_1_.5), custom_call_target="tpu_custom_call" | custom-call | bytes 1 | tf_op jit(solution)/shard_map/payload/pallas_call | solution.py:38
  1.6 4.9 %collective-permute-start = (bf16[128,1024]{1,0:T(8,128)(2,1)S(1)}, bf16[128,1024]{1,0:T(8,128)(2,1)S(1)}, u32[]{:S(2)}, u32[]{:S(2)}) collective-permute-start(bf16[128,1024]{1,0:T(8,128)(2,1)S(1)} %payload.2.refs_5_.refs_1_.refs_3_), channel_id=1, source_target_pairs={{0,2},{1,3},{2,4},{3,5},{4,6},{5,7},{8,10},{9,11},{10,12},{11,13},... | collective-permute-start | bytes 786440 | tf_op jit(solution)/shard_map/ppermute | solution.py:207
  6.5 1.0 %payload.3 = (bf16[128,1024]{1,0:T(8,128)(2,1)S(1)}, s32[1,1024]{1,0:T(1,128)S(1)}, f32[1,256]{1,0:T(1,128)S(1)}, f32[1,256]{1,0:T(1,128)S(1)}) custom-call(bf16[1,128,1024]{2,1,0:T(8,128)(2,1)} %refs_0_.7, bf16[1,128,1024]{2,1,0:T(8,128)(2,1)} %refs_1_.5, s32[1,1024]{1,0:T(1,128)} %refs_2_.3, f32[1,256]{1,0:T(1,128)} %bitcast.4, f32[1,256]{1,0:T(1,128)} %bitcast.5, ...), custom_call_target="tpu_custom_call" | custom-call | bytes 1 | tf_op jit(solution)/shard_map/payload/pallas_call | solution.py:38
  7.6 3.5 %collective-permute-start.3 = (bf16[128,1024]{1,0:T(8,128)(2,1)S(1)}, bf16[128,1024]{1,0:T(8,128)(2,1)S(1)}, u32[]{:S(2)}, u32[]{:S(2)}) collective-permute-start(bf16[128,1024]{1,0:T(8,128)(2,1)S(1)} %get-tuple-element.47.refs_1_.refs_3_), channel_id=1, source_target_pairs={{0,2},{1,3},{2,4},{3,5},{4,6},{5,7},{8,10},{9,11},{10,12},{11,13},... | collective-permute-start | bytes 786440 | tf_op jit(solution)/shard_map/ppermute | solution.py:207
  11.1 2.2 %collective-permute-done.refs_0_.refs_5_ = bf16[128,1024]{1,0:T(8,128)(2,1)S(1)} collective-permute-done((bf16[128,1024]{1,0:T(8,128)(2,1)S(1)}, bf16[128,1024]{1,0:T(8,128)(2,1)S(1)}, u32[]{:S(2)}, u32[]{:S(2)}) %collective-permute-start) | collective-permute-done | bytes 262176 | tf_op jit(solution)/shard_map/ppermute | solution.py:207
  13.3 4.4 %collective-permute-start.2 = (bf16[128,1024]{1,0:T(8,128)(2,1)S(1)}, bf16[128,1024]{1,0:T(8,128)(2,1)S(1)}, u32[]{:S(2)}, u32[]{:S(2)}) collective-permute-start(bf16[128,1024]{1,0:T(8,128)(2,1)S(1)} %get-tuple-element.46.refs_2_), channel_id=1, source_target_pairs={{0,2},{1,3},{2,4},{3,5},{4,6},{5,7},{8,10},{9,11},{10,12},{11,13},... | collective-permute-start | bytes 786440 | tf_op jit(solution)/shard_map/ppermute | solution.py:207
  17.7 1.1 %collective-permute-done.3.refs_0_.refs_5_ = bf16[128,1024]{1,0:T(8,128)(2,1)S(1)} collective-permute-done((bf16[128,1024]{1,0:T(8,128)(2,1)S(1)}, bf16[128,1024]{1,0:T(8,128)(2,1)S(1)}, u32[]{:S(2)}, u32[]{:S(2)}) %collective-permute-start.3) | collective-permute-done | bytes 262176 | tf_op jit(solution)/shard_map/ppermute | solution.py:207
  18.9 4.5 %collective-permute-start.7 = (bf16[128,1024]{1,0:T(8,128)(2,1)S(1)}, bf16[128,1024]{1,0:T(8,128)(2,1)S(1)}, u32[]{:S(2)}, u32[]{:S(2)}) collective-permute-start(bf16[128,1024]{1,0:T(8,128)(2,1)S(1)} %get-tuple-element.48.refs_2_), channel_id=1, source_target_pairs={{0,2},{1,3},{2,4},{3,5},{4,6},{5,7},{8,10},{9,11},{10,12},{11,13},... | collective-permute-start | bytes 786440 | tf_op jit(solution)/shard_map/ppermute | solution.py:207
  23.4 1.0 %collective-permute-done.2.refs_1_.refs_6_ = bf16[128,1024]{1,0:T(8,128)(2,1)S(1)} collective-permute-done((bf16[128,1024]{1,0:T(8,128)(2,1)S(1)}, bf16[128,1024]{1,0:T(8,128)(2,1)S(1)}, u32[]{:S(2)}, u32[]{:S(2)}) %collective-permute-start.2) | collective-permute-done | bytes 262176 | tf_op jit(solution)/shard_map/ppermute | solution.py:207
  25.1 0.8 %collective-permute-done.4.refs_7_ = bf16[128,512]{1,0:T(8,128)(2,1)S(1)} collective-permute-done((bf16[128,512]{1,0:T(8,128)(2,1)S(1)}, bf16[128,512]{1,0:T(8,128)(2,1)S(1)}, u32[]{:S(2)}, u32[]{:S(2)}) %collective-permute-start.4) | collective-permute-done | bytes 131104 | tf_op jit(solution)/shard_map/ppermute | solution.py:207
  26.1 2.3 %attend.2 = (bf16[128,1024]{1,0:T(8,128)(2,1)S(1)}, bf16[128,1024]{1,0:T(8,128)(2,1)S(1)}, f32[128,1024]{1,0:T(8,128)S(1)}, f32[128,1024]{1,0:T(8,128)S(1)}, f32...) custom-call(s32[1,1024]{1,0:T(1,128)S(1)} %get-tuple-element.44.refs, ...), custom_call_target="tpu_custom_call" | custom-call | bytes 1 | tf_op jit(solution)/shard_map/attend/pallas_call | solution.py:38
  30.1 1.3 %collective-permute-start.17 = (bf16[128,1024]{1,0:T(8,128)(2,1)S(1)}, bf16[128,1024]{1,0:T(8,128)(2,1)S(1)}, u32[]{:S(2)}, u32[]{:S(2)}) collective-permute-start(bf16[128,1024]{1,0:T(8,128)(2,1)S(1)} %sink.4.refs_11_.refs_3_), channel_id=1, source_target_pairs={{2,0},{3,1},{4,2},{5,3},{6,4},{7,5},{10,8},{11,9},{12,10},{13,11},... | collective-permute-start | bytes 786440 | tf_op jit(solution)/shard_map/ppermute | solution.py:207
  31.5 2.3 %attend.3 = (bf16[128,1024]{1,0:T(8,128)(2,1)S(1)}, bf16[128,1024]{1,0:T(8,128)(2,1)S(1)}, f32[128,1024]{1,0:T(8,128)S(1)}, f32[128,1024]{1,0:T(8,128)S(1)}, f32...) custom-call(s32[1,1024]{1,0:T(1,128)S(1)} %get-tuple-element.44.refs, ...), custom_call_target="tpu_custom_call" | custom-call | bytes 1 | tf_op jit(solution)/shard_map/attend/pallas_call | solution.py:38
  34.8 0.6 %collective-permute-done.14.refs_1_ = f32[2,256]{1,0:T(2,128)S(1)} collective-permute-done((f32[2,256]{1,0:T(2,128)S(1)}, f32[2,256]{1,0:T(2,128)S(1)}, u32[]{:S(2)}, u32[]{:S(2)}) %collective-permute-start.14) | collective-permute-done | bytes 2080 | tf_op jit(solution)/shard_map/ppermute | solution.py:207
  35.8 1.3 %collective-permute-start.15 = (bf16[128,1024]{1,0:T(8,128)(2,1)S(1)}, bf16[128,1024]{1,0:T(8,128)(2,1)S(1)}, u32[]{:S(2)}, u32[]{:S(2)}) collective-permute-start(bf16[128,1024]{1,0:T(8,128)(2,1)S(1)} %sink.5.refs_5_), channel_id=1, source_target_pairs={{2,0},{3,1},{4,2},{5,3},{6,4},{7,5},{10,8},{11,9},{12,10},{13,11},... | collective-permute-start | bytes 786440 | tf_op jit(solution)/shard_map/ppermute | solution.py:207
  37.1 4.1 %collective-permute-done.17.refs_1_ = bf16[128,1024]{1,0:T(8,128)(2,1)S(1)} collective-permute-done((bf16[128,1024]{1,0:T(8,128)(2,1)S(1)}, bf16[128,1024]{1,0:T(8,128)(2,1)S(1)}, u32[]{:S(2)}, u32[]{:S(2)}) %collective-permute-start.17) | collective-permute-done | bytes 262176 | tf_op jit(solution)/shard_map/ppermute | solution.py:207
  41.2 1.7 %collective-permute-start.21 = (f32[2,256]{1,0:T(2,128)S(1)}, f32[2,256]{1,0:T(2,128)S(1)}, u32[]{:S(2)}, u32[]{:S(2)}) collective-permute-start(f32[2,256]{1,0:T(2,128)S(1)} %add.7.refs_0_), channel_id=1, source_target_pairs={{0,2},{1,3},{2,0},{3,1},{4,6},{5,7},{6,4},{7,5},{8,10},{9,11},{10,... | collective-permute-start | bytes 6152 | tf_op jit(solution)/shard_map/ppermute | solution.py:207
  42.9 1.4 %collective-permute-start.22 = (f32[2,256]{1,0:T(2,128)S(1)}, f32[2,256]{1,0:T(2,128)S(1)}, u32[]{:S(2)}, u32[]{:S(2)}) collective-permute-start(f32[2,256]{1,0:T(2,128)S(1)} %add.7.refs_0_), channel_id=1, source_target_pairs={{0,4},{1,5},{2,6},{3,7},{4,0},{5,1},{6,2},{7,3},{8,12},{9,13},{10,... | collective-permute-start | bytes 6152 | tf_op jit(solution)/shard_map/ppermute | solution.py:207
  44.4 1.2 %collective-permute-start.23 = (f32[2,256]{1,0:T(2,128)S(1)}, f32[2,256]{1,0:T(2,128)S(1)}, u32[]{:S(2)}, u32[]{:S(2)}) collective-permute-start(f32[2,256]{1,0:T(2,128)S(1)} %add.7.refs_0_), channel_id=1, source_target_pairs={{0,6},{1,7},{2,4},{3,5},{4,2},{5,3},{6,0},{7,1},{8,14},{9,15},{10,... | collective-permute-start | bytes 6152 | tf_op jit(solution)/shard_map/ppermute | solution.py:207
  45.7 1.3 %collective-permute-start.20 = (bf16[128,1024]{1,0:T(8,128)(2,1)S(1)}, bf16[128,1024]{1,0:T(8,128)(2,1)S(1)}, u32[]{:S(2)}, u32[]{:S(2)}) collective-permute-start(bf16[128,1024]{1,0:T(8,128)(2,1)S(1)} %sink.6.refs_5_), channel_id=1, source_target_pairs={{2,0},{3,1},{4,2},{5,3},{6,4},{7,5},{10,8},{11,9},{12,10},{13,11},... | collective-permute-start | bytes 786440 | tf_op jit(solution)/shard_map/ppermute | solution.py:207
  47.0 0.6 collective-permute-done.15.refs_1_.refs_4_
  47.7 1.3 %collective-permute-start.19 = (bf16[128,1024]{1,0:T(8,128)(2,1)S(1)}, bf16[128,1024]{1,0:T(8,128)(2,1)S(1)}, u32[]{:S(2)}, u32[]{:S(2)}) collective-permute-start(bf16[128,1024]{1,0:T(8,128)(2,1)S(1)} %sink.7.refs_4_), channel_id=1, source_target_pairs={{2,0},{3,1},{4,2},{5,3},{6,4},{7,5},{10,8},{11,9},{12,10},{13,11},... | collective-permute-start | bytes 786440 | tf_op jit(solution)/shard_map/ppermute | solution.py:207
  49.1 1.5 %collective-permute-done.23.refs_3_ = f32[2,256]{1,0:T(2,128)S(1)} collective-permute-done((f32[2,256]{1,0:T(2,128)S(1)}, f32[2,256]{1,0:T(2,128)S(1)}, u32[]{:S(2)}, u32[]{:S(2)}) %collective-permute-start.23) | collective-permute-done | bytes 2080 | tf_op jit(solution)/shard_map/ppermute | solution.py:207
  50.6 1.5 %collective-permute-start.24 = (f32[2,256]{1,0:T(2,128)S(1)}, f32[2,256]{1,0:T(2,128)S(1)}, u32[]{:S(2)}, u32[]{:S(2)}) collective-permute-start(f32[2,256]{1,0:T(2,128)S(1)} %add.8.refs_0_), channel_id=1, source_target_pairs={{0,8},{8,0},{16,24},{24,16},{1,9},{9,1},{17,25},{25,17},{2,10},{10... | collective-permute-start | bytes 6152 | tf_op jit(solution)/shard_map/ppermute | solution.py:207
  52.1 2.1 %collective-permute-done.24.refs_1_ = f32[2,256]{1,0:T(2,128)S(1)} collective-permute-done((f32[2,256]{1,0:T(2,128)S(1)}, f32[2,256]{1,0:T(2,128)S(1)}, u32[]{:S(2)}, u32[]{:S(2)}) %collective-permute-start.24) | collective-permute-done | bytes 2080 | tf_op jit(solution)/shard_map/ppermute | solution.py:207
  54.2 1.5 %collective-permute-start.25 = (f32[2,256]{1,0:T(2,128)S(1)}, f32[2,256]{1,0:T(2,128)S(1)}, u32[]{:S(2)}, u32[]{:S(2)}) collective-permute-start(f32[2,256]{1,0:T(2,128)S(1)} %add.9.refs_0_), channel_id=1, source_target_pairs={{0,16},{8,24},{16,0},{24,8},{1,17},{9,25},{17,1},{25,9},{2,18},{10... | collective-permute-start | bytes 6152 | tf_op jit(solution)/shard_map/ppermute | solution.py:207
  55.7 1.0 %assemble.1 = (bf16[1,128,2048]{2,1,0:T(8,128)(2,1)}, bf16[1,128,2048]{2,1,0:T(8,128)(2,1)}) custom-call(bf16[128,1024]{1,0:T(8,128)(2,1)S(1)} %get-tuple-element.53.refs_0_, bf16[128,1024]{1,0:T(8,128)(2,1)S(1)} %get-tuple-element.61.refs_1_, bf16[128,1024]{1,0:T(8,128)(2,1)S(1)} %get-tuple-element.62.refs_2_, ...), custom_call_target="tpu_custom_call" | custom-call | bytes 1 | tf_op jit(solution)/shard_map/assemble/pallas_call | solution.py:38
  56.7 1.0 %collective-permute-done.25.refs_1_ = f32[2,256]{1,0:T(2,128)S(1)} collective-permute-done((f32[2,256]{1,0:T(2,128)S(1)}, f32[2,256]{1,0:T(2,128)S(1)}, u32[]{:S(2)}, u32[]{:S(2)}) %collective-permute-start.25) | collective-permute-done | bytes 2080 | tf_op jit(solution)/shard_map/ppermute | solution.py:207
  57.8 0.6 scale.1
  58.3 0.9 %finish.2 = (bf16[1,128,1024]{2,1,0:T(8,128)(2,1)}, bf16[1,128,1024]{2,1,0:T(8,128)(2,1)}) custom-call(bf16[1,128,1024]{2,1,0:T(8,128)(2,1)S(1)} %copy-done.2, f32[1,256]{1,0:T(1,128)S(1)} %get-tuple-element.52.refs_10_.refs_1_, f32[128,1024]{1,0:T(8,128)S(1)} %get-tuple-element.75.refs_2_, bf16[128,1024]{1,0:T(8,128)(2,1)S(1)} %collective-permute-done.18.refs_4_.refs_3_, ...), custom_call_target="tpu_custom_call" | custom-call | flops 2147483648 | bytes 1 | tf_op jit(solution)/shard_map/finish/pallas_call | solution.py:38
  59.3 1.1 %collective-permute-done.19.refs_4_ = bf16[128,1024]{1,0:T(8,128)(2,1)S(1)} collective-permute-done((bf16[128,1024]{1,0:T(8,128)(2,1)S(1)}, bf16[128,1024]{1,0:T(8,128)(2,1)S(1)}, u32[]{:S(2)}, u32[]{:S(2)}) %collective-permute-start.19) | collective-permute-done | bytes 262176 | tf_op jit(solution)/shard_map/ppermute | solution.py:207
  60.3 0.9 %finish.3 = (bf16[1,128,1024]{2,1,0:T(8,128)(2,1)}, bf16[1,128,1024]{2,1,0:T(8,128)(2,1)}) custom-call(bf16[1,128,1024]{2,1,0:T(8,128)(2,1)S(1)} %copy-done.2, f32[1,256]{1,0:T(1,128)S(1)} %get-tuple-element.52.refs_10_.refs_1_, f32[128,1024]{1,0:T(8,128)S(1)} %get-tuple-element.74.refs_2_, ...), custom_call_target="tpu_custom_call", output_to_operand_aliasing={{0}: (5, {}), {1}: (6, {})} | custom-call | flops 4294967296 | bytes 1 | tf_op jit(solution)/shard_map/finish/pallas_call | solution.py:38
  (47 shorter events, 4.5 us)
Async XLA Ops:
  1.6 11.6 %collective-permute-start = (bf16[128,1024]{1,0:T(8,128)(2,1)S(1)}, bf16[128,1024]{1,0:T(8,128)(2,1)S(1)}, u32[]{:S(2)}, u32[]{:S(2)}) collective-permute-start(bf16[128,1024]{1,0:T(8,128)(2,1)S(1)} %payload.2.refs_5_.refs_1_.refs_3_), channel_id=1, source_target_pairs={{0,2},{1,3},{2,4},{3,5},{4,6},{5,7},{8,10},{9,11},{10,12},{11,13},... | collective-permute-start | bytes 786440 | tf_op jit(solution)/shard_map/ppermute | solution.py:207
  7.6 11.3 %collective-permute-start.3 = (bf16[128,1024]{1,0:T(8,128)(2,1)S(1)}, bf16[128,1024]{1,0:T(8,128)(2,1)S(1)}, u32[]{:S(2)}, u32[]{:S(2)}) collective-permute-start(bf16[128,1024]{1,0:T(8,128)(2,1)S(1)} %get-tuple-element.47.refs_1_.refs_3_), channel_id=1, source_target_pairs={{0,2},{1,3},{2,4},{3,5},{4,6},{5,7},{8,10},{9,11},{10,12},{11,13},... | collective-permute-start | bytes 786440 | tf_op jit(solution)/shard_map/ppermute | solution.py:207
  13.3 11.2 %collective-permute-start.2 = (bf16[128,1024]{1,0:T(8,128)(2,1)S(1)}, bf16[128,1024]{1,0:T(8,128)(2,1)S(1)}, u32[]{:S(2)}, u32[]{:S(2)}) collective-permute-start(bf16[128,1024]{1,0:T(8,128)(2,1)S(1)} %get-tuple-element.46.refs_2_), channel_id=1, source_target_pairs={{0,2},{1,3},{2,4},{3,5},{4,6},{5,7},{8,10},{9,11},{10,12},{11,13},... | collective-permute-start | bytes 786440 | tf_op jit(solution)/shard_map/ppermute | solution.py:207
  17.7 7.5 %collective-permute-start.1 = (bf16[128,1024]{1,0:T(8,128)(2,1)S(1)}, bf16[128,1024]{1,0:T(8,128)(2,1)S(1)}, u32[]{:S(2)}, u32[]{:S(2)}) collective-permute-start(bf16[128,1024]{1,0:T(8,128)(2,1)S(1)} %get-tuple-element.45), channel_id=1, source_target_pairs={{0,1},{1,0},{2,3},{3,2},{4,5},{5,4},{6,7},{7,6},{8,9},{9,8},{10,11... | collective-permute-start | bytes 786440 | tf_op jit(solution)/shard_map/ppermute | solution.py:207
  18.9 7.2 %copy-start = (bf16[1,128,2048]{2,1,0:T(8,128)(2,1)S(1)}, bf16[1,128,2048]{2,1,0:T(8,128)(2,1)}, u32[]{:S(2)}) copy-start(bf16[1,128,2048]{2,1,0:T(8,128)(2,1)} %refs_1_.7) | copy-start | bytes 1572868
  18.9 7.2 %copy-start.1 = (bf16[1,128,2048]{2,1,0:T(8,128)(2,1)S(1)}, bf16[1,128,2048]{2,1,0:T(8,128)(2,1)}, u32[]{:S(2)}) copy-start(bf16[1,128,2048]{2,1,0:T(8,128)(2,1)} %refs_2_.5) | copy-start | bytes 1572868
  18.9 10.0 %collective-permute-start.7 = (bf16[128,1024]{1,0:T(8,128)(2,1)S(1)}, bf16[128,1024]{1,0:T(8,128)(2,1)S(1)}, u32[]{:S(2)}, u32[]{:S(2)}) collective-permute-start(bf16[128,1024]{1,0:T(8,128)(2,1)S(1)} %get-tuple-element.48.refs_2_), channel_id=1, source_target_pairs={{0,2},{1,3},{2,4},{3,5},{4,6},{5,7},{8,10},{9,11},{10,12},{11,13},... | collective-permute-start | bytes 786440 | tf_op jit(solution)/shard_map/ppermute | solution.py:207
  24.5 1.4 %collective-permute-start.4 = (bf16[128,512]{1,0:T(8,128)(2,1)S(1)}, bf16[128,512]{1,0:T(8,128)(2,1)S(1)}, u32[]{:S(2)}, u32[]{:S(2)}) collective-permute-start(bf16[128,512]{1,0:T(8,128)(2,1)S(1)} %get-tuple-element.49.refs_2_), channel_id=1, source_target_pairs={{0,1},{1,0},{2,3},{3,2},{4,5},{5,4},{6,7},{7,6},{8,9},{9,8},{10,11... | collective-permute-start | bytes 393224 | tf_op jit(solution)/shard_map/ppermute | solution.py:207
  24.6 1.5 %collective-permute-start.5 = (bf16[128,512]{1,0:T(8,128)(2,1)S(1)}, bf16[128,512]{1,0:T(8,128)(2,1)S(1)}, u32[]{:S(2)}, u32[]{:S(2)}) collective-permute-start(bf16[128,512]{1,0:T(8,128)(2,1)S(1)} %get-tuple-element.50), channel_id=1, source_target_pairs={{0,1},{1,0},{2,3},{3,2},{4,5},{5,4},{6,7},{7,6},{8,9},{9,8},{10,11... | collective-permute-start | bytes 393224 | tf_op jit(solution)/shard_map/ppermute | solution.py:207
  25.1 6.4 %collective-permute-start.6 = (bf16[128,1024]{1,0:T(8,128)(2,1)S(1)}, bf16[128,1024]{1,0:T(8,128)(2,1)S(1)}, u32[]{:S(2)}, u32[]{:S(2)}) collective-permute-start(bf16[128,1024]{1,0:T(8,128)(2,1)S(1)} %get-tuple-element.54), channel_id=1, source_target_pairs={{0,1},{1,0},{2,3},{3,2},{4,5},{5,4},{6,7},{7,6},{8,9},{9,8},{10,11... | collective-permute-start | bytes 786440 | tf_op jit(solution)/shard_map/ppermute | solution.py:207
  28.4 1.4 %collective-permute-start.10 = (bf16[128,512]{1,0:T(8,128)(2,1)S(1)}, bf16[128,512]{1,0:T(8,128)(2,1)S(1)}, u32[]{:S(2)}, u32[]{:S(2)}) collective-permute-start(bf16[128,512]{1,0:T(8,128)(2,1)S(1)} %get-tuple-element.59), channel_id=1, source_target_pairs={{0,1},{1,0},{2,3},{3,2},{4,5},{5,4},{6,7},{7,6},{8,9},{9,8},{10,11... | collective-permute-start | bytes 393224 | tf_op jit(solution)/shard_map/ppermute | solution.py:207
  28.7 1.3 %collective-permute-start.11 = (bf16[128,512]{1,0:T(8,128)(2,1)S(1)}, bf16[128,512]{1,0:T(8,128)(2,1)S(1)}, u32[]{:S(2)}, u32[]{:S(2)}) collective-permute-start(bf16[128,512]{1,0:T(8,128)(2,1)S(1)} %get-tuple-element.60), channel_id=1, source_target_pairs={{0,1},{1,0},{2,3},{3,2},{4,5},{5,4},{6,7},{7,6},{8,9},{9,8},{10,11... | collective-permute-start | bytes 393224 | tf_op jit(solution)/shard_map/ppermute | solution.py:207
  29.0 2.5 %collective-permute-start.8 = (bf16[128,512]{1,0:T(8,128)(2,1)S(1)}, bf16[128,512]{1,0:T(8,128)(2,1)S(1)}, u32[]{:S(2)}, u32[]{:S(2)}) collective-permute-start(bf16[128,512]{1,0:T(8,128)(2,1)S(1)} %get-tuple-element.56), channel_id=1, source_target_pairs={{0,1},{1,0},{2,3},{3,2},{4,5},{5,4},{6,7},{7,6},{8,9},{9,8},{10,11... | collective-permute-start | bytes 393224 | tf_op jit(solution)/shard_map/ppermute | solution.py:207
  29.3 2.1 %collective-permute-start.9 = (bf16[128,512]{1,0:T(8,128)(2,1)S(1)}, bf16[128,512]{1,0:T(8,128)(2,1)S(1)}, u32[]{:S(2)}, u32[]{:S(2)}) collective-permute-start(bf16[128,512]{1,0:T(8,128)(2,1)S(1)} %get-tuple-element.57), channel_id=1, source_target_pairs={{0,1},{1,0},{2,3},{3,2},{4,5},{5,4},{6,7},{7,6},{8,9},{9,8},{10,11... | collective-permute-start | bytes 393224 | tf_op jit(solution)/shard_map/ppermute | solution.py:207
  30.1 11.1 %collective-permute-start.17 = (bf16[128,1024]{1,0:T(8,128)(2,1)S(1)}, bf16[128,1024]{1,0:T(8,128)(2,1)S(1)}, u32[]{:S(2)}, u32[]{:S(2)}) collective-permute-start(bf16[128,1024]{1,0:T(8,128)(2,1)S(1)} %sink.4.refs_11_.refs_3_), channel_id=1, source_target_pairs={{2,0},{3,1},{4,2},{5,3},{6,4},{7,5},{10,8},{11,9},{12,10},{13,11},... | collective-permute-start | bytes 786440 | tf_op jit(solution)/shard_map/ppermute | solution.py:207
  33.7 1.9 %collective-permute-start.12 = (bf16[128,512]{1,0:T(8,128)(2,1)S(1)}, bf16[128,512]{1,0:T(8,128)(2,1)S(1)}, u32[]{:S(2)}, u32[]{:S(2)}) collective-permute-start(bf16[128,512]{1,0:T(8,128)(2,1)S(1)} %get-tuple-element.66), channel_id=1, source_target_pairs={{0,1},{1,0},{2,3},{3,2},{4,5},{5,4},{6,7},{7,6},{8,9},{9,8},{10,11... | collective-permute-start | bytes 393224 | tf_op jit(solution)/shard_map/ppermute | solution.py:207
  34.0 1.7 %collective-permute-start.13 = (bf16[128,512]{1,0:T(8,128)(2,1)S(1)}, bf16[128,512]{1,0:T(8,128)(2,1)S(1)}, u32[]{:S(2)}, u32[]{:S(2)}) collective-permute-start(bf16[128,512]{1,0:T(8,128)(2,1)S(1)} %get-tuple-element.67), channel_id=1, source_target_pairs={{0,1},{1,0},{2,3},{3,2},{4,5},{5,4},{6,7},{7,6},{8,9},{9,8},{10,11... | collective-permute-start | bytes 393224 | tf_op jit(solution)/shard_map/ppermute | solution.py:207
  34.3 1.2 %collective-permute-start.14 = (f32[2,256]{1,0:T(2,128)S(1)}, f32[2,256]{1,0:T(2,128)S(1)}, u32[]{:S(2)}, u32[]{:S(2)}) collective-permute-start(f32[2,256]{1,0:T(2,128)S(1)} %add.5.refs_0_), channel_id=1, source_target_pairs={{0,1},{1,0},{2,3},{3,2},{4,5},{5,4},{6,7},{7,6},{8,9},{9,8},{10,11... | collective-permute-start | bytes 6152 | tf_op jit(solution)/shard_map/ppermute | solution.py:207
  34.5 9.9 %collective-permute-start.18 = (bf16[128,1024]{1,0:T(8,128)(2,1)S(1)}, bf16[128,1024]{1,0:T(8,128)(2,1)S(1)}, u32[]{:S(2)}, u32[]{:S(2)}) collective-permute-start(bf16[128,1024]{1,0:T(8,128)(2,1)S(1)} %get-tuple-element.71), channel_id=1, source_target_pairs={{0,1},{1,0},{2,3},{3,2},{4,5},{5,4},{6,7},{7,6},{8,9},{9,8},{10,11... | collective-permute-start | bytes 786440 | tf_op jit(solution)/shard_map/ppermute | solution.py:207
  35.5 10.2 %collective-permute-start.16 = (bf16[128,1024]{1,0:T(8,128)(2,1)S(1)}, bf16[128,1024]{1,0:T(8,128)(2,1)S(1)}, u32[]{:S(2)}, u32[]{:S(2)}) collective-permute-start(bf16[128,1024]{1,0:T(8,128)(2,1)S(1)} %get-tuple-element.69), channel_id=1, source_target_pairs={{0,1},{1,0},{2,3},{3,2},{4,5},{5,4},{6,7},{7,6},{8,9},{9,8},{10,11... | collective-permute-start | bytes 786440 | tf_op jit(solution)/shard_map/ppermute | solution.py:207
  35.8 11.8 %collective-permute-start.15 = (bf16[128,1024]{1,0:T(8,128)(2,1)S(1)}, bf16[128,1024]{1,0:T(8,128)(2,1)S(1)}, u32[]{:S(2)}, u32[]{:S(2)}) collective-permute-start(bf16[128,1024]{1,0:T(8,128)(2,1)S(1)} %sink.5.refs_5_), channel_id=1, source_target_pairs={{2,0},{3,1},{4,2},{5,3},{6,4},{7,5},{10,8},{11,9},{12,10},{13,11},... | collective-permute-start | bytes 786440 | tf_op jit(solution)/shard_map/ppermute | solution.py:207
  41.2 7.8 %collective-permute-start.21 = (f32[2,256]{1,0:T(2,128)S(1)}, f32[2,256]{1,0:T(2,128)S(1)}, u32[]{:S(2)}, u32[]{:S(2)}) collective-permute-start(f32[2,256]{1,0:T(2,128)S(1)} %add.7.refs_0_), channel_id=1, source_target_pairs={{0,2},{1,3},{2,0},{3,1},{4,6},{5,7},{6,4},{7,5},{8,10},{9,11},{10,... | collective-permute-start | bytes 6152 | tf_op jit(solution)/shard_map/ppermute | solution.py:207
  42.9 6.2 %collective-permute-start.22 = (f32[2,256]{1,0:T(2,128)S(1)}, f32[2,256]{1,0:T(2,128)S(1)}, u32[]{:S(2)}, u32[]{:S(2)}) collective-permute-start(f32[2,256]{1,0:T(2,128)S(1)} %add.7.refs_0_), channel_id=1, source_target_pairs={{0,4},{1,5},{2,6},{3,7},{4,0},{5,1},{6,2},{7,3},{8,12},{9,13},{10,... | collective-permute-start | bytes 6152 | tf_op jit(solution)/shard_map/ppermute | solution.py:207
  44.4 6.2 %collective-permute-start.23 = (f32[2,256]{1,0:T(2,128)S(1)}, f32[2,256]{1,0:T(2,128)S(1)}, u32[]{:S(2)}, u32[]{:S(2)}) collective-permute-start(f32[2,256]{1,0:T(2,128)S(1)} %add.7.refs_0_), channel_id=1, source_target_pairs={{0,6},{1,7},{2,4},{3,5},{4,2},{5,3},{6,0},{7,1},{8,14},{9,15},{10,... | collective-permute-start | bytes 6152 | tf_op jit(solution)/shard_map/ppermute | solution.py:207
  45.7 12.6 %collective-permute-start.20 = (bf16[128,1024]{1,0:T(8,128)(2,1)S(1)}, bf16[128,1024]{1,0:T(8,128)(2,1)S(1)}, u32[]{:S(2)}, u32[]{:S(2)}) collective-permute-start(bf16[128,1024]{1,0:T(8,128)(2,1)S(1)} %sink.6.refs_5_), channel_id=1, source_target_pairs={{2,0},{3,1},{4,2},{5,3},{6,4},{7,5},{10,8},{11,9},{12,10},{13,11},... | collective-permute-start | bytes 786440 | tf_op jit(solution)/shard_map/ppermute | solution.py:207
  47.7 12.6 %collective-permute-start.19 = (bf16[128,1024]{1,0:T(8,128)(2,1)S(1)}, bf16[128,1024]{1,0:T(8,128)(2,1)S(1)}, u32[]{:S(2)}, u32[]{:S(2)}) collective-permute-start(bf16[128,1024]{1,0:T(8,128)(2,1)S(1)} %sink.7.refs_4_), channel_id=1, source_target_pairs={{2,0},{3,1},{4,2},{5,3},{6,4},{7,5},{10,8},{11,9},{12,10},{13,11},... | collective-permute-start | bytes 786440 | tf_op jit(solution)/shard_map/ppermute | solution.py:207
  50.6 3.6 %collective-permute-start.24 = (f32[2,256]{1,0:T(2,128)S(1)}, f32[2,256]{1,0:T(2,128)S(1)}, u32[]{:S(2)}, u32[]{:S(2)}) collective-permute-start(f32[2,256]{1,0:T(2,128)S(1)} %add.8.refs_0_), channel_id=1, source_target_pairs={{0,8},{8,0},{16,24},{24,16},{1,9},{9,1},{17,25},{25,17},{2,10},{10... | collective-permute-start | bytes 6152 | tf_op jit(solution)/shard_map/ppermute | solution.py:207
  54.2 3.6 %collective-permute-start.25 = (f32[2,256]{1,0:T(2,128)S(1)}, f32[2,256]{1,0:T(2,128)S(1)}, u32[]{:S(2)}, u32[]{:S(2)}) collective-permute-start(f32[2,256]{1,0:T(2,128)S(1)} %add.9.refs_0_), channel_id=1, source_target_pairs={{0,16},{8,24},{16,0},{24,8},{1,17},{9,25},{17,1},{25,9},{2,18},{10... | collective-permute-start | bytes 6152 | tf_op jit(solution)/shard_map/ppermute | solution.py:207
  55.7 2.6 %copy-start.2 = (bf16[1,128,1024]{2,1,0:T(8,128)(2,1)S(1)}, bf16[1,128,1024]{2,1,0:T(8,128)(2,1)}, u32[]{:S(2)}) copy-start(bf16[1,128,1024]{2,1,0:T(8,128)(2,1)} %refs_0_.7) | copy-start | bytes 786436

commit v10 on v9

--- a/solution.py
+++ b/solution.py
@@ -21,7 +21,7 @@
 
 PIECES = 4
 
-COSTS = 2**32, 0, 0, 2**31, 2**32, 2**32
+COSTS = 2**32, 0, 0, 2**31, 2**32, 2**31
 
 VMEM = pl.BlockSpec(memory_space=pltpu.VMEM)
 ANY = pl.BlockSpec(memory_space=pl.ANY)
@@ -376,13 +376,15 @@
             last = [*last, total]
         last = [sink(chunk, last)]
 
+    first_sink = last
     for step in range(amount, amount + LAG):
-        last = [sink(step, last)]
+        hold = call(add, "hold", dict(total=total), dict(o=shape(2, HEAD_DIM, F32)), [sunk[step - LAG]], cost=COSTS[5])
+        last = [sink(step, [*last, *(hold if step == amount else [])])]
 
     factor = (lax.axis_size("dp") * queries.shape[0] * lax.axis_size("ctx") * rows) ** (-0.5)
     row = shape(1, HEAD_DIM, F32)
     chips = lax.axis_size("ctx") // 2
-    (total,) = call(add, "add", dict(total=total), dict(o=shape(2, HEAD_DIM, F32)), [sunk[0]], cost=COSTS[5])
+    (total,) = call(add, "add", dict(total=total), dict(o=shape(2, HEAD_DIM, F32)), first_sink)
     while chips > 4:
         total = total_over(total, "ctx", chips, 2 * chips, 2)
         chips //= 2

time: 61.7 us -> 61.2 us (level)
  waiting for transfers between devices: 16.8 us -> 13.4 us
  starting transfers between devices: 33.1 us -> 36 us
    ppermute x26, waiting for transfers between devices: 16.8 us -> 13.4 us  [move(): lax.ppermute(field, axis, [(i, target(i)) for i in range(size) if 0 <= ta...]
    ppermute x26, starting transfers between devices: 33.1 us -> 36 us  [move(): lax.ppermute(field, axis, [(i, target(i)) for i in range(size) if 0 <= ta...]
    pallas_call x21 -> x22, Pallas kernels: 10.4 us -> 10.4 us  [call(): pl.pallas_call(kernel, out_shape=list(outs.values()), in_specs=specs, out...]
  transfers between devices with their start and end apart: 26 -> 26, of which waited for: 15 -> 13; matrix products, arithmetic and copies ran while one was open for 0% -> 0% of each run, Pallas kernels for 14% -> 14%
where the time goes in v10:
time: 61.2 us; the launch traced here: 60.7 us
  starting transfers between devices  36 us (59%)
  waiting for transfers between devices  13.4 us (22%)
  Pallas kernels  10.4 us (17%)
  between operations  0.85 us (1%)
    ppermute x26, starting transfers between devices, move(): lax.ppermute(field, axis, [(i, target(i)) for i in range(size) if 0 <= ta...  36 us
    ppermute x26, waiting for transfers between devices, move(): lax.ppermute(field, axis, [(i, target(i)) for i in range(size) if 0 <= ta...  13.4 us
    pallas_call x22, Pallas kernels, call(): pl.pallas_call(kernel, out_shape=list(outs.values()), in_specs=specs, out...  10.4 us
  transfers between devices with their start and end apart: 26, of which 13 were waited for; matrix products, arithmetic and copies ran while one was open for 0% of the time, Pallas kernels for 14%

profile of v10, /device:TPU:0, one launch (start us, length us, event | category | flops | bytes accessed | tf_op | source)
XLA Modules:
  0.0 60.7 jit_solution(7296796615321728500)
XLA Ops:
  0.6 0.9 %payload.2.refs_5_.refs_1_.refs_3_ = bf16[128,1024]{1,0:T(8,128)(2,1)S(1)} custom-call(bf16[1,128,1024]{2,1,0:T(8,128)(2,1)} %refs_0_.7, bf16[1,128,1024]{2,1,0:T(8,128)(2,1)} %refs_1_.5), custom_call_target="tpu_custom_call" | custom-call | bytes 1 | tf_op jit(solution)/shard_map/payload/pallas_call | solution.py:38
  1.6 4.9 %collective-permute-start = (bf16[128,1024]{1,0:T(8,128)(2,1)S(1)}, bf16[128,1024]{1,0:T(8,128)(2,1)S(1)}, u32[]{:S(2)}, u32[]{:S(2)}) collective-permute-start(bf16[128,1024]{1,0:T(8,128)(2,1)S(1)} %payload.2.refs_5_.refs_1_.refs_3_), channel_id=1, source_target_pairs={{0,2},{1,3},{2,4},{3,5},{4,6},{5,7},{8,10},{9,11},{10,12},{11,13},... | collective-permute-start | bytes 786440 | tf_op jit(solution)/shard_map/ppermute | solution.py:207
  6.5 1.0 %payload.3 = (bf16[128,1024]{1,0:T(8,128)(2,1)S(1)}, s32[1,1024]{1,0:T(1,128)S(1)}, f32[1,256]{1,0:T(1,128)S(1)}, f32[1,256]{1,0:T(1,128)S(1)}) custom-call(bf16[1,128,1024]{2,1,0:T(8,128)(2,1)} %refs_0_.7, bf16[1,128,1024]{2,1,0:T(8,128)(2,1)} %refs_1_.5, s32[1,1024]{1,0:T(1,128)} %refs_2_.3, f32[1,256]{1,0:T(1,128)} %bitcast.4, f32[1,256]{1,0:T(1,128)} %bitcast.5, ...), custom_call_target="tpu_custom_call" | custom-call | bytes 1 | tf_op jit(solution)/shard_map/payload/pallas_call | solution.py:38
  7.6 3.5 %collective-permute-start.3 = (bf16[128,1024]{1,0:T(8,128)(2,1)S(1)}, bf16[128,1024]{1,0:T(8,128)(2,1)S(1)}, u32[]{:S(2)}, u32[]{:S(2)}) collective-permute-start(bf16[128,1024]{1,0:T(8,128)(2,1)S(1)} %get-tuple-element.47.refs_1_.refs_3_), channel_id=1, source_target_pairs={{0,2},{1,3},{2,4},{3,5},{4,6},{5,7},{8,10},{9,11},{10,12},{11,13},... | collective-permute-start | bytes 786440 | tf_op jit(solution)/shard_map/ppermute | solution.py:207
  11.1 2.2 %collective-permute-done.refs_0_.refs_5_ = bf16[128,1024]{1,0:T(8,128)(2,1)S(1)} collective-permute-done((bf16[128,1024]{1,0:T(8,128)(2,1)S(1)}, bf16[128,1024]{1,0:T(8,128)(2,1)S(1)}, u32[]{:S(2)}, u32[]{:S(2)}) %collective-permute-start) | collective-permute-done | bytes 262176 | tf_op jit(solution)/shard_map/ppermute | solution.py:207
  13.3 4.4 %collective-permute-start.2 = (bf16[128,1024]{1,0:T(8,128)(2,1)S(1)}, bf16[128,1024]{1,0:T(8,128)(2,1)S(1)}, u32[]{:S(2)}, u32[]{:S(2)}) collective-permute-start(bf16[128,1024]{1,0:T(8,128)(2,1)S(1)} %get-tuple-element.46.refs_2_), channel_id=1, source_target_pairs={{0,2},{1,3},{2,4},{3,5},{4,6},{5,7},{8,10},{9,11},{10,12},{11,13},... | collective-permute-start | bytes 786440 | tf_op jit(solution)/shard_map/ppermute | solution.py:207
  17.7 1.1 %collective-permute-done.3.refs_0_.refs_5_ = bf16[128,1024]{1,0:T(8,128)(2,1)S(1)} collective-permute-done((bf16[128,1024]{1,0:T(8,128)(2,1)S(1)}, bf16[128,1024]{1,0:T(8,128)(2,1)S(1)}, u32[]{:S(2)}, u32[]{:S(2)}) %collective-permute-start.3) | collective-permute-done | bytes 262176 | tf_op jit(solution)/shard_map/ppermute | solution.py:207
  18.9 4.5 %collective-permute-start.7 = (bf16[128,1024]{1,0:T(8,128)(2,1)S(1)}, bf16[128,1024]{1,0:T(8,128)(2,1)S(1)}, u32[]{:S(2)}, u32[]{:S(2)}) collective-permute-start(bf16[128,1024]{1,0:T(8,128)(2,1)S(1)} %get-tuple-element.48.refs_2_), channel_id=1, source_target_pairs={{0,2},{1,3},{2,4},{3,5},{4,6},{5,7},{8,10},{9,11},{10,12},{11,13},... | collective-permute-start | bytes 786440 | tf_op jit(solution)/shard_map/ppermute | solution.py:207
  23.4 1.0 %collective-permute-done.2.refs_1_.refs_6_ = bf16[128,1024]{1,0:T(8,128)(2,1)S(1)} collective-permute-done((bf16[128,1024]{1,0:T(8,128)(2,1)S(1)}, bf16[128,1024]{1,0:T(8,128)(2,1)S(1)}, u32[]{:S(2)}, u32[]{:S(2)}) %collective-permute-start.2) | collective-permute-done | bytes 262176 | tf_op jit(solution)/shard_map/ppermute | solution.py:207
  24.6 0.5 collective-permute-start.5
  25.1 0.8 %collective-permute-done.4.refs_7_ = bf16[128,512]{1,0:T(8,128)(2,1)S(1)} collective-permute-done((bf16[128,512]{1,0:T(8,128)(2,1)S(1)}, bf16[128,512]{1,0:T(8,128)(2,1)S(1)}, u32[]{:S(2)}, u32[]{:S(2)}) %collective-permute-start.4) | collective-permute-done | bytes 131104 | tf_op jit(solution)/shard_map/ppermute | solution.py:207
  26.1 2.3 %attend.2 = (bf16[128,1024]{1,0:T(8,128)(2,1)S(1)}, bf16[128,1024]{1,0:T(8,128)(2,1)S(1)}, f32[128,1024]{1,0:T(8,128)S(1)}, f32[128,1024]{1,0:T(8,128)S(1)}, f32...) custom-call(s32[1,1024]{1,0:T(1,128)S(1)} %get-tuple-element.44.refs, ...), custom_call_target="tpu_custom_call" | custom-call | bytes 1 | tf_op jit(solution)/shard_map/attend/pallas_call | solution.py:38
  28.4 0.4 collective-permute-start.10
  29.0 0.4 collective-permute-start.8
  30.2 1.3 %collective-permute-start.17 = (bf16[128,1024]{1,0:T(8,128)(2,1)S(1)}, bf16[128,1024]{1,0:T(8,128)(2,1)S(1)}, u32[]{:S(2)}, u32[]{:S(2)}) collective-permute-start(bf16[128,1024]{1,0:T(8,128)(2,1)S(1)} %sink.4.refs_11_.refs_3_), channel_id=1, source_target_pairs={{2,0},{3,1},{4,2},{5,3},{6,4},{7,5},{10,8},{11,9},{12,10},{13,11},... | collective-permute-start | bytes 786440 | tf_op jit(solution)/shard_map/ppermute | solution.py:207
  31.5 2.2 %attend.3 = (bf16[128,1024]{1,0:T(8,128)(2,1)S(1)}, bf16[128,1024]{1,0:T(8,128)(2,1)S(1)}, f32[128,1024]{1,0:T(8,128)S(1)}, f32[128,1024]{1,0:T(8,128)S(1)}, f32...) custom-call(s32[1,1024]{1,0:T(1,128)S(1)} %get-tuple-element.44.refs, ...), custom_call_target="tpu_custom_call" | custom-call | bytes 1 | tf_op jit(solution)/shard_map/attend/pallas_call | solution.py:38
  34.5 0.9 %collective-permute-done.14.refs_1_ = f32[2,256]{1,0:T(2,128)S(1)} collective-permute-done((f32[2,256]{1,0:T(2,128)S(1)}, f32[2,256]{1,0:T(2,128)S(1)}, u32[]{:S(2)}, u32[]{:S(2)}) %collective-permute-start.14) | collective-permute-done | bytes 2080 | tf_op jit(solution)/shard_map/ppermute | solution.py:207
  35.8 1.3 %collective-permute-start.15 = (bf16[128,1024]{1,0:T(8,128)(2,1)S(1)}, bf16[128,1024]{1,0:T(8,128)(2,1)S(1)}, u32[]{:S(2)}, u32[]{:S(2)}) collective-permute-start(bf16[128,1024]{1,0:T(8,128)(2,1)S(1)} %sink.5.refs_5_.refs_1_), channel_id=1, source_target_pairs={{2,0},{3,1},{4,2},{5,3},{6,4},{7,5},{10,8},{11,9},{12,10},{13,11},... | collective-permute-start | bytes 786440 | tf_op jit(solution)/shard_map/ppermute | solution.py:207
  37.1 3.8 %collective-permute-start.21 = (f32[2,256]{1,0:T(2,128)S(1)}, f32[2,256]{1,0:T(2,128)S(1)}, u32[]{:S(2)}, u32[]{:S(2)}) collective-permute-start(f32[2,256]{1,0:T(2,128)S(1)} %add.7.refs_0_), channel_id=1, source_target_pairs={{0,2},{1,3},{2,0},{3,1},{4,6},{5,7},{6,4},{7,5},{8,10},{9,11},{10,... | collective-permute-start | bytes 6152 | tf_op jit(solution)/shard_map/ppermute | solution.py:207
  40.9 3.5 %collective-permute-start.22 = (f32[2,256]{1,0:T(2,128)S(1)}, f32[2,256]{1,0:T(2,128)S(1)}, u32[]{:S(2)}, u32[]{:S(2)}) collective-permute-start(f32[2,256]{1,0:T(2,128)S(1)} %add.7.refs_0_), channel_id=1, source_target_pairs={{0,4},{1,5},{2,6},{3,7},{4,0},{5,1},{6,2},{7,3},{8,12},{9,13},{10,... | collective-permute-start | bytes 6152 | tf_op jit(solution)/shard_map/ppermute | solution.py:207
  44.5 1.3 %collective-permute-start.20 = (bf16[128,1024]{1,0:T(8,128)(2,1)S(1)}, bf16[128,1024]{1,0:T(8,128)(2,1)S(1)}, u32[]{:S(2)}, u32[]{:S(2)}) collective-permute-start(bf16[128,1024]{1,0:T(8,128)(2,1)S(1)} %sink.6.refs_5_), channel_id=1, source_target_pairs={{2,0},{3,1},{4,2},{5,3},{6,4},{7,5},{10,8},{11,9},{12,10},{13,11},... | collective-permute-start | bytes 786440 | tf_op jit(solution)/shard_map/ppermute | solution.py:207
  45.8 1.8 %collective-permute-done.15.refs_1_.refs_4_ = bf16[128,1024]{1,0:T(8,128)(2,1)S(1)} collective-permute-done((bf16[128,1024]{1,0:T(8,128)(2,1)S(1)}, bf16[128,1024]{1,0:T(8,128)(2,1)S(1)}, u32[]{:S(2)}, u32[]{:S(2)}) %collective-permute-start.15) | collective-permute-done | bytes 262176 | tf_op jit(solution)/shard_map/ppermute | solution.py:207
  47.7 1.3 %collective-permute-start.19 = (bf16[128,1024]{1,0:T(8,128)(2,1)S(1)}, bf16[128,1024]{1,0:T(8,128)(2,1)S(1)}, u32[]{:S(2)}, u32[]{:S(2)}) collective-permute-start(bf16[128,1024]{1,0:T(8,128)(2,1)S(1)} %sink.7.refs_4_), channel_id=1, source_target_pairs={{2,0},{3,1},{4,2},{5,3},{6,4},{7,5},{10,8},{11,9},{12,10},{13,11},... | collective-permute-start | bytes 786440 | tf_op jit(solution)/shard_map/ppermute | solution.py:207
  49.3 1.6 %collective-permute-done.23.refs_3_ = f32[2,256]{1,0:T(2,128)S(1)} collective-permute-done((f32[2,256]{1,0:T(2,128)S(1)}, f32[2,256]{1,0:T(2,128)S(1)}, u32[]{:S(2)}, u32[]{:S(2)}) %collective-permute-start.23) | collective-permute-done | bytes 2080 | tf_op jit(solution)/shard_map/ppermute | solution.py:207
  50.9 1.5 %collective-permute-start.24 = (f32[2,256]{1,0:T(2,128)S(1)}, f32[2,256]{1,0:T(2,128)S(1)}, u32[]{:S(2)}, u32[]{:S(2)}) collective-permute-start(f32[2,256]{1,0:T(2,128)S(1)} %add.8.refs_0_), channel_id=1, source_target_pairs={{0,8},{8,0},{16,24},{24,16},{1,9},{9,1},{17,25},{25,17},{2,10},{10... | collective-permute-start | bytes 6152 | tf_op jit(solution)/shard_map/ppermute | solution.py:207
  52.4 2.1 %collective-permute-done.24.refs_1_ = f32[2,256]{1,0:T(2,128)S(1)} collective-permute-done((f32[2,256]{1,0:T(2,128)S(1)}, f32[2,256]{1,0:T(2,128)S(1)}, u32[]{:S(2)}, u32[]{:S(2)}) %collective-permute-start.24) | collective-permute-done | bytes 2080 | tf_op jit(solution)/shard_map/ppermute | solution.py:207
  54.5 1.5 %collective-permute-start.25 = (f32[2,256]{1,0:T(2,128)S(1)}, f32[2,256]{1,0:T(2,128)S(1)}, u32[]{:S(2)}, u32[]{:S(2)}) collective-permute-start(f32[2,256]{1,0:T(2,128)S(1)} %add.9.refs_0_), channel_id=1, source_target_pairs={{0,16},{8,24},{16,0},{24,8},{1,17},{9,25},{17,1},{25,9},{2,18},{10... | collective-permute-start | bytes 6152 | tf_op jit(solution)/shard_map/ppermute | solution.py:207
  56.0 1.0 %assemble.1 = (bf16[1,128,2048]{2,1,0:T(8,128)(2,1)}, bf16[1,128,2048]{2,1,0:T(8,128)(2,1)}) custom-call(bf16[128,1024]{1,0:T(8,128)(2,1)S(1)} %get-tuple-element.53.refs_0_, bf16[128,1024]{1,0:T(8,128)(2,1)S(1)} %get-tuple-element.61.refs_1_, bf16[128,1024]{1,0:T(8,128)(2,1)S(1)} %get-tuple-element.62.refs_2_, ...), custom_call_target="tpu_custom_call" | custom-call | bytes 1 | tf_op jit(solution)/shard_map/assemble/pallas_call | solution.py:38
  57.1 1.0 %collective-permute-done.25.refs_1_ = f32[2,256]{1,0:T(2,128)S(1)} collective-permute-done((f32[2,256]{1,0:T(2,128)S(1)}, f32[2,256]{1,0:T(2,128)S(1)}, u32[]{:S(2)}, u32[]{:S(2)}) %collective-permute-start.25) | collective-permute-done | bytes 2080 | tf_op jit(solution)/shard_map/ppermute | solution.py:207
  58.1 0.6 scale.1
  58.7 0.9 %finish.2 = (bf16[1,128,1024]{2,1,0:T(8,128)(2,1)}, bf16[1,128,1024]{2,1,0:T(8,128)(2,1)}) custom-call(bf16[1,128,1024]{2,1,0:T(8,128)(2,1)S(1)} %copy-done.2, f32[1,256]{1,0:T(1,128)S(1)} %get-tuple-element.52.refs_10_.refs_1_, f32[128,1024]{1,0:T(8,128)S(1)} %get-tuple-element.75.refs_2_, bf16[128,1024]{1,0:T(8,128)(2,1)S(1)} %collective-permute-done.18.refs_4_.refs_3_, ...), custom_call_target="tpu_custom_call" | custom-call | flops 2147483648 | bytes 1 | tf_op jit(solution)/shard_map/finish/pallas_call | solution.py:38
  59.8 0.9 %finish.3 = (bf16[1,128,1024]{2,1,0:T(8,128)(2,1)}, bf16[1,128,1024]{2,1,0:T(8,128)(2,1)}) custom-call(bf16[1,128,1024]{2,1,0:T(8,128)(2,1)S(1)} %copy-done.2, f32[1,256]{1,0:T(1,128)S(1)} %get-tuple-element.52.refs_10_.refs_1_, f32[128,1024]{1,0:T(8,128)S(1)} %get-tuple-element.74.refs_2_, ...), custom_call_target="tpu_custom_call", output_to_operand_aliasing={{0}: (5, {}), {1}: (6, {})} | custom-call | flops 4294967296 | bytes 1 | tf_op jit(solution)/shard_map/finish/pallas_call | solution.py:38
  (48 shorter events, 3.5 us)
Async XLA Ops:
  1.6 11.6 %collective-permute-start = (bf16[128,1024]{1,0:T(8,128)(2,1)S(1)}, bf16[128,1024]{1,0:T(8,128)(2,1)S(1)}, u32[]{:S(2)}, u32[]{:S(2)}) collective-permute-start(bf16[128,1024]{1,0:T(8,128)(2,1)S(1)} %payload.2.refs_5_.refs_1_.refs_3_), channel_id=1, source_target_pairs={{0,2},{1,3},{2,4},{3,5},{4,6},{5,7},{8,10},{9,11},{10,12},{11,13},... | collective-permute-start | bytes 786440 | tf_op jit(solution)/shard_map/ppermute | solution.py:207
  7.6 11.3 %collective-permute-start.3 = (bf16[128,1024]{1,0:T(8,128)(2,1)S(1)}, bf16[128,1024]{1,0:T(8,128)(2,1)S(1)}, u32[]{:S(2)}, u32[]{:S(2)}) collective-permute-start(bf16[128,1024]{1,0:T(8,128)(2,1)S(1)} %get-tuple-element.47.refs_1_.refs_3_), channel_id=1, source_target_pairs={{0,2},{1,3},{2,4},{3,5},{4,6},{5,7},{8,10},{9,11},{10,12},{11,13},... | collective-permute-start | bytes 786440 | tf_op jit(solution)/shard_map/ppermute | solution.py:207
  13.3 11.2 %collective-permute-start.2 = (bf16[128,1024]{1,0:T(8,128)(2,1)S(1)}, bf16[128,1024]{1,0:T(8,128)(2,1)S(1)}, u32[]{:S(2)}, u32[]{:S(2)}) collective-permute-start(bf16[128,1024]{1,0:T(8,128)(2,1)S(1)} %get-tuple-element.46.refs_2_), channel_id=1, source_target_pairs={{0,2},{1,3},{2,4},{3,5},{4,6},{5,7},{8,10},{9,11},{10,12},{11,13},... | collective-permute-start | bytes 786440 | tf_op jit(solution)/shard_map/ppermute | solution.py:207
  17.7 7.5 %collective-permute-start.1 = (bf16[128,1024]{1,0:T(8,128)(2,1)S(1)}, bf16[128,1024]{1,0:T(8,128)(2,1)S(1)}, u32[]{:S(2)}, u32[]{:S(2)}) collective-permute-start(bf16[128,1024]{1,0:T(8,128)(2,1)S(1)} %get-tuple-element.45), channel_id=1, source_target_pairs={{0,1},{1,0},{2,3},{3,2},{4,5},{5,4},{6,7},{7,6},{8,9},{9,8},{10,11... | collective-permute-start | bytes 786440 | tf_op jit(solution)/shard_map/ppermute | solution.py:207
  18.9 7.2 %copy-start = (bf16[1,128,2048]{2,1,0:T(8,128)(2,1)S(1)}, bf16[1,128,2048]{2,1,0:T(8,128)(2,1)}, u32[]{:S(2)}) copy-start(bf16[1,128,2048]{2,1,0:T(8,128)(2,1)} %refs_1_.7) | copy-start | bytes 1572868
  18.9 7.2 %copy-start.1 = (bf16[1,128,2048]{2,1,0:T(8,128)(2,1)S(1)}, bf16[1,128,2048]{2,1,0:T(8,128)(2,1)}, u32[]{:S(2)}) copy-start(bf16[1,128,2048]{2,1,0:T(8,128)(2,1)} %refs_2_.5) | copy-start | bytes 1572868
  18.9 10.0 %collective-permute-start.7 = (bf16[128,1024]{1,0:T(8,128)(2,1)S(1)}, bf16[128,1024]{1,0:T(8,128)(2,1)S(1)}, u32[]{:S(2)}, u32[]{:S(2)}) collective-permute-start(bf16[128,1024]{1,0:T(8,128)(2,1)S(1)} %get-tuple-element.48.refs_2_), channel_id=1, source_target_pairs={{0,2},{1,3},{2,4},{3,5},{4,6},{5,7},{8,10},{9,11},{10,12},{11,13},... | collective-permute-start | bytes 786440 | tf_op jit(solution)/shard_map/ppermute | solution.py:207
  24.5 1.4 %collective-permute-start.4 = (bf16[128,512]{1,0:T(8,128)(2,1)S(1)}, bf16[128,512]{1,0:T(8,128)(2,1)S(1)}, u32[]{:S(2)}, u32[]{:S(2)}) collective-permute-start(bf16[128,512]{1,0:T(8,128)(2,1)S(1)} %get-tuple-element.49.refs_2_), channel_id=1, source_target_pairs={{0,1},{1,0},{2,3},{3,2},{4,5},{5,4},{6,7},{7,6},{8,9},{9,8},{10,11... | collective-permute-start | bytes 393224 | tf_op jit(solution)/shard_map/ppermute | solution.py:207
  24.6 1.5 %collective-permute-start.5 = (bf16[128,512]{1,0:T(8,128)(2,1)S(1)}, bf16[128,512]{1,0:T(8,128)(2,1)S(1)}, u32[]{:S(2)}, u32[]{:S(2)}) collective-permute-start(bf16[128,512]{1,0:T(8,128)(2,1)S(1)} %get-tuple-element.50), channel_id=1, source_target_pairs={{0,1},{1,0},{2,3},{3,2},{4,5},{5,4},{6,7},{7,6},{8,9},{9,8},{10,11... | collective-permute-start | bytes 393224 | tf_op jit(solution)/shard_map/ppermute | solution.py:207
  25.1 6.4 %collective-permute-start.6 = (bf16[128,1024]{1,0:T(8,128)(2,1)S(1)}, bf16[128,1024]{1,0:T(8,128)(2,1)S(1)}, u32[]{:S(2)}, u32[]{:S(2)}) collective-permute-start(bf16[128,1024]{1,0:T(8,128)(2,1)S(1)} %get-tuple-element.54), channel_id=1, source_target_pairs={{0,1},{1,0},{2,3},{3,2},{4,5},{5,4},{6,7},{7,6},{8,9},{9,8},{10,11... | collective-permute-start | bytes 786440 | tf_op jit(solution)/shard_map/ppermute | solution.py:207
  28.4 1.4 %collective-permute-start.10 = (bf16[128,512]{1,0:T(8,128)(2,1)S(1)}, bf16[128,512]{1,0:T(8,128)(2,1)S(1)}, u32[]{:S(2)}, u32[]{:S(2)}) collective-permute-start(bf16[128,512]{1,0:T(8,128)(2,1)S(1)} %get-tuple-element.59), channel_id=1, source_target_pairs={{0,1},{1,0},{2,3},{3,2},{4,5},{5,4},{6,7},{7,6},{8,9},{9,8},{10,11... | collective-permute-start | bytes 393224 | tf_op jit(solution)/shard_map/ppermute | solution.py:207
  28.7 1.4 %collective-permute-start.11 = (bf16[128,512]{1,0:T(8,128)(2,1)S(1)}, bf16[128,512]{1,0:T(8,128)(2,1)S(1)}, u32[]{:S(2)}, u32[]{:S(2)}) collective-permute-start(bf16[128,512]{1,0:T(8,128)(2,1)S(1)} %get-tuple-element.60), channel_id=1, source_target_pairs={{0,1},{1,0},{2,3},{3,2},{4,5},{5,4},{6,7},{7,6},{8,9},{9,8},{10,11... | collective-permute-start | bytes 393224 | tf_op jit(solution)/shard_map/ppermute | solution.py:207
  29.0 2.5 %collective-permute-start.8 = (bf16[128,512]{1,0:T(8,128)(2,1)S(1)}, bf16[128,512]{1,0:T(8,128)(2,1)S(1)}, u32[]{:S(2)}, u32[]{:S(2)}) collective-permute-start(bf16[128,512]{1,0:T(8,128)(2,1)S(1)} %get-tuple-element.56), channel_id=1, source_target_pairs={{0,1},{1,0},{2,3},{3,2},{4,5},{5,4},{6,7},{7,6},{8,9},{9,8},{10,11... | collective-permute-start | bytes 393224 | tf_op jit(solution)/shard_map/ppermute | solution.py:207
  29.3 2.1 %collective-permute-start.9 = (bf16[128,512]{1,0:T(8,128)(2,1)S(1)}, bf16[128,512]{1,0:T(8,128)(2,1)S(1)}, u32[]{:S(2)}, u32[]{:S(2)}) collective-permute-start(bf16[128,512]{1,0:T(8,128)(2,1)S(1)} %get-tuple-element.57), channel_id=1, source_target_pairs={{0,1},{1,0},{2,3},{3,2},{4,5},{5,4},{6,7},{7,6},{8,9},{9,8},{10,11... | collective-permute-start | bytes 393224 | tf_op jit(solution)/shard_map/ppermute | solution.py:207
  29.8 11.1 %collective-permute-start.18 = (bf16[128,1024]{1,0:T(8,128)(2,1)S(1)}, bf16[128,1024]{1,0:T(8,128)(2,1)S(1)}, u32[]{:S(2)}, u32[]{:S(2)}) collective-permute-start(bf16[128,1024]{1,0:T(8,128)(2,1)S(1)} %get-tuple-element.71), channel_id=1, source_target_pairs={{0,1},{1,0},{2,3},{3,2},{4,5},{5,4},{6,7},{7,6},{8,9},{9,8},{10,11... | collective-permute-start | bytes 786440 | tf_op jit(solution)/shard_map/ppermute | solution.py:207
  30.2 14.2 %collective-permute-start.17 = (bf16[128,1024]{1,0:T(8,128)(2,1)S(1)}, bf16[128,1024]{1,0:T(8,128)(2,1)S(1)}, u32[]{:S(2)}, u32[]{:S(2)}) collective-permute-start(bf16[128,1024]{1,0:T(8,128)(2,1)S(1)} %sink.4.refs_11_.refs_3_), channel_id=1, source_target_pairs={{2,0},{3,1},{4,2},{5,3},{6,4},{7,5},{10,8},{11,9},{12,10},{13,11},... | collective-permute-start | bytes 786440 | tf_op jit(solution)/shard_map/ppermute | solution.py:207
  33.7 2.0 %collective-permute-start.12 = (bf16[128,512]{1,0:T(8,128)(2,1)S(1)}, bf16[128,512]{1,0:T(8,128)(2,1)S(1)}, u32[]{:S(2)}, u32[]{:S(2)}) collective-permute-start(bf16[128,512]{1,0:T(8,128)(2,1)S(1)} %get-tuple-element.66), channel_id=1, source_target_pairs={{0,1},{1,0},{2,3},{3,2},{4,5},{5,4},{6,7},{7,6},{8,9},{9,8},{10,11... | collective-permute-start | bytes 393224 | tf_op jit(solution)/shard_map/ppermute | solution.py:207
  34.0 1.7 %collective-permute-start.13 = (bf16[128,512]{1,0:T(8,128)(2,1)S(1)}, bf16[128,512]{1,0:T(8,128)(2,1)S(1)}, u32[]{:S(2)}, u32[]{:S(2)}) collective-permute-start(bf16[128,512]{1,0:T(8,128)(2,1)S(1)} %get-tuple-element.67), channel_id=1, source_target_pairs={{0,1},{1,0},{2,3},{3,2},{4,5},{5,4},{6,7},{7,6},{8,9},{9,8},{10,11... | collective-permute-start | bytes 393224 | tf_op jit(solution)/shard_map/ppermute | solution.py:207
  34.3 1.2 %collective-permute-start.14 = (f32[2,256]{1,0:T(2,128)S(1)}, f32[2,256]{1,0:T(2,128)S(1)}, u32[]{:S(2)}, u32[]{:S(2)}) collective-permute-start(f32[2,256]{1,0:T(2,128)S(1)} %add.5.refs_0_), channel_id=1, source_target_pairs={{0,1},{1,0},{2,3},{3,2},{4,5},{5,4},{6,7},{7,6},{8,9},{9,8},{10,11... | collective-permute-start | bytes 6152 | tf_op jit(solution)/shard_map/ppermute | solution.py:207
  35.5 9.0 %collective-permute-start.16 = (bf16[128,1024]{1,0:T(8,128)(2,1)S(1)}, bf16[128,1024]{1,0:T(8,128)(2,1)S(1)}, u32[]{:S(2)}, u32[]{:S(2)}) collective-permute-start(bf16[128,1024]{1,0:T(8,128)(2,1)S(1)} %get-tuple-element.69), channel_id=1, source_target_pairs={{0,1},{1,0},{2,3},{3,2},{4,5},{5,4},{6,7},{7,6},{8,9},{9,8},{10,11... | collective-permute-start | bytes 786440 | tf_op jit(solution)/shard_map/ppermute | solution.py:207
  35.8 11.8 %collective-permute-start.15 = (bf16[128,1024]{1,0:T(8,128)(2,1)S(1)}, bf16[128,1024]{1,0:T(8,128)(2,1)S(1)}, u32[]{:S(2)}, u32[]{:S(2)}) collective-permute-start(bf16[128,1024]{1,0:T(8,128)(2,1)S(1)} %sink.5.refs_5_.refs_1_), channel_id=1, source_target_pairs={{2,0},{3,1},{4,2},{5,3},{6,4},{7,5},{10,8},{11,9},{12,10},{13,11},... | collective-permute-start | bytes 786440 | tf_op jit(solution)/shard_map/ppermute | solution.py:207
  37.1 11.9 %collective-permute-start.21 = (f32[2,256]{1,0:T(2,128)S(1)}, f32[2,256]{1,0:T(2,128)S(1)}, u32[]{:S(2)}, u32[]{:S(2)}) collective-permute-start(f32[2,256]{1,0:T(2,128)S(1)} %add.7.refs_0_), channel_id=1, source_target_pairs={{0,2},{1,3},{2,0},{3,1},{4,6},{5,7},{6,4},{7,5},{8,10},{9,11},{10,... | collective-permute-start | bytes 6152 | tf_op jit(solution)/shard_map/ppermute | solution.py:207
  40.9 8.5 %collective-permute-start.22 = (f32[2,256]{1,0:T(2,128)S(1)}, f32[2,256]{1,0:T(2,128)S(1)}, u32[]{:S(2)}, u32[]{:S(2)}) collective-permute-start(f32[2,256]{1,0:T(2,128)S(1)} %add.7.refs_0_), channel_id=1, source_target_pairs={{0,4},{1,5},{2,6},{3,7},{4,0},{5,1},{6,2},{7,3},{8,12},{9,13},{10,... | collective-permute-start | bytes 6152 | tf_op jit(solution)/shard_map/ppermute | solution.py:207
  44.4 6.6 %collective-permute-start.23 = (f32[2,256]{1,0:T(2,128)S(1)}, f32[2,256]{1,0:T(2,128)S(1)}, u32[]{:S(2)}, u32[]{:S(2)}) collective-permute-start(f32[2,256]{1,0:T(2,128)S(1)} %add.7.refs_0_), channel_id=1, source_target_pairs={{0,6},{1,7},{2,4},{3,5},{4,2},{5,3},{6,0},{7,1},{8,14},{9,15},{10,... | collective-permute-start | bytes 6152 | tf_op jit(solution)/shard_map/ppermute | solution.py:207
  44.5 14.2 %collective-permute-start.20 = (bf16[128,1024]{1,0:T(8,128)(2,1)S(1)}, bf16[128,1024]{1,0:T(8,128)(2,1)S(1)}, u32[]{:S(2)}, u32[]{:S(2)}) collective-permute-start(bf16[128,1024]{1,0:T(8,128)(2,1)S(1)} %sink.6.refs_5_), channel_id=1, source_target_pairs={{2,0},{3,1},{4,2},{5,3},{6,4},{7,5},{10,8},{11,9},{12,10},{13,11},... | collective-permute-start | bytes 786440 | tf_op jit(solution)/shard_map/ppermute | solution.py:207
  47.7 12.1 %collective-permute-start.19 = (bf16[128,1024]{1,0:T(8,128)(2,1)S(1)}, bf16[128,1024]{1,0:T(8,128)(2,1)S(1)}, u32[]{:S(2)}, u32[]{:S(2)}) collective-permute-start(bf16[128,1024]{1,0:T(8,128)(2,1)S(1)} %sink.7.refs_4_), channel_id=1, source_target_pairs={{2,0},{3,1},{4,2},{5,3},{6,4},{7,5},{10,8},{11,9},{12,10},{13,11},... | collective-permute-start | bytes 786440 | tf_op jit(solution)/shard_map/ppermute | solution.py:207
  50.9 3.6 %collective-permute-start.24 = (f32[2,256]{1,0:T(2,128)S(1)}, f32[2,256]{1,0:T(2,128)S(1)}, u32[]{:S(2)}, u32[]{:S(2)}) collective-permute-start(f32[2,256]{1,0:T(2,128)S(1)} %add.8.refs_0_), channel_id=1, source_target_pairs={{0,8},{8,0},{16,24},{24,16},{1,9},{9,1},{17,25},{25,17},{2,10},{10... | collective-permute-start | bytes 6152 | tf_op jit(solution)/shard_map/ppermute | solution.py:207
  54.5 3.6 %collective-permute-start.25 = (f32[2,256]{1,0:T(2,128)S(1)}, f32[2,256]{1,0:T(2,128)S(1)}, u32[]{:S(2)}, u32[]{:S(2)}) collective-permute-start(f32[2,256]{1,0:T(2,128)S(1)} %add.9.refs_0_), channel_id=1, source_target_pairs={{0,16},{8,24},{16,0},{24,8},{1,17},{9,25},{17,1},{25,9},{2,18},{10... | collective-permute-start | bytes 6152 | tf_op jit(solution)/shard_map/ppermute | solution.py:207
  56.0 2.6 %copy-start.2 = (bf16[1,128,1024]{2,1,0:T(8,128)(2,1)S(1)}, bf16[1,128,1024]{2,1,0:T(8,128)(2,1)}, u32[]{:S(2)}) copy-start(bf16[1,128,1024]{2,1,0:T(8,128)(2,1)} %refs_0_.7) | copy-start | bytes 786436

commit v11 on v10

--- a/solution.py
+++ b/solution.py
@@ -172,14 +172,14 @@
     refs[-1][...] = sum(ref[...] for ref in refs[1:-1]) + refs[0][...]
 
 
-def scale(factor, *refs):
-    total = sum(ref[...] for ref in refs[1:-2]) + refs[0][...]
-    refs[-2][...] = total[0:1, :] * factor
-    refs[-1][...] = total[1:2, :] * factor
-
-
-def finish(count, at, keys, key_gain, part_own, swapped, arrived, *rest):
-    key_grad, value_grad = rest[-2:]
+def finish(count, at, factor, keys, key_gain, part_own, swapped, arrived, *rest):
+    if factor is None:
+        key_grad, value_grad = rest
+    else:
+        gains, (key_grad, value_grad, query_gains, key_gains) = rest[:-4], rest[-4:]
+        total = sum(ref[...] for ref in gains[1:]) + gains[0][...]
+        query_gains[...] = total[0:1, :] * factor
+        key_gains[...] = total[1:2, :] * factor
     rows = part_own.shape[0]
     gain_k = key_gain[...]
     for head in range(count):
@@ -381,6 +381,14 @@
         hold = call(add, "hold", dict(total=total), dict(o=shape(2, HEAD_DIM, F32)), [sunk[step - LAG]], cost=COSTS[5])
         last = [sink(step, [*last, *(hold if step == amount else [])])]
 
+    attended, query_grad = call(
+        assemble,
+        "assemble",
+        {(i, chunk): made[chunk][i] for i in range(2) for chunk in range(amount)},
+        dict(a=jax.ShapeDtypeStruct(queries.shape, BF16), b=jax.ShapeDtypeStruct(queries.shape, BF16)),
+        last,
+    )
+
     factor = (lax.axis_size("dp") * queries.shape[0] * lax.axis_size("ctx") * rows) ** (-0.5)
     row = shape(1, HEAD_DIM, F32)
     chips = lax.axis_size("ctx") // 2
@@ -390,43 +398,35 @@
         chips //= 2
     total = total_over(total, "ctx", 2, 2 * chips, 4, COSTS[0], [sunk[amount - 1]])
     half = lax.axis_size("dp") // 2
-    total = total_over(total, "dp", 1, half, 2, COSTS[1])
+    total = total_over(total, "dp", 1, half, 2, COSTS[1], [pltpu.with_memory_space_constraint(attended, pltpu.HBM)])
     others = [move(total, "dp", lambda i: i ^ half)] if half else []
-    query_gains, key_gains = call(
-        functools.partial(scale, factor),
-        "scale",
-        dict(enumerate([total, *others])),
-        dict(a=row, b=row),
-        cost=COSTS[2],
-    )
-    attended, query_grad = call(
-        assemble,
-        "assemble",
-        {(i, chunk): made[chunk][i] for i in range(2) for chunk in range(amount)},
-        dict(a=jax.ShapeDtypeStruct(queries.shape, BF16), b=jax.ShapeDtypeStruct(queries.shape, BF16)),
-        last,
-    )
-    before = [pltpu.with_memory_space_constraint(field, pltpu.HBM) for field in (attended, query_gains)]
     key_outputs = []
     for chunk, (first, count) in enumerate(CHUNKS):
         narrow = columns(rows, count * HEAD_DIM, first * HEAD_DIM)
+        ins = dict(
+            keys=keys, gain=gain_k, own=parts[chunk]["own"], next=parts[chunk]["next"], arrived=sunk[chunk + LAG]
+        )
+        outs = dict(
+            key_grad=jax.ShapeDtypeStruct(keys.shape, BF16), value_grad=jax.ShapeDtypeStruct(keys.shape, BF16)
+        )
+        final = chunk == amount - 1
+        if final:
+            ins.update(enumerate([total, *others]))
+            outs.update(query_gains=row, key_gains=row)
         key_outputs = call(
-            functools.partial(finish, count, width[chunk + LAG]),
+            functools.partial(finish, count, width[chunk + LAG], factor if final else None),
             "finish",
-            dict(
-                keys=keys, gain=gain_k, own=parts[chunk]["own"], next=parts[chunk]["next"], arrived=sunk[chunk + LAG]
-            ),
-            dict(
-                key_grad=jax.ShapeDtypeStruct(keys.shape, BF16), value_grad=jax.ShapeDtypeStruct(keys.shape, BF16)
-            ),
-            [*key_outputs, *(before if chunk == amount - 1 else [])],
+            ins,
+            outs,
+            key_outputs,
             cost=COSTS[3 + chunk],
             grid=(1,),
             in_specs=dict(keys=narrow),
             out_specs=dict(key_grad=narrow, value_grad=narrow),
-            input_output_aliases={5 + i: i for i in range(len(key_outputs))},
-        )
-    return attended, query_grad, *key_outputs, query_gains[0], key_gains[0]
+            input_output_aliases={len(ins) + i: i for i in range(len(key_outputs))},
+        )
+    key_grad, value_grad, query_gains, key_gains = key_outputs
+    return attended, query_grad, key_grad, value_grad, query_gains[0], key_gains[0]
 
 
 def solution(mesh):

time: 61.2 us -> 61.2 us (level)
    pallas_call x22 -> x21, Pallas kernels: 10.4 us -> 9.88 us  [call(): pl.pallas_call(kernel, out_shape=list(outs.values()), in_specs=specs, out...]
  transfers between devices with their start and end apart: 26 -> 26, of which waited for: 13 -> 13; matrix products, arithmetic and copies ran while one was open for 0% -> 0% of each run, Pallas kernels for 14% -> 13%
where the time goes in v11:
time: 61.2 us; the launch traced here: 60.7 us
  starting transfers between devices  36 us (59%)
  waiting for transfers between devices  14 us (23%)
  Pallas kernels  9.88 us (16%)
  between operations  0.85 us (1%)
    ppermute x26, starting transfers between devices, move(): lax.ppermute(field, axis, [(i, target(i)) for i in range(size) if 0 <= ta...  36 us
    ppermute x26, waiting for transfers between devices, move(): lax.ppermute(field, axis, [(i, target(i)) for i in range(size) if 0 <= ta...  14 us
    pallas_call x21, Pallas kernels, call(): pl.pallas_call(kernel, out_shape=list(outs.values()), in_specs=specs, out...  9.88 us
  transfers between devices with their start and end apart: 26, of which 13 were waited for; matrix products, arithmetic and copies ran while one was open for 0% of the time, Pallas kernels for 13%

profile of v11, /device:TPU:0, one launch (start us, length us, event | category | flops | bytes accessed | tf_op | source)
XLA Modules:
  0.0 60.7 jit_solution(15968073363126363301)
XLA Ops:
  0.6 0.9 %payload.2.refs_5_.refs_1_.refs_3_ = bf16[128,1024]{1,0:T(8,128)(2,1)S(1)} custom-call(bf16[1,128,1024]{2,1,0:T(8,128)(2,1)} %refs_0_.7, bf16[1,128,1024]{2,1,0:T(8,128)(2,1)} %refs_1_.5), custom_call_target="tpu_custom_call" | custom-call | bytes 1 | tf_op jit(solution)/shard_map/payload/pallas_call | solution.py:38
  1.6 4.9 %collective-permute-start = (bf16[128,1024]{1,0:T(8,128)(2,1)S(1)}, bf16[128,1024]{1,0:T(8,128)(2,1)S(1)}, u32[]{:S(2)}, u32[]{:S(2)}) collective-permute-start(bf16[128,1024]{1,0:T(8,128)(2,1)S(1)} %payload.2.refs_5_.refs_1_.refs_3_), channel_id=1, source_target_pairs={{0,2},{1,3},{2,4},{3,5},{4,6},{5,7},{8,10},{9,11},{10,12},{11,13},... | collective-permute-start | bytes 786440 | tf_op jit(solution)/shard_map/ppermute | solution.py:207
  6.5 1.0 %payload.3 = (bf16[128,1024]{1,0:T(8,128)(2,1)S(1)}, s32[1,1024]{1,0:T(1,128)S(1)}, f32[1,256]{1,0:T(1,128)S(1)}, f32[1,256]{1,0:T(1,128)S(1)}) custom-call(bf16[1,128,1024]{2,1,0:T(8,128)(2,1)} %refs_0_.7, bf16[1,128,1024]{2,1,0:T(8,128)(2,1)} %refs_1_.5, s32[1,1024]{1,0:T(1,128)} %refs_2_.3, f32[1,256]{1,0:T(1,128)} %bitcast.4, f32[1,256]{1,0:T(1,128)} %bitcast.5, ...), custom_call_target="tpu_custom_call" | custom-call | bytes 1 | tf_op jit(solution)/shard_map/payload/pallas_call | solution.py:38
  7.6 3.5 %collective-permute-start.3 = (bf16[128,1024]{1,0:T(8,128)(2,1)S(1)}, bf16[128,1024]{1,0:T(8,128)(2,1)S(1)}, u32[]{:S(2)}, u32[]{:S(2)}) collective-permute-start(bf16[128,1024]{1,0:T(8,128)(2,1)S(1)} %get-tuple-element.47.refs_1_.refs_3_), channel_id=1, source_target_pairs={{0,2},{1,3},{2,4},{3,5},{4,6},{5,7},{8,10},{9,11},{10,12},{11,13},... | collective-permute-start | bytes 786440 | tf_op jit(solution)/shard_map/ppermute | solution.py:207
  11.1 2.2 %collective-permute-done.refs_0_.refs_5_ = bf16[128,1024]{1,0:T(8,128)(2,1)S(1)} collective-permute-done((bf16[128,1024]{1,0:T(8,128)(2,1)S(1)}, bf16[128,1024]{1,0:T(8,128)(2,1)S(1)}, u32[]{:S(2)}, u32[]{:S(2)}) %collective-permute-start) | collective-permute-done | bytes 262176 | tf_op jit(solution)/shard_map/ppermute | solution.py:207
  13.3 4.4 %collective-permute-start.2 = (bf16[128,1024]{1,0:T(8,128)(2,1)S(1)}, bf16[128,1024]{1,0:T(8,128)(2,1)S(1)}, u32[]{:S(2)}, u32[]{:S(2)}) collective-permute-start(bf16[128,1024]{1,0:T(8,128)(2,1)S(1)} %get-tuple-element.46.refs_2_), channel_id=1, source_target_pairs={{0,2},{1,3},{2,4},{3,5},{4,6},{5,7},{8,10},{9,11},{10,12},{11,13},... | collective-permute-start | bytes 786440 | tf_op jit(solution)/shard_map/ppermute | solution.py:207
  17.7 1.1 %collective-permute-done.3.refs_0_.refs_5_ = bf16[128,1024]{1,0:T(8,128)(2,1)S(1)} collective-permute-done((bf16[128,1024]{1,0:T(8,128)(2,1)S(1)}, bf16[128,1024]{1,0:T(8,128)(2,1)S(1)}, u32[]{:S(2)}, u32[]{:S(2)}) %collective-permute-start.3) | collective-permute-done | bytes 262176 | tf_op jit(solution)/shard_map/ppermute | solution.py:207
  18.9 4.5 %collective-permute-start.7 = (bf16[128,1024]{1,0:T(8,128)(2,1)S(1)}, bf16[128,1024]{1,0:T(8,128)(2,1)S(1)}, u32[]{:S(2)}, u32[]{:S(2)}) collective-permute-start(bf16[128,1024]{1,0:T(8,128)(2,1)S(1)} %get-tuple-element.48.refs_2_), channel_id=1, source_target_pairs={{0,2},{1,3},{2,4},{3,5},{4,6},{5,7},{8,10},{9,11},{10,12},{11,13},... | collective-permute-start | bytes 786440 | tf_op jit(solution)/shard_map/ppermute | solution.py:207
  23.4 1.0 %collective-permute-done.2.refs_1_.refs_6_ = bf16[128,1024]{1,0:T(8,128)(2,1)S(1)} collective-permute-done((bf16[128,1024]{1,0:T(8,128)(2,1)S(1)}, bf16[128,1024]{1,0:T(8,128)(2,1)S(1)}, u32[]{:S(2)}, u32[]{:S(2)}) %collective-permute-start.2) | collective-permute-done | bytes 262176 | tf_op jit(solution)/shard_map/ppermute | solution.py:207
  24.6 0.5 collective-permute-start.5
  25.1 0.8 %collective-permute-done.4.refs_7_ = bf16[128,512]{1,0:T(8,128)(2,1)S(1)} collective-permute-done((bf16[128,512]{1,0:T(8,128)(2,1)S(1)}, bf16[128,512]{1,0:T(8,128)(2,1)S(1)}, u32[]{:S(2)}, u32[]{:S(2)}) %collective-permute-start.4) | collective-permute-done | bytes 131104 | tf_op jit(solution)/shard_map/ppermute | solution.py:207
  26.1 2.3 %attend.2 = (bf16[128,1024]{1,0:T(8,128)(2,1)S(1)}, bf16[128,1024]{1,0:T(8,128)(2,1)S(1)}, f32[128,1024]{1,0:T(8,128)S(1)}, f32[128,1024]{1,0:T(8,128)S(1)}, f32...) custom-call(s32[1,1024]{1,0:T(1,128)S(1)} %get-tuple-element.44.refs, ...), custom_call_target="tpu_custom_call" | custom-call | bytes 1 | tf_op jit(solution)/shard_map/attend/pallas_call | solution.py:38
  28.4 0.4 collective-permute-start.10
  29.0 0.4 collective-permute-start.8
  30.2 1.3 %collective-permute-start.17 = (bf16[128,1024]{1,0:T(8,128)(2,1)S(1)}, bf16[128,1024]{1,0:T(8,128)(2,1)S(1)}, u32[]{:S(2)}, u32[]{:S(2)}) collective-permute-start(bf16[128,1024]{1,0:T(8,128)(2,1)S(1)} %sink.4.refs_11_.refs_3_), channel_id=1, source_target_pairs={{2,0},{3,1},{4,2},{5,3},{6,4},{7,5},{10,8},{11,9},{12,10},{13,11},... | collective-permute-start | bytes 786440 | tf_op jit(solution)/shard_map/ppermute | solution.py:207
  31.5 2.3 %attend.3 = (bf16[128,1024]{1,0:T(8,128)(2,1)S(1)}, bf16[128,1024]{1,0:T(8,128)(2,1)S(1)}, f32[128,1024]{1,0:T(8,128)S(1)}, f32[128,1024]{1,0:T(8,128)S(1)}, f32...) custom-call(s32[1,1024]{1,0:T(1,128)S(1)} %get-tuple-element.44.refs, ...), custom_call_target="tpu_custom_call" | custom-call | bytes 1 | tf_op jit(solution)/shard_map/attend/pallas_call | solution.py:38
  34.5 0.9 %collective-permute-done.14.refs_1_ = f32[2,256]{1,0:T(2,128)S(1)} collective-permute-done((f32[2,256]{1,0:T(2,128)S(1)}, f32[2,256]{1,0:T(2,128)S(1)}, u32[]{:S(2)}, u32[]{:S(2)}) %collective-permute-start.14) | collective-permute-done | bytes 2080 | tf_op jit(solution)/shard_map/ppermute | solution.py:207
  35.8 1.3 %collective-permute-start.15 = (bf16[128,1024]{1,0:T(8,128)(2,1)S(1)}, bf16[128,1024]{1,0:T(8,128)(2,1)S(1)}, u32[]{:S(2)}, u32[]{:S(2)}) collective-permute-start(bf16[128,1024]{1,0:T(8,128)(2,1)S(1)} %sink.5.refs_5_.refs_1_), channel_id=1, source_target_pairs={{2,0},{3,1},{4,2},{5,3},{6,4},{7,5},{10,8},{11,9},{12,10},{13,11},... | collective-permute-start | bytes 786440 | tf_op jit(solution)/shard_map/ppermute | solution.py:207
  37.1 3.8 %collective-permute-start.20 = (f32[2,256]{1,0:T(2,128)S(1)}, f32[2,256]{1,0:T(2,128)S(1)}, u32[]{:S(2)}, u32[]{:S(2)}) collective-permute-start(f32[2,256]{1,0:T(2,128)S(1)} %add.7.refs_0_), channel_id=1, source_target_pairs={{0,2},{1,3},{2,0},{3,1},{4,6},{5,7},{6,4},{7,5},{8,10},{9,11},{10,... | collective-permute-start | bytes 6152 | tf_op jit(solution)/shard_map/ppermute | solution.py:207
  40.9 3.5 %collective-permute-start.21 = (f32[2,256]{1,0:T(2,128)S(1)}, f32[2,256]{1,0:T(2,128)S(1)}, u32[]{:S(2)}, u32[]{:S(2)}) collective-permute-start(f32[2,256]{1,0:T(2,128)S(1)} %add.7.refs_0_), channel_id=1, source_target_pairs={{0,4},{1,5},{2,6},{3,7},{4,0},{5,1},{6,2},{7,3},{8,12},{9,13},{10,... | collective-permute-start | bytes 6152 | tf_op jit(solution)/shard_map/ppermute | solution.py:207
  44.5 1.3 %collective-permute-start.25 = (bf16[128,1024]{1,0:T(8,128)(2,1)S(1)}, bf16[128,1024]{1,0:T(8,128)(2,1)S(1)}, u32[]{:S(2)}, u32[]{:S(2)}) collective-permute-start(bf16[128,1024]{1,0:T(8,128)(2,1)S(1)} %sink.6.refs_5_), channel_id=1, source_target_pairs={{2,0},{3,1},{4,2},{5,3},{6,4},{7,5},{10,8},{11,9},{12,10},{13,11},... | collective-permute-start | bytes 786440 | tf_op jit(solution)/shard_map/ppermute | solution.py:207
  45.8 1.8 %collective-permute-done.15.refs_1_.refs_4_ = bf16[128,1024]{1,0:T(8,128)(2,1)S(1)} collective-permute-done((bf16[128,1024]{1,0:T(8,128)(2,1)S(1)}, bf16[128,1024]{1,0:T(8,128)(2,1)S(1)}, u32[]{:S(2)}, u32[]{:S(2)}) %collective-permute-start.15) | collective-permute-done | bytes 262176 | tf_op jit(solution)/shard_map/ppermute | solution.py:207
  47.7 1.3 %collective-permute-start.19 = (bf16[128,1024]{1,0:T(8,128)(2,1)S(1)}, bf16[128,1024]{1,0:T(8,128)(2,1)S(1)}, u32[]{:S(2)}, u32[]{:S(2)}) collective-permute-start(bf16[128,1024]{1,0:T(8,128)(2,1)S(1)} %sink.7.refs_4_), channel_id=1, source_target_pairs={{2,0},{3,1},{4,2},{5,3},{6,4},{7,5},{10,8},{11,9},{12,10},{13,11},... | collective-permute-start | bytes 786440 | tf_op jit(solution)/shard_map/ppermute | solution.py:207
  49.3 1.6 %collective-permute-done.22.refs_3_ = f32[2,256]{1,0:T(2,128)S(1)} collective-permute-done((f32[2,256]{1,0:T(2,128)S(1)}, f32[2,256]{1,0:T(2,128)S(1)}, u32[]{:S(2)}, u32[]{:S(2)}) %collective-permute-start.22) | collective-permute-done | bytes 2080 | tf_op jit(solution)/shard_map/ppermute | solution.py:207
  50.9 1.5 %collective-permute-start.23 = (f32[2,256]{1,0:T(2,128)S(1)}, f32[2,256]{1,0:T(2,128)S(1)}, u32[]{:S(2)}, u32[]{:S(2)}) collective-permute-start(f32[2,256]{1,0:T(2,128)S(1)} %add.8.refs_0_), channel_id=1, source_target_pairs={{0,8},{8,0},{16,24},{24,16},{1,9},{9,1},{17,25},{25,17},{2,10},{10... | collective-permute-start | bytes 6152 | tf_op jit(solution)/shard_map/ppermute | solution.py:207
  52.4 1.0 %assemble.1 = (bf16[1,128,2048]{2,1,0:T(8,128)(2,1)}, bf16[1,128,2048]{2,1,0:T(8,128)(2,1)}) custom-call(bf16[128,1024]{1,0:T(8,128)(2,1)S(1)} %get-tuple-element.53.refs_0_, bf16[128,1024]{1,0:T(8,128)(2,1)S(1)} %get-tuple-element.61.refs_1_, bf16[128,1024]{1,0:T(8,128)(2,1)S(1)} %get-tuple-element.62.refs_2_, ...), custom_call_target="tpu_custom_call" | custom-call | bytes 1 | tf_op jit(solution)/shard_map/assemble/pallas_call | solution.py:38
  53.5 1.1 %collective-permute-done.23.refs_1_ = f32[2,256]{1,0:T(2,128)S(1)} collective-permute-done((f32[2,256]{1,0:T(2,128)S(1)}, f32[2,256]{1,0:T(2,128)S(1)}, u32[]{:S(2)}, u32[]{:S(2)}) %collective-permute-start.23) | collective-permute-done | bytes 2080 | tf_op jit(solution)/shard_map/ppermute | solution.py:207
  54.5 1.5 %collective-permute-start.24 = (f32[2,256]{1,0:T(2,128)S(1)}, f32[2,256]{1,0:T(2,128)S(1)}, u32[]{:S(2)}, u32[]{:S(2)}) collective-permute-start(f32[2,256]{1,0:T(2,128)S(1)} %add.9.refs_5_), channel_id=1, source_target_pairs={{0,16},{8,24},{16,0},{24,8},{1,17},{9,25},{17,1},{25,9},{2,18},{10... | collective-permute-start | bytes 6152 | tf_op jit(solution)/shard_map/ppermute | solution.py:207
  56.0 0.9 %finish.2 = (bf16[1,128,1024]{2,1,0:T(8,128)(2,1)}, bf16[1,128,1024]{2,1,0:T(8,128)(2,1)}) custom-call(bf16[1,128,1024]{2,1,0:T(8,128)(2,1)S(1)} %copy-done.2, f32[1,256]{1,0:T(1,128)S(1)} %get-tuple-element.52.refs_10_.refs_1_, f32[128,1024]{1,0:T(8,128)S(1)} %get-tuple-element.75.refs_2_, bf16[128,1024]{1,0:T(8,128)(2,1)S(1)} %collective-permute-done.18.refs_4_.refs_3_, ...), custom_call_target="tpu_custom_call" | custom-call | flops 2147483648 | bytes 1 | tf_op jit(solution)/shard_map/finish/pallas_call | solution.py:38
  57.0 1.1 %collective-permute-done.24.refs_6_ = f32[2,256]{1,0:T(2,128)S(1)} collective-permute-done((f32[2,256]{1,0:T(2,128)S(1)}, f32[2,256]{1,0:T(2,128)S(1)}, u32[]{:S(2)}, u32[]{:S(2)}) %collective-permute-start.24) | collective-permute-done | bytes 2080 | tf_op jit(solution)/shard_map/ppermute | solution.py:207
  58.1 1.7 %collective-permute-done.19.refs_4_ = bf16[128,1024]{1,0:T(8,128)(2,1)S(1)} collective-permute-done((bf16[128,1024]{1,0:T(8,128)(2,1)S(1)}, bf16[128,1024]{1,0:T(8,128)(2,1)S(1)}, u32[]{:S(2)}, u32[]{:S(2)}) %collective-permute-start.19) | collective-permute-done | bytes 262176 | tf_op jit(solution)/shard_map/ppermute | solution.py:207
  59.8 0.9 %finish.3 = (bf16[1,128,1024]{2,1,0:T(8,128)(2,1)}, bf16[1,128,1024]{2,1,0:T(8,128)(2,1)}, f32[1,256]{1,0:T(1,128)}, f32[1,256]{1,0:T(1,128)}) custom-call(bf16[1,128,1024]{2,1,0:T(8,128)(2,1)S(1)} %copy-done.2, f32[1,256]{1,0:T(1,128)S(1)} %get-tuple-element.52.refs_10_.refs_1_, ...), custom_call_target="tpu_custom_call", output_to_operand_aliasing={{0}: (7, {}), {1}: (8, {})} | custom-call | flops 4294967296 | bytes 1 | tf_op jit(solution)/shard_map/finish/pallas_call | solution.py:38
  (47 shorter events, 3.3 us)
Async XLA Ops:
  1.6 11.6 %collective-permute-start = (bf16[128,1024]{1,0:T(8,128)(2,1)S(1)}, bf16[128,1024]{1,0:T(8,128)(2,1)S(1)}, u32[]{:S(2)}, u32[]{:S(2)}) collective-permute-start(bf16[128,1024]{1,0:T(8,128)(2,1)S(1)} %payload.2.refs_5_.refs_1_.refs_3_), channel_id=1, source_target_pairs={{0,2},{1,3},{2,4},{3,5},{4,6},{5,7},{8,10},{9,11},{10,12},{11,13},... | collective-permute-start | bytes 786440 | tf_op jit(solution)/shard_map/ppermute | solution.py:207
  7.6 11.3 %collective-permute-start.3 = (bf16[128,1024]{1,0:T(8,128)(2,1)S(1)}, bf16[128,1024]{1,0:T(8,128)(2,1)S(1)}, u32[]{:S(2)}, u32[]{:S(2)}) collective-permute-start(bf16[128,1024]{1,0:T(8,128)(2,1)S(1)} %get-tuple-element.47.refs_1_.refs_3_), channel_id=1, source_target_pairs={{0,2},{1,3},{2,4},{3,5},{4,6},{5,7},{8,10},{9,11},{10,12},{11,13},... | collective-permute-start | bytes 786440 | tf_op jit(solution)/shard_map/ppermute | solution.py:207
  13.3 11.2 %collective-permute-start.2 = (bf16[128,1024]{1,0:T(8,128)(2,1)S(1)}, bf16[128,1024]{1,0:T(8,128)(2,1)S(1)}, u32[]{:S(2)}, u32[]{:S(2)}) collective-permute-start(bf16[128,1024]{1,0:T(8,128)(2,1)S(1)} %get-tuple-element.46.refs_2_), channel_id=1, source_target_pairs={{0,2},{1,3},{2,4},{3,5},{4,6},{5,7},{8,10},{9,11},{10,12},{11,13},... | collective-permute-start | bytes 786440 | tf_op jit(solution)/shard_map/ppermute | solution.py:207
  17.7 7.5 %collective-permute-start.1 = (bf16[128,1024]{1,0:T(8,128)(2,1)S(1)}, bf16[128,1024]{1,0:T(8,128)(2,1)S(1)}, u32[]{:S(2)}, u32[]{:S(2)}) collective-permute-start(bf16[128,1024]{1,0:T(8,128)(2,1)S(1)} %get-tuple-element.45), channel_id=1, source_target_pairs={{0,1},{1,0},{2,3},{3,2},{4,5},{5,4},{6,7},{7,6},{8,9},{9,8},{10,11... | collective-permute-start | bytes 786440 | tf_op jit(solution)/shard_map/ppermute | solution.py:207
  18.9 7.2 %copy-start = (bf16[1,128,2048]{2,1,0:T(8,128)(2,1)S(1)}, bf16[1,128,2048]{2,1,0:T(8,128)(2,1)}, u32[]{:S(2)}) copy-start(bf16[1,128,2048]{2,1,0:T(8,128)(2,1)} %refs_1_.7) | copy-start | bytes 1572868
  18.9 7.2 %copy-start.1 = (bf16[1,128,2048]{2,1,0:T(8,128)(2,1)S(1)}, bf16[1,128,2048]{2,1,0:T(8,128)(2,1)}, u32[]{:S(2)}) copy-start(bf16[1,128,2048]{2,1,0:T(8,128)(2,1)} %refs_2_.5) | copy-start | bytes 1572868
  18.9 10.0 %collective-permute-start.7 = (bf16[128,1024]{1,0:T(8,128)(2,1)S(1)}, bf16[128,1024]{1,0:T(8,128)(2,1)S(1)}, u32[]{:S(2)}, u32[]{:S(2)}) collective-permute-start(bf16[128,1024]{1,0:T(8,128)(2,1)S(1)} %get-tuple-element.48.refs_2_), channel_id=1, source_target_pairs={{0,2},{1,3},{2,4},{3,5},{4,6},{5,7},{8,10},{9,11},{10,12},{11,13},... | collective-permute-start | bytes 786440 | tf_op jit(solution)/shard_map/ppermute | solution.py:207
  24.5 1.4 %collective-permute-start.4 = (bf16[128,512]{1,0:T(8,128)(2,1)S(1)}, bf16[128,512]{1,0:T(8,128)(2,1)S(1)}, u32[]{:S(2)}, u32[]{:S(2)}) collective-permute-start(bf16[128,512]{1,0:T(8,128)(2,1)S(1)} %get-tuple-element.49.refs_2_), channel_id=1, source_target_pairs={{0,1},{1,0},{2,3},{3,2},{4,5},{5,4},{6,7},{7,6},{8,9},{9,8},{10,11... | collective-permute-start | bytes 393224 | tf_op jit(solution)/shard_map/ppermute | solution.py:207
  24.6 1.5 %collective-permute-start.5 = (bf16[128,512]{1,0:T(8,128)(2,1)S(1)}, bf16[128,512]{1,0:T(8,128)(2,1)S(1)}, u32[]{:S(2)}, u32[]{:S(2)}) collective-permute-start(bf16[128,512]{1,0:T(8,128)(2,1)S(1)} %get-tuple-element.50), channel_id=1, source_target_pairs={{0,1},{1,0},{2,3},{3,2},{4,5},{5,4},{6,7},{7,6},{8,9},{9,8},{10,11... | collective-permute-start | bytes 393224 | tf_op jit(solution)/shard_map/ppermute | solution.py:207
  25.1 6.4 %collective-permute-start.6 = (bf16[128,1024]{1,0:T(8,128)(2,1)S(1)}, bf16[128,1024]{1,0:T(8,128)(2,1)S(1)}, u32[]{:S(2)}, u32[]{:S(2)}) collective-permute-start(bf16[128,1024]{1,0:T(8,128)(2,1)S(1)} %get-tuple-element.54), channel_id=1, source_target_pairs={{0,1},{1,0},{2,3},{3,2},{4,5},{5,4},{6,7},{7,6},{8,9},{9,8},{10,11... | collective-permute-start | bytes 786440 | tf_op jit(solution)/shard_map/ppermute | solution.py:207
  28.4 1.4 %collective-permute-start.10 = (bf16[128,512]{1,0:T(8,128)(2,1)S(1)}, bf16[128,512]{1,0:T(8,128)(2,1)S(1)}, u32[]{:S(2)}, u32[]{:S(2)}) collective-permute-start(bf16[128,512]{1,0:T(8,128)(2,1)S(1)} %get-tuple-element.59), channel_id=1, source_target_pairs={{0,1},{1,0},{2,3},{3,2},{4,5},{5,4},{6,7},{7,6},{8,9},{9,8},{10,11... | collective-permute-start | bytes 393224 | tf_op jit(solution)/shard_map/ppermute | solution.py:207
  28.7 1.4 %collective-permute-start.11 = (bf16[128,512]{1,0:T(8,128)(2,1)S(1)}, bf16[128,512]{1,0:T(8,128)(2,1)S(1)}, u32[]{:S(2)}, u32[]{:S(2)}) collective-permute-start(bf16[128,512]{1,0:T(8,128)(2,1)S(1)} %get-tuple-element.60), channel_id=1, source_target_pairs={{0,1},{1,0},{2,3},{3,2},{4,5},{5,4},{6,7},{7,6},{8,9},{9,8},{10,11... | collective-permute-start | bytes 393224 | tf_op jit(solution)/shard_map/ppermute | solution.py:207
  29.0 2.5 %collective-permute-start.8 = (bf16[128,512]{1,0:T(8,128)(2,1)S(1)}, bf16[128,512]{1,0:T(8,128)(2,1)S(1)}, u32[]{:S(2)}, u32[]{:S(2)}) collective-permute-start(bf16[128,512]{1,0:T(8,128)(2,1)S(1)} %get-tuple-element.56), channel_id=1, source_target_pairs={{0,1},{1,0},{2,3},{3,2},{4,5},{5,4},{6,7},{7,6},{8,9},{9,8},{10,11... | collective-permute-start | bytes 393224 | tf_op jit(solution)/shard_map/ppermute | solution.py:207
  29.3 2.1 %collective-permute-start.9 = (bf16[128,512]{1,0:T(8,128)(2,1)S(1)}, bf16[128,512]{1,0:T(8,128)(2,1)S(1)}, u32[]{:S(2)}, u32[]{:S(2)}) collective-permute-start(bf16[128,512]{1,0:T(8,128)(2,1)S(1)} %get-tuple-element.57), channel_id=1, source_target_pairs={{0,1},{1,0},{2,3},{3,2},{4,5},{5,4},{6,7},{7,6},{8,9},{9,8},{10,11... | collective-permute-start | bytes 393224 | tf_op jit(solution)/shard_map/ppermute | solution.py:207
  29.8 11.1 %collective-permute-start.18 = (bf16[128,1024]{1,0:T(8,128)(2,1)S(1)}, bf16[128,1024]{1,0:T(8,128)(2,1)S(1)}, u32[]{:S(2)}, u32[]{:S(2)}) collective-permute-start(bf16[128,1024]{1,0:T(8,128)(2,1)S(1)} %get-tuple-element.71), channel_id=1, source_target_pairs={{0,1},{1,0},{2,3},{3,2},{4,5},{5,4},{6,7},{7,6},{8,9},{9,8},{10,11... | collective-permute-start | bytes 786440 | tf_op jit(solution)/shard_map/ppermute | solution.py:207
  30.2 14.2 %collective-permute-start.17 = (bf16[128,1024]{1,0:T(8,128)(2,1)S(1)}, bf16[128,1024]{1,0:T(8,128)(2,1)S(1)}, u32[]{:S(2)}, u32[]{:S(2)}) collective-permute-start(bf16[128,1024]{1,0:T(8,128)(2,1)S(1)} %sink.4.refs_11_.refs_3_), channel_id=1, source_target_pairs={{2,0},{3,1},{4,2},{5,3},{6,4},{7,5},{10,8},{11,9},{12,10},{13,11},... | collective-permute-start | bytes 786440 | tf_op jit(solution)/shard_map/ppermute | solution.py:207
  33.7 2.0 %collective-permute-start.12 = (bf16[128,512]{1,0:T(8,128)(2,1)S(1)}, bf16[128,512]{1,0:T(8,128)(2,1)S(1)}, u32[]{:S(2)}, u32[]{:S(2)}) collective-permute-start(bf16[128,512]{1,0:T(8,128)(2,1)S(1)} %get-tuple-element.66), channel_id=1, source_target_pairs={{0,1},{1,0},{2,3},{3,2},{4,5},{5,4},{6,7},{7,6},{8,9},{9,8},{10,11... | collective-permute-start | bytes 393224 | tf_op jit(solution)/shard_map/ppermute | solution.py:207
  34.0 1.7 %collective-permute-start.13 = (bf16[128,512]{1,0:T(8,128)(2,1)S(1)}, bf16[128,512]{1,0:T(8,128)(2,1)S(1)}, u32[]{:S(2)}, u32[]{:S(2)}) collective-permute-start(bf16[128,512]{1,0:T(8,128)(2,1)S(1)} %get-tuple-element.67), channel_id=1, source_target_pairs={{0,1},{1,0},{2,3},{3,2},{4,5},{5,4},{6,7},{7,6},{8,9},{9,8},{10,11... | collective-permute-start | bytes 393224 | tf_op jit(solution)/shard_map/ppermute | solution.py:207
  34.3 1.2 %collective-permute-start.14 = (f32[2,256]{1,0:T(2,128)S(1)}, f32[2,256]{1,0:T(2,128)S(1)}, u32[]{:S(2)}, u32[]{:S(2)}) collective-permute-start(f32[2,256]{1,0:T(2,128)S(1)} %add.5.refs_0_), channel_id=1, source_target_pairs={{0,1},{1,0},{2,3},{3,2},{4,5},{5,4},{6,7},{7,6},{8,9},{9,8},{10,11... | collective-permute-start | bytes 6152 | tf_op jit(solution)/shard_map/ppermute | solution.py:207
  35.5 9.0 %collective-permute-start.16 = (bf16[128,1024]{1,0:T(8,128)(2,1)S(1)}, bf16[128,1024]{1,0:T(8,128)(2,1)S(1)}, u32[]{:S(2)}, u32[]{:S(2)}) collective-permute-start(bf16[128,1024]{1,0:T(8,128)(2,1)S(1)} %get-tuple-element.69), channel_id=1, source_target_pairs={{0,1},{1,0},{2,3},{3,2},{4,5},{5,4},{6,7},{7,6},{8,9},{9,8},{10,11... | collective-permute-start | bytes 786440 | tf_op jit(solution)/shard_map/ppermute | solution.py:207
  35.8 11.8 %collective-permute-start.15 = (bf16[128,1024]{1,0:T(8,128)(2,1)S(1)}, bf16[128,1024]{1,0:T(8,128)(2,1)S(1)}, u32[]{:S(2)}, u32[]{:S(2)}) collective-permute-start(bf16[128,1024]{1,0:T(8,128)(2,1)S(1)} %sink.5.refs_5_.refs_1_), channel_id=1, source_target_pairs={{2,0},{3,1},{4,2},{5,3},{6,4},{7,5},{10,8},{11,9},{12,10},{13,11},... | collective-permute-start | bytes 786440 | tf_op jit(solution)/shard_map/ppermute | solution.py:207
  37.1 11.9 %collective-permute-start.20 = (f32[2,256]{1,0:T(2,128)S(1)}, f32[2,256]{1,0:T(2,128)S(1)}, u32[]{:S(2)}, u32[]{:S(2)}) collective-permute-start(f32[2,256]{1,0:T(2,128)S(1)} %add.7.refs_0_), channel_id=1, source_target_pairs={{0,2},{1,3},{2,0},{3,1},{4,6},{5,7},{6,4},{7,5},{8,10},{9,11},{10,... | collective-permute-start | bytes 6152 | tf_op jit(solution)/shard_map/ppermute | solution.py:207
  40.9 8.5 %collective-permute-start.21 = (f32[2,256]{1,0:T(2,128)S(1)}, f32[2,256]{1,0:T(2,128)S(1)}, u32[]{:S(2)}, u32[]{:S(2)}) collective-permute-start(f32[2,256]{1,0:T(2,128)S(1)} %add.7.refs_0_), channel_id=1, source_target_pairs={{0,4},{1,5},{2,6},{3,7},{4,0},{5,1},{6,2},{7,3},{8,12},{9,13},{10,... | collective-permute-start | bytes 6152 | tf_op jit(solution)/shard_map/ppermute | solution.py:207
  44.4 6.6 %collective-permute-start.22 = (f32[2,256]{1,0:T(2,128)S(1)}, f32[2,256]{1,0:T(2,128)S(1)}, u32[]{:S(2)}, u32[]{:S(2)}) collective-permute-start(f32[2,256]{1,0:T(2,128)S(1)} %add.7.refs_0_), channel_id=1, source_target_pairs={{0,6},{1,7},{2,4},{3,5},{4,2},{5,3},{6,0},{7,1},{8,14},{9,15},{10,... | collective-permute-start | bytes 6152 | tf_op jit(solution)/shard_map/ppermute | solution.py:207
  44.5 11.5 %collective-permute-start.25 = (bf16[128,1024]{1,0:T(8,128)(2,1)S(1)}, bf16[128,1024]{1,0:T(8,128)(2,1)S(1)}, u32[]{:S(2)}, u32[]{:S(2)}) collective-permute-start(bf16[128,1024]{1,0:T(8,128)(2,1)S(1)} %sink.6.refs_5_), channel_id=1, source_target_pairs={{2,0},{3,1},{4,2},{5,3},{6,4},{7,5},{10,8},{11,9},{12,10},{13,11},... | collective-permute-start | bytes 786440 | tf_op jit(solution)/shard_map/ppermute | solution.py:207
  47.7 12.1 %collective-permute-start.19 = (bf16[128,1024]{1,0:T(8,128)(2,1)S(1)}, bf16[128,1024]{1,0:T(8,128)(2,1)S(1)}, u32[]{:S(2)}, u32[]{:S(2)}) collective-permute-start(bf16[128,1024]{1,0:T(8,128)(2,1)S(1)} %sink.7.refs_4_), channel_id=1, source_target_pairs={{2,0},{3,1},{4,2},{5,3},{6,4},{7,5},{10,8},{11,9},{12,10},{13,11},... | collective-permute-start | bytes 786440 | tf_op jit(solution)/shard_map/ppermute | solution.py:207
  50.9 3.6 %collective-permute-start.23 = (f32[2,256]{1,0:T(2,128)S(1)}, f32[2,256]{1,0:T(2,128)S(1)}, u32[]{:S(2)}, u32[]{:S(2)}) collective-permute-start(f32[2,256]{1,0:T(2,128)S(1)} %add.8.refs_0_), channel_id=1, source_target_pairs={{0,8},{8,0},{16,24},{24,16},{1,9},{9,1},{17,25},{25,17},{2,10},{10... | collective-permute-start | bytes 6152 | tf_op jit(solution)/shard_map/ppermute | solution.py:207
  54.5 1.5 %copy-start.2 = (bf16[1,128,1024]{2,1,0:T(8,128)(2,1)S(1)}, bf16[1,128,1024]{2,1,0:T(8,128)(2,1)}, u32[]{:S(2)}) copy-start(bf16[1,128,1024]{2,1,0:T(8,128)(2,1)} %refs_0_.7) | copy-start | bytes 786436
  54.5 3.6 %collective-permute-start.24 = (f32[2,256]{1,0:T(2,128)S(1)}, f32[2,256]{1,0:T(2,128)S(1)}, u32[]{:S(2)}, u32[]{:S(2)}) collective-permute-start(f32[2,256]{1,0:T(2,128)S(1)} %add.9.refs_5_), channel_id=1, source_target_pairs={{0,16},{8,24},{16,0},{24,8},{1,17},{9,25},{17,1},{25,9},{2,18},{10... | collective-permute-start | bytes 6152 | tf_op jit(solution)/shard_map/ppermute | solution.py:207

commit v12 on v11

--- a/solution.py
+++ b/solution.py
@@ -109,9 +109,6 @@
     live = (query_seg == key_seg) & (back >= 0) & (back < WINDOW)
     live = jnp.concatenate([live] * GROUPS, 0)
 
-    query_gains = jnp.zeros((1, HEAD_DIM), F32)
-    key_gains = jnp.zeros((1, HEAD_DIM), F32)
-
     def band_of(index):
         third = (across_k, 0) if index < count else (across_v, -count * HEAD_DIM)
         blocks = ((arrived_far, at_far), third, (arrived_near, at_near), (across_x, at_x), (own, at_own))
@@ -119,44 +116,58 @@
             [field[:, at + index * HEAD_DIM : at + (index + 1) * HEAD_DIM] for field, at in blocks], 0
         )
 
-    for head in range(count):
-        at_k = slice(head * HEAD_DIM, (head + 1) * HEAD_DIM)
-        at_v = slice((count + head) * HEAD_DIM, (count + head + 1) * HEAD_DIM)
-        at_q = [slice((head * GROUPS + g) * HEAD_DIM, (head * GROUPS + g + 1) * HEAD_DIM) for g in range(GROUPS)]
-        from_q = [slice(at.start + first * GROUPS * HEAD_DIM, at.stop + first * GROUPS * HEAD_DIM) for at in at_q]
-        band_v = band_of(count + head)
-        k_normed, _ = normalize(band_of(head).astype(F32))
-        k_rounded = (k_normed * gain_k).astype(BF16)
-        q_normed, q_inverse = normalize(jnp.concatenate([queries[0, :, at] for at in from_q], 0).astype(F32))
-        q_scaled = (q_normed * gain_q * HEAD_DIM ** (-0.5)).astype(BF16)
-        grads = jnp.concatenate([out_grad[0, :, at] for at in from_q], 0)
-
-        scores = dot(q_scaled, k_rounded, (1, 1))
-        weights = jnp.where(live, jnp.exp(scores), 0.0)
+    def columns_of(index):
+        return slice(index * HEAD_DIM, (index + 1) * HEAD_DIM)
+
+    def query_rows(field, head):
+        start = (first + head) * GROUPS
+        return jnp.concatenate([field[0, :, columns_of(start + g)] for g in range(GROUPS)], 0)
+
+    heads = range(count)
+    grads = [query_rows(out_grad, head) for head in heads]
+    band_v = [band_of(count + head) for head in heads]
+    q_normed, q_inverse, q_scaled, k_normed, k_rounded, scores = [], [], [], [], [], []
+    for head in heads:
+        normed, inverse = normalize(query_rows(queries, head).astype(F32))
+        q_normed.append(normed)
+        q_inverse.append(inverse)
+        q_scaled.append((normed * gain_q * HEAD_DIM ** (-0.5)).astype(BF16))
+        k_normed.append(normalize(band_of(head).astype(F32))[0])
+        k_rounded.append((k_normed[head] * gain_k).astype(BF16))
+        scores.append(dot(q_scaled[head], k_rounded[head], (1, 1)))
+    dprob = [dot(grads[head], band_v[head], (1, 1)) for head in heads]
+    probs_low, dscore = [], []
+    for head in heads:
+        weights = jnp.where(live, jnp.exp(scores[head]), 0.0)
         probs = weights * (1.0 / jnp.sum(weights, -1, keepdims=True))
-        probs_low = probs.astype(BF16)
-        dprob = dot(grads, band_v, (1, 1))
-        centre = jnp.sum(probs * dprob, -1, keepdims=True)
-        dscore = (probs * (dprob - centre)).astype(BF16)
-        key_parts = dot(dscore, q_scaled, (0, 0))
-        value_parts = dot(probs_low, grads, (0, 0))
-        for at, parts, third in ((at_k, key_parts, third_k), (at_v, value_parts, third_v)):
-            part_far[:, at] = parts[:rows]
-            third[:, at_k] = parts[rows : 2 * rows].astype(BF16)
-            part_near[:, at] = parts[2 * rows : 3 * rows]
-            part_next[:, at] = parts[3 * rows : 4 * rows].astype(BF16)
-            part_own[:, at] = parts[4 * rows :]
-
-        output = dot(probs_low, band_v, (1, 0)).astype(BF16)
-        dq = dot(dscore, k_rounded, (1, 0)) * HEAD_DIM ** (-0.5)
+        probs_low.append(probs.astype(BF16))
+        centre = jnp.sum(probs * dprob[head], -1, keepdims=True)
+        dscore.append((probs * (dprob[head] - centre)).astype(BF16))
+
+    def give(parts, at):
+        part_far[:, at] = parts[:rows]
+        part_near[:, at] = parts[2 * rows : 3 * rows]
+        part_next[:, at] = parts[3 * rows : 4 * rows].astype(BF16)
+        part_own[:, at] = parts[4 * rows :]
+        return parts[rows : 2 * rows].astype(BF16)
+
+    for head in heads:
+        third_v[:, columns_of(head)] = give(dot(probs_low[head], grads[head], (0, 0)), columns_of(count + head))
+        output = dot(probs_low[head], band_v[head], (1, 0)).astype(BF16)
+        for g in range(GROUPS):
+            attended[:, columns_of(head * GROUPS + g)] = output[g * rows : (g + 1) * rows]
+    query_gains = jnp.zeros((1, HEAD_DIM), F32)
+    key_gains = jnp.zeros((1, HEAD_DIM), F32)
+    for head in heads:
+        key_parts = dot(dscore[head], q_scaled[head], (0, 0))
+        third_k[:, columns_of(head)] = give(key_parts, columns_of(head))
+        key_gains = key_gains + jnp.sum(key_parts * k_normed[head], 0, keepdims=True)
+        dq = dot(dscore[head], k_rounded[head], (1, 0)) * HEAD_DIM ** (-0.5)
         scaled = dq * gain_q
-        grad = q_inverse * (scaled - q_normed * jnp.mean(scaled * q_normed, -1, keepdims=True))
-        grad = grad.astype(BF16)
-        for g, at in enumerate(at_q):
-            attended[:, at] = output[g * rows : (g + 1) * rows]
-            query_grad[:, at] = grad[g * rows : (g + 1) * rows]
-        query_gains = query_gains + jnp.sum(dq * q_normed, 0, keepdims=True)
-        key_gains = key_gains + jnp.sum(key_parts * k_normed, 0, keepdims=True)
+        grad = q_inverse[head] * (scaled - q_normed[head] * jnp.mean(scaled * q_normed[head], -1, keepdims=True))
+        for g in range(GROUPS):
+            query_grad[:, columns_of(head * GROUPS + g)] = grad[g * rows : (g + 1) * rows].astype(BF16)
+        query_gains = query_gains + jnp.sum(dq * q_normed[head], 0, keepdims=True)
     gains[0:1, :] = query_gains
     gains[1:2, :] = key_gains
 

time: 61.2 us -> 60.5 us (0.989)
  Pallas kernels: 9.88 us -> 9.13 us
    pallas_call x21, Pallas kernels: 9.88 us -> 9.13 us  [call(): pl.pallas_call(kernel, out_shape=list(outs.values()), in_specs=specs, out...]
  transfers between devices with their start and end apart: 26 -> 26, of which waited for: 13 -> 13; matrix products, arithmetic and copies ran while one was open for 0% -> 0% of each run, Pallas kernels for 13% -> 12%
where the time goes in v12:
time: 60.5 us; the launch traced here: 60 us
  starting transfers between devices  35.9 us (59%)
  waiting for transfers between devices  14 us (23%)
  Pallas kernels  9.13 us (15%)
  between operations  0.86 us (1%)
    ppermute x26, starting transfers between devices, move(): lax.ppermute(field, axis, [(i, target(i)) for i in range(size) if 0 <= ta...  35.9 us
    ppermute x26, waiting for transfers between devices, move(): lax.ppermute(field, axis, [(i, target(i)) for i in range(size) if 0 <= ta...  14 us
    pallas_call x21, Pallas kernels, call(): pl.pallas_call(kernel, out_shape=list(outs.values()), in_specs=specs, out...  9.13 us
  transfers between devices with their start and end apart: 26, of which 13 were waited for; matrix products, arithmetic and copies ran while one was open for 0% of the time, Pallas kernels for 12%

profile of v12, /device:TPU:0, one launch (start us, length us, event | category | flops | bytes accessed | tf_op | source)
XLA Modules:
  0.0 60.0 jit_solution(15295160497834227549)
XLA Ops:
  0.6 0.9 %payload.2.refs_5_.refs_1_.refs_3_ = bf16[128,1024]{1,0:T(8,128)(2,1)S(1)} custom-call(bf16[1,128,1024]{2,1,0:T(8,128)(2,1)} %refs_0_.7, bf16[1,128,1024]{2,1,0:T(8,128)(2,1)} %refs_1_.5), custom_call_target="tpu_custom_call" | custom-call | bytes 1 | tf_op jit(solution)/shard_map/payload/pallas_call | solution.py:38
  1.6 4.9 %collective-permute-start = (bf16[128,1024]{1,0:T(8,128)(2,1)S(1)}, bf16[128,1024]{1,0:T(8,128)(2,1)S(1)}, u32[]{:S(2)}, u32[]{:S(2)}) collective-permute-start(bf16[128,1024]{1,0:T(8,128)(2,1)S(1)} %payload.2.refs_5_.refs_1_.refs_3_), channel_id=1, source_target_pairs={{0,2},{1,3},{2,4},{3,5},{4,6},{5,7},{8,10},{9,11},{10,12},{11,13},... | collective-permute-start | bytes 786440 | tf_op jit(solution)/shard_map/ppermute | solution.py:218
  6.5 1.0 %payload.3 = (bf16[128,1024]{1,0:T(8,128)(2,1)S(1)}, s32[1,1024]{1,0:T(1,128)S(1)}, f32[1,256]{1,0:T(1,128)S(1)}, f32[1,256]{1,0:T(1,128)S(1)}) custom-call(bf16[1,128,1024]{2,1,0:T(8,128)(2,1)} %refs_0_.7, bf16[1,128,1024]{2,1,0:T(8,128)(2,1)} %refs_1_.5, s32[1,1024]{1,0:T(1,128)} %refs_2_.3, f32[1,256]{1,0:T(1,128)} %bitcast.4, f32[1,256]{1,0:T(1,128)} %bitcast.5, ...), custom_call_target="tpu_custom_call" | custom-call | bytes 1 | tf_op jit(solution)/shard_map/payload/pallas_call | solution.py:38
  7.6 3.5 %collective-permute-start.3 = (bf16[128,1024]{1,0:T(8,128)(2,1)S(1)}, bf16[128,1024]{1,0:T(8,128)(2,1)S(1)}, u32[]{:S(2)}, u32[]{:S(2)}) collective-permute-start(bf16[128,1024]{1,0:T(8,128)(2,1)S(1)} %get-tuple-element.47.refs_1_.refs_3_), channel_id=1, source_target_pairs={{0,2},{1,3},{2,4},{3,5},{4,6},{5,7},{8,10},{9,11},{10,12},{11,13},... | collective-permute-start | bytes 786440 | tf_op jit(solution)/shard_map/ppermute | solution.py:218
  11.1 2.2 %collective-permute-done.refs_0_.refs_5_ = bf16[128,1024]{1,0:T(8,128)(2,1)S(1)} collective-permute-done((bf16[128,1024]{1,0:T(8,128)(2,1)S(1)}, bf16[128,1024]{1,0:T(8,128)(2,1)S(1)}, u32[]{:S(2)}, u32[]{:S(2)}) %collective-permute-start) | collective-permute-done | bytes 262176 | tf_op jit(solution)/shard_map/ppermute | solution.py:218
  13.3 4.4 %collective-permute-start.2 = (bf16[128,1024]{1,0:T(8,128)(2,1)S(1)}, bf16[128,1024]{1,0:T(8,128)(2,1)S(1)}, u32[]{:S(2)}, u32[]{:S(2)}) collective-permute-start(bf16[128,1024]{1,0:T(8,128)(2,1)S(1)} %get-tuple-element.46.refs_2_), channel_id=1, source_target_pairs={{0,2},{1,3},{2,4},{3,5},{4,6},{5,7},{8,10},{9,11},{10,12},{11,13},... | collective-permute-start | bytes 786440 | tf_op jit(solution)/shard_map/ppermute | solution.py:218
  17.7 1.1 %collective-permute-done.3.refs_0_.refs_5_ = bf16[128,1024]{1,0:T(8,128)(2,1)S(1)} collective-permute-done((bf16[128,1024]{1,0:T(8,128)(2,1)S(1)}, bf16[128,1024]{1,0:T(8,128)(2,1)S(1)}, u32[]{:S(2)}, u32[]{:S(2)}) %collective-permute-start.3) | collective-permute-done | bytes 262176 | tf_op jit(solution)/shard_map/ppermute | solution.py:218
  18.9 4.5 %collective-permute-start.7 = (bf16[128,1024]{1,0:T(8,128)(2,1)S(1)}, bf16[128,1024]{1,0:T(8,128)(2,1)S(1)}, u32[]{:S(2)}, u32[]{:S(2)}) collective-permute-start(bf16[128,1024]{1,0:T(8,128)(2,1)S(1)} %get-tuple-element.48.refs_2_), channel_id=1, source_target_pairs={{0,2},{1,3},{2,4},{3,5},{4,6},{5,7},{8,10},{9,11},{10,12},{11,13},... | collective-permute-start | bytes 786440 | tf_op jit(solution)/shard_map/ppermute | solution.py:218
  23.4 1.0 %collective-permute-done.2.refs_1_.refs_6_ = bf16[128,1024]{1,0:T(8,128)(2,1)S(1)} collective-permute-done((bf16[128,1024]{1,0:T(8,128)(2,1)S(1)}, bf16[128,1024]{1,0:T(8,128)(2,1)S(1)}, u32[]{:S(2)}, u32[]{:S(2)}) %collective-permute-start.2) | collective-permute-done | bytes 262176 | tf_op jit(solution)/shard_map/ppermute | solution.py:218
  24.6 0.5 collective-permute-start.5
  25.1 0.8 %collective-permute-done.4.refs_7_ = bf16[128,512]{1,0:T(8,128)(2,1)S(1)} collective-permute-done((bf16[128,512]{1,0:T(8,128)(2,1)S(1)}, bf16[128,512]{1,0:T(8,128)(2,1)S(1)}, u32[]{:S(2)}, u32[]{:S(2)}) %collective-permute-start.4) | collective-permute-done | bytes 131104 | tf_op jit(solution)/shard_map/ppermute | solution.py:218
  26.1 1.9 %attend.2 = (bf16[128,1024]{1,0:T(8,128)(2,1)S(1)}, bf16[128,1024]{1,0:T(8,128)(2,1)S(1)}, f32[128,1024]{1,0:T(8,128)S(1)}, f32[128,1024]{1,0:T(8,128)S(1)}, f32...) custom-call(s32[1,1024]{1,0:T(1,128)S(1)} %get-tuple-element.44.refs, ...), custom_call_target="tpu_custom_call" | custom-call | bytes 1 | tf_op jit(solution)/shard_map/attend/pallas_call | solution.py:38
  29.0 0.5 collective-permute-start.9
  29.8 1.3 %collective-permute-start.17 = (bf16[128,1024]{1,0:T(8,128)(2,1)S(1)}, bf16[128,1024]{1,0:T(8,128)(2,1)S(1)}, u32[]{:S(2)}, u32[]{:S(2)}) collective-permute-start(bf16[128,1024]{1,0:T(8,128)(2,1)S(1)} %sink.4.refs_11_.refs_3_), channel_id=1, source_target_pairs={{2,0},{3,1},{4,2},{5,3},{6,4},{7,5},{10,8},{11,9},{12,10},{13,11},... | collective-permute-start | bytes 786440 | tf_op jit(solution)/shard_map/ppermute | solution.py:218
  31.1 1.9 %attend.3 = (bf16[128,1024]{1,0:T(8,128)(2,1)S(1)}, bf16[128,1024]{1,0:T(8,128)(2,1)S(1)}, f32[128,1024]{1,0:T(8,128)S(1)}, f32[128,1024]{1,0:T(8,128)S(1)}, f32...) custom-call(s32[1,1024]{1,0:T(1,128)S(1)} %get-tuple-element.44.refs, ...), custom_call_target="tpu_custom_call" | custom-call | bytes 1 | tf_op jit(solution)/shard_map/attend/pallas_call | solution.py:38
  33.9 0.8 %collective-permute-done.14.refs_1_ = f32[2,256]{1,0:T(2,128)S(1)} collective-permute-done((f32[2,256]{1,0:T(2,128)S(1)}, f32[2,256]{1,0:T(2,128)S(1)}, u32[]{:S(2)}, u32[]{:S(2)}) %collective-permute-start.14) | collective-permute-done | bytes 2080 | tf_op jit(solution)/shard_map/ppermute | solution.py:218
  35.2 1.3 %collective-permute-start.15 = (bf16[128,1024]{1,0:T(8,128)(2,1)S(1)}, bf16[128,1024]{1,0:T(8,128)(2,1)S(1)}, u32[]{:S(2)}, u32[]{:S(2)}) collective-permute-start(bf16[128,1024]{1,0:T(8,128)(2,1)S(1)} %sink.5.refs_5_.refs_1_), channel_id=1, source_target_pairs={{2,0},{3,1},{4,2},{5,3},{6,4},{7,5},{10,8},{11,9},{12,10},{13,11},... | collective-permute-start | bytes 786440 | tf_op jit(solution)/shard_map/ppermute | solution.py:218
  36.5 3.8 %collective-permute-start.20 = (f32[2,256]{1,0:T(2,128)S(1)}, f32[2,256]{1,0:T(2,128)S(1)}, u32[]{:S(2)}, u32[]{:S(2)}) collective-permute-start(f32[2,256]{1,0:T(2,128)S(1)} %add.7.refs_0_), channel_id=1, source_target_pairs={{0,2},{1,3},{2,0},{3,1},{4,6},{5,7},{6,4},{7,5},{8,10},{9,11},{10,... | collective-permute-start | bytes 6152 | tf_op jit(solution)/shard_map/ppermute | solution.py:218
  40.3 3.3 %collective-permute-start.21 = (f32[2,256]{1,0:T(2,128)S(1)}, f32[2,256]{1,0:T(2,128)S(1)}, u32[]{:S(2)}, u32[]{:S(2)}) collective-permute-start(f32[2,256]{1,0:T(2,128)S(1)} %add.7.refs_0_), channel_id=1, source_target_pairs={{0,4},{1,5},{2,6},{3,7},{4,0},{5,1},{6,2},{7,3},{8,12},{9,13},{10,... | collective-permute-start | bytes 6152 | tf_op jit(solution)/shard_map/ppermute | solution.py:218
  43.8 1.3 %collective-permute-start.25 = (bf16[128,1024]{1,0:T(8,128)(2,1)S(1)}, bf16[128,1024]{1,0:T(8,128)(2,1)S(1)}, u32[]{:S(2)}, u32[]{:S(2)}) collective-permute-start(bf16[128,1024]{1,0:T(8,128)(2,1)S(1)} %sink.6.refs_5_), channel_id=1, source_target_pairs={{2,0},{3,1},{4,2},{5,3},{6,4},{7,5},{10,8},{11,9},{12,10},{13,11},... | collective-permute-start | bytes 786440 | tf_op jit(solution)/shard_map/ppermute | solution.py:218
  45.1 1.8 %collective-permute-done.15.refs_1_.refs_4_ = bf16[128,1024]{1,0:T(8,128)(2,1)S(1)} collective-permute-done((bf16[128,1024]{1,0:T(8,128)(2,1)S(1)}, bf16[128,1024]{1,0:T(8,128)(2,1)S(1)}, u32[]{:S(2)}, u32[]{:S(2)}) %collective-permute-start.15) | collective-permute-done | bytes 262176 | tf_op jit(solution)/shard_map/ppermute | solution.py:218
  47.0 1.3 %collective-permute-start.19 = (bf16[128,1024]{1,0:T(8,128)(2,1)S(1)}, bf16[128,1024]{1,0:T(8,128)(2,1)S(1)}, u32[]{:S(2)}, u32[]{:S(2)}) collective-permute-start(bf16[128,1024]{1,0:T(8,128)(2,1)S(1)} %sink.7.refs_4_), channel_id=1, source_target_pairs={{2,0},{3,1},{4,2},{5,3},{6,4},{7,5},{10,8},{11,9},{12,10},{13,11},... | collective-permute-start | bytes 786440 | tf_op jit(solution)/shard_map/ppermute | solution.py:218
  48.3 0.5 collective-permute-done.21.refs_2_
  48.8 1.4 %collective-permute-done.22.refs_3_ = f32[2,256]{1,0:T(2,128)S(1)} collective-permute-done((f32[2,256]{1,0:T(2,128)S(1)}, f32[2,256]{1,0:T(2,128)S(1)}, u32[]{:S(2)}, u32[]{:S(2)}) %collective-permute-start.22) | collective-permute-done | bytes 2080 | tf_op jit(solution)/shard_map/ppermute | solution.py:218
  50.2 1.5 %collective-permute-start.23 = (f32[2,256]{1,0:T(2,128)S(1)}, f32[2,256]{1,0:T(2,128)S(1)}, u32[]{:S(2)}, u32[]{:S(2)}) collective-permute-start(f32[2,256]{1,0:T(2,128)S(1)} %add.8.refs_0_), channel_id=1, source_target_pairs={{0,8},{8,0},{16,24},{24,16},{1,9},{9,1},{17,25},{25,17},{2,10},{10... | collective-permute-start | bytes 6152 | tf_op jit(solution)/shard_map/ppermute | solution.py:218
  51.7 1.0 %assemble.1 = (bf16[1,128,2048]{2,1,0:T(8,128)(2,1)}, bf16[1,128,2048]{2,1,0:T(8,128)(2,1)}) custom-call(bf16[128,1024]{1,0:T(8,128)(2,1)S(1)} %get-tuple-element.53.refs_0_, bf16[128,1024]{1,0:T(8,128)(2,1)S(1)} %get-tuple-element.61.refs_1_, bf16[128,1024]{1,0:T(8,128)(2,1)S(1)} %get-tuple-element.62.refs_2_, ...), custom_call_target="tpu_custom_call" | custom-call | bytes 1 | tf_op jit(solution)/shard_map/assemble/pallas_call | solution.py:38
  52.7 1.1 %collective-permute-done.23.refs_1_ = f32[2,256]{1,0:T(2,128)S(1)} collective-permute-done((f32[2,256]{1,0:T(2,128)S(1)}, f32[2,256]{1,0:T(2,128)S(1)}, u32[]{:S(2)}, u32[]{:S(2)}) %collective-permute-start.23) | collective-permute-done | bytes 2080 | tf_op jit(solution)/shard_map/ppermute | solution.py:218
  53.8 1.5 %collective-permute-start.24 = (f32[2,256]{1,0:T(2,128)S(1)}, f32[2,256]{1,0:T(2,128)S(1)}, u32[]{:S(2)}, u32[]{:S(2)}) collective-permute-start(f32[2,256]{1,0:T(2,128)S(1)} %add.9.refs_5_), channel_id=1, source_target_pairs={{0,16},{8,24},{16,0},{24,8},{1,17},{9,25},{17,1},{25,9},{2,18},{10... | collective-permute-start | bytes 6152 | tf_op jit(solution)/shard_map/ppermute | solution.py:218
  55.3 0.9 %finish.2 = (bf16[1,128,1024]{2,1,0:T(8,128)(2,1)}, bf16[1,128,1024]{2,1,0:T(8,128)(2,1)}) custom-call(bf16[1,128,1024]{2,1,0:T(8,128)(2,1)S(1)} %copy-done.2, f32[1,256]{1,0:T(1,128)S(1)} %get-tuple-element.52.refs_10_.refs_1_, f32[128,1024]{1,0:T(8,128)S(1)} %get-tuple-element.75.refs_2_, bf16[128,1024]{1,0:T(8,128)(2,1)S(1)} %collective-permute-done.18.refs_4_.refs_3_, ...), custom_call_target="tpu_custom_call" | custom-call | flops 2147483648 | bytes 1 | tf_op jit(solution)/shard_map/finish/pallas_call | solution.py:38
  56.2 1.2 %collective-permute-done.24.refs_6_ = f32[2,256]{1,0:T(2,128)S(1)} collective-permute-done((f32[2,256]{1,0:T(2,128)S(1)}, f32[2,256]{1,0:T(2,128)S(1)}, u32[]{:S(2)}, u32[]{:S(2)}) %collective-permute-start.24) | collective-permute-done | bytes 2080 | tf_op jit(solution)/shard_map/ppermute | solution.py:218
  57.4 1.7 %collective-permute-done.19.refs_4_ = bf16[128,1024]{1,0:T(8,128)(2,1)S(1)} collective-permute-done((bf16[128,1024]{1,0:T(8,128)(2,1)S(1)}, bf16[128,1024]{1,0:T(8,128)(2,1)S(1)}, u32[]{:S(2)}, u32[]{:S(2)}) %collective-permute-start.19) | collective-permute-done | bytes 262176 | tf_op jit(solution)/shard_map/ppermute | solution.py:218
  59.1 0.9 %finish.3 = (bf16[1,128,1024]{2,1,0:T(8,128)(2,1)}, bf16[1,128,1024]{2,1,0:T(8,128)(2,1)}, f32[1,256]{1,0:T(1,128)}, f32[1,256]{1,0:T(1,128)}) custom-call(bf16[1,128,1024]{2,1,0:T(8,128)(2,1)S(1)} %copy-done.2, f32[1,256]{1,0:T(1,128)S(1)} %get-tuple-element.52.refs_10_.refs_1_, ...), custom_call_target="tpu_custom_call", output_to_operand_aliasing={{0}: (7, {}), {1}: (8, {})} | custom-call | flops 4294967296 | bytes 1 | tf_op jit(solution)/shard_map/finish/pallas_call | solution.py:38
  (47 shorter events, 3.4 us)
Async XLA Ops:
  1.6 11.6 %collective-permute-start = (bf16[128,1024]{1,0:T(8,128)(2,1)S(1)}, bf16[128,1024]{1,0:T(8,128)(2,1)S(1)}, u32[]{:S(2)}, u32[]{:S(2)}) collective-permute-start(bf16[128,1024]{1,0:T(8,128)(2,1)S(1)} %payload.2.refs_5_.refs_1_.refs_3_), channel_id=1, source_target_pairs={{0,2},{1,3},{2,4},{3,5},{4,6},{5,7},{8,10},{9,11},{10,12},{11,13},... | collective-permute-start | bytes 786440 | tf_op jit(solution)/shard_map/ppermute | solution.py:218
  7.6 11.3 %collective-permute-start.3 = (bf16[128,1024]{1,0:T(8,128)(2,1)S(1)}, bf16[128,1024]{1,0:T(8,128)(2,1)S(1)}, u32[]{:S(2)}, u32[]{:S(2)}) collective-permute-start(bf16[128,1024]{1,0:T(8,128)(2,1)S(1)} %get-tuple-element.47.refs_1_.refs_3_), channel_id=1, source_target_pairs={{0,2},{1,3},{2,4},{3,5},{4,6},{5,7},{8,10},{9,11},{10,12},{11,13},... | collective-permute-start | bytes 786440 | tf_op jit(solution)/shard_map/ppermute | solution.py:218
  13.3 11.2 %collective-permute-start.2 = (bf16[128,1024]{1,0:T(8,128)(2,1)S(1)}, bf16[128,1024]{1,0:T(8,128)(2,1)S(1)}, u32[]{:S(2)}, u32[]{:S(2)}) collective-permute-start(bf16[128,1024]{1,0:T(8,128)(2,1)S(1)} %get-tuple-element.46.refs_2_), channel_id=1, source_target_pairs={{0,2},{1,3},{2,4},{3,5},{4,6},{5,7},{8,10},{9,11},{10,12},{11,13},... | collective-permute-start | bytes 786440 | tf_op jit(solution)/shard_map/ppermute | solution.py:218
  17.7 7.5 %collective-permute-start.1 = (bf16[128,1024]{1,0:T(8,128)(2,1)S(1)}, bf16[128,1024]{1,0:T(8,128)(2,1)S(1)}, u32[]{:S(2)}, u32[]{:S(2)}) collective-permute-start(bf16[128,1024]{1,0:T(8,128)(2,1)S(1)} %get-tuple-element.45), channel_id=1, source_target_pairs={{0,1},{1,0},{2,3},{3,2},{4,5},{5,4},{6,7},{7,6},{8,9},{9,8},{10,11... | collective-permute-start | bytes 786440 | tf_op jit(solution)/shard_map/ppermute | solution.py:218
  18.9 7.2 %copy-start = (bf16[1,128,2048]{2,1,0:T(8,128)(2,1)S(1)}, bf16[1,128,2048]{2,1,0:T(8,128)(2,1)}, u32[]{:S(2)}) copy-start(bf16[1,128,2048]{2,1,0:T(8,128)(2,1)} %refs_1_.7) | copy-start | bytes 1572868
  18.9 7.2 %copy-start.1 = (bf16[1,128,2048]{2,1,0:T(8,128)(2,1)S(1)}, bf16[1,128,2048]{2,1,0:T(8,128)(2,1)}, u32[]{:S(2)}) copy-start(bf16[1,128,2048]{2,1,0:T(8,128)(2,1)} %refs_2_.5) | copy-start | bytes 1572868
  18.9 10.0 %collective-permute-start.7 = (bf16[128,1024]{1,0:T(8,128)(2,1)S(1)}, bf16[128,1024]{1,0:T(8,128)(2,1)S(1)}, u32[]{:S(2)}, u32[]{:S(2)}) collective-permute-start(bf16[128,1024]{1,0:T(8,128)(2,1)S(1)} %get-tuple-element.48.refs_2_), channel_id=1, source_target_pairs={{0,2},{1,3},{2,4},{3,5},{4,6},{5,7},{8,10},{9,11},{10,12},{11,13},... | collective-permute-start | bytes 786440 | tf_op jit(solution)/shard_map/ppermute | solution.py:218
  24.5 1.4 %collective-permute-start.4 = (bf16[128,512]{1,0:T(8,128)(2,1)S(1)}, bf16[128,512]{1,0:T(8,128)(2,1)S(1)}, u32[]{:S(2)}, u32[]{:S(2)}) collective-permute-start(bf16[128,512]{1,0:T(8,128)(2,1)S(1)} %get-tuple-element.49.refs_2_), channel_id=1, source_target_pairs={{0,1},{1,0},{2,3},{3,2},{4,5},{5,4},{6,7},{7,6},{8,9},{9,8},{10,11... | collective-permute-start | bytes 393224 | tf_op jit(solution)/shard_map/ppermute | solution.py:218
  24.6 1.5 %collective-permute-start.5 = (bf16[128,512]{1,0:T(8,128)(2,1)S(1)}, bf16[128,512]{1,0:T(8,128)(2,1)S(1)}, u32[]{:S(2)}, u32[]{:S(2)}) collective-permute-start(bf16[128,512]{1,0:T(8,128)(2,1)S(1)} %get-tuple-element.50), channel_id=1, source_target_pairs={{0,1},{1,0},{2,3},{3,2},{4,5},{5,4},{6,7},{7,6},{8,9},{9,8},{10,11... | collective-permute-start | bytes 393224 | tf_op jit(solution)/shard_map/ppermute | solution.py:218
  25.1 6.0 %collective-permute-start.6 = (bf16[128,1024]{1,0:T(8,128)(2,1)S(1)}, bf16[128,1024]{1,0:T(8,128)(2,1)S(1)}, u32[]{:S(2)}, u32[]{:S(2)}) collective-permute-start(bf16[128,1024]{1,0:T(8,128)(2,1)S(1)} %get-tuple-element.54), channel_id=1, source_target_pairs={{0,1},{1,0},{2,3},{3,2},{4,5},{5,4},{6,7},{7,6},{8,9},{9,8},{10,11... | collective-permute-start | bytes 786440 | tf_op jit(solution)/shard_map/ppermute | solution.py:218
  28.0 1.6 %collective-permute-start.10 = (bf16[128,512]{1,0:T(8,128)(2,1)S(1)}, bf16[128,512]{1,0:T(8,128)(2,1)S(1)}, u32[]{:S(2)}, u32[]{:S(2)}) collective-permute-start(bf16[128,512]{1,0:T(8,128)(2,1)S(1)} %get-tuple-element.59), channel_id=1, source_target_pairs={{0,1},{1,0},{2,3},{3,2},{4,5},{5,4},{6,7},{7,6},{8,9},{9,8},{10,11... | collective-permute-start | bytes 393224 | tf_op jit(solution)/shard_map/ppermute | solution.py:218
  28.4 1.4 %collective-permute-start.11 = (bf16[128,512]{1,0:T(8,128)(2,1)S(1)}, bf16[128,512]{1,0:T(8,128)(2,1)S(1)}, u32[]{:S(2)}, u32[]{:S(2)}) collective-permute-start(bf16[128,512]{1,0:T(8,128)(2,1)S(1)} %get-tuple-element.60), channel_id=1, source_target_pairs={{0,1},{1,0},{2,3},{3,2},{4,5},{5,4},{6,7},{7,6},{8,9},{9,8},{10,11... | collective-permute-start | bytes 393224 | tf_op jit(solution)/shard_map/ppermute | solution.py:218
  29.0 2.1 %collective-permute-start.8 = (bf16[128,512]{1,0:T(8,128)(2,1)S(1)}, bf16[128,512]{1,0:T(8,128)(2,1)S(1)}, u32[]{:S(2)}, u32[]{:S(2)}) collective-permute-start(bf16[128,512]{1,0:T(8,128)(2,1)S(1)} %get-tuple-element.56), channel_id=1, source_target_pairs={{0,1},{1,0},{2,3},{3,2},{4,5},{5,4},{6,7},{7,6},{8,9},{9,8},{10,11... | collective-permute-start | bytes 393224 | tf_op jit(solution)/shard_map/ppermute | solution.py:218
  29.0 2.1 %collective-permute-start.9 = (bf16[128,512]{1,0:T(8,128)(2,1)S(1)}, bf16[128,512]{1,0:T(8,128)(2,1)S(1)}, u32[]{:S(2)}, u32[]{:S(2)}) collective-permute-start(bf16[128,512]{1,0:T(8,128)(2,1)S(1)} %get-tuple-element.57), channel_id=1, source_target_pairs={{0,1},{1,0},{2,3},{3,2},{4,5},{5,4},{6,7},{7,6},{8,9},{9,8},{10,11... | collective-permute-start | bytes 393224 | tf_op jit(solution)/shard_map/ppermute | solution.py:218
  29.5 10.8 %collective-permute-start.18 = (bf16[128,1024]{1,0:T(8,128)(2,1)S(1)}, bf16[128,1024]{1,0:T(8,128)(2,1)S(1)}, u32[]{:S(2)}, u32[]{:S(2)}) collective-permute-start(bf16[128,1024]{1,0:T(8,128)(2,1)S(1)} %get-tuple-element.71), channel_id=1, source_target_pairs={{0,1},{1,0},{2,3},{3,2},{4,5},{5,4},{6,7},{7,6},{8,9},{9,8},{10,11... | collective-permute-start | bytes 786440 | tf_op jit(solution)/shard_map/ppermute | solution.py:218
  29.8 13.8 %collective-permute-start.17 = (bf16[128,1024]{1,0:T(8,128)(2,1)S(1)}, bf16[128,1024]{1,0:T(8,128)(2,1)S(1)}, u32[]{:S(2)}, u32[]{:S(2)}) collective-permute-start(bf16[128,1024]{1,0:T(8,128)(2,1)S(1)} %sink.4.refs_11_.refs_3_), channel_id=1, source_target_pairs={{2,0},{3,1},{4,2},{5,3},{6,4},{7,5},{10,8},{11,9},{12,10},{13,11},... | collective-permute-start | bytes 786440 | tf_op jit(solution)/shard_map/ppermute | solution.py:218
  33.0 2.1 %collective-permute-start.12 = (bf16[128,512]{1,0:T(8,128)(2,1)S(1)}, bf16[128,512]{1,0:T(8,128)(2,1)S(1)}, u32[]{:S(2)}, u32[]{:S(2)}) collective-permute-start(bf16[128,512]{1,0:T(8,128)(2,1)S(1)} %get-tuple-element.66), channel_id=1, source_target_pairs={{0,1},{1,0},{2,3},{3,2},{4,5},{5,4},{6,7},{7,6},{8,9},{9,8},{10,11... | collective-permute-start | bytes 393224 | tf_op jit(solution)/shard_map/ppermute | solution.py:218
  33.4 1.7 %collective-permute-start.13 = (bf16[128,512]{1,0:T(8,128)(2,1)S(1)}, bf16[128,512]{1,0:T(8,128)(2,1)S(1)}, u32[]{:S(2)}, u32[]{:S(2)}) collective-permute-start(bf16[128,512]{1,0:T(8,128)(2,1)S(1)} %get-tuple-element.67), channel_id=1, source_target_pairs={{0,1},{1,0},{2,3},{3,2},{4,5},{5,4},{6,7},{7,6},{8,9},{9,8},{10,11... | collective-permute-start | bytes 393224 | tf_op jit(solution)/shard_map/ppermute | solution.py:218
  33.6 1.2 %collective-permute-start.14 = (f32[2,256]{1,0:T(2,128)S(1)}, f32[2,256]{1,0:T(2,128)S(1)}, u32[]{:S(2)}, u32[]{:S(2)}) collective-permute-start(f32[2,256]{1,0:T(2,128)S(1)} %add.5.refs_0_), channel_id=1, source_target_pairs={{0,1},{1,0},{2,3},{3,2},{4,5},{5,4},{6,7},{7,6},{8,9},{9,8},{10,11... | collective-permute-start | bytes 6152 | tf_op jit(solution)/shard_map/ppermute | solution.py:218
  34.8 9.0 %collective-permute-start.16 = (bf16[128,1024]{1,0:T(8,128)(2,1)S(1)}, bf16[128,1024]{1,0:T(8,128)(2,1)S(1)}, u32[]{:S(2)}, u32[]{:S(2)}) collective-permute-start(bf16[128,1024]{1,0:T(8,128)(2,1)S(1)} %get-tuple-element.69), channel_id=1, source_target_pairs={{0,1},{1,0},{2,3},{3,2},{4,5},{5,4},{6,7},{7,6},{8,9},{9,8},{10,11... | collective-permute-start | bytes 786440 | tf_op jit(solution)/shard_map/ppermute | solution.py:218
  35.2 11.7 %collective-permute-start.15 = (bf16[128,1024]{1,0:T(8,128)(2,1)S(1)}, bf16[128,1024]{1,0:T(8,128)(2,1)S(1)}, u32[]{:S(2)}, u32[]{:S(2)}) collective-permute-start(bf16[128,1024]{1,0:T(8,128)(2,1)S(1)} %sink.5.refs_5_.refs_1_), channel_id=1, source_target_pairs={{2,0},{3,1},{4,2},{5,3},{6,4},{7,5},{10,8},{11,9},{12,10},{13,11},... | collective-permute-start | bytes 786440 | tf_op jit(solution)/shard_map/ppermute | solution.py:218
  36.5 11.8 %collective-permute-start.20 = (f32[2,256]{1,0:T(2,128)S(1)}, f32[2,256]{1,0:T(2,128)S(1)}, u32[]{:S(2)}, u32[]{:S(2)}) collective-permute-start(f32[2,256]{1,0:T(2,128)S(1)} %add.7.refs_0_), channel_id=1, source_target_pairs={{0,2},{1,3},{2,0},{3,1},{4,6},{5,7},{6,4},{7,5},{8,10},{9,11},{10,... | collective-permute-start | bytes 6152 | tf_op jit(solution)/shard_map/ppermute | solution.py:218
  40.3 8.5 %collective-permute-start.21 = (f32[2,256]{1,0:T(2,128)S(1)}, f32[2,256]{1,0:T(2,128)S(1)}, u32[]{:S(2)}, u32[]{:S(2)}) collective-permute-start(f32[2,256]{1,0:T(2,128)S(1)} %add.7.refs_0_), channel_id=1, source_target_pairs={{0,4},{1,5},{2,6},{3,7},{4,0},{5,1},{6,2},{7,3},{8,12},{9,13},{10,... | collective-permute-start | bytes 6152 | tf_op jit(solution)/shard_map/ppermute | solution.py:218
  43.6 6.6 %collective-permute-start.22 = (f32[2,256]{1,0:T(2,128)S(1)}, f32[2,256]{1,0:T(2,128)S(1)}, u32[]{:S(2)}, u32[]{:S(2)}) collective-permute-start(f32[2,256]{1,0:T(2,128)S(1)} %add.7.refs_0_), channel_id=1, source_target_pairs={{0,6},{1,7},{2,4},{3,5},{4,2},{5,3},{6,0},{7,1},{8,14},{9,15},{10,... | collective-permute-start | bytes 6152 | tf_op jit(solution)/shard_map/ppermute | solution.py:218
  43.8 11.5 %collective-permute-start.25 = (bf16[128,1024]{1,0:T(8,128)(2,1)S(1)}, bf16[128,1024]{1,0:T(8,128)(2,1)S(1)}, u32[]{:S(2)}, u32[]{:S(2)}) collective-permute-start(bf16[128,1024]{1,0:T(8,128)(2,1)S(1)} %sink.6.refs_5_), channel_id=1, source_target_pairs={{2,0},{3,1},{4,2},{5,3},{6,4},{7,5},{10,8},{11,9},{12,10},{13,11},... | collective-permute-start | bytes 786440 | tf_op jit(solution)/shard_map/ppermute | solution.py:218
  47.0 12.1 %collective-permute-start.19 = (bf16[128,1024]{1,0:T(8,128)(2,1)S(1)}, bf16[128,1024]{1,0:T(8,128)(2,1)S(1)}, u32[]{:S(2)}, u32[]{:S(2)}) collective-permute-start(bf16[128,1024]{1,0:T(8,128)(2,1)S(1)} %sink.7.refs_4_), channel_id=1, source_target_pairs={{2,0},{3,1},{4,2},{5,3},{6,4},{7,5},{10,8},{11,9},{12,10},{13,11},... | collective-permute-start | bytes 786440 | tf_op jit(solution)/shard_map/ppermute | solution.py:218
  50.2 3.6 %collective-permute-start.23 = (f32[2,256]{1,0:T(2,128)S(1)}, f32[2,256]{1,0:T(2,128)S(1)}, u32[]{:S(2)}, u32[]{:S(2)}) collective-permute-start(f32[2,256]{1,0:T(2,128)S(1)} %add.8.refs_0_), channel_id=1, source_target_pairs={{0,8},{8,0},{16,24},{24,16},{1,9},{9,1},{17,25},{25,17},{2,10},{10... | collective-permute-start | bytes 6152 | tf_op jit(solution)/shard_map/ppermute | solution.py:218
  53.8 1.5 %copy-start.2 = (bf16[1,128,1024]{2,1,0:T(8,128)(2,1)S(1)}, bf16[1,128,1024]{2,1,0:T(8,128)(2,1)}, u32[]{:S(2)}) copy-start(bf16[1,128,1024]{2,1,0:T(8,128)(2,1)} %refs_0_.7) | copy-start | bytes 786436
  53.8 3.6 %collective-permute-start.24 = (f32[2,256]{1,0:T(2,128)S(1)}, f32[2,256]{1,0:T(2,128)S(1)}, u32[]{:S(2)}, u32[]{:S(2)}) collective-permute-start(f32[2,256]{1,0:T(2,128)S(1)} %add.9.refs_5_), channel_id=1, source_target_pairs={{0,16},{8,24},{16,0},{24,8},{1,17},{9,25},{17,1},{25,9},{2,18},{10... | collective-permute-start | bytes 6152 | tf_op jit(solution)/shard_map/ppermute | solution.py:218

commit v13 on v12

--- a/solution.py
+++ b/solution.py
@@ -136,13 +136,6 @@
         k_rounded.append((k_normed[head] * gain_k).astype(BF16))
         scores.append(dot(q_scaled[head], k_rounded[head], (1, 1)))
     dprob = [dot(grads[head], band_v[head], (1, 1)) for head in heads]
-    probs_low, dscore = [], []
-    for head in heads:
-        weights = jnp.where(live, jnp.exp(scores[head]), 0.0)
-        probs = weights * (1.0 / jnp.sum(weights, -1, keepdims=True))
-        probs_low.append(probs.astype(BF16))
-        centre = jnp.sum(probs * dprob[head], -1, keepdims=True)
-        dscore.append((probs * (dprob[head] - centre)).astype(BF16))
 
     def give(parts, at):
         part_far[:, at] = parts[:rows]
@@ -151,9 +144,15 @@
         part_own[:, at] = parts[4 * rows :]
         return parts[rows : 2 * rows].astype(BF16)
 
+    dscore = []
     for head in heads:
-        third_v[:, columns_of(head)] = give(dot(probs_low[head], grads[head], (0, 0)), columns_of(count + head))
-        output = dot(probs_low[head], band_v[head], (1, 0)).astype(BF16)
+        weights = jnp.where(live, jnp.exp(scores[head]), 0.0)
+        probs = weights * (1.0 / jnp.sum(weights, -1, keepdims=True))
+        probs_low = probs.astype(BF16)
+        centre = jnp.sum(probs * dprob[head], -1, keepdims=True)
+        dscore.append((probs * (dprob[head] - centre)).astype(BF16))
+        third_v[:, columns_of(head)] = give(dot(probs_low, grads[head], (0, 0)), columns_of(count + head))
+        output = dot(probs_low, band_v[head], (1, 0)).astype(BF16)
         for g in range(GROUPS):
             attended[:, columns_of(head * GROUPS + g)] = output[g * rows : (g + 1) * rows]
     query_gains = jnp.zeros((1, HEAD_DIM), F32)
@@ -183,7 +182,7 @@
     refs[-1][...] = sum(ref[...] for ref in refs[1:-1]) + refs[0][...]
 
 
-def finish(count, at, factor, keys, key_gain, part_own, swapped, arrived, *rest):
+def finish(count, at, factor, own, key_gain, part_own, swapped, arrived, *rest):
     if factor is None:
         key_grad, value_grad = rest
     else:
@@ -202,7 +201,7 @@
             return part_own[:, here] + extra + arrived[:, there].astype(F32)
 
         out = slice(head * HEAD_DIM, (head + 1) * HEAD_DIM)
-        normed, inverse = normalize(keys[0, :, out].astype(F32))
+        normed, inverse = normalize(own[:, out].astype(F32))
         scaled = total(head) * gain_k
         grad = inverse * (scaled - normed * jnp.mean(scaled * normed, -1, keepdims=True))
         key_grad[0, :, out] = grad.astype(BF16)
@@ -415,7 +414,7 @@
     for chunk, (first, count) in enumerate(CHUNKS):
         narrow = columns(rows, count * HEAD_DIM, first * HEAD_DIM)
         ins = dict(
-            keys=keys, gain=gain_k, own=parts[chunk]["own"], next=parts[chunk]["next"], arrived=sunk[chunk + LAG]
+            keys=own[chunk][0], gain=gain_k, own=parts[chunk]["own"], next=parts[chunk]["next"], arrived=sunk[chunk + LAG]
         )
         outs = dict(
             key_grad=jax.ShapeDtypeStruct(keys.shape, BF16), value_grad=jax.ShapeDtypeStruct(keys.shape, BF16)
@@ -432,7 +431,6 @@
             key_outputs,
             cost=COSTS[3 + chunk],
             grid=(1,),
-            in_specs=dict(keys=narrow),
             out_specs=dict(key_grad=narrow, value_grad=narrow),
             input_output_aliases={len(ins) + i: i for i in range(len(key_outputs))},
         )

time: 60.5 us -> 60.4 us (level)
  no operation moved by 1% of the time
where the time goes in v13:
time: 60.4 us; the launch traced here: 60 us
  starting transfers between devices  35.9 us (59%)
  waiting for transfers between devices  14 us (23%)
  Pallas kernels  9.13 us (15%)
  between operations  0.86 us (1%)
    ppermute x26, starting transfers between devices, move(): lax.ppermute(field, axis, [(i, target(i)) for i in range(size) if 0 <= ta...  35.9 us
    ppermute x26, waiting for transfers between devices, move(): lax.ppermute(field, axis, [(i, target(i)) for i in range(size) if 0 <= ta...  14 us
    pallas_call x21, Pallas kernels, call(): pl.pallas_call(kernel, out_shape=list(outs.values()), in_specs=specs, out...  9.13 us
  transfers between devices with their start and end apart: 26, of which 13 were waited for; matrix products, arithmetic and copies ran while one was open for 0% of the time, Pallas kernels for 12%

profile of v13, /device:TPU:0, one launch (start us, length us, event | category | flops | bytes accessed | tf_op | source)
XLA Modules:
  0.0 60.0 jit_solution(14622700399949703395)
XLA Ops:
  0.6 0.9 %payload.2.refs_5_.refs_1_.refs_3_.refs_0_ = bf16[128,1024]{1,0:T(8,128)(2,1)S(1)} custom-call(bf16[1,128,1024]{2,1,0:T(8,128)(2,1)} %refs_0_.3, bf16[1,128,1024]{2,1,0:T(8,128)(2,1)} %refs_1_.5), custom_call_target="tpu_custom_call" | custom-call | bytes 1 | tf_op jit(solution)/shard_map/payload/pallas_call | solution.py:38
  1.6 4.9 %collective-permute-start = (bf16[128,1024]{1,0:T(8,128)(2,1)S(1)}, bf16[128,1024]{1,0:T(8,128)(2,1)S(1)}, u32[]{:S(2)}, u32[]{:S(2)}) collective-permute-start(bf16[128,1024]{1,0:T(8,128)(2,1)S(1)} %payload.2.refs_5_.refs_1_.refs_3_.refs_0_), channel_id=1, source_target_pairs={{0,2},{1,3},{2,4},{3,5},{4,6},{5,7},{8,10},{9,11},{10,12},{11,13},... | collective-permute-start | bytes 786440 | tf_op jit(solution)/shard_map/ppermute | solution.py:217
  6.5 1.0 %payload.3 = (bf16[128,1024]{1,0:T(8,128)(2,1)S(1)}, s32[1,1024]{1,0:T(1,128)S(1)}, f32[1,256]{1,0:T(1,128)S(1)}, f32[1,256]{1,0:T(1,128)S(1)}) custom-call(bf16[1,128,1024]{2,1,0:T(8,128)(2,1)} %refs_0_.3, bf16[1,128,1024]{2,1,0:T(8,128)(2,1)} %refs_1_.5, s32[1,1024]{1,0:T(1,128)} %refs_2_.3, f32[1,256]{1,0:T(1,128)} %bitcast.4, f32[1,256]{1,0:T(1,128)} %bitcast.5, ...), custom_call_target="tpu_custom_call" | custom-call | bytes 1 | tf_op jit(solution)/shard_map/payload/pallas_call | solution.py:38
  7.6 3.5 %collective-permute-start.3 = (bf16[128,1024]{1,0:T(8,128)(2,1)S(1)}, bf16[128,1024]{1,0:T(8,128)(2,1)S(1)}, u32[]{:S(2)}, u32[]{:S(2)}) collective-permute-start(bf16[128,1024]{1,0:T(8,128)(2,1)S(1)} %get-tuple-element.47.refs_1_.refs_3_.refs_0_), channel_id=1, source_target_pairs={{0,2},{1,3},{2,4},{3,5},{4,6},{5,7},{8,10},{9,11},{10,12},{11,13},... | collective-permute-start | bytes 786440 | tf_op jit(solution)/shard_map/ppermute | solution.py:217
  11.1 2.2 %collective-permute-done.refs_0_.refs_5_ = bf16[128,1024]{1,0:T(8,128)(2,1)S(1)} collective-permute-done((bf16[128,1024]{1,0:T(8,128)(2,1)S(1)}, bf16[128,1024]{1,0:T(8,128)(2,1)S(1)}, u32[]{:S(2)}, u32[]{:S(2)}) %collective-permute-start) | collective-permute-done | bytes 262176 | tf_op jit(solution)/shard_map/ppermute | solution.py:217
  13.3 4.4 %collective-permute-start.2 = (bf16[128,1024]{1,0:T(8,128)(2,1)S(1)}, bf16[128,1024]{1,0:T(8,128)(2,1)S(1)}, u32[]{:S(2)}, u32[]{:S(2)}) collective-permute-start(bf16[128,1024]{1,0:T(8,128)(2,1)S(1)} %get-tuple-element.46.refs_2_), channel_id=1, source_target_pairs={{0,2},{1,3},{2,4},{3,5},{4,6},{5,7},{8,10},{9,11},{10,12},{11,13},... | collective-permute-start | bytes 786440 | tf_op jit(solution)/shard_map/ppermute | solution.py:217
  17.7 1.1 %collective-permute-done.3.refs_0_.refs_5_ = bf16[128,1024]{1,0:T(8,128)(2,1)S(1)} collective-permute-done((bf16[128,1024]{1,0:T(8,128)(2,1)S(1)}, bf16[128,1024]{1,0:T(8,128)(2,1)S(1)}, u32[]{:S(2)}, u32[]{:S(2)}) %collective-permute-start.3) | collective-permute-done | bytes 262176 | tf_op jit(solution)/shard_map/ppermute | solution.py:217
  18.9 4.5 %collective-permute-start.7 = (bf16[128,1024]{1,0:T(8,128)(2,1)S(1)}, bf16[128,1024]{1,0:T(8,128)(2,1)S(1)}, u32[]{:S(2)}, u32[]{:S(2)}) collective-permute-start(bf16[128,1024]{1,0:T(8,128)(2,1)S(1)} %get-tuple-element.48.refs_2_), channel_id=1, source_target_pairs={{0,2},{1,3},{2,4},{3,5},{4,6},{5,7},{8,10},{9,11},{10,12},{11,13},... | collective-permute-start | bytes 786440 | tf_op jit(solution)/shard_map/ppermute | solution.py:217
  23.4 1.0 %collective-permute-done.2.refs_1_.refs_6_ = bf16[128,1024]{1,0:T(8,128)(2,1)S(1)} collective-permute-done((bf16[128,1024]{1,0:T(8,128)(2,1)S(1)}, bf16[128,1024]{1,0:T(8,128)(2,1)S(1)}, u32[]{:S(2)}, u32[]{:S(2)}) %collective-permute-start.2) | collective-permute-done | bytes 262176 | tf_op jit(solution)/shard_map/ppermute | solution.py:217
  24.6 0.5 collective-permute-start.5
  25.1 0.8 %collective-permute-done.4.refs_7_ = bf16[128,512]{1,0:T(8,128)(2,1)S(1)} collective-permute-done((bf16[128,512]{1,0:T(8,128)(2,1)S(1)}, bf16[128,512]{1,0:T(8,128)(2,1)S(1)}, u32[]{:S(2)}, u32[]{:S(2)}) %collective-permute-start.4) | collective-permute-done | bytes 131104 | tf_op jit(solution)/shard_map/ppermute | solution.py:217
  26.1 1.9 %attend.2 = (bf16[128,1024]{1,0:T(8,128)(2,1)S(1)}, bf16[128,1024]{1,0:T(8,128)(2,1)S(1)}, f32[128,1024]{1,0:T(8,128)S(1)}, f32[128,1024]{1,0:T(8,128)S(1)}, f32...) custom-call(s32[1,1024]{1,0:T(1,128)S(1)} %get-tuple-element.44.refs, ...), custom_call_target="tpu_custom_call" | custom-call | bytes 1 | tf_op jit(solution)/shard_map/attend/pallas_call | solution.py:38
  29.0 0.5 collective-permute-start.9
  29.8 1.3 %collective-permute-start.17 = (bf16[128,1024]{1,0:T(8,128)(2,1)S(1)}, bf16[128,1024]{1,0:T(8,128)(2,1)S(1)}, u32[]{:S(2)}, u32[]{:S(2)}) collective-permute-start(bf16[128,1024]{1,0:T(8,128)(2,1)S(1)} %sink.4.refs_11_.refs_3_), channel_id=1, source_target_pairs={{2,0},{3,1},{4,2},{5,3},{6,4},{7,5},{10,8},{11,9},{12,10},{13,11},... | collective-permute-start | bytes 786440 | tf_op jit(solution)/shard_map/ppermute | solution.py:217
  31.1 1.9 %attend.3 = (bf16[128,1024]{1,0:T(8,128)(2,1)S(1)}, bf16[128,1024]{1,0:T(8,128)(2,1)S(1)}, f32[128,1024]{1,0:T(8,128)S(1)}, f32[128,1024]{1,0:T(8,128)S(1)}, f32...) custom-call(s32[1,1024]{1,0:T(1,128)S(1)} %get-tuple-element.44.refs, ...), custom_call_target="tpu_custom_call" | custom-call | bytes 1 | tf_op jit(solution)/shard_map/attend/pallas_call | solution.py:38
  33.9 0.8 %collective-permute-done.14.refs_1_ = f32[2,256]{1,0:T(2,128)S(1)} collective-permute-done((f32[2,256]{1,0:T(2,128)S(1)}, f32[2,256]{1,0:T(2,128)S(1)}, u32[]{:S(2)}, u32[]{:S(2)}) %collective-permute-start.14) | collective-permute-done | bytes 2080 | tf_op jit(solution)/shard_map/ppermute | solution.py:217
  35.2 1.3 %collective-permute-start.15 = (bf16[128,1024]{1,0:T(8,128)(2,1)S(1)}, bf16[128,1024]{1,0:T(8,128)(2,1)S(1)}, u32[]{:S(2)}, u32[]{:S(2)}) collective-permute-start(bf16[128,1024]{1,0:T(8,128)(2,1)S(1)} %sink.5.refs_5_.refs_1_), channel_id=1, source_target_pairs={{2,0},{3,1},{4,2},{5,3},{6,4},{7,5},{10,8},{11,9},{12,10},{13,11},... | collective-permute-start | bytes 786440 | tf_op jit(solution)/shard_map/ppermute | solution.py:217
  36.5 3.8 %collective-permute-start.20 = (f32[2,256]{1,0:T(2,128)S(1)}, f32[2,256]{1,0:T(2,128)S(1)}, u32[]{:S(2)}, u32[]{:S(2)}) collective-permute-start(f32[2,256]{1,0:T(2,128)S(1)} %add.7.refs_0_), channel_id=1, source_target_pairs={{0,2},{1,3},{2,0},{3,1},{4,6},{5,7},{6,4},{7,5},{8,10},{9,11},{10,... | collective-permute-start | bytes 6152 | tf_op jit(solution)/shard_map/ppermute | solution.py:217
  40.3 3.3 %collective-permute-start.21 = (f32[2,256]{1,0:T(2,128)S(1)}, f32[2,256]{1,0:T(2,128)S(1)}, u32[]{:S(2)}, u32[]{:S(2)}) collective-permute-start(f32[2,256]{1,0:T(2,128)S(1)} %add.7.refs_0_), channel_id=1, source_target_pairs={{0,4},{1,5},{2,6},{3,7},{4,0},{5,1},{6,2},{7,3},{8,12},{9,13},{10,... | collective-permute-start | bytes 6152 | tf_op jit(solution)/shard_map/ppermute | solution.py:217
  43.8 1.3 %collective-permute-start.25 = (bf16[128,1024]{1,0:T(8,128)(2,1)S(1)}, bf16[128,1024]{1,0:T(8,128)(2,1)S(1)}, u32[]{:S(2)}, u32[]{:S(2)}) collective-permute-start(bf16[128,1024]{1,0:T(8,128)(2,1)S(1)} %sink.6.refs_5_), channel_id=1, source_target_pairs={{2,0},{3,1},{4,2},{5,3},{6,4},{7,5},{10,8},{11,9},{12,10},{13,11},... | collective-permute-start | bytes 786440 | tf_op jit(solution)/shard_map/ppermute | solution.py:217
  45.1 1.8 %collective-permute-done.15.refs_1_.refs_4_ = bf16[128,1024]{1,0:T(8,128)(2,1)S(1)} collective-permute-done((bf16[128,1024]{1,0:T(8,128)(2,1)S(1)}, bf16[128,1024]{1,0:T(8,128)(2,1)S(1)}, u32[]{:S(2)}, u32[]{:S(2)}) %collective-permute-start.15) | collective-permute-done | bytes 262176 | tf_op jit(solution)/shard_map/ppermute | solution.py:217
  47.0 1.3 %collective-permute-start.19 = (bf16[128,1024]{1,0:T(8,128)(2,1)S(1)}, bf16[128,1024]{1,0:T(8,128)(2,1)S(1)}, u32[]{:S(2)}, u32[]{:S(2)}) collective-permute-start(bf16[128,1024]{1,0:T(8,128)(2,1)S(1)} %sink.7.refs_4_), channel_id=1, source_target_pairs={{2,0},{3,1},{4,2},{5,3},{6,4},{7,5},{10,8},{11,9},{12,10},{13,11},... | collective-permute-start | bytes 786440 | tf_op jit(solution)/shard_map/ppermute | solution.py:217
  48.3 0.5 collective-permute-done.21.refs_2_
  48.8 1.4 %collective-permute-done.22.refs_3_ = f32[2,256]{1,0:T(2,128)S(1)} collective-permute-done((f32[2,256]{1,0:T(2,128)S(1)}, f32[2,256]{1,0:T(2,128)S(1)}, u32[]{:S(2)}, u32[]{:S(2)}) %collective-permute-start.22) | collective-permute-done | bytes 2080 | tf_op jit(solution)/shard_map/ppermute | solution.py:217
  50.2 1.5 %collective-permute-start.23 = (f32[2,256]{1,0:T(2,128)S(1)}, f32[2,256]{1,0:T(2,128)S(1)}, u32[]{:S(2)}, u32[]{:S(2)}) collective-permute-start(f32[2,256]{1,0:T(2,128)S(1)} %add.8.refs_0_), channel_id=1, source_target_pairs={{0,8},{8,0},{16,24},{24,16},{1,9},{9,1},{17,25},{25,17},{2,10},{10... | collective-permute-start | bytes 6152 | tf_op jit(solution)/shard_map/ppermute | solution.py:217
  51.7 1.0 %assemble.1 = (bf16[1,128,2048]{2,1,0:T(8,128)(2,1)}, bf16[1,128,2048]{2,1,0:T(8,128)(2,1)}) custom-call(bf16[128,1024]{1,0:T(8,128)(2,1)S(1)} %get-tuple-element.53.refs_0_, bf16[128,1024]{1,0:T(8,128)(2,1)S(1)} %get-tuple-element.61.refs_1_, bf16[128,1024]{1,0:T(8,128)(2,1)S(1)} %get-tuple-element.62.refs_2_, ...), custom_call_target="tpu_custom_call" | custom-call | bytes 1 | tf_op jit(solution)/shard_map/assemble/pallas_call | solution.py:38
  52.7 1.1 %collective-permute-done.23.refs_1_ = f32[2,256]{1,0:T(2,128)S(1)} collective-permute-done((f32[2,256]{1,0:T(2,128)S(1)}, f32[2,256]{1,0:T(2,128)S(1)}, u32[]{:S(2)}, u32[]{:S(2)}) %collective-permute-start.23) | collective-permute-done | bytes 2080 | tf_op jit(solution)/shard_map/ppermute | solution.py:217
  53.8 1.5 %collective-permute-start.24 = (f32[2,256]{1,0:T(2,128)S(1)}, f32[2,256]{1,0:T(2,128)S(1)}, u32[]{:S(2)}, u32[]{:S(2)}) collective-permute-start(f32[2,256]{1,0:T(2,128)S(1)} %add.9.refs_5_), channel_id=1, source_target_pairs={{0,16},{8,24},{16,0},{24,8},{1,17},{9,25},{17,1},{25,9},{2,18},{10... | collective-permute-start | bytes 6152 | tf_op jit(solution)/shard_map/ppermute | solution.py:217
  55.3 0.9 %finish.2 = (bf16[1,128,1024]{2,1,0:T(8,128)(2,1)}, bf16[1,128,1024]{2,1,0:T(8,128)(2,1)}) custom-call(bf16[128,1024]{1,0:T(8,128)(2,1)S(1)} %payload.2.refs_5_.refs_1_.refs_3_.refs_0_, f32[1,256]{1,0:T(1,128)S(1)} %get-tuple-element.52.refs_10_.refs_1_, f32[128,1024]{1,0:T(8,128)S(1)} %get-tuple-element.75.refs_2_, ...), custom_call_target="tpu_custom_call" | custom-call | flops 2147483648 | bytes 1 | tf_op jit(solution)/shard_map/finish/pallas_call | solution.py:38
  56.2 1.2 %collective-permute-done.24.refs_6_ = f32[2,256]{1,0:T(2,128)S(1)} collective-permute-done((f32[2,256]{1,0:T(2,128)S(1)}, f32[2,256]{1,0:T(2,128)S(1)}, u32[]{:S(2)}, u32[]{:S(2)}) %collective-permute-start.24) | collective-permute-done | bytes 2080 | tf_op jit(solution)/shard_map/ppermute | solution.py:217
  57.4 1.7 %collective-permute-done.19.refs_4_ = bf16[128,1024]{1,0:T(8,128)(2,1)S(1)} collective-permute-done((bf16[128,1024]{1,0:T(8,128)(2,1)S(1)}, bf16[128,1024]{1,0:T(8,128)(2,1)S(1)}, u32[]{:S(2)}, u32[]{:S(2)}) %collective-permute-start.19) | collective-permute-done | bytes 262176 | tf_op jit(solution)/shard_map/ppermute | solution.py:217
  59.1 0.9 %finish.3 = (bf16[1,128,1024]{2,1,0:T(8,128)(2,1)}, bf16[1,128,1024]{2,1,0:T(8,128)(2,1)}, f32[1,256]{1,0:T(1,128)}, f32[1,256]{1,0:T(1,128)}) custom-call(bf16[128,1024]{1,0:T(8,128)(2,1)S(1)} %get-tuple-element.47.refs_1_.refs_3_.refs_0_, f32[1,256]{1,0:T(1,128)S(1)} %get-tuple-element.52.refs_10_.refs_1_, ...), custom_call_target="tpu_custom_call", output_to_operand_aliasing={{0}: (7, {}), {1}: (8, {})} | custom-call | flops 4294967296 | bytes 1 | tf_op jit(solution)/shard_map/finish/pallas_call | solution.py:38
  (45 shorter events, 3.4 us)
Async XLA Ops:
  1.6 11.6 %collective-permute-start = (bf16[128,1024]{1,0:T(8,128)(2,1)S(1)}, bf16[128,1024]{1,0:T(8,128)(2,1)S(1)}, u32[]{:S(2)}, u32[]{:S(2)}) collective-permute-start(bf16[128,1024]{1,0:T(8,128)(2,1)S(1)} %payload.2.refs_5_.refs_1_.refs_3_.refs_0_), channel_id=1, source_target_pairs={{0,2},{1,3},{2,4},{3,5},{4,6},{5,7},{8,10},{9,11},{10,12},{11,13},... | collective-permute-start | bytes 786440 | tf_op jit(solution)/shard_map/ppermute | solution.py:217
  7.6 11.3 %collective-permute-start.3 = (bf16[128,1024]{1,0:T(8,128)(2,1)S(1)}, bf16[128,1024]{1,0:T(8,128)(2,1)S(1)}, u32[]{:S(2)}, u32[]{:S(2)}) collective-permute-start(bf16[128,1024]{1,0:T(8,128)(2,1)S(1)} %get-tuple-element.47.refs_1_.refs_3_.refs_0_), channel_id=1, source_target_pairs={{0,2},{1,3},{2,4},{3,5},{4,6},{5,7},{8,10},{9,11},{10,12},{11,13},... | collective-permute-start | bytes 786440 | tf_op jit(solution)/shard_map/ppermute | solution.py:217
  13.3 11.2 %collective-permute-start.2 = (bf16[128,1024]{1,0:T(8,128)(2,1)S(1)}, bf16[128,1024]{1,0:T(8,128)(2,1)S(1)}, u32[]{:S(2)}, u32[]{:S(2)}) collective-permute-start(bf16[128,1024]{1,0:T(8,128)(2,1)S(1)} %get-tuple-element.46.refs_2_), channel_id=1, source_target_pairs={{0,2},{1,3},{2,4},{3,5},{4,6},{5,7},{8,10},{9,11},{10,12},{11,13},... | collective-permute-start | bytes 786440 | tf_op jit(solution)/shard_map/ppermute | solution.py:217
  17.7 7.5 %collective-permute-start.1 = (bf16[128,1024]{1,0:T(8,128)(2,1)S(1)}, bf16[128,1024]{1,0:T(8,128)(2,1)S(1)}, u32[]{:S(2)}, u32[]{:S(2)}) collective-permute-start(bf16[128,1024]{1,0:T(8,128)(2,1)S(1)} %get-tuple-element.45), channel_id=1, source_target_pairs={{0,1},{1,0},{2,3},{3,2},{4,5},{5,4},{6,7},{7,6},{8,9},{9,8},{10,11... | collective-permute-start | bytes 786440 | tf_op jit(solution)/shard_map/ppermute | solution.py:217
  18.9 7.2 %copy-start = (bf16[1,128,2048]{2,1,0:T(8,128)(2,1)S(1)}, bf16[1,128,2048]{2,1,0:T(8,128)(2,1)}, u32[]{:S(2)}) copy-start(bf16[1,128,2048]{2,1,0:T(8,128)(2,1)} %refs_1_.7) | copy-start | bytes 1572868
  18.9 7.2 %copy-start.1 = (bf16[1,128,2048]{2,1,0:T(8,128)(2,1)S(1)}, bf16[1,128,2048]{2,1,0:T(8,128)(2,1)}, u32[]{:S(2)}) copy-start(bf16[1,128,2048]{2,1,0:T(8,128)(2,1)} %refs_2_.5) | copy-start | bytes 1572868
  18.9 10.0 %collective-permute-start.7 = (bf16[128,1024]{1,0:T(8,128)(2,1)S(1)}, bf16[128,1024]{1,0:T(8,128)(2,1)S(1)}, u32[]{:S(2)}, u32[]{:S(2)}) collective-permute-start(bf16[128,1024]{1,0:T(8,128)(2,1)S(1)} %get-tuple-element.48.refs_2_), channel_id=1, source_target_pairs={{0,2},{1,3},{2,4},{3,5},{4,6},{5,7},{8,10},{9,11},{10,12},{11,13},... | collective-permute-start | bytes 786440 | tf_op jit(solution)/shard_map/ppermute | solution.py:217
  24.5 1.4 %collective-permute-start.4 = (bf16[128,512]{1,0:T(8,128)(2,1)S(1)}, bf16[128,512]{1,0:T(8,128)(2,1)S(1)}, u32[]{:S(2)}, u32[]{:S(2)}) collective-permute-start(bf16[128,512]{1,0:T(8,128)(2,1)S(1)} %get-tuple-element.49.refs_2_), channel_id=1, source_target_pairs={{0,1},{1,0},{2,3},{3,2},{4,5},{5,4},{6,7},{7,6},{8,9},{9,8},{10,11... | collective-permute-start | bytes 393224 | tf_op jit(solution)/shard_map/ppermute | solution.py:217
  24.6 1.5 %collective-permute-start.5 = (bf16[128,512]{1,0:T(8,128)(2,1)S(1)}, bf16[128,512]{1,0:T(8,128)(2,1)S(1)}, u32[]{:S(2)}, u32[]{:S(2)}) collective-permute-start(bf16[128,512]{1,0:T(8,128)(2,1)S(1)} %get-tuple-element.50), channel_id=1, source_target_pairs={{0,1},{1,0},{2,3},{3,2},{4,5},{5,4},{6,7},{7,6},{8,9},{9,8},{10,11... | collective-permute-start | bytes 393224 | tf_op jit(solution)/shard_map/ppermute | solution.py:217
  25.1 6.0 %collective-permute-start.6 = (bf16[128,1024]{1,0:T(8,128)(2,1)S(1)}, bf16[128,1024]{1,0:T(8,128)(2,1)S(1)}, u32[]{:S(2)}, u32[]{:S(2)}) collective-permute-start(bf16[128,1024]{1,0:T(8,128)(2,1)S(1)} %get-tuple-element.54), channel_id=1, source_target_pairs={{0,1},{1,0},{2,3},{3,2},{4,5},{5,4},{6,7},{7,6},{8,9},{9,8},{10,11... | collective-permute-start | bytes 786440 | tf_op jit(solution)/shard_map/ppermute | solution.py:217
  28.0 1.6 %collective-permute-start.10 = (bf16[128,512]{1,0:T(8,128)(2,1)S(1)}, bf16[128,512]{1,0:T(8,128)(2,1)S(1)}, u32[]{:S(2)}, u32[]{:S(2)}) collective-permute-start(bf16[128,512]{1,0:T(8,128)(2,1)S(1)} %get-tuple-element.59), channel_id=1, source_target_pairs={{0,1},{1,0},{2,3},{3,2},{4,5},{5,4},{6,7},{7,6},{8,9},{9,8},{10,11... | collective-permute-start | bytes 393224 | tf_op jit(solution)/shard_map/ppermute | solution.py:217
  28.4 1.4 %collective-permute-start.11 = (bf16[128,512]{1,0:T(8,128)(2,1)S(1)}, bf16[128,512]{1,0:T(8,128)(2,1)S(1)}, u32[]{:S(2)}, u32[]{:S(2)}) collective-permute-start(bf16[128,512]{1,0:T(8,128)(2,1)S(1)} %get-tuple-element.60), channel_id=1, source_target_pairs={{0,1},{1,0},{2,3},{3,2},{4,5},{5,4},{6,7},{7,6},{8,9},{9,8},{10,11... | collective-permute-start | bytes 393224 | tf_op jit(solution)/shard_map/ppermute | solution.py:217
  29.0 2.1 %collective-permute-start.8 = (bf16[128,512]{1,0:T(8,128)(2,1)S(1)}, bf16[128,512]{1,0:T(8,128)(2,1)S(1)}, u32[]{:S(2)}, u32[]{:S(2)}) collective-permute-start(bf16[128,512]{1,0:T(8,128)(2,1)S(1)} %get-tuple-element.56), channel_id=1, source_target_pairs={{0,1},{1,0},{2,3},{3,2},{4,5},{5,4},{6,7},{7,6},{8,9},{9,8},{10,11... | collective-permute-start | bytes 393224 | tf_op jit(solution)/shard_map/ppermute | solution.py:217
  29.0 2.1 %collective-permute-start.9 = (bf16[128,512]{1,0:T(8,128)(2,1)S(1)}, bf16[128,512]{1,0:T(8,128)(2,1)S(1)}, u32[]{:S(2)}, u32[]{:S(2)}) collective-permute-start(bf16[128,512]{1,0:T(8,128)(2,1)S(1)} %get-tuple-element.57), channel_id=1, source_target_pairs={{0,1},{1,0},{2,3},{3,2},{4,5},{5,4},{6,7},{7,6},{8,9},{9,8},{10,11... | collective-permute-start | bytes 393224 | tf_op jit(solution)/shard_map/ppermute | solution.py:217
  29.5 10.8 %collective-permute-start.18 = (bf16[128,1024]{1,0:T(8,128)(2,1)S(1)}, bf16[128,1024]{1,0:T(8,128)(2,1)S(1)}, u32[]{:S(2)}, u32[]{:S(2)}) collective-permute-start(bf16[128,1024]{1,0:T(8,128)(2,1)S(1)} %get-tuple-element.71), channel_id=1, source_target_pairs={{0,1},{1,0},{2,3},{3,2},{4,5},{5,4},{6,7},{7,6},{8,9},{9,8},{10,11... | collective-permute-start | bytes 786440 | tf_op jit(solution)/shard_map/ppermute | solution.py:217
  29.8 13.8 %collective-permute-start.17 = (bf16[128,1024]{1,0:T(8,128)(2,1)S(1)}, bf16[128,1024]{1,0:T(8,128)(2,1)S(1)}, u32[]{:S(2)}, u32[]{:S(2)}) collective-permute-start(bf16[128,1024]{1,0:T(8,128)(2,1)S(1)} %sink.4.refs_11_.refs_3_), channel_id=1, source_target_pairs={{2,0},{3,1},{4,2},{5,3},{6,4},{7,5},{10,8},{11,9},{12,10},{13,11},... | collective-permute-start | bytes 786440 | tf_op jit(solution)/shard_map/ppermute | solution.py:217
  33.0 2.1 %collective-permute-start.12 = (bf16[128,512]{1,0:T(8,128)(2,1)S(1)}, bf16[128,512]{1,0:T(8,128)(2,1)S(1)}, u32[]{:S(2)}, u32[]{:S(2)}) collective-permute-start(bf16[128,512]{1,0:T(8,128)(2,1)S(1)} %get-tuple-element.66), channel_id=1, source_target_pairs={{0,1},{1,0},{2,3},{3,2},{4,5},{5,4},{6,7},{7,6},{8,9},{9,8},{10,11... | collective-permute-start | bytes 393224 | tf_op jit(solution)/shard_map/ppermute | solution.py:217
  33.4 1.7 %collective-permute-start.13 = (bf16[128,512]{1,0:T(8,128)(2,1)S(1)}, bf16[128,512]{1,0:T(8,128)(2,1)S(1)}, u32[]{:S(2)}, u32[]{:S(2)}) collective-permute-start(bf16[128,512]{1,0:T(8,128)(2,1)S(1)} %get-tuple-element.67), channel_id=1, source_target_pairs={{0,1},{1,0},{2,3},{3,2},{4,5},{5,4},{6,7},{7,6},{8,9},{9,8},{10,11... | collective-permute-start | bytes 393224 | tf_op jit(solution)/shard_map/ppermute | solution.py:217
  33.6 1.2 %collective-permute-start.14 = (f32[2,256]{1,0:T(2,128)S(1)}, f32[2,256]{1,0:T(2,128)S(1)}, u32[]{:S(2)}, u32[]{:S(2)}) collective-permute-start(f32[2,256]{1,0:T(2,128)S(1)} %add.5.refs_0_), channel_id=1, source_target_pairs={{0,1},{1,0},{2,3},{3,2},{4,5},{5,4},{6,7},{7,6},{8,9},{9,8},{10,11... | collective-permute-start | bytes 6152 | tf_op jit(solution)/shard_map/ppermute | solution.py:217
  34.8 9.0 %collective-permute-start.16 = (bf16[128,1024]{1,0:T(8,128)(2,1)S(1)}, bf16[128,1024]{1,0:T(8,128)(2,1)S(1)}, u32[]{:S(2)}, u32[]{:S(2)}) collective-permute-start(bf16[128,1024]{1,0:T(8,128)(2,1)S(1)} %get-tuple-element.69), channel_id=1, source_target_pairs={{0,1},{1,0},{2,3},{3,2},{4,5},{5,4},{6,7},{7,6},{8,9},{9,8},{10,11... | collective-permute-start | bytes 786440 | tf_op jit(solution)/shard_map/ppermute | solution.py:217
  35.2 11.7 %collective-permute-start.15 = (bf16[128,1024]{1,0:T(8,128)(2,1)S(1)}, bf16[128,1024]{1,0:T(8,128)(2,1)S(1)}, u32[]{:S(2)}, u32[]{:S(2)}) collective-permute-start(bf16[128,1024]{1,0:T(8,128)(2,1)S(1)} %sink.5.refs_5_.refs_1_), channel_id=1, source_target_pairs={{2,0},{3,1},{4,2},{5,3},{6,4},{7,5},{10,8},{11,9},{12,10},{13,11},... | collective-permute-start | bytes 786440 | tf_op jit(solution)/shard_map/ppermute | solution.py:217
  36.5 11.8 %collective-permute-start.20 = (f32[2,256]{1,0:T(2,128)S(1)}, f32[2,256]{1,0:T(2,128)S(1)}, u32[]{:S(2)}, u32[]{:S(2)}) collective-permute-start(f32[2,256]{1,0:T(2,128)S(1)} %add.7.refs_0_), channel_id=1, source_target_pairs={{0,2},{1,3},{2,0},{3,1},{4,6},{5,7},{6,4},{7,5},{8,10},{9,11},{10,... | collective-permute-start | bytes 6152 | tf_op jit(solution)/shard_map/ppermute | solution.py:217
  40.3 8.5 %collective-permute-start.21 = (f32[2,256]{1,0:T(2,128)S(1)}, f32[2,256]{1,0:T(2,128)S(1)}, u32[]{:S(2)}, u32[]{:S(2)}) collective-permute-start(f32[2,256]{1,0:T(2,128)S(1)} %add.7.refs_0_), channel_id=1, source_target_pairs={{0,4},{1,5},{2,6},{3,7},{4,0},{5,1},{6,2},{7,3},{8,12},{9,13},{10,... | collective-permute-start | bytes 6152 | tf_op jit(solution)/shard_map/ppermute | solution.py:217
  43.6 6.6 %collective-permute-start.22 = (f32[2,256]{1,0:T(2,128)S(1)}, f32[2,256]{1,0:T(2,128)S(1)}, u32[]{:S(2)}, u32[]{:S(2)}) collective-permute-start(f32[2,256]{1,0:T(2,128)S(1)} %add.7.refs_0_), channel_id=1, source_target_pairs={{0,6},{1,7},{2,4},{3,5},{4,2},{5,3},{6,0},{7,1},{8,14},{9,15},{10,... | collective-permute-start | bytes 6152 | tf_op jit(solution)/shard_map/ppermute | solution.py:217
  43.8 11.5 %collective-permute-start.25 = (bf16[128,1024]{1,0:T(8,128)(2,1)S(1)}, bf16[128,1024]{1,0:T(8,128)(2,1)S(1)}, u32[]{:S(2)}, u32[]{:S(2)}) collective-permute-start(bf16[128,1024]{1,0:T(8,128)(2,1)S(1)} %sink.6.refs_5_), channel_id=1, source_target_pairs={{2,0},{3,1},{4,2},{5,3},{6,4},{7,5},{10,8},{11,9},{12,10},{13,11},... | collective-permute-start | bytes 786440 | tf_op jit(solution)/shard_map/ppermute | solution.py:217
  47.0 12.1 %collective-permute-start.19 = (bf16[128,1024]{1,0:T(8,128)(2,1)S(1)}, bf16[128,1024]{1,0:T(8,128)(2,1)S(1)}, u32[]{:S(2)}, u32[]{:S(2)}) collective-permute-start(bf16[128,1024]{1,0:T(8,128)(2,1)S(1)} %sink.7.refs_4_), channel_id=1, source_target_pairs={{2,0},{3,1},{4,2},{5,3},{6,4},{7,5},{10,8},{11,9},{12,10},{13,11},... | collective-permute-start | bytes 786440 | tf_op jit(solution)/shard_map/ppermute | solution.py:217
  50.2 3.6 %collective-permute-start.23 = (f32[2,256]{1,0:T(2,128)S(1)}, f32[2,256]{1,0:T(2,128)S(1)}, u32[]{:S(2)}, u32[]{:S(2)}) collective-permute-start(f32[2,256]{1,0:T(2,128)S(1)} %add.8.refs_0_), channel_id=1, source_target_pairs={{0,8},{8,0},{16,24},{24,16},{1,9},{9,1},{17,25},{25,17},{2,10},{10... | collective-permute-start | bytes 6152 | tf_op jit(solution)/shard_map/ppermute | solution.py:217
  53.8 3.6 %collective-permute-start.24 = (f32[2,256]{1,0:T(2,128)S(1)}, f32[2,256]{1,0:T(2,128)S(1)}, u32[]{:S(2)}, u32[]{:S(2)}) collective-permute-start(f32[2,256]{1,0:T(2,128)S(1)} %add.9.refs_5_), channel_id=1, source_target_pairs={{0,16},{8,24},{16,0},{24,8},{1,17},{9,25},{17,1},{25,9},{2,18},{10... | collective-permute-start | bytes 6152 | tf_op jit(solution)/shard_map/ppermute | solution.py:217

commit v14 on v13

--- a/solution.py
+++ b/solution.py
@@ -217,12 +217,12 @@
     return lax.ppermute(field, axis, [(i, target(i)) for i in range(size) if 0 <= target(i) < size])
 
 
-def up(field):
-    return move(field, "ctx", lambda i: i + 2)
-
-
-def down(field):
-    return move(field, "ctx", lambda i: i - 2)
+def up(field, lowest=0):
+    return move(field, "ctx", lambda i: i + 2 if i >= 2 * lowest else -1)
+
+
+def down(field, lowest=0):
+    return move(field, "ctx", lambda i: i - 2 if i - 2 >= 2 * lowest else -1)
 
 
 def swap(field):
@@ -310,7 +310,7 @@
         made = dict(zip(outs, call(body, "climb", ins, outs, after, cost=10**9 * steps[0])))
         for step in steps:
             if step < amount:
-                arrived = up(made[f"rise{step}"])
+                arrived = up(made[f"rise{step}"], 0 if step + LAG < amount else 1)
                 ahead = 0
                 if step + LAG < amount:
                     near[step + LAG] = (arrived, 0)
@@ -348,7 +348,7 @@
                     ref["out"][:, mine + half.start : mine + half.stop] = total.astype(BF16)
 
         (total,) = call(body, "sink", ins, dict(out=shape(rows, mine + below)), after)
-        sunk[step] = down(total)
+        sunk[step] = down(total, 0 if older else 1)
         return total
 
     made, gains, last, token = [], [], [], []

time: 60.4 us -> 60 us (level)
  starting transfers between devices: 35.9 us -> 34.1 us
  waiting for transfers between devices: 14 us -> 15.4 us
    ppermute x26, starting transfers between devices: 35.9 us -> 34.1 us  [move(): lax.ppermute(field, axis, [(i, target(i)) for i in range(size) if 0 <= ta...]
    ppermute x26, waiting for transfers between devices: 14 us -> 15.4 us  [move(): lax.ppermute(field, axis, [(i, target(i)) for i in range(size) if 0 <= ta...]
  transfers between devices with their start and end apart: 26 -> 26, of which waited for: 13 -> 11; matrix products, arithmetic and copies ran while one was open for 0% -> 0% of each run, Pallas kernels for 12% -> 12%
where the time goes in v14:
time: 60 us; the launch traced here: 59.6 us
  starting transfers between devices  34.1 us (57%)
  waiting for transfers between devices  15.4 us (26%)
  Pallas kernels  9.14 us (15%)
  between operations  0.88 us (1%)
    ppermute x26, starting transfers between devices, move(): lax.ppermute(field, axis, [(i, target(i)) for i in range(size) if 0 <= ta...  34.1 us
    ppermute x26, waiting for transfers between devices, move(): lax.ppermute(field, axis, [(i, target(i)) for i in range(size) if 0 <= ta...  15.4 us
    pallas_call x21, Pallas kernels, call(): pl.pallas_call(kernel, out_shape=list(outs.values()), in_specs=specs, out...  9.14 us
  transfers between devices with their start and end apart: 26, of which 11 were waited for; matrix products, arithmetic and copies ran while one was open for 0% of the time, Pallas kernels for 12%

profile of v14, /device:TPU:0, one launch (start us, length us, event | category | flops | bytes accessed | tf_op | source)
XLA Modules:
  0.0 59.6 jit_solution(3279595492602131410)
XLA Ops:
  0.6 0.9 %payload.2.refs_5_.refs_1_.refs_3_.refs_0_ = bf16[128,1024]{1,0:T(8,128)(2,1)S(1)} custom-call(bf16[1,128,1024]{2,1,0:T(8,128)(2,1)} %refs_0_.3, bf16[1,128,1024]{2,1,0:T(8,128)(2,1)} %refs_1_.5), custom_call_target="tpu_custom_call" | custom-call | bytes 1 | tf_op jit(solution)/shard_map/payload/pallas_call | solution.py:38
  1.6 4.9 %collective-permute-start = (bf16[128,1024]{1,0:T(8,128)(2,1)S(1)}, bf16[128,1024]{1,0:T(8,128)(2,1)S(1)}, u32[]{:S(2)}, u32[]{:S(2)}) collective-permute-start(bf16[128,1024]{1,0:T(8,128)(2,1)S(1)} %payload.2.refs_5_.refs_1_.refs_3_.refs_0_), channel_id=1, source_target_pairs={{0,2},{1,3},{2,4},{3,5},{4,6},{5,7},{8,10},{9,11},{10,12},{11,13},... | collective-permute-start | bytes 786440 | tf_op jit(solution)/shard_map/ppermute | solution.py:217
  6.5 1.0 %payload.3 = (bf16[128,1024]{1,0:T(8,128)(2,1)S(1)}, s32[1,1024]{1,0:T(1,128)S(1)}, f32[1,256]{1,0:T(1,128)S(1)}, f32[1,256]{1,0:T(1,128)S(1)}) custom-call(bf16[1,128,1024]{2,1,0:T(8,128)(2,1)} %refs_0_.3, bf16[1,128,1024]{2,1,0:T(8,128)(2,1)} %refs_1_.5, s32[1,1024]{1,0:T(1,128)} %refs_2_.3, f32[1,256]{1,0:T(1,128)} %bitcast.4, f32[1,256]{1,0:T(1,128)} %bitcast.5, ...), custom_call_target="tpu_custom_call" | custom-call | bytes 1 | tf_op jit(solution)/shard_map/payload/pallas_call | solution.py:38
  7.6 3.5 %collective-permute-start.3 = (bf16[128,1024]{1,0:T(8,128)(2,1)S(1)}, bf16[128,1024]{1,0:T(8,128)(2,1)S(1)}, u32[]{:S(2)}, u32[]{:S(2)}) collective-permute-start(bf16[128,1024]{1,0:T(8,128)(2,1)S(1)} %get-tuple-element.47.refs_1_.refs_3_.refs_0_), channel_id=1, source_target_pairs={{0,2},{1,3},{2,4},{3,5},{4,6},{5,7},{8,10},{9,11},{10,12},{11,13},... | collective-permute-start | bytes 786440 | tf_op jit(solution)/shard_map/ppermute | solution.py:217
  11.1 2.2 %collective-permute-done.refs_0_.refs_5_ = bf16[128,1024]{1,0:T(8,128)(2,1)S(1)} collective-permute-done((bf16[128,1024]{1,0:T(8,128)(2,1)S(1)}, bf16[128,1024]{1,0:T(8,128)(2,1)S(1)}, u32[]{:S(2)}, u32[]{:S(2)}) %collective-permute-start) | collective-permute-done | bytes 262176 | tf_op jit(solution)/shard_map/ppermute | solution.py:217
  13.3 0.7 %collective-permute-start.2 = (bf16[128,1024]{1,0:T(8,128)(2,1)S(1)}, bf16[128,1024]{1,0:T(8,128)(2,1)S(1)}, u32[]{:S(2)}, u32[]{:S(2)}) collective-permute-start(bf16[128,1024]{1,0:T(8,128)(2,1)S(1)} %get-tuple-element.46.refs_2_), channel_id=1, source_target_pairs={{2,4},{3,5},{4,6},{5,7},{10,12},{11,13},{12,14},{13,15},{18,20},{1... | collective-permute-start | bytes 786440 | tf_op jit(solution)/shard_map/ppermute | solution.py:217
  14.0 3.7 %collective-permute-done.3.refs_0_.refs_5_ = bf16[128,1024]{1,0:T(8,128)(2,1)S(1)} collective-permute-done((bf16[128,1024]{1,0:T(8,128)(2,1)S(1)}, bf16[128,1024]{1,0:T(8,128)(2,1)S(1)}, u32[]{:S(2)}, u32[]{:S(2)}) %collective-permute-start.3) | collective-permute-done | bytes 262176 | tf_op jit(solution)/shard_map/ppermute | solution.py:217
  17.8 0.8 %collective-permute-start.7 = (bf16[128,1024]{1,0:T(8,128)(2,1)S(1)}, bf16[128,1024]{1,0:T(8,128)(2,1)S(1)}, u32[]{:S(2)}, u32[]{:S(2)}) collective-permute-start(bf16[128,1024]{1,0:T(8,128)(2,1)S(1)} %get-tuple-element.48.refs_2_), channel_id=1, source_target_pairs={{2,4},{3,5},{4,6},{5,7},{10,12},{11,13},{12,14},{13,15},{18,20},{1... | collective-permute-start | bytes 786440 | tf_op jit(solution)/shard_map/ppermute | solution.py:217
  18.7 0.5 collective-permute-start.5
  19.3 0.8 %collective-permute-done.4.refs_7_ = bf16[128,512]{1,0:T(8,128)(2,1)S(1)} collective-permute-done((bf16[128,512]{1,0:T(8,128)(2,1)S(1)}, bf16[128,512]{1,0:T(8,128)(2,1)S(1)}, u32[]{:S(2)}, u32[]{:S(2)}) %collective-permute-start.4) | collective-permute-done | bytes 131104 | tf_op jit(solution)/shard_map/ppermute | solution.py:217
  20.2 1.9 %attend.2 = (bf16[128,1024]{1,0:T(8,128)(2,1)S(1)}, bf16[128,1024]{1,0:T(8,128)(2,1)S(1)}, f32[128,1024]{1,0:T(8,128)S(1)}, f32[128,1024]{1,0:T(8,128)S(1)}, f32...) custom-call(s32[1,1024]{1,0:T(1,128)S(1)} %get-tuple-element.44.refs, ...), custom_call_target="tpu_custom_call" | custom-call | bytes 1 | tf_op jit(solution)/shard_map/attend/pallas_call | solution.py:38
  22.1 0.4 collective-permute-start.10
  22.7 0.4 collective-permute-start.8
  23.9 0.7 %collective-permute-start.17 = (bf16[128,1024]{1,0:T(8,128)(2,1)S(1)}, bf16[128,1024]{1,0:T(8,128)(2,1)S(1)}, u32[]{:S(2)}, u32[]{:S(2)}) collective-permute-start(bf16[128,1024]{1,0:T(8,128)(2,1)S(1)} %sink.4.refs_11_.refs_3_), channel_id=1, source_target_pairs={{4,2},{5,3},{6,4},{7,5},{12,10},{13,11},{14,12},{15,13},{20,18},{2... | collective-permute-start | bytes 786440 | tf_op jit(solution)/shard_map/ppermute | solution.py:217
  24.6 1.9 %attend.3 = (bf16[128,1024]{1,0:T(8,128)(2,1)S(1)}, bf16[128,1024]{1,0:T(8,128)(2,1)S(1)}, f32[128,1024]{1,0:T(8,128)S(1)}, f32[128,1024]{1,0:T(8,128)S(1)}, f32...) custom-call(s32[1,1024]{1,0:T(1,128)S(1)} %get-tuple-element.44.refs, ...), custom_call_target="tpu_custom_call" | custom-call | bytes 1 | tf_op jit(solution)/shard_map/attend/pallas_call | solution.py:38
  26.8 0.3 collective-permute-start.13
  27.3 1.0 %collective-permute-done.14.refs_1_ = f32[2,256]{1,0:T(2,128)S(1)} collective-permute-done((f32[2,256]{1,0:T(2,128)S(1)}, f32[2,256]{1,0:T(2,128)S(1)}, u32[]{:S(2)}, u32[]{:S(2)}) %collective-permute-start.14) | collective-permute-done | bytes 2080 | tf_op jit(solution)/shard_map/ppermute | solution.py:217
  28.6 0.7 %collective-permute-start.15 = (bf16[128,1024]{1,0:T(8,128)(2,1)S(1)}, bf16[128,1024]{1,0:T(8,128)(2,1)S(1)}, u32[]{:S(2)}, u32[]{:S(2)}) collective-permute-start(bf16[128,1024]{1,0:T(8,128)(2,1)S(1)} %sink.5.refs_5_.refs_1_), channel_id=1, source_target_pairs={{4,2},{5,3},{6,4},{7,5},{12,10},{13,11},{14,12},{15,13},{20,18},{2... | collective-permute-start | bytes 786440 | tf_op jit(solution)/shard_map/ppermute | solution.py:217
  29.3 8.9 %collective-permute-start.20 = (f32[2,256]{1,0:T(2,128)S(1)}, f32[2,256]{1,0:T(2,128)S(1)}, u32[]{:S(2)}, u32[]{:S(2)}) collective-permute-start(f32[2,256]{1,0:T(2,128)S(1)} %add.7.refs_0_), channel_id=1, source_target_pairs={{0,2},{1,3},{2,0},{3,1},{4,6},{5,7},{6,4},{7,5},{8,10},{9,11},{10,... | collective-permute-start | bytes 6152 | tf_op jit(solution)/shard_map/ppermute | solution.py:217
  38.1 5.2 %collective-permute-start.21 = (f32[2,256]{1,0:T(2,128)S(1)}, f32[2,256]{1,0:T(2,128)S(1)}, u32[]{:S(2)}, u32[]{:S(2)}) collective-permute-start(f32[2,256]{1,0:T(2,128)S(1)} %add.7.refs_0_), channel_id=1, source_target_pairs={{0,4},{1,5},{2,6},{3,7},{4,0},{5,1},{6,2},{7,3},{8,12},{9,13},{10,... | collective-permute-start | bytes 6152 | tf_op jit(solution)/shard_map/ppermute | solution.py:217
  43.5 1.3 %collective-permute-start.25 = (bf16[128,1024]{1,0:T(8,128)(2,1)S(1)}, bf16[128,1024]{1,0:T(8,128)(2,1)S(1)}, u32[]{:S(2)}, u32[]{:S(2)}) collective-permute-start(bf16[128,1024]{1,0:T(8,128)(2,1)S(1)} %sink.6.refs_5_), channel_id=1, source_target_pairs={{2,0},{3,1},{4,2},{5,3},{6,4},{7,5},{10,8},{11,9},{12,10},{13,11},... | collective-permute-start | bytes 786440 | tf_op jit(solution)/shard_map/ppermute | solution.py:217
  44.9 1.3 %collective-permute-start.19 = (bf16[128,1024]{1,0:T(8,128)(2,1)S(1)}, bf16[128,1024]{1,0:T(8,128)(2,1)S(1)}, u32[]{:S(2)}, u32[]{:S(2)}) collective-permute-start(bf16[128,1024]{1,0:T(8,128)(2,1)S(1)} %sink.7.refs_4_), channel_id=1, source_target_pairs={{2,0},{3,1},{4,2},{5,3},{6,4},{7,5},{10,8},{11,9},{12,10},{13,11},... | collective-permute-start | bytes 786440 | tf_op jit(solution)/shard_map/ppermute | solution.py:217
  46.2 2.0 %collective-permute-done.21.refs_2_ = f32[2,256]{1,0:T(2,128)S(1)} collective-permute-done((f32[2,256]{1,0:T(2,128)S(1)}, f32[2,256]{1,0:T(2,128)S(1)}, u32[]{:S(2)}, u32[]{:S(2)}) %collective-permute-start.21) | collective-permute-done | bytes 2080 | tf_op jit(solution)/shard_map/ppermute | solution.py:217
  48.2 1.6 %collective-permute-done.22.refs_3_ = f32[2,256]{1,0:T(2,128)S(1)} collective-permute-done((f32[2,256]{1,0:T(2,128)S(1)}, f32[2,256]{1,0:T(2,128)S(1)}, u32[]{:S(2)}, u32[]{:S(2)}) %collective-permute-start.22) | collective-permute-done | bytes 2080 | tf_op jit(solution)/shard_map/ppermute | solution.py:217
  49.8 1.5 %collective-permute-start.23 = (f32[2,256]{1,0:T(2,128)S(1)}, f32[2,256]{1,0:T(2,128)S(1)}, u32[]{:S(2)}, u32[]{:S(2)}) collective-permute-start(f32[2,256]{1,0:T(2,128)S(1)} %add.8.refs_0_), channel_id=1, source_target_pairs={{0,8},{8,0},{16,24},{24,16},{1,9},{9,1},{17,25},{25,17},{2,10},{10... | collective-permute-start | bytes 6152 | tf_op jit(solution)/shard_map/ppermute | solution.py:217
  51.3 1.0 %assemble.1 = (bf16[1,128,2048]{2,1,0:T(8,128)(2,1)}, bf16[1,128,2048]{2,1,0:T(8,128)(2,1)}) custom-call(bf16[128,1024]{1,0:T(8,128)(2,1)S(1)} %get-tuple-element.53.refs_0_, bf16[128,1024]{1,0:T(8,128)(2,1)S(1)} %get-tuple-element.61.refs_1_, bf16[128,1024]{1,0:T(8,128)(2,1)S(1)} %get-tuple-element.62.refs_2_, ...), custom_call_target="tpu_custom_call" | custom-call | bytes 1 | tf_op jit(solution)/shard_map/assemble/pallas_call | solution.py:38
  52.3 1.1 %collective-permute-done.23.refs_1_ = f32[2,256]{1,0:T(2,128)S(1)} collective-permute-done((f32[2,256]{1,0:T(2,128)S(1)}, f32[2,256]{1,0:T(2,128)S(1)}, u32[]{:S(2)}, u32[]{:S(2)}) %collective-permute-start.23) | collective-permute-done | bytes 2080 | tf_op jit(solution)/shard_map/ppermute | solution.py:217
  53.4 1.5 %collective-permute-start.24 = (f32[2,256]{1,0:T(2,128)S(1)}, f32[2,256]{1,0:T(2,128)S(1)}, u32[]{:S(2)}, u32[]{:S(2)}) collective-permute-start(f32[2,256]{1,0:T(2,128)S(1)} %add.9.refs_5_), channel_id=1, source_target_pairs={{0,16},{8,24},{16,0},{24,8},{1,17},{9,25},{17,1},{25,9},{2,18},{10... | collective-permute-start | bytes 6152 | tf_op jit(solution)/shard_map/ppermute | solution.py:217
  54.9 0.9 %finish.2 = (bf16[1,128,1024]{2,1,0:T(8,128)(2,1)}, bf16[1,128,1024]{2,1,0:T(8,128)(2,1)}) custom-call(bf16[128,1024]{1,0:T(8,128)(2,1)S(1)} %payload.2.refs_5_.refs_1_.refs_3_.refs_0_, f32[1,256]{1,0:T(1,128)S(1)} %get-tuple-element.52.refs_10_.refs_1_, f32[128,1024]{1,0:T(8,128)S(1)} %get-tuple-element.75.refs_2_, ...), custom_call_target="tpu_custom_call" | custom-call | flops 2147483648 | bytes 1 | tf_op jit(solution)/shard_map/finish/pallas_call | solution.py:38
  55.8 1.2 %collective-permute-done.24.refs_6_ = f32[2,256]{1,0:T(2,128)S(1)} collective-permute-done((f32[2,256]{1,0:T(2,128)S(1)}, f32[2,256]{1,0:T(2,128)S(1)}, u32[]{:S(2)}, u32[]{:S(2)}) %collective-permute-start.24) | collective-permute-done | bytes 2080 | tf_op jit(solution)/shard_map/ppermute | solution.py:217
  57.0 1.7 %collective-permute-done.19.refs_4_ = bf16[128,1024]{1,0:T(8,128)(2,1)S(1)} collective-permute-done((bf16[128,1024]{1,0:T(8,128)(2,1)S(1)}, bf16[128,1024]{1,0:T(8,128)(2,1)S(1)}, u32[]{:S(2)}, u32[]{:S(2)}) %collective-permute-start.19) | collective-permute-done | bytes 262176 | tf_op jit(solution)/shard_map/ppermute | solution.py:217
  58.6 0.9 %finish.3 = (bf16[1,128,1024]{2,1,0:T(8,128)(2,1)}, bf16[1,128,1024]{2,1,0:T(8,128)(2,1)}, f32[1,256]{1,0:T(1,128)}, f32[1,256]{1,0:T(1,128)}) custom-call(bf16[128,1024]{1,0:T(8,128)(2,1)S(1)} %get-tuple-element.47.refs_1_.refs_3_.refs_0_, f32[1,256]{1,0:T(1,128)S(1)} %get-tuple-element.52.refs_10_.refs_1_, ...), custom_call_target="tpu_custom_call", output_to_operand_aliasing={{0}: (7, {}), {1}: (8, {})} | custom-call | flops 4294967296 | bytes 1 | tf_op jit(solution)/shard_map/finish/pallas_call | solution.py:38
  (45 shorter events, 2.6 us)
Async XLA Ops:
  1.6 11.6 %collective-permute-start = (bf16[128,1024]{1,0:T(8,128)(2,1)S(1)}, bf16[128,1024]{1,0:T(8,128)(2,1)S(1)}, u32[]{:S(2)}, u32[]{:S(2)}) collective-permute-start(bf16[128,1024]{1,0:T(8,128)(2,1)S(1)} %payload.2.refs_5_.refs_1_.refs_3_.refs_0_), channel_id=1, source_target_pairs={{0,2},{1,3},{2,4},{3,5},{4,6},{5,7},{8,10},{9,11},{10,12},{11,13},... | collective-permute-start | bytes 786440 | tf_op jit(solution)/shard_map/ppermute | solution.py:217
  7.6 10.1 %collective-permute-start.3 = (bf16[128,1024]{1,0:T(8,128)(2,1)S(1)}, bf16[128,1024]{1,0:T(8,128)(2,1)S(1)}, u32[]{:S(2)}, u32[]{:S(2)}) collective-permute-start(bf16[128,1024]{1,0:T(8,128)(2,1)S(1)} %get-tuple-element.47.refs_1_.refs_3_.refs_0_), channel_id=1, source_target_pairs={{0,2},{1,3},{2,4},{3,5},{4,6},{5,7},{8,10},{9,11},{10,12},{11,13},... | collective-permute-start | bytes 786440 | tf_op jit(solution)/shard_map/ppermute | solution.py:217
  13.3 5.3 %collective-permute-start.2 = (bf16[128,1024]{1,0:T(8,128)(2,1)S(1)}, bf16[128,1024]{1,0:T(8,128)(2,1)S(1)}, u32[]{:S(2)}, u32[]{:S(2)}) collective-permute-start(bf16[128,1024]{1,0:T(8,128)(2,1)S(1)} %get-tuple-element.46.refs_2_), channel_id=1, source_target_pairs={{2,4},{3,5},{4,6},{5,7},{10,12},{11,13},{12,14},{13,15},{18,20},{1... | collective-permute-start | bytes 786440 | tf_op jit(solution)/shard_map/ppermute | solution.py:217
  13.9 5.3 %collective-permute-start.1 = (bf16[128,1024]{1,0:T(8,128)(2,1)S(1)}, bf16[128,1024]{1,0:T(8,128)(2,1)S(1)}, u32[]{:S(2)}, u32[]{:S(2)}) collective-permute-start(bf16[128,1024]{1,0:T(8,128)(2,1)S(1)} %get-tuple-element.45), channel_id=1, source_target_pairs={{0,1},{1,0},{2,3},{3,2},{4,5},{5,4},{6,7},{7,6},{8,9},{9,8},{10,11... | collective-permute-start | bytes 786440 | tf_op jit(solution)/shard_map/ppermute | solution.py:217
  17.7 2.5 %copy-start = (bf16[1,128,2048]{2,1,0:T(8,128)(2,1)S(1)}, bf16[1,128,2048]{2,1,0:T(8,128)(2,1)}, u32[]{:S(2)}) copy-start(bf16[1,128,2048]{2,1,0:T(8,128)(2,1)} %refs_1_.7) | copy-start | bytes 1572868
  17.7 2.5 %copy-start.1 = (bf16[1,128,2048]{2,1,0:T(8,128)(2,1)S(1)}, bf16[1,128,2048]{2,1,0:T(8,128)(2,1)}, u32[]{:S(2)}) copy-start(bf16[1,128,2048]{2,1,0:T(8,128)(2,1)} %refs_2_.5) | copy-start | bytes 1572868
  17.8 4.9 %collective-permute-start.7 = (bf16[128,1024]{1,0:T(8,128)(2,1)S(1)}, bf16[128,1024]{1,0:T(8,128)(2,1)S(1)}, u32[]{:S(2)}, u32[]{:S(2)}) collective-permute-start(bf16[128,1024]{1,0:T(8,128)(2,1)S(1)} %get-tuple-element.48.refs_2_), channel_id=1, source_target_pairs={{2,4},{3,5},{4,6},{5,7},{10,12},{11,13},{12,14},{13,15},{18,20},{1... | collective-permute-start | bytes 786440 | tf_op jit(solution)/shard_map/ppermute | solution.py:217
  18.6 1.4 %collective-permute-start.4 = (bf16[128,512]{1,0:T(8,128)(2,1)S(1)}, bf16[128,512]{1,0:T(8,128)(2,1)S(1)}, u32[]{:S(2)}, u32[]{:S(2)}) collective-permute-start(bf16[128,512]{1,0:T(8,128)(2,1)S(1)} %get-tuple-element.49.refs_2_), channel_id=1, source_target_pairs={{0,1},{1,0},{2,3},{3,2},{4,5},{5,4},{6,7},{7,6},{8,9},{9,8},{10,11... | collective-permute-start | bytes 393224 | tf_op jit(solution)/shard_map/ppermute | solution.py:217
  18.7 1.5 %collective-permute-start.5 = (bf16[128,512]{1,0:T(8,128)(2,1)S(1)}, bf16[128,512]{1,0:T(8,128)(2,1)S(1)}, u32[]{:S(2)}, u32[]{:S(2)}) collective-permute-start(bf16[128,512]{1,0:T(8,128)(2,1)S(1)} %get-tuple-element.50), channel_id=1, source_target_pairs={{0,1},{1,0},{2,3},{3,2},{4,5},{5,4},{6,7},{7,6},{8,9},{9,8},{10,11... | collective-permute-start | bytes 393224 | tf_op jit(solution)/shard_map/ppermute | solution.py:217
  19.2 5.4 %collective-permute-start.6 = (bf16[128,1024]{1,0:T(8,128)(2,1)S(1)}, bf16[128,1024]{1,0:T(8,128)(2,1)S(1)}, u32[]{:S(2)}, u32[]{:S(2)}) collective-permute-start(bf16[128,1024]{1,0:T(8,128)(2,1)S(1)} %get-tuple-element.54), channel_id=1, source_target_pairs={{0,1},{1,0},{2,3},{3,2},{4,5},{5,4},{6,7},{7,6},{8,9},{9,8},{10,11... | collective-permute-start | bytes 786440 | tf_op jit(solution)/shard_map/ppermute | solution.py:217
  22.1 1.4 %collective-permute-start.10 = (bf16[128,512]{1,0:T(8,128)(2,1)S(1)}, bf16[128,512]{1,0:T(8,128)(2,1)S(1)}, u32[]{:S(2)}, u32[]{:S(2)}) collective-permute-start(bf16[128,512]{1,0:T(8,128)(2,1)S(1)} %get-tuple-element.59), channel_id=1, source_target_pairs={{0,1},{1,0},{2,3},{3,2},{4,5},{5,4},{6,7},{7,6},{8,9},{9,8},{10,11... | collective-permute-start | bytes 393224 | tf_op jit(solution)/shard_map/ppermute | solution.py:217
  22.5 1.4 %collective-permute-start.11 = (bf16[128,512]{1,0:T(8,128)(2,1)S(1)}, bf16[128,512]{1,0:T(8,128)(2,1)S(1)}, u32[]{:S(2)}, u32[]{:S(2)}) collective-permute-start(bf16[128,512]{1,0:T(8,128)(2,1)S(1)} %get-tuple-element.60), channel_id=1, source_target_pairs={{0,1},{1,0},{2,3},{3,2},{4,5},{5,4},{6,7},{7,6},{8,9},{9,8},{10,11... | collective-permute-start | bytes 393224 | tf_op jit(solution)/shard_map/ppermute | solution.py:217
  22.7 1.9 %collective-permute-start.8 = (bf16[128,512]{1,0:T(8,128)(2,1)S(1)}, bf16[128,512]{1,0:T(8,128)(2,1)S(1)}, u32[]{:S(2)}, u32[]{:S(2)}) collective-permute-start(bf16[128,512]{1,0:T(8,128)(2,1)S(1)} %get-tuple-element.56), channel_id=1, source_target_pairs={{0,1},{1,0},{2,3},{3,2},{4,5},{5,4},{6,7},{7,6},{8,9},{9,8},{10,11... | collective-permute-start | bytes 393224 | tf_op jit(solution)/shard_map/ppermute | solution.py:217
  23.1 1.5 %collective-permute-start.9 = (bf16[128,512]{1,0:T(8,128)(2,1)S(1)}, bf16[128,512]{1,0:T(8,128)(2,1)S(1)}, u32[]{:S(2)}, u32[]{:S(2)}) collective-permute-start(bf16[128,512]{1,0:T(8,128)(2,1)S(1)} %get-tuple-element.57), channel_id=1, source_target_pairs={{0,1},{1,0},{2,3},{3,2},{4,5},{5,4},{6,7},{7,6},{8,9},{9,8},{10,11... | collective-permute-start | bytes 393224 | tf_op jit(solution)/shard_map/ppermute | solution.py:217
  23.5 14.6 %collective-permute-start.18 = (bf16[128,1024]{1,0:T(8,128)(2,1)S(1)}, bf16[128,1024]{1,0:T(8,128)(2,1)S(1)}, u32[]{:S(2)}, u32[]{:S(2)}) collective-permute-start(bf16[128,1024]{1,0:T(8,128)(2,1)S(1)} %get-tuple-element.71), channel_id=1, source_target_pairs={{0,1},{1,0},{2,3},{3,2},{4,5},{5,4},{6,7},{7,6},{8,9},{9,8},{10,11... | collective-permute-start | bytes 786440 | tf_op jit(solution)/shard_map/ppermute | solution.py:217
  23.9 19.4 %collective-permute-start.17 = (bf16[128,1024]{1,0:T(8,128)(2,1)S(1)}, bf16[128,1024]{1,0:T(8,128)(2,1)S(1)}, u32[]{:S(2)}, u32[]{:S(2)}) collective-permute-start(bf16[128,1024]{1,0:T(8,128)(2,1)S(1)} %sink.4.refs_11_.refs_3_), channel_id=1, source_target_pairs={{4,2},{5,3},{6,4},{7,5},{12,10},{13,11},{14,12},{15,13},{20,18},{2... | collective-permute-start | bytes 786440 | tf_op jit(solution)/shard_map/ppermute | solution.py:217
  26.5 1.9 %collective-permute-start.12 = (bf16[128,512]{1,0:T(8,128)(2,1)S(1)}, bf16[128,512]{1,0:T(8,128)(2,1)S(1)}, u32[]{:S(2)}, u32[]{:S(2)}) collective-permute-start(bf16[128,512]{1,0:T(8,128)(2,1)S(1)} %get-tuple-element.66), channel_id=1, source_target_pairs={{0,1},{1,0},{2,3},{3,2},{4,5},{5,4},{6,7},{7,6},{8,9},{9,8},{10,11... | collective-permute-start | bytes 393224 | tf_op jit(solution)/shard_map/ppermute | solution.py:217
  26.8 1.7 %collective-permute-start.13 = (bf16[128,512]{1,0:T(8,128)(2,1)S(1)}, bf16[128,512]{1,0:T(8,128)(2,1)S(1)}, u32[]{:S(2)}, u32[]{:S(2)}) collective-permute-start(bf16[128,512]{1,0:T(8,128)(2,1)S(1)} %get-tuple-element.67), channel_id=1, source_target_pairs={{0,1},{1,0},{2,3},{3,2},{4,5},{5,4},{6,7},{7,6},{8,9},{9,8},{10,11... | collective-permute-start | bytes 393224 | tf_op jit(solution)/shard_map/ppermute | solution.py:217
  27.1 1.2 %collective-permute-start.14 = (f32[2,256]{1,0:T(2,128)S(1)}, f32[2,256]{1,0:T(2,128)S(1)}, u32[]{:S(2)}, u32[]{:S(2)}) collective-permute-start(f32[2,256]{1,0:T(2,128)S(1)} %add.5.refs_0_), channel_id=1, source_target_pairs={{0,1},{1,0},{2,3},{3,2},{4,5},{5,4},{6,7},{7,6},{8,9},{9,8},{10,11... | collective-permute-start | bytes 6152 | tf_op jit(solution)/shard_map/ppermute | solution.py:217
  28.3 15.2 %collective-permute-start.16 = (bf16[128,1024]{1,0:T(8,128)(2,1)S(1)}, bf16[128,1024]{1,0:T(8,128)(2,1)S(1)}, u32[]{:S(2)}, u32[]{:S(2)}) collective-permute-start(bf16[128,1024]{1,0:T(8,128)(2,1)S(1)} %get-tuple-element.69), channel_id=1, source_target_pairs={{0,1},{1,0},{2,3},{3,2},{4,5},{5,4},{6,7},{7,6},{8,9},{9,8},{10,11... | collective-permute-start | bytes 786440 | tf_op jit(solution)/shard_map/ppermute | solution.py:217
  28.6 16.2 %collective-permute-start.15 = (bf16[128,1024]{1,0:T(8,128)(2,1)S(1)}, bf16[128,1024]{1,0:T(8,128)(2,1)S(1)}, u32[]{:S(2)}, u32[]{:S(2)}) collective-permute-start(bf16[128,1024]{1,0:T(8,128)(2,1)S(1)} %sink.5.refs_5_.refs_1_), channel_id=1, source_target_pairs={{4,2},{5,3},{6,4},{7,5},{12,10},{13,11},{14,12},{15,13},{20,18},{2... | collective-permute-start | bytes 786440 | tf_op jit(solution)/shard_map/ppermute | solution.py:217
  29.3 16.9 %collective-permute-start.20 = (f32[2,256]{1,0:T(2,128)S(1)}, f32[2,256]{1,0:T(2,128)S(1)}, u32[]{:S(2)}, u32[]{:S(2)}) collective-permute-start(f32[2,256]{1,0:T(2,128)S(1)} %add.7.refs_0_), channel_id=1, source_target_pairs={{0,2},{1,3},{2,0},{3,1},{4,6},{5,7},{6,4},{7,5},{8,10},{9,11},{10,... | collective-permute-start | bytes 6152 | tf_op jit(solution)/shard_map/ppermute | solution.py:217
  38.1 10.1 %collective-permute-start.21 = (f32[2,256]{1,0:T(2,128)S(1)}, f32[2,256]{1,0:T(2,128)S(1)}, u32[]{:S(2)}, u32[]{:S(2)}) collective-permute-start(f32[2,256]{1,0:T(2,128)S(1)} %add.7.refs_0_), channel_id=1, source_target_pairs={{0,4},{1,5},{2,6},{3,7},{4,0},{5,1},{6,2},{7,3},{8,12},{9,13},{10,... | collective-permute-start | bytes 6152 | tf_op jit(solution)/shard_map/ppermute | solution.py:217
  43.3 6.4 %collective-permute-start.22 = (f32[2,256]{1,0:T(2,128)S(1)}, f32[2,256]{1,0:T(2,128)S(1)}, u32[]{:S(2)}, u32[]{:S(2)}) collective-permute-start(f32[2,256]{1,0:T(2,128)S(1)} %add.7.refs_0_), channel_id=1, source_target_pairs={{0,6},{1,7},{2,4},{3,5},{4,2},{5,3},{6,0},{7,1},{8,14},{9,15},{10,... | collective-permute-start | bytes 6152 | tf_op jit(solution)/shard_map/ppermute | solution.py:217
  43.5 11.4 %collective-permute-start.25 = (bf16[128,1024]{1,0:T(8,128)(2,1)S(1)}, bf16[128,1024]{1,0:T(8,128)(2,1)S(1)}, u32[]{:S(2)}, u32[]{:S(2)}) collective-permute-start(bf16[128,1024]{1,0:T(8,128)(2,1)S(1)} %sink.6.refs_5_), channel_id=1, source_target_pairs={{2,0},{3,1},{4,2},{5,3},{6,4},{7,5},{10,8},{11,9},{12,10},{13,11},... | collective-permute-start | bytes 786440 | tf_op jit(solution)/shard_map/ppermute | solution.py:217
  44.9 13.7 %collective-permute-start.19 = (bf16[128,1024]{1,0:T(8,128)(2,1)S(1)}, bf16[128,1024]{1,0:T(8,128)(2,1)S(1)}, u32[]{:S(2)}, u32[]{:S(2)}) collective-permute-start(bf16[128,1024]{1,0:T(8,128)(2,1)S(1)} %sink.7.refs_4_), channel_id=1, source_target_pairs={{2,0},{3,1},{4,2},{5,3},{6,4},{7,5},{10,8},{11,9},{12,10},{13,11},... | collective-permute-start | bytes 786440 | tf_op jit(solution)/shard_map/ppermute | solution.py:217
  49.8 3.6 %collective-permute-start.23 = (f32[2,256]{1,0:T(2,128)S(1)}, f32[2,256]{1,0:T(2,128)S(1)}, u32[]{:S(2)}, u32[]{:S(2)}) collective-permute-start(f32[2,256]{1,0:T(2,128)S(1)} %add.8.refs_0_), channel_id=1, source_target_pairs={{0,8},{8,0},{16,24},{24,16},{1,9},{9,1},{17,25},{25,17},{2,10},{10... | collective-permute-start | bytes 6152 | tf_op jit(solution)/shard_map/ppermute | solution.py:217
  53.4 3.6 %collective-permute-start.24 = (f32[2,256]{1,0:T(2,128)S(1)}, f32[2,256]{1,0:T(2,128)S(1)}, u32[]{:S(2)}, u32[]{:S(2)}) collective-permute-start(f32[2,256]{1,0:T(2,128)S(1)} %add.9.refs_5_), channel_id=1, source_target_pairs={{0,16},{8,24},{16,0},{24,8},{1,17},{9,25},{17,1},{25,9},{2,18},{10... | collective-permute-start | bytes 6152 | tf_op jit(solution)/shard_map/ppermute | solution.py:217

commit v15 on v14

--- a/solution.py
+++ b/solution.py
@@ -83,59 +83,92 @@
     return lax.dot_general(left, right, ((over[:1], over[1:]), ((), ())), preferred_element_type=F32)
 
 
-def attend(
-    first, count, at_own, at_x, at_near, at_far, segments, queries, out_grad, own, across_x, arrived_near, arrived_far,
-    across_k, across_v,    query_gain, key_gain, *rest,
-):
-    attended, query_grad, part_own, part_near, part_far, third_k, third_v, part_next, gains = rest
+def columns_of(index):
+    return slice(index * HEAD_DIM, (index + 1) * HEAD_DIM)
+
+
+def live_pairs(segments, rows, distances):
     position = lax.axis_index("ctx")
-    rows = queries.shape[1]
-    band = (GREACH + 1) * rows
-    gain_q = query_gain[...]
-    gain_k = key_gain[...]
 
     def segment(distance):
         block = position - distance
         first = pl.multiple_of(jnp.maximum(block, 0) * rows, rows)
         return jnp.where(block >= 0, segments[:, pl.ds(first, rows)], -1)
 
-    key_seg = jnp.concatenate([segment(distance) for distance in range(GREACH, -1, -1)], 1)
+    key_seg = jnp.concatenate([segment(distance) for distance in distances], 1)
     query_seg = jnp.broadcast_to(segment(0), (rows, rows)).T[:, :1]
-    back = (
-        lax.broadcasted_iota(jnp.int32, (rows, band), 0)
-        - lax.broadcasted_iota(jnp.int32, (rows, band), 1)
-        + GREACH * rows
-    )
+    span = (rows, len(distances) * rows)
+    back = lax.broadcasted_iota(jnp.int32, span, 0) - lax.broadcasted_iota(jnp.int32, span, 1) + distances[0] * rows
     live = (query_seg == key_seg) & (back >= 0) & (back < WINDOW)
-    live = jnp.concatenate([live] * GROUPS, 0)
+    return jnp.concatenate([live] * GROUPS, 0)
+
+
+def query_rows(field, head):
+    return jnp.concatenate([field[0, :, columns_of(head * GROUPS + g)] for g in range(GROUPS)], 0)
+
+
+def scored(live, queries, grads, keys, values, gain_q, gain_k):
+    k_normed = normalize(keys.astype(F32))[0]
+    k_rounded = (k_normed * gain_k).astype(BF16)
+    weights = jnp.where(live, jnp.exp(dot(queries, k_rounded, (1, 1))), 0.0)
+    return k_normed, k_rounded, weights, dot(grads, values, (1, 1))
+
+
+def normed_queries(queries, head, gain_q):
+    q_normed, q_inverse = normalize(query_rows(queries, head).astype(F32))
+    return q_normed, q_inverse, (q_normed * gain_q * HEAD_DIM ** (-0.5)).astype(BF16)
+
+
+def begin(first, count, places, segments, queries, out_grad, own, across_x, arrived_near, query_gain, key_gain, *outs):
+    live = live_pairs(segments, queries.shape[1], (2, 1, 0))
+    gain_q, gain_k = query_gain[...], key_gain[...]
+    blocks = list(zip((arrived_near, across_x, own), places))
 
     def band_of(index):
+        return jnp.concatenate([field[:, at + index * HEAD_DIM : at + (index + 1) * HEAD_DIM] for field, at in blocks], 0)
+
+    for head in range(count):
+        q_scaled = normed_queries(queries, first + head, gain_q)[2]
+        grads = query_rows(out_grad, first + head)
+        made = scored(live, q_scaled, grads, band_of(head), band_of(count + head), gain_q, gain_k)
+        for out, value in zip(outs, made):
+            share = value.shape[0]
+            out[head * share : (head + 1) * share, :] = value
+
+
+def attend(
+    first, count, places, at_far, segments, queries, out_grad, own, across_x, arrived_near, arrived_far, across_k,
+    across_v, query_gain, key_gain, begun_normed, begun_rounded, begun_weights, begun_dprob, *rest,
+):
+    attended, query_grad, part_own, part_near, part_far, third_k, third_v, part_next, gains = rest
+    rows = queries.shape[1]
+    gain_q, gain_k = query_gain[...], key_gain[...]
+    live = live_pairs(segments, rows, (4, 3))
+    blocks = list(zip((arrived_near, across_x, own), places))
+
+    def far_of(index):
         third = (across_k, 0) if index < count else (across_v, -count * HEAD_DIM)
-        blocks = ((arrived_far, at_far), third, (arrived_near, at_near), (across_x, at_x), (own, at_own))
-        return jnp.concatenate(
-            [field[:, at + index * HEAD_DIM : at + (index + 1) * HEAD_DIM] for field, at in blocks], 0
-        )
-
-    def columns_of(index):
-        return slice(index * HEAD_DIM, (index + 1) * HEAD_DIM)
-
-    def query_rows(field, head):
-        start = (first + head) * GROUPS
-        return jnp.concatenate([field[0, :, columns_of(start + g)] for g in range(GROUPS)], 0)
+        return [field[:, at + index * HEAD_DIM : at + (index + 1) * HEAD_DIM] for field, at in ((arrived_far, at_far), third)]
+
+    def near_of(index):
+        return [field[:, at + index * HEAD_DIM : at + (index + 1) * HEAD_DIM] for field, at in blocks]
+
+    def begun(field, head):
+        share = field.shape[0] // count
+        return field[head * share : (head + 1) * share, :]
 
     heads = range(count)
-    grads = [query_rows(out_grad, head) for head in heads]
-    band_v = [band_of(count + head) for head in heads]
-    q_normed, q_inverse, q_scaled, k_normed, k_rounded, scores = [], [], [], [], [], []
+    grads = [query_rows(out_grad, first + head) for head in heads]
+    band_v = [jnp.concatenate(far_of(count + head) + near_of(count + head), 0) for head in heads]
+    query = [normed_queries(queries, first + head, gain_q) for head in heads]
+    k_normed, k_rounded, weights, dprob = [], [], [], []
     for head in heads:
-        normed, inverse = normalize(query_rows(queries, head).astype(F32))
-        q_normed.append(normed)
-        q_inverse.append(inverse)
-        q_scaled.append((normed * gain_q * HEAD_DIM ** (-0.5)).astype(BF16))
-        k_normed.append(normalize(band_of(head).astype(F32))[0])
-        k_rounded.append((k_normed[head] * gain_k).astype(BF16))
-        scores.append(dot(q_scaled[head], k_rounded[head], (1, 1)))
-    dprob = [dot(grads[head], band_v[head], (1, 1)) for head in heads]
+        far_keys, far_values = (jnp.concatenate(far_of(index), 0) for index in (head, count + head))
+        made = scored(live, query[head][2], grads[head], far_keys, far_values, gain_q, gain_k)
+        k_normed.append(jnp.concatenate([made[0], begun(begun_normed, head)], 0))
+        k_rounded.append(jnp.concatenate([made[1], begun(begun_rounded, head)], 0))
+        weights.append(jnp.concatenate([made[2], begun(begun_weights, head)], 1))
+        dprob.append(jnp.concatenate([made[3], begun(begun_dprob, head)], 1))
 
     def give(parts, at):
         part_far[:, at] = parts[:rows]
@@ -146,8 +179,7 @@
 
     dscore = []
     for head in heads:
-        weights = jnp.where(live, jnp.exp(scores[head]), 0.0)
-        probs = weights * (1.0 / jnp.sum(weights, -1, keepdims=True))
+        probs = weights[head] * (1.0 / jnp.sum(weights[head], -1, keepdims=True))
         probs_low = probs.astype(BF16)
         centre = jnp.sum(probs * dprob[head], -1, keepdims=True)
         dscore.append((probs * (dprob[head] - centre)).astype(BF16))
@@ -158,15 +190,16 @@
     query_gains = jnp.zeros((1, HEAD_DIM), F32)
     key_gains = jnp.zeros((1, HEAD_DIM), F32)
     for head in heads:
-        key_parts = dot(dscore[head], q_scaled[head], (0, 0))
+        q_normed, q_inverse, q_scaled = query[head]
+        key_parts = dot(dscore[head], q_scaled, (0, 0))
         third_k[:, columns_of(head)] = give(key_parts, columns_of(head))
         key_gains = key_gains + jnp.sum(key_parts * k_normed[head], 0, keepdims=True)
         dq = dot(dscore[head], k_rounded[head], (1, 0)) * HEAD_DIM ** (-0.5)
         scaled = dq * gain_q
-        grad = q_inverse[head] * (scaled - q_normed[head] * jnp.mean(scaled * q_normed[head], -1, keepdims=True))
+        grad = q_inverse * (scaled - q_normed * jnp.mean(scaled * q_normed, -1, keepdims=True))
         for g in range(GROUPS):
             query_grad[:, columns_of(head * GROUPS + g)] = grad[g * rows : (g + 1) * rows].astype(BF16)
-        query_gains = query_gains + jnp.sum(dq * q_normed[head], 0, keepdims=True)
+        query_gains = query_gains + jnp.sum(dq * q_normed, 0, keepdims=True)
     gains[0:1, :] = query_gains
     gains[1:2, :] = key_gains
 
@@ -356,17 +389,28 @@
     for step in range(LAG):
         order = climb([step], order)
     for chunk, (first, count) in enumerate(CHUNKS):
-        order = climb([chunk + LAG], order + token)
-        held = (own, next_behind, near, far)
+        tall, square = count * (GREACH - 1) * rows, count * GROUPS * rows
+        held = dict(own=own[chunk], across_x=next_behind[chunk], near=near[chunk])
+        places = [held[key][1] for key in ("near", "across_x", "own")]
+        common = dict(segments=segments, queries=queries, out_grad=out_grad, **{key: held[key][0] for key in held})
+        begun = call(
+            functools.partial(begin, first, count, places),
+            "begin",
+            dict(**common, gain_q=gain_q, gain_k=gain_k),
+            dict(
+                normed=shape(tall, HEAD_DIM, F32), rounded=shape(tall, HEAD_DIM),
+                weights=shape(square, (GREACH - 1) * rows, F32), dprob=shape(square, (GREACH - 1) * rows, F32),
+            ),
+        )
+        order = climb([chunk + LAG], order + token + list(begun[1:2]))
         wide = shape(rows, GROUPS * count * HEAD_DIM)
         whole, low, half = shape(rows, width[chunk], F32), shape(rows, width[chunk]), shape(rows, width[chunk] // 2)
         result = call(
-            functools.partial(attend, first, count, *(place[chunk][1] for place in held)),
+            functools.partial(attend, first, count, places, far[chunk][1]),
             "attend",
             dict(
-                segments=segments, queries=queries, out_grad=out_grad, own=own[chunk][0],
-                **{f"behind{i}": place[chunk][0] for i, place in enumerate(held[1:])},
-                third_k=third_behind[chunk][0], third_v=third_behind[chunk][1], gain_q=gain_q, gain_k=gain_k,
+                **common, far=far[chunk][0], third_k=third_behind[chunk][0], third_v=third_behind[chunk][1],
+                gain_q=gain_q, gain_k=gain_k, **dict(zip(("b0", "b1", "b2", "b3"), begun)),
             ),
             dict(
                 attended=wide, query_grad=wide, own=whole, near=whole, far=whole,

time: 60 us -> 60.5 us (level)
  Pallas kernels: 9.14 us -> 10 us
    pallas_call x21 -> x23, Pallas kernels: 9.14 us -> 10 us  [call(): pl.pallas_call(kernel, out_shape=list(outs.values()), in_specs=specs, out...]
  transfers between devices with their start and end apart: 26 -> 26, of which waited for: 11 -> 11; matrix products, arithmetic and copies ran while one was open for 0% -> 0% of each run, Pallas kernels for 12% -> 14%
where the time goes in v15:
time: 60.5 us; the launch traced here: 60.1 us
  starting transfers between devices  34.3 us (57%)
  waiting for transfers between devices  14.8 us (24%)
  Pallas kernels  10 us (17%)
  between operations  0.89 us (1%)
    ppermute x26, starting transfers between devices, move(): lax.ppermute(field, axis, [(i, target(i)) for i in range(size) if 0 <= ta...  34.3 us
    ppermute x26, waiting for transfers between devices, move(): lax.ppermute(field, axis, [(i, target(i)) for i in range(size) if 0 <= ta...  14.8 us
    pallas_call x23, Pallas kernels, call(): pl.pallas_call(kernel, out_shape=list(outs.values()), in_specs=specs, out...  10 us
  transfers between devices with their start and end apart: 26, of which 11 were waited for; matrix products, arithmetic and copies ran while one was open for 0% of the time, Pallas kernels for 14%

profile of v15, /device:TPU:0, one launch (start us, length us, event | category | flops | bytes accessed | tf_op | source)
XLA Modules:
  0.0 60.1 jit_solution(7218429569098148664)
XLA Ops:
  0.6 0.9 %payload.2.refs_5_.refs_1_.refs_3_.refs_0_ = bf16[128,1024]{1,0:T(8,128)(2,1)S(1)} custom-call(bf16[1,128,1024]{2,1,0:T(8,128)(2,1)} %refs_0_.3, bf16[1,128,1024]{2,1,0:T(8,128)(2,1)} %refs_1_.7), custom_call_target="tpu_custom_call" | custom-call | bytes 1 | tf_op jit(solution)/shard_map/payload/pallas_call | solution.py:38
  1.6 4.9 %collective-permute-start = (bf16[128,1024]{1,0:T(8,128)(2,1)S(1)}, bf16[128,1024]{1,0:T(8,128)(2,1)S(1)}, u32[]{:S(2)}, u32[]{:S(2)}) collective-permute-start(bf16[128,1024]{1,0:T(8,128)(2,1)S(1)} %payload.2.refs_5_.refs_1_.refs_3_.refs_0_), channel_id=1, source_target_pairs={{0,2},{1,3},{2,4},{3,5},{4,6},{5,7},{8,10},{9,11},{10,12},{11,13},... | collective-permute-start | bytes 786440 | tf_op jit(solution)/shard_map/ppermute | solution.py:250
  6.5 1.0 %payload.3 = (bf16[128,1024]{1,0:T(8,128)(2,1)S(1)}, s32[1,1024]{1,0:T(1,128)S(1)}, f32[1,256]{1,0:T(1,128)S(1)}, f32[1,256]{1,0:T(1,128)S(1)}) custom-call(bf16[1,128,1024]{2,1,0:T(8,128)(2,1)} %refs_0_.3, bf16[1,128,1024]{2,1,0:T(8,128)(2,1)} %refs_1_.7, s32[1,1024]{1,0:T(1,128)} %refs_2_.5, f32[1,256]{1,0:T(1,128)} %bitcast.4, f32[1,256]{1,0:T(1,128)} %bitcast.5, ...), custom_call_target="tpu_custom_call" | custom-call | bytes 1 | tf_op jit(solution)/shard_map/payload/pallas_call | solution.py:38
  7.6 3.5 %collective-permute-start.3 = (bf16[128,1024]{1,0:T(8,128)(2,1)S(1)}, bf16[128,1024]{1,0:T(8,128)(2,1)S(1)}, u32[]{:S(2)}, u32[]{:S(2)}) collective-permute-start(bf16[128,1024]{1,0:T(8,128)(2,1)S(1)} %get-tuple-element.55.refs_1_.refs_3_.refs_0_), channel_id=1, source_target_pairs={{0,2},{1,3},{2,4},{3,5},{4,6},{5,7},{8,10},{9,11},{10,12},{11,13},... | collective-permute-start | bytes 786440 | tf_op jit(solution)/shard_map/ppermute | solution.py:250
  11.1 2.2 %collective-permute-done.refs_0_.refs_5_ = bf16[128,1024]{1,0:T(8,128)(2,1)S(1)} collective-permute-done((bf16[128,1024]{1,0:T(8,128)(2,1)S(1)}, bf16[128,1024]{1,0:T(8,128)(2,1)S(1)}, u32[]{:S(2)}, u32[]{:S(2)}) %collective-permute-start) | collective-permute-done | bytes 262176 | tf_op jit(solution)/shard_map/ppermute | solution.py:250
  13.4 0.8 %collective-permute-start.2 = (bf16[128,1024]{1,0:T(8,128)(2,1)S(1)}, bf16[128,1024]{1,0:T(8,128)(2,1)S(1)}, u32[]{:S(2)}, u32[]{:S(2)}) collective-permute-start(bf16[128,1024]{1,0:T(8,128)(2,1)S(1)} %get-tuple-element.54.refs_2_), channel_id=1, source_target_pairs={{2,4},{3,5},{4,6},{5,7},{10,12},{11,13},{12,14},{13,15},{18,20},{1... | collective-permute-start | bytes 786440 | tf_op jit(solution)/shard_map/ppermute | solution.py:250
  14.2 3.5 %collective-permute-done.3.refs_0_.refs_5_ = bf16[128,1024]{1,0:T(8,128)(2,1)S(1)} collective-permute-done((bf16[128,1024]{1,0:T(8,128)(2,1)S(1)}, bf16[128,1024]{1,0:T(8,128)(2,1)S(1)}, u32[]{:S(2)}, u32[]{:S(2)}) %collective-permute-start.3) | collective-permute-done | bytes 262176 | tf_op jit(solution)/shard_map/ppermute | solution.py:250
  17.8 0.7 %collective-permute-start.7 = (bf16[128,1024]{1,0:T(8,128)(2,1)S(1)}, bf16[128,1024]{1,0:T(8,128)(2,1)S(1)}, u32[]{:S(2)}, u32[]{:S(2)}) collective-permute-start(bf16[128,1024]{1,0:T(8,128)(2,1)S(1)} %get-tuple-element.56.refs_2_), channel_id=1, source_target_pairs={{2,4},{3,5},{4,6},{5,7},{10,12},{11,13},{12,14},{13,15},{18,20},{1... | collective-permute-start | bytes 786440 | tf_op jit(solution)/shard_map/ppermute | solution.py:250
  18.5 0.6 %begin.2 = (f32[768,256]{1,0:T(8,128)S(1)}, bf16[768,256]{1,0:T(8,128)(2,1)S(1)}, f32[512,384]{1,0:T(8,128)S(1)}, f32[512,384]{1,0:T(8,128)S(1)}) custom-call(s32[1,1024]{1,0:T(1,128)S(1)} %get-tuple-element.52.refs_0_, bf16[1,128,2048]{2,1,0:T(8,128)(2,1)S(1)} %copy-done, bf16[1,128,2048]{2,1,0:T(8,128)(2,1)S(1)} %copy-done.1, ...), custom_call_target="tpu_custom_call" | custom-call | bytes 1 | tf_op jit(solution)/shard_map/begin/pallas_call | solution.py:38
  19.2 0.5 collective-permute-start.4
  19.8 0.6 %begin.3 = (f32[768,256]{1,0:T(8,128)S(1)}, bf16[768,256]{1,0:T(8,128)(2,1)S(1)}, f32[512,384]{1,0:T(8,128)S(1)}, f32[512,384]{1,0:T(8,128)S(1)}) custom-call(s32[1,1024]{1,0:T(1,128)S(1)} %get-tuple-element.52.refs_0_, bf16[1,128,2048]{2,1,0:T(8,128)(2,1)S(1)} %copy-done, bf16[1,128,2048]{2,1,0:T(8,128)(2,1)S(1)} %copy-done.1, ...), custom_call_target="tpu_custom_call" | custom-call | bytes 1 | tf_op jit(solution)/shard_map/begin/pallas_call | solution.py:38
  20.7 0.4 collective-permute-done.5.refs_8_
  21.1 1.7 %attend.2 = (bf16[128,1024]{1,0:T(8,128)(2,1)S(1)}, bf16[128,1024]{1,0:T(8,128)(2,1)S(1)}, f32[128,1024]{1,0:T(8,128)S(1)}, f32[128,1024]{1,0:T(8,128)S(1)}, f32...) custom-call(s32[1,1024]{1,0:T(1,128)S(1)} %get-tuple-element.52.refs, ...), custom_call_target="tpu_custom_call" | custom-call | bytes 1 | tf_op jit(solution)/shard_map/attend/pallas_call | solution.py:38
  24.5 0.7 %collective-permute-start.17 = (bf16[128,1024]{1,0:T(8,128)(2,1)S(1)}, bf16[128,1024]{1,0:T(8,128)(2,1)S(1)}, u32[]{:S(2)}, u32[]{:S(2)}) collective-permute-start(bf16[128,1024]{1,0:T(8,128)(2,1)S(1)} %sink.4.refs_15_.refs_3_), channel_id=1, source_target_pairs={{4,2},{5,3},{6,4},{7,5},{12,10},{13,11},{14,12},{15,13},{20,18},{2... | collective-permute-start | bytes 786440 | tf_op jit(solution)/shard_map/ppermute | solution.py:250
  25.2 1.7 %attend.3 = (bf16[128,1024]{1,0:T(8,128)(2,1)S(1)}, bf16[128,1024]{1,0:T(8,128)(2,1)S(1)}, f32[128,1024]{1,0:T(8,128)S(1)}, f32[128,1024]{1,0:T(8,128)S(1)}, f32...) custom-call(s32[1,1024]{1,0:T(1,128)S(1)} %get-tuple-element.52.refs, ...), custom_call_target="tpu_custom_call" | custom-call | bytes 1 | tf_op jit(solution)/shard_map/attend/pallas_call | solution.py:38
  26.9 0.4 collective-permute-start.12
  27.8 0.8 %collective-permute-done.14.refs_1_ = f32[2,256]{1,0:T(2,128)S(1)} collective-permute-done((f32[2,256]{1,0:T(2,128)S(1)}, f32[2,256]{1,0:T(2,128)S(1)}, u32[]{:S(2)}, u32[]{:S(2)}) %collective-permute-start.14) | collective-permute-done | bytes 2080 | tf_op jit(solution)/shard_map/ppermute | solution.py:250
  29.0 0.7 %collective-permute-start.15 = (bf16[128,1024]{1,0:T(8,128)(2,1)S(1)}, bf16[128,1024]{1,0:T(8,128)(2,1)S(1)}, u32[]{:S(2)}, u32[]{:S(2)}) collective-permute-start(bf16[128,1024]{1,0:T(8,128)(2,1)S(1)} %sink.5.refs_5_.refs_1_), channel_id=1, source_target_pairs={{4,2},{5,3},{6,4},{7,5},{12,10},{13,11},{14,12},{15,13},{20,18},{2... | collective-permute-start | bytes 786440 | tf_op jit(solution)/shard_map/ppermute | solution.py:250
  29.7 8.9 %collective-permute-start.20 = (f32[2,256]{1,0:T(2,128)S(1)}, f32[2,256]{1,0:T(2,128)S(1)}, u32[]{:S(2)}, u32[]{:S(2)}) collective-permute-start(f32[2,256]{1,0:T(2,128)S(1)} %add.7.refs_0_), channel_id=1, source_target_pairs={{0,2},{1,3},{2,0},{3,1},{4,6},{5,7},{6,4},{7,5},{8,10},{9,11},{10,... | collective-permute-start | bytes 6152 | tf_op jit(solution)/shard_map/ppermute | solution.py:250
  38.7 5.2 %collective-permute-start.21 = (f32[2,256]{1,0:T(2,128)S(1)}, f32[2,256]{1,0:T(2,128)S(1)}, u32[]{:S(2)}, u32[]{:S(2)}) collective-permute-start(f32[2,256]{1,0:T(2,128)S(1)} %add.7.refs_0_), channel_id=1, source_target_pairs={{0,4},{1,5},{2,6},{3,7},{4,0},{5,1},{6,2},{7,3},{8,12},{9,13},{10,... | collective-permute-start | bytes 6152 | tf_op jit(solution)/shard_map/ppermute | solution.py:250
  44.0 1.3 %collective-permute-start.25 = (bf16[128,1024]{1,0:T(8,128)(2,1)S(1)}, bf16[128,1024]{1,0:T(8,128)(2,1)S(1)}, u32[]{:S(2)}, u32[]{:S(2)}) collective-permute-start(bf16[128,1024]{1,0:T(8,128)(2,1)S(1)} %sink.6.refs_5_), channel_id=1, source_target_pairs={{2,0},{3,1},{4,2},{5,3},{6,4},{7,5},{10,8},{11,9},{12,10},{13,11},... | collective-permute-start | bytes 786440 | tf_op jit(solution)/shard_map/ppermute | solution.py:250
  45.4 1.3 %collective-permute-start.19 = (bf16[128,1024]{1,0:T(8,128)(2,1)S(1)}, bf16[128,1024]{1,0:T(8,128)(2,1)S(1)}, u32[]{:S(2)}, u32[]{:S(2)}) collective-permute-start(bf16[128,1024]{1,0:T(8,128)(2,1)S(1)} %sink.7.refs_4_), channel_id=1, source_target_pairs={{2,0},{3,1},{4,2},{5,3},{6,4},{7,5},{10,8},{11,9},{12,10},{13,11},... | collective-permute-start | bytes 786440 | tf_op jit(solution)/shard_map/ppermute | solution.py:250
  46.7 1.8 %collective-permute-done.21.refs_2_ = f32[2,256]{1,0:T(2,128)S(1)} collective-permute-done((f32[2,256]{1,0:T(2,128)S(1)}, f32[2,256]{1,0:T(2,128)S(1)}, u32[]{:S(2)}, u32[]{:S(2)}) %collective-permute-start.21) | collective-permute-done | bytes 2080 | tf_op jit(solution)/shard_map/ppermute | solution.py:250
  48.6 1.7 %collective-permute-done.22.refs_3_ = f32[2,256]{1,0:T(2,128)S(1)} collective-permute-done((f32[2,256]{1,0:T(2,128)S(1)}, f32[2,256]{1,0:T(2,128)S(1)}, u32[]{:S(2)}, u32[]{:S(2)}) %collective-permute-start.22) | collective-permute-done | bytes 2080 | tf_op jit(solution)/shard_map/ppermute | solution.py:250
  50.3 1.5 %collective-permute-start.23 = (f32[2,256]{1,0:T(2,128)S(1)}, f32[2,256]{1,0:T(2,128)S(1)}, u32[]{:S(2)}, u32[]{:S(2)}) collective-permute-start(f32[2,256]{1,0:T(2,128)S(1)} %add.8.refs_0_), channel_id=1, source_target_pairs={{0,8},{8,0},{16,24},{24,16},{1,9},{9,1},{17,25},{25,17},{2,10},{10... | collective-permute-start | bytes 6152 | tf_op jit(solution)/shard_map/ppermute | solution.py:250
  51.8 1.0 %assemble.1 = (bf16[1,128,2048]{2,1,0:T(8,128)(2,1)}, bf16[1,128,2048]{2,1,0:T(8,128)(2,1)}) custom-call(bf16[128,1024]{1,0:T(8,128)(2,1)S(1)} %get-tuple-element.65.refs_0_, bf16[128,1024]{1,0:T(8,128)(2,1)S(1)} %get-tuple-element.77.refs_1_, bf16[128,1024]{1,0:T(8,128)(2,1)S(1)} %get-tuple-element.78.refs_2_, ...), custom_call_target="tpu_custom_call" | custom-call | bytes 1 | tf_op jit(solution)/shard_map/assemble/pallas_call | solution.py:38
  52.8 1.1 %collective-permute-done.23.refs_1_ = f32[2,256]{1,0:T(2,128)S(1)} collective-permute-done((f32[2,256]{1,0:T(2,128)S(1)}, f32[2,256]{1,0:T(2,128)S(1)}, u32[]{:S(2)}, u32[]{:S(2)}) %collective-permute-start.23) | collective-permute-done | bytes 2080 | tf_op jit(solution)/shard_map/ppermute | solution.py:250
  53.9 1.5 %collective-permute-start.24 = (f32[2,256]{1,0:T(2,128)S(1)}, f32[2,256]{1,0:T(2,128)S(1)}, u32[]{:S(2)}, u32[]{:S(2)}) collective-permute-start(f32[2,256]{1,0:T(2,128)S(1)} %add.9.refs_5_), channel_id=1, source_target_pairs={{0,16},{8,24},{16,0},{24,8},{1,17},{9,25},{17,1},{25,9},{2,18},{10... | collective-permute-start | bytes 6152 | tf_op jit(solution)/shard_map/ppermute | solution.py:250
  55.4 0.9 %finish.2 = (bf16[1,128,1024]{2,1,0:T(8,128)(2,1)}, bf16[1,128,1024]{2,1,0:T(8,128)(2,1)}) custom-call(bf16[128,1024]{1,0:T(8,128)(2,1)S(1)} %payload.2.refs_5_.refs_1_.refs_3_.refs_0_, f32[1,256]{1,0:T(1,128)S(1)} %get-tuple-element.58.refs_7_.refs_10_.refs_1_, f32[128,1024]{1,0:T(8,128)S(1)} %get-tuple-element.91.refs_2_, ...), custom_call_target="tpu_custom_call" | custom-call | flops 2147483648 | bytes 1 | tf_op jit(solution)/shard_map/finish/pallas_call | solution.py:38
  56.3 1.1 %collective-permute-done.24.refs_6_ = f32[2,256]{1,0:T(2,128)S(1)} collective-permute-done((f32[2,256]{1,0:T(2,128)S(1)}, f32[2,256]{1,0:T(2,128)S(1)}, u32[]{:S(2)}, u32[]{:S(2)}) %collective-permute-start.24) | collective-permute-done | bytes 2080 | tf_op jit(solution)/shard_map/ppermute | solution.py:250
  57.5 1.7 %collective-permute-done.19.refs_4_ = bf16[128,1024]{1,0:T(8,128)(2,1)S(1)} collective-permute-done((bf16[128,1024]{1,0:T(8,128)(2,1)S(1)}, bf16[128,1024]{1,0:T(8,128)(2,1)S(1)}, u32[]{:S(2)}, u32[]{:S(2)}) %collective-permute-start.19) | collective-permute-done | bytes 262176 | tf_op jit(solution)/shard_map/ppermute | solution.py:250
  59.2 0.9 %finish.3 = (bf16[1,128,1024]{2,1,0:T(8,128)(2,1)}, bf16[1,128,1024]{2,1,0:T(8,128)(2,1)}, f32[1,256]{1,0:T(1,128)}, f32[1,256]{1,0:T(1,128)}) custom-call(bf16[128,1024]{1,0:T(8,128)(2,1)S(1)} %get-tuple-element.55.refs_1_.refs_3_.refs_0_, f32[1,256]{1,0:T(1,128)S(1)} %get-tuple-element.58.refs_7_.refs_10_.refs_1_, ...), custom_call_target="tpu_custom_call", output_to_operand_aliasing={{0}: (7, {}), {1}: (8, {})} | custom-call | flops 4294967296 | bytes 1 | tf_op jit(solution)/shard_map/finish/pallas_call | solution.py:38
  (47 shorter events, 3.5 us)
Async XLA Ops:
  1.6 11.6 %collective-permute-start = (bf16[128,1024]{1,0:T(8,128)(2,1)S(1)}, bf16[128,1024]{1,0:T(8,128)(2,1)S(1)}, u32[]{:S(2)}, u32[]{:S(2)}) collective-permute-start(bf16[128,1024]{1,0:T(8,128)(2,1)S(1)} %payload.2.refs_5_.refs_1_.refs_3_.refs_0_), channel_id=1, source_target_pairs={{0,2},{1,3},{2,4},{3,5},{4,6},{5,7},{8,10},{9,11},{10,12},{11,13},... | collective-permute-start | bytes 786440 | tf_op jit(solution)/shard_map/ppermute | solution.py:250
  7.6 10.1 %collective-permute-start.3 = (bf16[128,1024]{1,0:T(8,128)(2,1)S(1)}, bf16[128,1024]{1,0:T(8,128)(2,1)S(1)}, u32[]{:S(2)}, u32[]{:S(2)}) collective-permute-start(bf16[128,1024]{1,0:T(8,128)(2,1)S(1)} %get-tuple-element.55.refs_1_.refs_3_.refs_0_), channel_id=1, source_target_pairs={{0,2},{1,3},{2,4},{3,5},{4,6},{5,7},{8,10},{9,11},{10,12},{11,13},... | collective-permute-start | bytes 786440 | tf_op jit(solution)/shard_map/ppermute | solution.py:250
  13.3 5.2 %collective-permute-start.1 = (bf16[128,1024]{1,0:T(8,128)(2,1)S(1)}, bf16[128,1024]{1,0:T(8,128)(2,1)S(1)}, u32[]{:S(2)}, u32[]{:S(2)}) collective-permute-start(bf16[128,1024]{1,0:T(8,128)(2,1)S(1)} %get-tuple-element.53), channel_id=1, source_target_pairs={{0,1},{1,0},{2,3},{3,2},{4,5},{5,4},{6,7},{7,6},{8,9},{9,8},{10,11... | collective-permute-start | bytes 786440 | tf_op jit(solution)/shard_map/ppermute | solution.py:250
  13.3 5.2 %copy-start = (bf16[1,128,2048]{2,1,0:T(8,128)(2,1)S(1)}, bf16[1,128,2048]{2,1,0:T(8,128)(2,1)}, u32[]{:S(2)}) copy-start(bf16[1,128,2048]{2,1,0:T(8,128)(2,1)} %refs_1_.11) | copy-start | bytes 1572868
  13.3 5.2 %copy-start.1 = (bf16[1,128,2048]{2,1,0:T(8,128)(2,1)S(1)}, bf16[1,128,2048]{2,1,0:T(8,128)(2,1)}, u32[]{:S(2)}) copy-start(bf16[1,128,2048]{2,1,0:T(8,128)(2,1)} %refs_2_.9) | copy-start | bytes 1572868
  13.4 5.8 %collective-permute-start.2 = (bf16[128,1024]{1,0:T(8,128)(2,1)S(1)}, bf16[128,1024]{1,0:T(8,128)(2,1)S(1)}, u32[]{:S(2)}, u32[]{:S(2)}) collective-permute-start(bf16[128,1024]{1,0:T(8,128)(2,1)S(1)} %get-tuple-element.54.refs_2_), channel_id=1, source_target_pairs={{2,4},{3,5},{4,6},{5,7},{10,12},{11,13},{12,14},{13,15},{18,20},{1... | collective-permute-start | bytes 786440 | tf_op jit(solution)/shard_map/ppermute | solution.py:250
  17.7 2.1 %collective-permute-start.6 = (bf16[128,1024]{1,0:T(8,128)(2,1)S(1)}, bf16[128,1024]{1,0:T(8,128)(2,1)S(1)}, u32[]{:S(2)}, u32[]{:S(2)}) collective-permute-start(bf16[128,1024]{1,0:T(8,128)(2,1)S(1)} %get-tuple-element.66), channel_id=1, source_target_pairs={{0,1},{1,0},{2,3},{3,2},{4,5},{5,4},{6,7},{7,6},{8,9},{9,8},{10,11... | collective-permute-start | bytes 786440 | tf_op jit(solution)/shard_map/ppermute | solution.py:250
  17.8 5.6 %collective-permute-start.7 = (bf16[128,1024]{1,0:T(8,128)(2,1)S(1)}, bf16[128,1024]{1,0:T(8,128)(2,1)S(1)}, u32[]{:S(2)}, u32[]{:S(2)}) collective-permute-start(bf16[128,1024]{1,0:T(8,128)(2,1)S(1)} %get-tuple-element.56.refs_2_), channel_id=1, source_target_pairs={{2,4},{3,5},{4,6},{5,7},{10,12},{11,13},{12,14},{13,15},{18,20},{1... | collective-permute-start | bytes 786440 | tf_op jit(solution)/shard_map/ppermute | solution.py:250
  19.2 1.5 %collective-permute-start.4 = (bf16[128,512]{1,0:T(8,128)(2,1)S(1)}, bf16[128,512]{1,0:T(8,128)(2,1)S(1)}, u32[]{:S(2)}, u32[]{:S(2)}) collective-permute-start(bf16[128,512]{1,0:T(8,128)(2,1)S(1)} %get-tuple-element.60.refs_2_), channel_id=1, source_target_pairs={{0,1},{1,0},{2,3},{3,2},{4,5},{5,4},{6,7},{7,6},{8,9},{9,8},{10,11... | collective-permute-start | bytes 393224 | tf_op jit(solution)/shard_map/ppermute | solution.py:250
  19.7 1.3 %collective-permute-start.5 = (bf16[128,512]{1,0:T(8,128)(2,1)S(1)}, bf16[128,512]{1,0:T(8,128)(2,1)S(1)}, u32[]{:S(2)}, u32[]{:S(2)}) collective-permute-start(bf16[128,512]{1,0:T(8,128)(2,1)S(1)} %get-tuple-element.61), channel_id=1, source_target_pairs={{0,1},{1,0},{2,3},{3,2},{4,5},{5,4},{6,7},{7,6},{8,9},{9,8},{10,11... | collective-permute-start | bytes 393224 | tf_op jit(solution)/shard_map/ppermute | solution.py:250
  22.8 1.4 %collective-permute-start.10 = (bf16[128,512]{1,0:T(8,128)(2,1)S(1)}, bf16[128,512]{1,0:T(8,128)(2,1)S(1)}, u32[]{:S(2)}, u32[]{:S(2)}) collective-permute-start(bf16[128,512]{1,0:T(8,128)(2,1)S(1)} %get-tuple-element.75), channel_id=1, source_target_pairs={{0,1},{1,0},{2,3},{3,2},{4,5},{5,4},{6,7},{7,6},{8,9},{9,8},{10,11... | collective-permute-start | bytes 393224 | tf_op jit(solution)/shard_map/ppermute | solution.py:250
  23.1 1.4 %collective-permute-start.11 = (bf16[128,512]{1,0:T(8,128)(2,1)S(1)}, bf16[128,512]{1,0:T(8,128)(2,1)S(1)}, u32[]{:S(2)}, u32[]{:S(2)}) collective-permute-start(bf16[128,512]{1,0:T(8,128)(2,1)S(1)} %get-tuple-element.76), channel_id=1, source_target_pairs={{0,1},{1,0},{2,3},{3,2},{4,5},{5,4},{6,7},{7,6},{8,9},{9,8},{10,11... | collective-permute-start | bytes 393224 | tf_op jit(solution)/shard_map/ppermute | solution.py:250
  23.4 1.7 %collective-permute-start.8 = (bf16[128,512]{1,0:T(8,128)(2,1)S(1)}, bf16[128,512]{1,0:T(8,128)(2,1)S(1)}, u32[]{:S(2)}, u32[]{:S(2)}) collective-permute-start(bf16[128,512]{1,0:T(8,128)(2,1)S(1)} %get-tuple-element.69), channel_id=1, source_target_pairs={{0,1},{1,0},{2,3},{3,2},{4,5},{5,4},{6,7},{7,6},{8,9},{9,8},{10,11... | collective-permute-start | bytes 393224 | tf_op jit(solution)/shard_map/ppermute | solution.py:250
  23.7 1.5 %collective-permute-start.9 = (bf16[128,512]{1,0:T(8,128)(2,1)S(1)}, bf16[128,512]{1,0:T(8,128)(2,1)S(1)}, u32[]{:S(2)}, u32[]{:S(2)}) collective-permute-start(bf16[128,512]{1,0:T(8,128)(2,1)S(1)} %get-tuple-element.70), channel_id=1, source_target_pairs={{0,1},{1,0},{2,3},{3,2},{4,5},{5,4},{6,7},{7,6},{8,9},{9,8},{10,11... | collective-permute-start | bytes 393224 | tf_op jit(solution)/shard_map/ppermute | solution.py:250
  24.0 14.6 %collective-permute-start.18 = (bf16[128,1024]{1,0:T(8,128)(2,1)S(1)}, bf16[128,1024]{1,0:T(8,128)(2,1)S(1)}, u32[]{:S(2)}, u32[]{:S(2)}) collective-permute-start(bf16[128,1024]{1,0:T(8,128)(2,1)S(1)} %get-tuple-element.87), channel_id=1, source_target_pairs={{0,1},{1,0},{2,3},{3,2},{4,5},{5,4},{6,7},{7,6},{8,9},{9,8},{10,11... | collective-permute-start | bytes 786440 | tf_op jit(solution)/shard_map/ppermute | solution.py:250
  24.5 19.4 %collective-permute-start.17 = (bf16[128,1024]{1,0:T(8,128)(2,1)S(1)}, bf16[128,1024]{1,0:T(8,128)(2,1)S(1)}, u32[]{:S(2)}, u32[]{:S(2)}) collective-permute-start(bf16[128,1024]{1,0:T(8,128)(2,1)S(1)} %sink.4.refs_15_.refs_3_), channel_id=1, source_target_pairs={{4,2},{5,3},{6,4},{7,5},{12,10},{13,11},{14,12},{15,13},{20,18},{2... | collective-permute-start | bytes 786440 | tf_op jit(solution)/shard_map/ppermute | solution.py:250
  26.9 2.1 %collective-permute-start.12 = (bf16[128,512]{1,0:T(8,128)(2,1)S(1)}, bf16[128,512]{1,0:T(8,128)(2,1)S(1)}, u32[]{:S(2)}, u32[]{:S(2)}) collective-permute-start(bf16[128,512]{1,0:T(8,128)(2,1)S(1)} %get-tuple-element.82), channel_id=1, source_target_pairs={{0,1},{1,0},{2,3},{3,2},{4,5},{5,4},{6,7},{7,6},{8,9},{9,8},{10,11... | collective-permute-start | bytes 393224 | tf_op jit(solution)/shard_map/ppermute | solution.py:250
  27.3 1.7 %collective-permute-start.13 = (bf16[128,512]{1,0:T(8,128)(2,1)S(1)}, bf16[128,512]{1,0:T(8,128)(2,1)S(1)}, u32[]{:S(2)}, u32[]{:S(2)}) collective-permute-start(bf16[128,512]{1,0:T(8,128)(2,1)S(1)} %get-tuple-element.83), channel_id=1, source_target_pairs={{0,1},{1,0},{2,3},{3,2},{4,5},{5,4},{6,7},{7,6},{8,9},{9,8},{10,11... | collective-permute-start | bytes 393224 | tf_op jit(solution)/shard_map/ppermute | solution.py:250
  27.5 1.2 %collective-permute-start.14 = (f32[2,256]{1,0:T(2,128)S(1)}, f32[2,256]{1,0:T(2,128)S(1)}, u32[]{:S(2)}, u32[]{:S(2)}) collective-permute-start(f32[2,256]{1,0:T(2,128)S(1)} %add.5.refs_0_), channel_id=1, source_target_pairs={{0,1},{1,0},{2,3},{3,2},{4,5},{5,4},{6,7},{7,6},{8,9},{9,8},{10,11... | collective-permute-start | bytes 6152 | tf_op jit(solution)/shard_map/ppermute | solution.py:250
  28.6 15.4 %collective-permute-start.16 = (bf16[128,1024]{1,0:T(8,128)(2,1)S(1)}, bf16[128,1024]{1,0:T(8,128)(2,1)S(1)}, u32[]{:S(2)}, u32[]{:S(2)}) collective-permute-start(bf16[128,1024]{1,0:T(8,128)(2,1)S(1)} %get-tuple-element.85), channel_id=1, source_target_pairs={{0,1},{1,0},{2,3},{3,2},{4,5},{5,4},{6,7},{7,6},{8,9},{9,8},{10,11... | collective-permute-start | bytes 786440 | tf_op jit(solution)/shard_map/ppermute | solution.py:250
  29.0 16.3 %collective-permute-start.15 = (bf16[128,1024]{1,0:T(8,128)(2,1)S(1)}, bf16[128,1024]{1,0:T(8,128)(2,1)S(1)}, u32[]{:S(2)}, u32[]{:S(2)}) collective-permute-start(bf16[128,1024]{1,0:T(8,128)(2,1)S(1)} %sink.5.refs_5_.refs_1_), channel_id=1, source_target_pairs={{4,2},{5,3},{6,4},{7,5},{12,10},{13,11},{14,12},{15,13},{20,18},{2... | collective-permute-start | bytes 786440 | tf_op jit(solution)/shard_map/ppermute | solution.py:250
  29.7 17.0 %collective-permute-start.20 = (f32[2,256]{1,0:T(2,128)S(1)}, f32[2,256]{1,0:T(2,128)S(1)}, u32[]{:S(2)}, u32[]{:S(2)}) collective-permute-start(f32[2,256]{1,0:T(2,128)S(1)} %add.7.refs_0_), channel_id=1, source_target_pairs={{0,2},{1,3},{2,0},{3,1},{4,6},{5,7},{6,4},{7,5},{8,10},{9,11},{10,... | collective-permute-start | bytes 6152 | tf_op jit(solution)/shard_map/ppermute | solution.py:250
  38.7 9.9 %collective-permute-start.21 = (f32[2,256]{1,0:T(2,128)S(1)}, f32[2,256]{1,0:T(2,128)S(1)}, u32[]{:S(2)}, u32[]{:S(2)}) collective-permute-start(f32[2,256]{1,0:T(2,128)S(1)} %add.7.refs_0_), channel_id=1, source_target_pairs={{0,4},{1,5},{2,6},{3,7},{4,0},{5,1},{6,2},{7,3},{8,12},{9,13},{10,... | collective-permute-start | bytes 6152 | tf_op jit(solution)/shard_map/ppermute | solution.py:250
  43.9 6.4 %collective-permute-start.22 = (f32[2,256]{1,0:T(2,128)S(1)}, f32[2,256]{1,0:T(2,128)S(1)}, u32[]{:S(2)}, u32[]{:S(2)}) collective-permute-start(f32[2,256]{1,0:T(2,128)S(1)} %add.7.refs_0_), channel_id=1, source_target_pairs={{0,6},{1,7},{2,4},{3,5},{4,2},{5,3},{6,0},{7,1},{8,14},{9,15},{10,... | collective-permute-start | bytes 6152 | tf_op jit(solution)/shard_map/ppermute | solution.py:250
  44.0 11.4 %collective-permute-start.25 = (bf16[128,1024]{1,0:T(8,128)(2,1)S(1)}, bf16[128,1024]{1,0:T(8,128)(2,1)S(1)}, u32[]{:S(2)}, u32[]{:S(2)}) collective-permute-start(bf16[128,1024]{1,0:T(8,128)(2,1)S(1)} %sink.6.refs_5_), channel_id=1, source_target_pairs={{2,0},{3,1},{4,2},{5,3},{6,4},{7,5},{10,8},{11,9},{12,10},{13,11},... | collective-permute-start | bytes 786440 | tf_op jit(solution)/shard_map/ppermute | solution.py:250
  45.4 13.7 %collective-permute-start.19 = (bf16[128,1024]{1,0:T(8,128)(2,1)S(1)}, bf16[128,1024]{1,0:T(8,128)(2,1)S(1)}, u32[]{:S(2)}, u32[]{:S(2)}) collective-permute-start(bf16[128,1024]{1,0:T(8,128)(2,1)S(1)} %sink.7.refs_4_), channel_id=1, source_target_pairs={{2,0},{3,1},{4,2},{5,3},{6,4},{7,5},{10,8},{11,9},{12,10},{13,11},... | collective-permute-start | bytes 786440 | tf_op jit(solution)/shard_map/ppermute | solution.py:250
  50.3 3.6 %collective-permute-start.23 = (f32[2,256]{1,0:T(2,128)S(1)}, f32[2,256]{1,0:T(2,128)S(1)}, u32[]{:S(2)}, u32[]{:S(2)}) collective-permute-start(f32[2,256]{1,0:T(2,128)S(1)} %add.8.refs_0_), channel_id=1, source_target_pairs={{0,8},{8,0},{16,24},{24,16},{1,9},{9,1},{17,25},{25,17},{2,10},{10... | collective-permute-start | bytes 6152 | tf_op jit(solution)/shard_map/ppermute | solution.py:250
  53.9 3.6 %collective-permute-start.24 = (f32[2,256]{1,0:T(2,128)S(1)}, f32[2,256]{1,0:T(2,128)S(1)}, u32[]{:S(2)}, u32[]{:S(2)}) collective-permute-start(f32[2,256]{1,0:T(2,128)S(1)} %add.9.refs_5_), channel_id=1, source_target_pairs={{0,16},{8,24},{16,0},{24,8},{1,17},{9,25},{17,1},{25,9},{2,18},{10... | collective-permute-start | bytes 6152 | tf_op jit(solution)/shard_map/ppermute | solution.py:250

commit v16 on v14

--- a/solution.py
+++ b/solution.py
@@ -329,15 +329,19 @@
         ins = {}
         if fresh:
             ins.update(far=parts[step]["far"], third_k=parts[step]["third_k"], third_v=parts[step]["third_v"])
+        if step == 0:
+            ins.update(next=parts[step]["next"])
         if older:
             chunk = step - LAG
             ins.update(near=parts[chunk]["near"], arrived=sunk[chunk])
             ins.update(old_k=parts[chunk]["third_k"], old_v=parts[chunk]["third_v"], next_old=parts[chunk]["next"])
 
         def body(*refs):
-            ref = dict(zip(list(ins) + ["out"], refs))
+            ref = dict(zip(list(ins) + list(outs), refs))
             first = core_index() == 0
             if fresh:
+                if step == 0:
+                    ref["give"][...] = ref["next"][...]
                 for half, extra in ((slice(0, mine // 2), ref["third_k"]), (slice(mine // 2, mine), ref["third_v"])):
                     extra = jnp.where(first, 0.0, extra[...].astype(F32))
                     ref["out"][:, half] = (ref["far"][:, half] + extra).astype(BF16)
@@ -347,8 +351,13 @@
                     total = ref["near"][:, half] + extra + ref["arrived"][:, half].astype(F32)
                     ref["out"][:, mine + half.start : mine + half.stop] = total.astype(BF16)
 
-        (total,) = call(body, "sink", ins, dict(out=shape(rows, mine + below)), after)
+        outs = dict(out=shape(rows, mine + below))
+        if step == 0:
+            outs.update(give=shape(rows, mine))
+        total, *give = call(body, "sink", ins, outs, after)
         sunk[step] = down(total, 0 if older else 1)
+        if step == 0:
+            parts[step]["next"] = swap(give[0])
         return total
 
     made, gains, last, token = [], [], [], []
@@ -379,7 +388,7 @@
         gains.append(result[8])
         token = [result[8]]
         parts.append(dict(zip(("own", "near", "far"), result[2:5])))
-        parts[-1].update(third_k=swap(result[5]), third_v=swap(result[6]), next=swap(result[7]))
+        parts[-1].update(third_k=swap(result[5]), third_v=swap(result[6]), next=swap(result[7]) if chunk else result[7])
         if chunk == amount - 1:
             (total,) = call(add, "add", dict(enumerate(gains)), dict(o=shape(2, HEAD_DIM, F32)))
             total = total_over(total, "ctx", 1, 2, 2)

time: 60 us -> 61.2 us (1.020)
  starting transfers between devices: 34.1 us -> 35.4 us
    ppermute x26, starting transfers between devices: 34.1 us -> 35.4 us  [move(): lax.ppermute(field, axis, [(i, target(i)) for i in range(size) if 0 <= ta...]
  transfers between devices with their start and end apart: 26 -> 26, of which waited for: 11 -> 13; matrix products, arithmetic and copies ran while one was open for 0% -> 0% of each run, Pallas kernels for 12% -> 12%
where the time goes in v16:
time: 61.2 us; the launch traced here: 60.7 us
  starting transfers between devices  35.4 us (58%)
  waiting for transfers between devices  15.4 us (25%)
  Pallas kernels  9.14 us (15%)
  between operations  0.85 us (1%)
    ppermute x26, starting transfers between devices, move(): lax.ppermute(field, axis, [(i, target(i)) for i in range(size) if 0 <= ta...  35.4 us
    ppermute x26, waiting for transfers between devices, move(): lax.ppermute(field, axis, [(i, target(i)) for i in range(size) if 0 <= ta...  15.4 us
    pallas_call x21, Pallas kernels, call(): pl.pallas_call(kernel, out_shape=list(outs.values()), in_specs=specs, out...  9.14 us
  transfers between devices with their start and end apart: 26, of which 13 were waited for; matrix products, arithmetic and copies ran while one was open for 0% of the time, Pallas kernels for 12%

profile of v16, /device:TPU:0, one launch (start us, length us, event | category | flops | bytes accessed | tf_op | source)
XLA Modules:
  0.0 60.7 jit_solution(10912433973733974530)
XLA Ops:
  0.6 0.9 %payload.2.refs_5_.refs_1_.refs_3_.refs_0_ = bf16[128,1024]{1,0:T(8,128)(2,1)S(1)} custom-call(bf16[1,128,1024]{2,1,0:T(8,128)(2,1)} %refs_0_.3, bf16[1,128,1024]{2,1,0:T(8,128)(2,1)} %refs_1_.5), custom_call_target="tpu_custom_call" | custom-call | bytes 1 | tf_op jit(solution)/shard_map/payload/pallas_call | solution.py:38
  1.6 4.9 %collective-permute-start = (bf16[128,1024]{1,0:T(8,128)(2,1)S(1)}, bf16[128,1024]{1,0:T(8,128)(2,1)S(1)}, u32[]{:S(2)}, u32[]{:S(2)}) collective-permute-start(bf16[128,1024]{1,0:T(8,128)(2,1)S(1)} %payload.2.refs_5_.refs_1_.refs_3_.refs_0_), channel_id=1, source_target_pairs={{0,2},{1,3},{2,4},{3,5},{4,6},{5,7},{8,10},{9,11},{10,12},{11,13},... | collective-permute-start | bytes 786440 | tf_op jit(solution)/shard_map/ppermute | solution.py:217
  6.5 1.0 %payload.3 = (bf16[128,1024]{1,0:T(8,128)(2,1)S(1)}, s32[1,1024]{1,0:T(1,128)S(1)}, f32[1,256]{1,0:T(1,128)S(1)}, f32[1,256]{1,0:T(1,128)S(1)}) custom-call(bf16[1,128,1024]{2,1,0:T(8,128)(2,1)} %refs_0_.3, bf16[1,128,1024]{2,1,0:T(8,128)(2,1)} %refs_1_.5, s32[1,1024]{1,0:T(1,128)} %refs_2_.3, f32[1,256]{1,0:T(1,128)} %bitcast.4, f32[1,256]{1,0:T(1,128)} %bitcast.5, ...), custom_call_target="tpu_custom_call" | custom-call | bytes 1 | tf_op jit(solution)/shard_map/payload/pallas_call | solution.py:38
  7.6 3.5 %collective-permute-start.3 = (bf16[128,1024]{1,0:T(8,128)(2,1)S(1)}, bf16[128,1024]{1,0:T(8,128)(2,1)S(1)}, u32[]{:S(2)}, u32[]{:S(2)}) collective-permute-start(bf16[128,1024]{1,0:T(8,128)(2,1)S(1)} %get-tuple-element.49.refs_1_.refs_3_.refs_0_), channel_id=1, source_target_pairs={{0,2},{1,3},{2,4},{3,5},{4,6},{5,7},{8,10},{9,11},{10,12},{11,13},... | collective-permute-start | bytes 786440 | tf_op jit(solution)/shard_map/ppermute | solution.py:217
  11.1 2.2 %collective-permute-done.refs_0_.refs_5_ = bf16[128,1024]{1,0:T(8,128)(2,1)S(1)} collective-permute-done((bf16[128,1024]{1,0:T(8,128)(2,1)S(1)}, bf16[128,1024]{1,0:T(8,128)(2,1)S(1)}, u32[]{:S(2)}, u32[]{:S(2)}) %collective-permute-start) | collective-permute-done | bytes 262176 | tf_op jit(solution)/shard_map/ppermute | solution.py:217
  13.3 0.7 %collective-permute-start.2 = (bf16[128,1024]{1,0:T(8,128)(2,1)S(1)}, bf16[128,1024]{1,0:T(8,128)(2,1)S(1)}, u32[]{:S(2)}, u32[]{:S(2)}) collective-permute-start(bf16[128,1024]{1,0:T(8,128)(2,1)S(1)} %get-tuple-element.48.refs_2_), channel_id=1, source_target_pairs={{2,4},{3,5},{4,6},{5,7},{10,12},{11,13},{12,14},{13,15},{18,20},{1... | collective-permute-start | bytes 786440 | tf_op jit(solution)/shard_map/ppermute | solution.py:217
  14.0 3.7 %collective-permute-done.3.refs_0_.refs_5_ = bf16[128,1024]{1,0:T(8,128)(2,1)S(1)} collective-permute-done((bf16[128,1024]{1,0:T(8,128)(2,1)S(1)}, bf16[128,1024]{1,0:T(8,128)(2,1)S(1)}, u32[]{:S(2)}, u32[]{:S(2)}) %collective-permute-start.3) | collective-permute-done | bytes 262176 | tf_op jit(solution)/shard_map/ppermute | solution.py:217
  17.8 0.8 %collective-permute-start.7 = (bf16[128,1024]{1,0:T(8,128)(2,1)S(1)}, bf16[128,1024]{1,0:T(8,128)(2,1)S(1)}, u32[]{:S(2)}, u32[]{:S(2)}) collective-permute-start(bf16[128,1024]{1,0:T(8,128)(2,1)S(1)} %get-tuple-element.50.refs_2_), channel_id=1, source_target_pairs={{2,4},{3,5},{4,6},{5,7},{10,12},{11,13},{12,14},{13,15},{18,20},{1... | collective-permute-start | bytes 786440 | tf_op jit(solution)/shard_map/ppermute | solution.py:217
  18.7 0.5 collective-permute-start.5
  19.3 0.8 %collective-permute-done.4.refs_7_ = bf16[128,512]{1,0:T(8,128)(2,1)S(1)} collective-permute-done((bf16[128,512]{1,0:T(8,128)(2,1)S(1)}, bf16[128,512]{1,0:T(8,128)(2,1)S(1)}, u32[]{:S(2)}, u32[]{:S(2)}) %collective-permute-start.4) | collective-permute-done | bytes 131104 | tf_op jit(solution)/shard_map/ppermute | solution.py:217
  20.2 1.9 %attend.2 = (bf16[128,1024]{1,0:T(8,128)(2,1)S(1)}, bf16[128,1024]{1,0:T(8,128)(2,1)S(1)}, f32[128,1024]{1,0:T(8,128)S(1)}, f32[128,1024]{1,0:T(8,128)S(1)}, f32...) custom-call(s32[1,1024]{1,0:T(1,128)S(1)} %get-tuple-element.46.refs, ...), custom_call_target="tpu_custom_call" | custom-call | bytes 1 | tf_op jit(solution)/shard_map/attend/pallas_call | solution.py:38
  22.1 0.4 collective-permute-start.10
  23.9 0.7 %collective-permute-start.17 = (bf16[128,1024]{1,0:T(8,128)(2,1)S(1)}, bf16[128,1024]{1,0:T(8,128)(2,1)S(1)}, u32[]{:S(2)}, u32[]{:S(2)}) collective-permute-start(bf16[128,1024]{1,0:T(8,128)(2,1)S(1)} %get-tuple-element.64.refs_11_.refs_3_), channel_id=1, source_target_pairs={{4,2},{5,3},{6,4},{7,5},{12,10},{13,11},{14,12},{15,13},{20,18},{2... | collective-permute-start | bytes 786440 | tf_op jit(solution)/shard_map/ppermute | solution.py:217
  24.9 1.9 %attend.3 = (bf16[128,1024]{1,0:T(8,128)(2,1)S(1)}, bf16[128,1024]{1,0:T(8,128)(2,1)S(1)}, f32[128,1024]{1,0:T(8,128)S(1)}, f32[128,1024]{1,0:T(8,128)S(1)}, f32...) custom-call(s32[1,1024]{1,0:T(1,128)S(1)} %get-tuple-element.46.refs, ...), custom_call_target="tpu_custom_call" | custom-call | bytes 1 | tf_op jit(solution)/shard_map/attend/pallas_call | solution.py:38
  26.8 0.4 collective-permute-start.12
  27.7 0.8 %collective-permute-done.14.refs_1_ = f32[2,256]{1,0:T(2,128)S(1)} collective-permute-done((f32[2,256]{1,0:T(2,128)S(1)}, f32[2,256]{1,0:T(2,128)S(1)}, u32[]{:S(2)}, u32[]{:S(2)}) %collective-permute-start.14) | collective-permute-done | bytes 2080 | tf_op jit(solution)/shard_map/ppermute | solution.py:217
  28.9 0.7 %collective-permute-start.15 = (bf16[128,1024]{1,0:T(8,128)(2,1)S(1)}, bf16[128,1024]{1,0:T(8,128)(2,1)S(1)}, u32[]{:S(2)}, u32[]{:S(2)}) collective-permute-start(bf16[128,1024]{1,0:T(8,128)(2,1)S(1)} %sink.5.refs_5_.refs_1_), channel_id=1, source_target_pairs={{4,2},{5,3},{6,4},{7,5},{12,10},{13,11},{14,12},{15,13},{20,18},{2... | collective-permute-start | bytes 786440 | tf_op jit(solution)/shard_map/ppermute | solution.py:217
  29.6 8.7 %collective-permute-start.20 = (f32[2,256]{1,0:T(2,128)S(1)}, f32[2,256]{1,0:T(2,128)S(1)}, u32[]{:S(2)}, u32[]{:S(2)}) collective-permute-start(f32[2,256]{1,0:T(2,128)S(1)} %add.7.refs_0_), channel_id=1, source_target_pairs={{0,2},{1,3},{2,0},{3,1},{4,6},{5,7},{6,4},{7,5},{8,10},{9,11},{10,... | collective-permute-start | bytes 6152 | tf_op jit(solution)/shard_map/ppermute | solution.py:217
  38.4 5.2 %collective-permute-start.21 = (f32[2,256]{1,0:T(2,128)S(1)}, f32[2,256]{1,0:T(2,128)S(1)}, u32[]{:S(2)}, u32[]{:S(2)}) collective-permute-start(f32[2,256]{1,0:T(2,128)S(1)} %add.7.refs_0_), channel_id=1, source_target_pairs={{0,4},{1,5},{2,6},{3,7},{4,0},{5,1},{6,2},{7,3},{8,12},{9,13},{10,... | collective-permute-start | bytes 6152 | tf_op jit(solution)/shard_map/ppermute | solution.py:217
  43.6 1.2 %collective-permute-start.22 = (f32[2,256]{1,0:T(2,128)S(1)}, f32[2,256]{1,0:T(2,128)S(1)}, u32[]{:S(2)}, u32[]{:S(2)}) collective-permute-start(f32[2,256]{1,0:T(2,128)S(1)} %add.7.refs_0_), channel_id=1, source_target_pairs={{0,6},{1,7},{2,4},{3,5},{4,2},{5,3},{6,0},{7,1},{8,14},{9,15},{10,... | collective-permute-start | bytes 6152 | tf_op jit(solution)/shard_map/ppermute | solution.py:217
  44.9 1.3 %collective-permute-start.25 = (bf16[128,1024]{1,0:T(8,128)(2,1)S(1)}, bf16[128,1024]{1,0:T(8,128)(2,1)S(1)}, u32[]{:S(2)}, u32[]{:S(2)}) collective-permute-start(bf16[128,1024]{1,0:T(8,128)(2,1)S(1)} %sink.6.refs_5_), channel_id=1, source_target_pairs={{2,0},{3,1},{4,2},{5,3},{6,4},{7,5},{10,8},{11,9},{12,10},{13,11},... | collective-permute-start | bytes 786440 | tf_op jit(solution)/shard_map/ppermute | solution.py:217
  46.3 1.3 %collective-permute-start.19 = (bf16[128,1024]{1,0:T(8,128)(2,1)S(1)}, bf16[128,1024]{1,0:T(8,128)(2,1)S(1)}, u32[]{:S(2)}, u32[]{:S(2)}) collective-permute-start(bf16[128,1024]{1,0:T(8,128)(2,1)S(1)} %sink.7.refs_4_), channel_id=1, source_target_pairs={{2,0},{3,1},{4,2},{5,3},{6,4},{7,5},{10,8},{11,9},{12,10},{13,11},... | collective-permute-start | bytes 786440 | tf_op jit(solution)/shard_map/ppermute | solution.py:217
  47.6 0.9 %collective-permute-done.21.refs_2_ = f32[2,256]{1,0:T(2,128)S(1)} collective-permute-done((f32[2,256]{1,0:T(2,128)S(1)}, f32[2,256]{1,0:T(2,128)S(1)}, u32[]{:S(2)}, u32[]{:S(2)}) %collective-permute-start.21) | collective-permute-done | bytes 2080 | tf_op jit(solution)/shard_map/ppermute | solution.py:217
  48.6 1.4 %collective-permute-done.22.refs_3_ = f32[2,256]{1,0:T(2,128)S(1)} collective-permute-done((f32[2,256]{1,0:T(2,128)S(1)}, f32[2,256]{1,0:T(2,128)S(1)}, u32[]{:S(2)}, u32[]{:S(2)}) %collective-permute-start.22) | collective-permute-done | bytes 2080 | tf_op jit(solution)/shard_map/ppermute | solution.py:217
  50.0 1.5 %collective-permute-start.23 = (f32[2,256]{1,0:T(2,128)S(1)}, f32[2,256]{1,0:T(2,128)S(1)}, u32[]{:S(2)}, u32[]{:S(2)}) collective-permute-start(f32[2,256]{1,0:T(2,128)S(1)} %add.8.refs_0_), channel_id=1, source_target_pairs={{0,8},{8,0},{16,24},{24,16},{1,9},{9,1},{17,25},{25,17},{2,10},{10... | collective-permute-start | bytes 6152 | tf_op jit(solution)/shard_map/ppermute | solution.py:217
  51.5 1.0 %assemble.1 = (bf16[1,128,2048]{2,1,0:T(8,128)(2,1)}, bf16[1,128,2048]{2,1,0:T(8,128)(2,1)}) custom-call(bf16[128,1024]{1,0:T(8,128)(2,1)S(1)} %get-tuple-element.55.refs_0_, bf16[128,1024]{1,0:T(8,128)(2,1)S(1)} %get-tuple-element.65.refs_1_, bf16[128,1024]{1,0:T(8,128)(2,1)S(1)} %get-tuple-element.66.refs_2_, ...), custom_call_target="tpu_custom_call" | custom-call | bytes 1 | tf_op jit(solution)/shard_map/assemble/pallas_call | solution.py:38
  52.5 1.1 %collective-permute-done.23.refs_1_ = f32[2,256]{1,0:T(2,128)S(1)} collective-permute-done((f32[2,256]{1,0:T(2,128)S(1)}, f32[2,256]{1,0:T(2,128)S(1)}, u32[]{:S(2)}, u32[]{:S(2)}) %collective-permute-start.23) | collective-permute-done | bytes 2080 | tf_op jit(solution)/shard_map/ppermute | solution.py:217
  53.6 1.5 %collective-permute-start.24 = (f32[2,256]{1,0:T(2,128)S(1)}, f32[2,256]{1,0:T(2,128)S(1)}, u32[]{:S(2)}, u32[]{:S(2)}) collective-permute-start(f32[2,256]{1,0:T(2,128)S(1)} %add.9.refs_5_), channel_id=1, source_target_pairs={{0,16},{8,24},{16,0},{24,8},{1,17},{9,25},{17,1},{25,9},{2,18},{10... | collective-permute-start | bytes 6152 | tf_op jit(solution)/shard_map/ppermute | solution.py:217
  55.1 0.9 %collective-permute-done.25.refs_4_ = bf16[128,1024]{1,0:T(8,128)(2,1)S(1)} collective-permute-done((bf16[128,1024]{1,0:T(8,128)(2,1)S(1)}, bf16[128,1024]{1,0:T(8,128)(2,1)S(1)}, u32[]{:S(2)}, u32[]{:S(2)}) %collective-permute-start.25) | collective-permute-done | bytes 262176 | tf_op jit(solution)/shard_map/ppermute | solution.py:217
  56.0 0.9 %finish.2 = (bf16[1,128,1024]{2,1,0:T(8,128)(2,1)}, bf16[1,128,1024]{2,1,0:T(8,128)(2,1)}) custom-call(bf16[128,1024]{1,0:T(8,128)(2,1)S(1)} %payload.2.refs_5_.refs_1_.refs_3_.refs_0_, f32[1,256]{1,0:T(1,128)S(1)} %get-tuple-element.54.refs_10_.refs_1_, f32[128,1024]{1,0:T(8,128)S(1)} %get-tuple-element.79.refs_2_, ...), custom_call_target="tpu_custom_call" | custom-call | flops 2147483648 | bytes 1 | tf_op jit(solution)/shard_map/finish/pallas_call | solution.py:38
  57.2 2.6 %collective-permute-done.19.refs_4_ = bf16[128,1024]{1,0:T(8,128)(2,1)S(1)} collective-permute-done((bf16[128,1024]{1,0:T(8,128)(2,1)S(1)}, bf16[128,1024]{1,0:T(8,128)(2,1)S(1)}, u32[]{:S(2)}, u32[]{:S(2)}) %collective-permute-start.19) | collective-permute-done | bytes 262176 | tf_op jit(solution)/shard_map/ppermute | solution.py:217
  59.8 0.9 %finish.3 = (bf16[1,128,1024]{2,1,0:T(8,128)(2,1)}, bf16[1,128,1024]{2,1,0:T(8,128)(2,1)}, f32[1,256]{1,0:T(1,128)}, f32[1,256]{1,0:T(1,128)}) custom-call(bf16[128,1024]{1,0:T(8,128)(2,1)S(1)} %get-tuple-element.49.refs_1_.refs_3_.refs_0_, f32[1,256]{1,0:T(1,128)S(1)} %get-tuple-element.54.refs_10_.refs_1_, ...), custom_call_target="tpu_custom_call", output_to_operand_aliasing={{0}: (7, {}), {1}: (8, {})} | custom-call | flops 4294967296 | bytes 1 | tf_op jit(solution)/shard_map/finish/pallas_call | solution.py:38
  (45 shorter events, 3.6 us)
Async XLA Ops:
  1.6 11.6 %collective-permute-start = (bf16[128,1024]{1,0:T(8,128)(2,1)S(1)}, bf16[128,1024]{1,0:T(8,128)(2,1)S(1)}, u32[]{:S(2)}, u32[]{:S(2)}) collective-permute-start(bf16[128,1024]{1,0:T(8,128)(2,1)S(1)} %payload.2.refs_5_.refs_1_.refs_3_.refs_0_), channel_id=1, source_target_pairs={{0,2},{1,3},{2,4},{3,5},{4,6},{5,7},{8,10},{9,11},{10,12},{11,13},... | collective-permute-start | bytes 786440 | tf_op jit(solution)/shard_map/ppermute | solution.py:217
  7.6 10.1 %collective-permute-start.3 = (bf16[128,1024]{1,0:T(8,128)(2,1)S(1)}, bf16[128,1024]{1,0:T(8,128)(2,1)S(1)}, u32[]{:S(2)}, u32[]{:S(2)}) collective-permute-start(bf16[128,1024]{1,0:T(8,128)(2,1)S(1)} %get-tuple-element.49.refs_1_.refs_3_.refs_0_), channel_id=1, source_target_pairs={{0,2},{1,3},{2,4},{3,5},{4,6},{5,7},{8,10},{9,11},{10,12},{11,13},... | collective-permute-start | bytes 786440 | tf_op jit(solution)/shard_map/ppermute | solution.py:217
  13.3 5.3 %collective-permute-start.2 = (bf16[128,1024]{1,0:T(8,128)(2,1)S(1)}, bf16[128,1024]{1,0:T(8,128)(2,1)S(1)}, u32[]{:S(2)}, u32[]{:S(2)}) collective-permute-start(bf16[128,1024]{1,0:T(8,128)(2,1)S(1)} %get-tuple-element.48.refs_2_), channel_id=1, source_target_pairs={{2,4},{3,5},{4,6},{5,7},{10,12},{11,13},{12,14},{13,15},{18,20},{1... | collective-permute-start | bytes 786440 | tf_op jit(solution)/shard_map/ppermute | solution.py:217
  13.9 5.3 %collective-permute-start.1 = (bf16[128,1024]{1,0:T(8,128)(2,1)S(1)}, bf16[128,1024]{1,0:T(8,128)(2,1)S(1)}, u32[]{:S(2)}, u32[]{:S(2)}) collective-permute-start(bf16[128,1024]{1,0:T(8,128)(2,1)S(1)} %get-tuple-element.47), channel_id=1, source_target_pairs={{0,1},{1,0},{2,3},{3,2},{4,5},{5,4},{6,7},{7,6},{8,9},{9,8},{10,11... | collective-permute-start | bytes 786440 | tf_op jit(solution)/shard_map/ppermute | solution.py:217
  17.7 2.5 %copy-start = (bf16[1,128,2048]{2,1,0:T(8,128)(2,1)S(1)}, bf16[1,128,2048]{2,1,0:T(8,128)(2,1)}, u32[]{:S(2)}) copy-start(bf16[1,128,2048]{2,1,0:T(8,128)(2,1)} %refs_1_.7) | copy-start | bytes 1572868
  17.7 2.5 %copy-start.1 = (bf16[1,128,2048]{2,1,0:T(8,128)(2,1)S(1)}, bf16[1,128,2048]{2,1,0:T(8,128)(2,1)}, u32[]{:S(2)}) copy-start(bf16[1,128,2048]{2,1,0:T(8,128)(2,1)} %refs_2_.5) | copy-start | bytes 1572868
  17.8 4.9 %collective-permute-start.7 = (bf16[128,1024]{1,0:T(8,128)(2,1)S(1)}, bf16[128,1024]{1,0:T(8,128)(2,1)S(1)}, u32[]{:S(2)}, u32[]{:S(2)}) collective-permute-start(bf16[128,1024]{1,0:T(8,128)(2,1)S(1)} %get-tuple-element.50.refs_2_), channel_id=1, source_target_pairs={{2,4},{3,5},{4,6},{5,7},{10,12},{11,13},{12,14},{13,15},{18,20},{1... | collective-permute-start | bytes 786440 | tf_op jit(solution)/shard_map/ppermute | solution.py:217
  18.6 1.4 %collective-permute-start.4 = (bf16[128,512]{1,0:T(8,128)(2,1)S(1)}, bf16[128,512]{1,0:T(8,128)(2,1)S(1)}, u32[]{:S(2)}, u32[]{:S(2)}) collective-permute-start(bf16[128,512]{1,0:T(8,128)(2,1)S(1)} %get-tuple-element.51.refs_2_), channel_id=1, source_target_pairs={{0,1},{1,0},{2,3},{3,2},{4,5},{5,4},{6,7},{7,6},{8,9},{9,8},{10,11... | collective-permute-start | bytes 393224 | tf_op jit(solution)/shard_map/ppermute | solution.py:217
  18.7 1.5 %collective-permute-start.5 = (bf16[128,512]{1,0:T(8,128)(2,1)S(1)}, bf16[128,512]{1,0:T(8,128)(2,1)S(1)}, u32[]{:S(2)}, u32[]{:S(2)}) collective-permute-start(bf16[128,512]{1,0:T(8,128)(2,1)S(1)} %get-tuple-element.52), channel_id=1, source_target_pairs={{0,1},{1,0},{2,3},{3,2},{4,5},{5,4},{6,7},{7,6},{8,9},{9,8},{10,11... | collective-permute-start | bytes 393224 | tf_op jit(solution)/shard_map/ppermute | solution.py:217
  19.2 5.7 %collective-permute-start.6 = (bf16[128,1024]{1,0:T(8,128)(2,1)S(1)}, bf16[128,1024]{1,0:T(8,128)(2,1)S(1)}, u32[]{:S(2)}, u32[]{:S(2)}) collective-permute-start(bf16[128,1024]{1,0:T(8,128)(2,1)S(1)} %get-tuple-element.56), channel_id=1, source_target_pairs={{0,1},{1,0},{2,3},{3,2},{4,5},{5,4},{6,7},{7,6},{8,9},{9,8},{10,11... | collective-permute-start | bytes 786440 | tf_op jit(solution)/shard_map/ppermute | solution.py:217
  22.1 1.4 %collective-permute-start.10 = (bf16[128,512]{1,0:T(8,128)(2,1)S(1)}, bf16[128,512]{1,0:T(8,128)(2,1)S(1)}, u32[]{:S(2)}, u32[]{:S(2)}) collective-permute-start(bf16[128,512]{1,0:T(8,128)(2,1)S(1)} %get-tuple-element.61), channel_id=1, source_target_pairs={{0,1},{1,0},{2,3},{3,2},{4,5},{5,4},{6,7},{7,6},{8,9},{9,8},{10,11... | collective-permute-start | bytes 393224 | tf_op jit(solution)/shard_map/ppermute | solution.py:217
  22.5 1.3 %collective-permute-start.11 = (bf16[128,512]{1,0:T(8,128)(2,1)S(1)}, bf16[128,512]{1,0:T(8,128)(2,1)S(1)}, u32[]{:S(2)}, u32[]{:S(2)}) collective-permute-start(bf16[128,512]{1,0:T(8,128)(2,1)S(1)} %get-tuple-element.62), channel_id=1, source_target_pairs={{0,1},{1,0},{2,3},{3,2},{4,5},{5,4},{6,7},{7,6},{8,9},{9,8},{10,11... | collective-permute-start | bytes 393224 | tf_op jit(solution)/shard_map/ppermute | solution.py:217
  22.7 2.1 %collective-permute-start.8 = (bf16[128,512]{1,0:T(8,128)(2,1)S(1)}, bf16[128,512]{1,0:T(8,128)(2,1)S(1)}, u32[]{:S(2)}, u32[]{:S(2)}) collective-permute-start(bf16[128,512]{1,0:T(8,128)(2,1)S(1)} %get-tuple-element.58), channel_id=1, source_target_pairs={{0,1},{1,0},{2,3},{3,2},{4,5},{5,4},{6,7},{7,6},{8,9},{9,8},{10,11... | collective-permute-start | bytes 393224 | tf_op jit(solution)/shard_map/ppermute | solution.py:217
  23.1 1.8 %collective-permute-start.9 = (bf16[128,512]{1,0:T(8,128)(2,1)S(1)}, bf16[128,512]{1,0:T(8,128)(2,1)S(1)}, u32[]{:S(2)}, u32[]{:S(2)}) collective-permute-start(bf16[128,512]{1,0:T(8,128)(2,1)S(1)} %get-tuple-element.59), channel_id=1, source_target_pairs={{0,1},{1,0},{2,3},{3,2},{4,5},{5,4},{6,7},{7,6},{8,9},{9,8},{10,11... | collective-permute-start | bytes 393224 | tf_op jit(solution)/shard_map/ppermute | solution.py:217
  23.9 14.4 %collective-permute-start.17 = (bf16[128,1024]{1,0:T(8,128)(2,1)S(1)}, bf16[128,1024]{1,0:T(8,128)(2,1)S(1)}, u32[]{:S(2)}, u32[]{:S(2)}) collective-permute-start(bf16[128,1024]{1,0:T(8,128)(2,1)S(1)} %get-tuple-element.64.refs_11_.refs_3_), channel_id=1, source_target_pairs={{4,2},{5,3},{6,4},{7,5},{12,10},{13,11},{14,12},{15,13},{20,18},{2... | collective-permute-start | bytes 786440 | tf_op jit(solution)/shard_map/ppermute | solution.py:217
  24.6 19.0 %collective-permute-start.18 = (bf16[128,1024]{1,0:T(8,128)(2,1)S(1)}, bf16[128,1024]{1,0:T(8,128)(2,1)S(1)}, u32[]{:S(2)}, u32[]{:S(2)}) collective-permute-start(bf16[128,1024]{1,0:T(8,128)(2,1)S(1)} %get-tuple-element.75), channel_id=1, source_target_pairs={{0,1},{1,0},{2,3},{3,2},{4,5},{5,4},{6,7},{7,6},{8,9},{9,8},{10,11... | collective-permute-start | bytes 786440 | tf_op jit(solution)/shard_map/ppermute | solution.py:217
  26.8 2.1 %collective-permute-start.12 = (bf16[128,512]{1,0:T(8,128)(2,1)S(1)}, bf16[128,512]{1,0:T(8,128)(2,1)S(1)}, u32[]{:S(2)}, u32[]{:S(2)}) collective-permute-start(bf16[128,512]{1,0:T(8,128)(2,1)S(1)} %get-tuple-element.70), channel_id=1, source_target_pairs={{0,1},{1,0},{2,3},{3,2},{4,5},{5,4},{6,7},{7,6},{8,9},{9,8},{10,11... | collective-permute-start | bytes 393224 | tf_op jit(solution)/shard_map/ppermute | solution.py:217
  27.2 1.7 %collective-permute-start.13 = (bf16[128,512]{1,0:T(8,128)(2,1)S(1)}, bf16[128,512]{1,0:T(8,128)(2,1)S(1)}, u32[]{:S(2)}, u32[]{:S(2)}) collective-permute-start(bf16[128,512]{1,0:T(8,128)(2,1)S(1)} %get-tuple-element.71), channel_id=1, source_target_pairs={{0,1},{1,0},{2,3},{3,2},{4,5},{5,4},{6,7},{7,6},{8,9},{9,8},{10,11... | collective-permute-start | bytes 393224 | tf_op jit(solution)/shard_map/ppermute | solution.py:217
  27.4 1.2 %collective-permute-start.14 = (f32[2,256]{1,0:T(2,128)S(1)}, f32[2,256]{1,0:T(2,128)S(1)}, u32[]{:S(2)}, u32[]{:S(2)}) collective-permute-start(f32[2,256]{1,0:T(2,128)S(1)} %add.5.refs_0_), channel_id=1, source_target_pairs={{0,1},{1,0},{2,3},{3,2},{4,5},{5,4},{6,7},{7,6},{8,9},{9,8},{10,11... | collective-permute-start | bytes 6152 | tf_op jit(solution)/shard_map/ppermute | solution.py:217
  28.5 16.4 %collective-permute-start.16 = (bf16[128,1024]{1,0:T(8,128)(2,1)S(1)}, bf16[128,1024]{1,0:T(8,128)(2,1)S(1)}, u32[]{:S(2)}, u32[]{:S(2)}) collective-permute-start(bf16[128,1024]{1,0:T(8,128)(2,1)S(1)} %get-tuple-element.73), channel_id=1, source_target_pairs={{0,1},{1,0},{2,3},{3,2},{4,5},{5,4},{6,7},{7,6},{8,9},{9,8},{10,11... | collective-permute-start | bytes 786440 | tf_op jit(solution)/shard_map/ppermute | solution.py:217
  28.9 17.3 %collective-permute-start.15 = (bf16[128,1024]{1,0:T(8,128)(2,1)S(1)}, bf16[128,1024]{1,0:T(8,128)(2,1)S(1)}, u32[]{:S(2)}, u32[]{:S(2)}) collective-permute-start(bf16[128,1024]{1,0:T(8,128)(2,1)S(1)} %sink.5.refs_5_.refs_1_), channel_id=1, source_target_pairs={{4,2},{5,3},{6,4},{7,5},{12,10},{13,11},{14,12},{15,13},{20,18},{2... | collective-permute-start | bytes 786440 | tf_op jit(solution)/shard_map/ppermute | solution.py:217
  29.6 18.0 %collective-permute-start.20 = (f32[2,256]{1,0:T(2,128)S(1)}, f32[2,256]{1,0:T(2,128)S(1)}, u32[]{:S(2)}, u32[]{:S(2)}) collective-permute-start(f32[2,256]{1,0:T(2,128)S(1)} %add.7.refs_0_), channel_id=1, source_target_pairs={{0,2},{1,3},{2,0},{3,1},{4,6},{5,7},{6,4},{7,5},{8,10},{9,11},{10,... | collective-permute-start | bytes 6152 | tf_op jit(solution)/shard_map/ppermute | solution.py:217
  38.4 10.2 %collective-permute-start.21 = (f32[2,256]{1,0:T(2,128)S(1)}, f32[2,256]{1,0:T(2,128)S(1)}, u32[]{:S(2)}, u32[]{:S(2)}) collective-permute-start(f32[2,256]{1,0:T(2,128)S(1)} %add.7.refs_0_), channel_id=1, source_target_pairs={{0,4},{1,5},{2,6},{3,7},{4,0},{5,1},{6,2},{7,3},{8,12},{9,13},{10,... | collective-permute-start | bytes 6152 | tf_op jit(solution)/shard_map/ppermute | solution.py:217
  43.6 6.4 %collective-permute-start.22 = (f32[2,256]{1,0:T(2,128)S(1)}, f32[2,256]{1,0:T(2,128)S(1)}, u32[]{:S(2)}, u32[]{:S(2)}) collective-permute-start(f32[2,256]{1,0:T(2,128)S(1)} %add.7.refs_0_), channel_id=1, source_target_pairs={{0,6},{1,7},{2,4},{3,5},{4,2},{5,3},{6,0},{7,1},{8,14},{9,15},{10,... | collective-permute-start | bytes 6152 | tf_op jit(solution)/shard_map/ppermute | solution.py:217
  44.9 11.1 %collective-permute-start.25 = (bf16[128,1024]{1,0:T(8,128)(2,1)S(1)}, bf16[128,1024]{1,0:T(8,128)(2,1)S(1)}, u32[]{:S(2)}, u32[]{:S(2)}) collective-permute-start(bf16[128,1024]{1,0:T(8,128)(2,1)S(1)} %sink.6.refs_5_), channel_id=1, source_target_pairs={{2,0},{3,1},{4,2},{5,3},{6,4},{7,5},{10,8},{11,9},{12,10},{13,11},... | collective-permute-start | bytes 786440 | tf_op jit(solution)/shard_map/ppermute | solution.py:217
  46.3 13.5 %collective-permute-start.19 = (bf16[128,1024]{1,0:T(8,128)(2,1)S(1)}, bf16[128,1024]{1,0:T(8,128)(2,1)S(1)}, u32[]{:S(2)}, u32[]{:S(2)}) collective-permute-start(bf16[128,1024]{1,0:T(8,128)(2,1)S(1)} %sink.7.refs_4_), channel_id=1, source_target_pairs={{2,0},{3,1},{4,2},{5,3},{6,4},{7,5},{10,8},{11,9},{12,10},{13,11},... | collective-permute-start | bytes 786440 | tf_op jit(solution)/shard_map/ppermute | solution.py:217
  50.0 3.6 %collective-permute-start.23 = (f32[2,256]{1,0:T(2,128)S(1)}, f32[2,256]{1,0:T(2,128)S(1)}, u32[]{:S(2)}, u32[]{:S(2)}) collective-permute-start(f32[2,256]{1,0:T(2,128)S(1)} %add.8.refs_0_), channel_id=1, source_target_pairs={{0,8},{8,0},{16,24},{24,16},{1,9},{9,1},{17,25},{25,17},{2,10},{10... | collective-permute-start | bytes 6152 | tf_op jit(solution)/shard_map/ppermute | solution.py:217
  53.6 3.6 %collective-permute-start.24 = (f32[2,256]{1,0:T(2,128)S(1)}, f32[2,256]{1,0:T(2,128)S(1)}, u32[]{:S(2)}, u32[]{:S(2)}) collective-permute-start(f32[2,256]{1,0:T(2,128)S(1)} %add.9.refs_5_), channel_id=1, source_target_pairs={{0,16},{8,24},{16,0},{24,8},{1,17},{9,25},{17,1},{25,9},{2,18},{10... | collective-permute-start | bytes 6152 | tf_op jit(solution)/shard_map/ppermute | solution.py:217

commit v17 on v14

--- a/solution.py
+++ b/solution.py
@@ -110,7 +110,7 @@
     live = jnp.concatenate([live] * GROUPS, 0)
 
     def band_of(index):
-        third = (across_k, 0) if index < count else (across_v, -count * HEAD_DIM)
+        third = (across_k, 0) if index < count else (across_v, across_v.shape[1] - 2 * count * HEAD_DIM)
         blocks = ((arrived_far, at_far), third, (arrived_near, at_near), (across_x, at_x), (own, at_own))
         return jnp.concatenate(
             [field[:, at + index * HEAD_DIM : at + (index + 1) * HEAD_DIM] for field, at in blocks], 0
@@ -297,7 +297,7 @@
                 outs[f"rise{step}"] = shape(rows, rise + width[step])
                 exchange("next", step, own, near)
             if step >= LAG:
-                exchange("third", step - LAG, near, far, 2)
+                exchange("third", step - LAG, near, far, 1 if step > LAG else 2)
 
         def body(*refs):
             ref = dict(zip(list(ins) + list(outs), refs))
@@ -318,7 +318,7 @@
                 far[step] = (arrived, ahead)
                 next_behind[step] = (swap(made["next0"]), 0)
             if step >= LAG:
-                third_behind[step - LAG] = [swap(made["third0"]), swap(made["third1"])]
+                third_behind[step - LAG] = [swap(made[key]) for key in ("third0", "third1") if key in made]
         return [next(iter(made.values()))]
 
     parts, sunk = [], {}
@@ -366,7 +366,7 @@
             dict(
                 segments=segments, queries=queries, out_grad=out_grad, own=own[chunk][0],
                 **{f"behind{i}": place[chunk][0] for i, place in enumerate(held[1:])},
-                third_k=third_behind[chunk][0], third_v=third_behind[chunk][1], gain_q=gain_q, gain_k=gain_k,
+                third_k=third_behind[chunk][0], third_v=third_behind[chunk][-1], gain_q=gain_q, gain_k=gain_k,
             ),
             dict(
                 attended=wide, query_grad=wide, own=whole, near=whole, far=whole,

time: 60 us -> 61.2 us (1.020)
  waiting for transfers between devices: 15.4 us -> 16.1 us
    ppermute x26 -> x25, waiting for transfers between devices: 15.4 us -> 16.1 us  [move(): lax.ppermute(field, axis, [(i, target(i)) for i in range(size) if 0 <= ta...]
    ppermute x26 -> x25, starting transfers between devices: 34.1 us -> 34.6 us  [move(): lax.ppermute(field, axis, [(i, target(i)) for i in range(size) if 0 <= ta...]
  transfers between devices with their start and end apart: 26 -> 25, of which waited for: 11 -> 12; matrix products, arithmetic and copies ran while one was open for 0% -> 0% of each run, Pallas kernels for 12% -> 12%
where the time goes in v17:
time: 61.2 us; the launch traced here: 60.7 us
  starting transfers between devices  34.6 us (57%)
  waiting for transfers between devices  16.1 us (26%)
  Pallas kernels  9.13 us (15%)
  between operations  0.88 us (1%)
    ppermute x25, starting transfers between devices, move(): lax.ppermute(field, axis, [(i, target(i)) for i in range(size) if 0 <= ta...  34.6 us
    ppermute x25, waiting for transfers between devices, move(): lax.ppermute(field, axis, [(i, target(i)) for i in range(size) if 0 <= ta...  16.1 us
    pallas_call x21, Pallas kernels, call(): pl.pallas_call(kernel, out_shape=list(outs.values()), in_specs=specs, out...  9.13 us
  transfers between devices with their start and end apart: 25, of which 12 were waited for; matrix products, arithmetic and copies ran while one was open for 0% of the time, Pallas kernels for 12%

profile of v17, /device:TPU:0, one launch (start us, length us, event | category | flops | bytes accessed | tf_op | source)
XLA Modules:
  0.0 60.7 jit_solution(3681184819965780983)
XLA Ops:
  0.6 0.9 %payload.2.refs_5_.refs_1_.refs_3_.refs_0_ = bf16[128,1024]{1,0:T(8,128)(2,1)S(1)} custom-call(bf16[1,128,1024]{2,1,0:T(8,128)(2,1)} %refs_0_.3, bf16[1,128,1024]{2,1,0:T(8,128)(2,1)} %refs_1_.5), custom_call_target="tpu_custom_call" | custom-call | bytes 1 | tf_op jit(solution)/shard_map/payload/pallas_call | solution.py:38
  1.6 4.9 %collective-permute-start = (bf16[128,1024]{1,0:T(8,128)(2,1)S(1)}, bf16[128,1024]{1,0:T(8,128)(2,1)S(1)}, u32[]{:S(2)}, u32[]{:S(2)}) collective-permute-start(bf16[128,1024]{1,0:T(8,128)(2,1)S(1)} %payload.2.refs_5_.refs_1_.refs_3_.refs_0_), channel_id=1, source_target_pairs={{0,2},{1,3},{2,4},{3,5},{4,6},{5,7},{8,10},{9,11},{10,12},{11,13},... | collective-permute-start | bytes 786440 | tf_op jit(solution)/shard_map/ppermute | solution.py:217
  6.5 1.0 %payload.3 = (bf16[128,1024]{1,0:T(8,128)(2,1)S(1)}, s32[1,1024]{1,0:T(1,128)S(1)}, f32[1,256]{1,0:T(1,128)S(1)}, f32[1,256]{1,0:T(1,128)S(1)}) custom-call(bf16[1,128,1024]{2,1,0:T(8,128)(2,1)} %refs_0_.3, bf16[1,128,1024]{2,1,0:T(8,128)(2,1)} %refs_1_.5, s32[1,1024]{1,0:T(1,128)} %refs_2_.3, f32[1,256]{1,0:T(1,128)} %bitcast.4, f32[1,256]{1,0:T(1,128)} %bitcast.5, ...), custom_call_target="tpu_custom_call" | custom-call | bytes 1 | tf_op jit(solution)/shard_map/payload/pallas_call | solution.py:38
  7.6 3.5 %collective-permute-start.3 = (bf16[128,1024]{1,0:T(8,128)(2,1)S(1)}, bf16[128,1024]{1,0:T(8,128)(2,1)S(1)}, u32[]{:S(2)}, u32[]{:S(2)}) collective-permute-start(bf16[128,1024]{1,0:T(8,128)(2,1)S(1)} %get-tuple-element.45.refs_1_.refs_3_.refs_0_), channel_id=1, source_target_pairs={{0,2},{1,3},{2,4},{3,5},{4,6},{5,7},{8,10},{9,11},{10,12},{11,13},... | collective-permute-start | bytes 786440 | tf_op jit(solution)/shard_map/ppermute | solution.py:217
  11.1 2.2 %collective-permute-done.refs_0_.refs_5_ = bf16[128,1024]{1,0:T(8,128)(2,1)S(1)} collective-permute-done((bf16[128,1024]{1,0:T(8,128)(2,1)S(1)}, bf16[128,1024]{1,0:T(8,128)(2,1)S(1)}, u32[]{:S(2)}, u32[]{:S(2)}) %collective-permute-start) | collective-permute-done | bytes 262176 | tf_op jit(solution)/shard_map/ppermute | solution.py:217
  13.3 0.7 %collective-permute-start.2 = (bf16[128,1024]{1,0:T(8,128)(2,1)S(1)}, bf16[128,1024]{1,0:T(8,128)(2,1)S(1)}, u32[]{:S(2)}, u32[]{:S(2)}) collective-permute-start(bf16[128,1024]{1,0:T(8,128)(2,1)S(1)} %get-tuple-element.44.refs_2_), channel_id=1, source_target_pairs={{2,4},{3,5},{4,6},{5,7},{10,12},{11,13},{12,14},{13,15},{18,20},{1... | collective-permute-start | bytes 786440 | tf_op jit(solution)/shard_map/ppermute | solution.py:217
  14.0 3.7 %collective-permute-done.3.refs_0_.refs_5_ = bf16[128,1024]{1,0:T(8,128)(2,1)S(1)} collective-permute-done((bf16[128,1024]{1,0:T(8,128)(2,1)S(1)}, bf16[128,1024]{1,0:T(8,128)(2,1)S(1)}, u32[]{:S(2)}, u32[]{:S(2)}) %collective-permute-start.3) | collective-permute-done | bytes 262176 | tf_op jit(solution)/shard_map/ppermute | solution.py:217
  17.8 0.8 %collective-permute-start.7 = (bf16[128,1024]{1,0:T(8,128)(2,1)S(1)}, bf16[128,1024]{1,0:T(8,128)(2,1)S(1)}, u32[]{:S(2)}, u32[]{:S(2)}) collective-permute-start(bf16[128,1024]{1,0:T(8,128)(2,1)S(1)} %get-tuple-element.46.refs_2_), channel_id=1, source_target_pairs={{2,4},{3,5},{4,6},{5,7},{10,12},{11,13},{12,14},{13,15},{18,20},{1... | collective-permute-start | bytes 786440 | tf_op jit(solution)/shard_map/ppermute | solution.py:217
  18.7 0.5 collective-permute-start.5
  19.3 0.8 %collective-permute-done.4.refs_7_ = bf16[128,512]{1,0:T(8,128)(2,1)S(1)} collective-permute-done((bf16[128,512]{1,0:T(8,128)(2,1)S(1)}, bf16[128,512]{1,0:T(8,128)(2,1)S(1)}, u32[]{:S(2)}, u32[]{:S(2)}) %collective-permute-start.4) | collective-permute-done | bytes 131104 | tf_op jit(solution)/shard_map/ppermute | solution.py:217
  20.2 1.9 %attend.2 = (bf16[128,1024]{1,0:T(8,128)(2,1)S(1)}, bf16[128,1024]{1,0:T(8,128)(2,1)S(1)}, f32[128,1024]{1,0:T(8,128)S(1)}, f32[128,1024]{1,0:T(8,128)S(1)}, f32...) custom-call(s32[1,1024]{1,0:T(1,128)S(1)} %get-tuple-element.42.refs, ...), custom_call_target="tpu_custom_call" | custom-call | bytes 1 | tf_op jit(solution)/shard_map/attend/pallas_call | solution.py:38
  22.2 0.4 collective-permute-start.8
  23.3 0.7 %collective-permute-done.10.refs_2_.refs_3_ = bf16[128,512]{1,0:T(8,128)(2,1)S(1)} collective-permute-done((bf16[128,512]{1,0:T(8,128)(2,1)S(1)}, bf16[128,512]{1,0:T(8,128)(2,1)S(1)}, u32[]{:S(2)}, u32[]{:S(2)}) %collective-permute-start.10) | collective-permute-done | bytes 131104 | tf_op jit(solution)/shard_map/ppermute | solution.py:217
  24.2 0.7 %collective-permute-start.16 = (bf16[128,1024]{1,0:T(8,128)(2,1)S(1)}, bf16[128,1024]{1,0:T(8,128)(2,1)S(1)}, u32[]{:S(2)}, u32[]{:S(2)}) collective-permute-start(bf16[128,1024]{1,0:T(8,128)(2,1)S(1)} %sink.4.refs_11_.refs_3_), channel_id=1, source_target_pairs={{4,2},{5,3},{6,4},{7,5},{12,10},{13,11},{14,12},{15,13},{20,18},{2... | collective-permute-start | bytes 786440 | tf_op jit(solution)/shard_map/ppermute | solution.py:217
  24.9 1.9 %attend.3 = (bf16[128,1024]{1,0:T(8,128)(2,1)S(1)}, bf16[128,1024]{1,0:T(8,128)(2,1)S(1)}, f32[128,1024]{1,0:T(8,128)S(1)}, f32[128,1024]{1,0:T(8,128)S(1)}, f32...) custom-call(s32[1,1024]{1,0:T(1,128)S(1)} %get-tuple-element.42.refs, ...), custom_call_target="tpu_custom_call" | custom-call | bytes 1 | tf_op jit(solution)/shard_map/attend/pallas_call | solution.py:38
  26.8 0.4 collective-permute-start.11
  27.7 0.8 %collective-permute-done.13.refs_1_ = f32[2,256]{1,0:T(2,128)S(1)} collective-permute-done((f32[2,256]{1,0:T(2,128)S(1)}, f32[2,256]{1,0:T(2,128)S(1)}, u32[]{:S(2)}, u32[]{:S(2)}) %collective-permute-start.13) | collective-permute-done | bytes 2080 | tf_op jit(solution)/shard_map/ppermute | solution.py:217
  29.0 0.7 %collective-permute-start.14 = (bf16[128,1024]{1,0:T(8,128)(2,1)S(1)}, bf16[128,1024]{1,0:T(8,128)(2,1)S(1)}, u32[]{:S(2)}, u32[]{:S(2)}) collective-permute-start(bf16[128,1024]{1,0:T(8,128)(2,1)S(1)} %sink.5.refs_5_.refs_1_), channel_id=1, source_target_pairs={{4,2},{5,3},{6,4},{7,5},{12,10},{13,11},{14,12},{15,13},{20,18},{2... | collective-permute-start | bytes 786440 | tf_op jit(solution)/shard_map/ppermute | solution.py:217
  29.7 9.5 %collective-permute-start.19 = (f32[2,256]{1,0:T(2,128)S(1)}, f32[2,256]{1,0:T(2,128)S(1)}, u32[]{:S(2)}, u32[]{:S(2)}) collective-permute-start(f32[2,256]{1,0:T(2,128)S(1)} %add.7.refs_0_), channel_id=1, source_target_pairs={{0,2},{1,3},{2,0},{3,1},{4,6},{5,7},{6,4},{7,5},{8,10},{9,11},{10,... | collective-permute-start | bytes 6152 | tf_op jit(solution)/shard_map/ppermute | solution.py:217
  39.2 5.2 %collective-permute-start.20 = (f32[2,256]{1,0:T(2,128)S(1)}, f32[2,256]{1,0:T(2,128)S(1)}, u32[]{:S(2)}, u32[]{:S(2)}) collective-permute-start(f32[2,256]{1,0:T(2,128)S(1)} %add.7.refs_0_), channel_id=1, source_target_pairs={{0,4},{1,5},{2,6},{3,7},{4,0},{5,1},{6,2},{7,3},{8,12},{9,13},{10,... | collective-permute-start | bytes 6152 | tf_op jit(solution)/shard_map/ppermute | solution.py:217
  44.5 1.3 %collective-permute-start.24 = (bf16[128,1024]{1,0:T(8,128)(2,1)S(1)}, bf16[128,1024]{1,0:T(8,128)(2,1)S(1)}, u32[]{:S(2)}, u32[]{:S(2)}) collective-permute-start(bf16[128,1024]{1,0:T(8,128)(2,1)S(1)} %sink.6.refs_5_), channel_id=1, source_target_pairs={{2,0},{3,1},{4,2},{5,3},{6,4},{7,5},{10,8},{11,9},{12,10},{13,11},... | collective-permute-start | bytes 786440 | tf_op jit(solution)/shard_map/ppermute | solution.py:217
  45.9 1.3 %collective-permute-start.18 = (bf16[128,1024]{1,0:T(8,128)(2,1)S(1)}, bf16[128,1024]{1,0:T(8,128)(2,1)S(1)}, u32[]{:S(2)}, u32[]{:S(2)}) collective-permute-start(bf16[128,1024]{1,0:T(8,128)(2,1)S(1)} %sink.7.refs_4_), channel_id=1, source_target_pairs={{2,0},{3,1},{4,2},{5,3},{6,4},{7,5},{10,8},{11,9},{12,10},{13,11},... | collective-permute-start | bytes 786440 | tf_op jit(solution)/shard_map/ppermute | solution.py:217
  47.3 2.1 %collective-permute-done.20.refs_2_ = f32[2,256]{1,0:T(2,128)S(1)} collective-permute-done((f32[2,256]{1,0:T(2,128)S(1)}, f32[2,256]{1,0:T(2,128)S(1)}, u32[]{:S(2)}, u32[]{:S(2)}) %collective-permute-start.20) | collective-permute-done | bytes 2080 | tf_op jit(solution)/shard_map/ppermute | solution.py:217
  49.4 1.6 %collective-permute-done.21.refs_3_ = f32[2,256]{1,0:T(2,128)S(1)} collective-permute-done((f32[2,256]{1,0:T(2,128)S(1)}, f32[2,256]{1,0:T(2,128)S(1)}, u32[]{:S(2)}, u32[]{:S(2)}) %collective-permute-start.21) | collective-permute-done | bytes 2080 | tf_op jit(solution)/shard_map/ppermute | solution.py:217
  51.0 1.5 %collective-permute-start.22 = (f32[2,256]{1,0:T(2,128)S(1)}, f32[2,256]{1,0:T(2,128)S(1)}, u32[]{:S(2)}, u32[]{:S(2)}) collective-permute-start(f32[2,256]{1,0:T(2,128)S(1)} %add.8.refs_0_), channel_id=1, source_target_pairs={{0,8},{8,0},{16,24},{24,16},{1,9},{9,1},{17,25},{25,17},{2,10},{10... | collective-permute-start | bytes 6152 | tf_op jit(solution)/shard_map/ppermute | solution.py:217
  52.5 1.0 %assemble.1 = (bf16[1,128,2048]{2,1,0:T(8,128)(2,1)}, bf16[1,128,2048]{2,1,0:T(8,128)(2,1)}) custom-call(bf16[128,1024]{1,0:T(8,128)(2,1)S(1)} %get-tuple-element.51.refs_0_, bf16[128,1024]{1,0:T(8,128)(2,1)S(1)} %get-tuple-element.57.refs_1_, bf16[128,1024]{1,0:T(8,128)(2,1)S(1)} %get-tuple-element.58.refs_2_, ...), custom_call_target="tpu_custom_call" | custom-call | bytes 1 | tf_op jit(solution)/shard_map/assemble/pallas_call | solution.py:38
  53.5 1.1 %collective-permute-done.22.refs_1_ = f32[2,256]{1,0:T(2,128)S(1)} collective-permute-done((f32[2,256]{1,0:T(2,128)S(1)}, f32[2,256]{1,0:T(2,128)S(1)}, u32[]{:S(2)}, u32[]{:S(2)}) %collective-permute-start.22) | collective-permute-done | bytes 2080 | tf_op jit(solution)/shard_map/ppermute | solution.py:217
  54.5 1.5 %collective-permute-start.23 = (f32[2,256]{1,0:T(2,128)S(1)}, f32[2,256]{1,0:T(2,128)S(1)}, u32[]{:S(2)}, u32[]{:S(2)}) collective-permute-start(f32[2,256]{1,0:T(2,128)S(1)} %add.9.refs_5_), channel_id=1, source_target_pairs={{0,16},{8,24},{16,0},{24,8},{1,17},{9,25},{17,1},{25,9},{2,18},{10... | collective-permute-start | bytes 6152 | tf_op jit(solution)/shard_map/ppermute | solution.py:217
  56.1 0.9 %finish.2 = (bf16[1,128,1024]{2,1,0:T(8,128)(2,1)}, bf16[1,128,1024]{2,1,0:T(8,128)(2,1)}) custom-call(bf16[128,1024]{1,0:T(8,128)(2,1)S(1)} %payload.2.refs_5_.refs_1_.refs_3_.refs_0_, f32[1,256]{1,0:T(1,128)S(1)} %get-tuple-element.50.refs_10_.refs_1_, f32[128,1024]{1,0:T(8,128)S(1)} %get-tuple-element.71.refs_2_, ...), custom_call_target="tpu_custom_call" | custom-call | flops 2147483648 | bytes 1 | tf_op jit(solution)/shard_map/finish/pallas_call | solution.py:38
  57.0 1.1 %collective-permute-done.23.refs_6_ = f32[2,256]{1,0:T(2,128)S(1)} collective-permute-done((f32[2,256]{1,0:T(2,128)S(1)}, f32[2,256]{1,0:T(2,128)S(1)}, u32[]{:S(2)}, u32[]{:S(2)}) %collective-permute-start.23) | collective-permute-done | bytes 2080 | tf_op jit(solution)/shard_map/ppermute | solution.py:217
  58.1 1.7 %collective-permute-done.18.refs_4_ = bf16[128,1024]{1,0:T(8,128)(2,1)S(1)} collective-permute-done((bf16[128,1024]{1,0:T(8,128)(2,1)S(1)}, bf16[128,1024]{1,0:T(8,128)(2,1)S(1)}, u32[]{:S(2)}, u32[]{:S(2)}) %collective-permute-start.18) | collective-permute-done | bytes 262176 | tf_op jit(solution)/shard_map/ppermute | solution.py:217
  59.8 0.9 %finish.3 = (bf16[1,128,1024]{2,1,0:T(8,128)(2,1)}, bf16[1,128,1024]{2,1,0:T(8,128)(2,1)}, f32[1,256]{1,0:T(1,128)}, f32[1,256]{1,0:T(1,128)}) custom-call(bf16[128,1024]{1,0:T(8,128)(2,1)S(1)} %get-tuple-element.45.refs_1_.refs_3_.refs_0_, f32[1,256]{1,0:T(1,128)S(1)} %get-tuple-element.50.refs_10_.refs_1_, ...), custom_call_target="tpu_custom_call", output_to_operand_aliasing={{0}: (7, {}), {1}: (8, {})} | custom-call | flops 4294967296 | bytes 1 | tf_op jit(solution)/shard_map/finish/pallas_call | solution.py:38
  (43 shorter events, 2.7 us)
Async XLA Ops:
  1.6 11.6 %collective-permute-start = (bf16[128,1024]{1,0:T(8,128)(2,1)S(1)}, bf16[128,1024]{1,0:T(8,128)(2,1)S(1)}, u32[]{:S(2)}, u32[]{:S(2)}) collective-permute-start(bf16[128,1024]{1,0:T(8,128)(2,1)S(1)} %payload.2.refs_5_.refs_1_.refs_3_.refs_0_), channel_id=1, source_target_pairs={{0,2},{1,3},{2,4},{3,5},{4,6},{5,7},{8,10},{9,11},{10,12},{11,13},... | collective-permute-start | bytes 786440 | tf_op jit(solution)/shard_map/ppermute | solution.py:217
  7.6 10.1 %collective-permute-start.3 = (bf16[128,1024]{1,0:T(8,128)(2,1)S(1)}, bf16[128,1024]{1,0:T(8,128)(2,1)S(1)}, u32[]{:S(2)}, u32[]{:S(2)}) collective-permute-start(bf16[128,1024]{1,0:T(8,128)(2,1)S(1)} %get-tuple-element.45.refs_1_.refs_3_.refs_0_), channel_id=1, source_target_pairs={{0,2},{1,3},{2,4},{3,5},{4,6},{5,7},{8,10},{9,11},{10,12},{11,13},... | collective-permute-start | bytes 786440 | tf_op jit(solution)/shard_map/ppermute | solution.py:217
  13.3 5.3 %collective-permute-start.2 = (bf16[128,1024]{1,0:T(8,128)(2,1)S(1)}, bf16[128,1024]{1,0:T(8,128)(2,1)S(1)}, u32[]{:S(2)}, u32[]{:S(2)}) collective-permute-start(bf16[128,1024]{1,0:T(8,128)(2,1)S(1)} %get-tuple-element.44.refs_2_), channel_id=1, source_target_pairs={{2,4},{3,5},{4,6},{5,7},{10,12},{11,13},{12,14},{13,15},{18,20},{1... | collective-permute-start | bytes 786440 | tf_op jit(solution)/shard_map/ppermute | solution.py:217
  13.9 5.3 %collective-permute-start.1 = (bf16[128,1024]{1,0:T(8,128)(2,1)S(1)}, bf16[128,1024]{1,0:T(8,128)(2,1)S(1)}, u32[]{:S(2)}, u32[]{:S(2)}) collective-permute-start(bf16[128,1024]{1,0:T(8,128)(2,1)S(1)} %get-tuple-element.43), channel_id=1, source_target_pairs={{0,1},{1,0},{2,3},{3,2},{4,5},{5,4},{6,7},{7,6},{8,9},{9,8},{10,11... | collective-permute-start | bytes 786440 | tf_op jit(solution)/shard_map/ppermute | solution.py:217
  17.7 2.5 %copy-start = (bf16[1,128,2048]{2,1,0:T(8,128)(2,1)S(1)}, bf16[1,128,2048]{2,1,0:T(8,128)(2,1)}, u32[]{:S(2)}) copy-start(bf16[1,128,2048]{2,1,0:T(8,128)(2,1)} %refs_1_.7) | copy-start | bytes 1572868
  17.7 2.5 %copy-start.1 = (bf16[1,128,2048]{2,1,0:T(8,128)(2,1)S(1)}, bf16[1,128,2048]{2,1,0:T(8,128)(2,1)}, u32[]{:S(2)}) copy-start(bf16[1,128,2048]{2,1,0:T(8,128)(2,1)} %refs_2_.5) | copy-start | bytes 1572868
  17.8 4.4 %collective-permute-start.7 = (bf16[128,1024]{1,0:T(8,128)(2,1)S(1)}, bf16[128,1024]{1,0:T(8,128)(2,1)S(1)}, u32[]{:S(2)}, u32[]{:S(2)}) collective-permute-start(bf16[128,1024]{1,0:T(8,128)(2,1)S(1)} %get-tuple-element.46.refs_2_), channel_id=1, source_target_pairs={{2,4},{3,5},{4,6},{5,7},{10,12},{11,13},{12,14},{13,15},{18,20},{1... | collective-permute-start | bytes 786440 | tf_op jit(solution)/shard_map/ppermute | solution.py:217
  18.6 1.4 %collective-permute-start.4 = (bf16[128,512]{1,0:T(8,128)(2,1)S(1)}, bf16[128,512]{1,0:T(8,128)(2,1)S(1)}, u32[]{:S(2)}, u32[]{:S(2)}) collective-permute-start(bf16[128,512]{1,0:T(8,128)(2,1)S(1)} %get-tuple-element.47.refs_2_), channel_id=1, source_target_pairs={{0,1},{1,0},{2,3},{3,2},{4,5},{5,4},{6,7},{7,6},{8,9},{9,8},{10,11... | collective-permute-start | bytes 393224 | tf_op jit(solution)/shard_map/ppermute | solution.py:217
  18.7 1.5 %collective-permute-start.5 = (bf16[128,512]{1,0:T(8,128)(2,1)S(1)}, bf16[128,512]{1,0:T(8,128)(2,1)S(1)}, u32[]{:S(2)}, u32[]{:S(2)}) collective-permute-start(bf16[128,512]{1,0:T(8,128)(2,1)S(1)} %get-tuple-element.48), channel_id=1, source_target_pairs={{0,1},{1,0},{2,3},{3,2},{4,5},{5,4},{6,7},{7,6},{8,9},{9,8},{10,11... | collective-permute-start | bytes 393224 | tf_op jit(solution)/shard_map/ppermute | solution.py:217
  19.2 5.7 %collective-permute-start.6 = (bf16[128,1024]{1,0:T(8,128)(2,1)S(1)}, bf16[128,1024]{1,0:T(8,128)(2,1)S(1)}, u32[]{:S(2)}, u32[]{:S(2)}) collective-permute-start(bf16[128,1024]{1,0:T(8,128)(2,1)S(1)} %get-tuple-element.52), channel_id=1, source_target_pairs={{0,1},{1,0},{2,3},{3,2},{4,5},{5,4},{6,7},{7,6},{8,9},{9,8},{10,11... | collective-permute-start | bytes 786440 | tf_op jit(solution)/shard_map/ppermute | solution.py:217
  22.2 2.7 %collective-permute-start.8 = (bf16[128,1024]{1,0:T(8,128)(2,1)S(1)}, bf16[128,1024]{1,0:T(8,128)(2,1)S(1)}, u32[]{:S(2)}, u32[]{:S(2)}) collective-permute-start(bf16[128,1024]{1,0:T(8,128)(2,1)S(1)} %climb.7), channel_id=1, source_target_pairs={{0,1},{1,0},{2,3},{3,2},{4,5},{5,4},{6,7},{7,6},{8,9},{9,8},{10,11... | collective-permute-start | bytes 786440 | tf_op jit(solution)/shard_map/ppermute | solution.py:217
  22.6 1.4 %collective-permute-start.10 = (bf16[128,512]{1,0:T(8,128)(2,1)S(1)}, bf16[128,512]{1,0:T(8,128)(2,1)S(1)}, u32[]{:S(2)}, u32[]{:S(2)}) collective-permute-start(bf16[128,512]{1,0:T(8,128)(2,1)S(1)} %get-tuple-element.56), channel_id=1, source_target_pairs={{0,1},{1,0},{2,3},{3,2},{4,5},{5,4},{6,7},{7,6},{8,9},{9,8},{10,11... | collective-permute-start | bytes 393224 | tf_op jit(solution)/shard_map/ppermute | solution.py:217
  22.7 1.4 %collective-permute-start.9 = (bf16[128,512]{1,0:T(8,128)(2,1)S(1)}, bf16[128,512]{1,0:T(8,128)(2,1)S(1)}, u32[]{:S(2)}, u32[]{:S(2)}) collective-permute-start(bf16[128,512]{1,0:T(8,128)(2,1)S(1)} %get-tuple-element.55), channel_id=1, source_target_pairs={{0,1},{1,0},{2,3},{3,2},{4,5},{5,4},{6,7},{7,6},{8,9},{9,8},{10,11... | collective-permute-start | bytes 393224 | tf_op jit(solution)/shard_map/ppermute | solution.py:217
  23.1 16.1 %collective-permute-start.17 = (bf16[128,1024]{1,0:T(8,128)(2,1)S(1)}, bf16[128,1024]{1,0:T(8,128)(2,1)S(1)}, u32[]{:S(2)}, u32[]{:S(2)}) collective-permute-start(bf16[128,1024]{1,0:T(8,128)(2,1)S(1)} %get-tuple-element.67), channel_id=1, source_target_pairs={{0,1},{1,0},{2,3},{3,2},{4,5},{5,4},{6,7},{7,6},{8,9},{9,8},{10,11... | collective-permute-start | bytes 786440 | tf_op jit(solution)/shard_map/ppermute | solution.py:217
  24.2 20.2 %collective-permute-start.16 = (bf16[128,1024]{1,0:T(8,128)(2,1)S(1)}, bf16[128,1024]{1,0:T(8,128)(2,1)S(1)}, u32[]{:S(2)}, u32[]{:S(2)}) collective-permute-start(bf16[128,1024]{1,0:T(8,128)(2,1)S(1)} %sink.4.refs_11_.refs_3_), channel_id=1, source_target_pairs={{4,2},{5,3},{6,4},{7,5},{12,10},{13,11},{14,12},{15,13},{20,18},{2... | collective-permute-start | bytes 786440 | tf_op jit(solution)/shard_map/ppermute | solution.py:217
  26.8 2.1 %collective-permute-start.11 = (bf16[128,512]{1,0:T(8,128)(2,1)S(1)}, bf16[128,512]{1,0:T(8,128)(2,1)S(1)}, u32[]{:S(2)}, u32[]{:S(2)}) collective-permute-start(bf16[128,512]{1,0:T(8,128)(2,1)S(1)} %get-tuple-element.62), channel_id=1, source_target_pairs={{0,1},{1,0},{2,3},{3,2},{4,5},{5,4},{6,7},{7,6},{8,9},{9,8},{10,11... | collective-permute-start | bytes 393224 | tf_op jit(solution)/shard_map/ppermute | solution.py:217
  27.2 1.7 %collective-permute-start.12 = (bf16[128,512]{1,0:T(8,128)(2,1)S(1)}, bf16[128,512]{1,0:T(8,128)(2,1)S(1)}, u32[]{:S(2)}, u32[]{:S(2)}) collective-permute-start(bf16[128,512]{1,0:T(8,128)(2,1)S(1)} %get-tuple-element.63), channel_id=1, source_target_pairs={{0,1},{1,0},{2,3},{3,2},{4,5},{5,4},{6,7},{7,6},{8,9},{9,8},{10,11... | collective-permute-start | bytes 393224 | tf_op jit(solution)/shard_map/ppermute | solution.py:217
  27.4 1.2 %collective-permute-start.13 = (f32[2,256]{1,0:T(2,128)S(1)}, f32[2,256]{1,0:T(2,128)S(1)}, u32[]{:S(2)}, u32[]{:S(2)}) collective-permute-start(f32[2,256]{1,0:T(2,128)S(1)} %add.5.refs_0_), channel_id=1, source_target_pairs={{0,1},{1,0},{2,3},{3,2},{4,5},{5,4},{6,7},{7,6},{8,9},{9,8},{10,11... | collective-permute-start | bytes 6152 | tf_op jit(solution)/shard_map/ppermute | solution.py:217
  28.5 16.0 %collective-permute-start.15 = (bf16[128,1024]{1,0:T(8,128)(2,1)S(1)}, bf16[128,1024]{1,0:T(8,128)(2,1)S(1)}, u32[]{:S(2)}, u32[]{:S(2)}) collective-permute-start(bf16[128,1024]{1,0:T(8,128)(2,1)S(1)} %get-tuple-element.65), channel_id=1, source_target_pairs={{0,1},{1,0},{2,3},{3,2},{4,5},{5,4},{6,7},{7,6},{8,9},{9,8},{10,11... | collective-permute-start | bytes 786440 | tf_op jit(solution)/shard_map/ppermute | solution.py:217
  29.0 16.9 %collective-permute-start.14 = (bf16[128,1024]{1,0:T(8,128)(2,1)S(1)}, bf16[128,1024]{1,0:T(8,128)(2,1)S(1)}, u32[]{:S(2)}, u32[]{:S(2)}) collective-permute-start(bf16[128,1024]{1,0:T(8,128)(2,1)S(1)} %sink.5.refs_5_.refs_1_), channel_id=1, source_target_pairs={{4,2},{5,3},{6,4},{7,5},{12,10},{13,11},{14,12},{15,13},{20,18},{2... | collective-permute-start | bytes 786440 | tf_op jit(solution)/shard_map/ppermute | solution.py:217
  29.7 17.6 %collective-permute-start.19 = (f32[2,256]{1,0:T(2,128)S(1)}, f32[2,256]{1,0:T(2,128)S(1)}, u32[]{:S(2)}, u32[]{:S(2)}) collective-permute-start(f32[2,256]{1,0:T(2,128)S(1)} %add.7.refs_0_), channel_id=1, source_target_pairs={{0,2},{1,3},{2,0},{3,1},{4,6},{5,7},{6,4},{7,5},{8,10},{9,11},{10,... | collective-permute-start | bytes 6152 | tf_op jit(solution)/shard_map/ppermute | solution.py:217
  39.2 10.2 %collective-permute-start.20 = (f32[2,256]{1,0:T(2,128)S(1)}, f32[2,256]{1,0:T(2,128)S(1)}, u32[]{:S(2)}, u32[]{:S(2)}) collective-permute-start(f32[2,256]{1,0:T(2,128)S(1)} %add.7.refs_0_), channel_id=1, source_target_pairs={{0,4},{1,5},{2,6},{3,7},{4,0},{5,1},{6,2},{7,3},{8,12},{9,13},{10,... | collective-permute-start | bytes 6152 | tf_op jit(solution)/shard_map/ppermute | solution.py:217
  44.4 6.6 %collective-permute-start.21 = (f32[2,256]{1,0:T(2,128)S(1)}, f32[2,256]{1,0:T(2,128)S(1)}, u32[]{:S(2)}, u32[]{:S(2)}) collective-permute-start(f32[2,256]{1,0:T(2,128)S(1)} %add.7.refs_0_), channel_id=1, source_target_pairs={{0,6},{1,7},{2,4},{3,5},{4,2},{5,3},{6,0},{7,1},{8,14},{9,15},{10,... | collective-permute-start | bytes 6152 | tf_op jit(solution)/shard_map/ppermute | solution.py:217
  44.5 11.5 %collective-permute-start.24 = (bf16[128,1024]{1,0:T(8,128)(2,1)S(1)}, bf16[128,1024]{1,0:T(8,128)(2,1)S(1)}, u32[]{:S(2)}, u32[]{:S(2)}) collective-permute-start(bf16[128,1024]{1,0:T(8,128)(2,1)S(1)} %sink.6.refs_5_), channel_id=1, source_target_pairs={{2,0},{3,1},{4,2},{5,3},{6,4},{7,5},{10,8},{11,9},{12,10},{13,11},... | collective-permute-start | bytes 786440 | tf_op jit(solution)/shard_map/ppermute | solution.py:217
  45.9 13.9 %collective-permute-start.18 = (bf16[128,1024]{1,0:T(8,128)(2,1)S(1)}, bf16[128,1024]{1,0:T(8,128)(2,1)S(1)}, u32[]{:S(2)}, u32[]{:S(2)}) collective-permute-start(bf16[128,1024]{1,0:T(8,128)(2,1)S(1)} %sink.7.refs_4_), channel_id=1, source_target_pairs={{2,0},{3,1},{4,2},{5,3},{6,4},{7,5},{10,8},{11,9},{12,10},{13,11},... | collective-permute-start | bytes 786440 | tf_op jit(solution)/shard_map/ppermute | solution.py:217
  51.0 3.6 %collective-permute-start.22 = (f32[2,256]{1,0:T(2,128)S(1)}, f32[2,256]{1,0:T(2,128)S(1)}, u32[]{:S(2)}, u32[]{:S(2)}) collective-permute-start(f32[2,256]{1,0:T(2,128)S(1)} %add.8.refs_0_), channel_id=1, source_target_pairs={{0,8},{8,0},{16,24},{24,16},{1,9},{9,1},{17,25},{25,17},{2,10},{10... | collective-permute-start | bytes 6152 | tf_op jit(solution)/shard_map/ppermute | solution.py:217
  54.5 3.6 %collective-permute-start.23 = (f32[2,256]{1,0:T(2,128)S(1)}, f32[2,256]{1,0:T(2,128)S(1)}, u32[]{:S(2)}, u32[]{:S(2)}) collective-permute-start(f32[2,256]{1,0:T(2,128)S(1)} %add.9.refs_5_), channel_id=1, source_target_pairs={{0,16},{8,24},{16,0},{24,8},{1,17},{9,25},{17,1},{25,9},{2,18},{10... | collective-permute-start | bytes 6152 | tf_op jit(solution)/shard_map/ppermute | solution.py:217
